TPU v7x, 256 devices: a whole 4x4x8 slice. The times are simulated.
256 devices in a mesh: dp: 16 (over z, core), expert: 16 (over y, x).
Axes of the slice: x: 4, y: 4, z: 8, core: 2. Of those that a mesh axis runs over, the one named last changes fastest.
Arguments:
- tokens: bfloat16 [32768, 1024], P(('dp', 'expert')), may hold values from -6 to 6
- tangent: bfloat16 [32768, 1024], P(('dp', 'expert')), may hold values from -6 to 6
- cotangent: bfloat16 [32768, 1024], P(('dp', 'expert')), may hold values from -6 to 6
- routes: int32 [32768, 2], P(('dp', 'expert')), may hold values from 0 to 15, all different within a row; in each aligned block of 128 rows (0 to 127, 128 to 255, ...) at most 24 rows name the same one
- gate_num: int32 [32768, 2], P(('dp', 'expert')), may hold values from 8 to 56
- w_up: bfloat16 [16, 4096, 1024], P('expert', 'dp'), may hold values from -0.1875 to 0.1875
- w_down: bfloat16 [16, 4096, 1024], P('expert', 'dp'), may hold values from -0.09375 to 0.09375
Outputs:
- hvp: float32 [32768, 1024], P(('dp', 'expert'))
Inputs may be any that keep to these rules, and one draw needn't show every extreme that they name: `routes`: the experts of a token are distinct. Within the 128 rows of one device no expert is named by more than 24 rows, and in some device one expert is named by exactly 24 rows.
All inputs are finite; a program needn't handle non-finite values.
Results may differ from a plain program's by a relative error of at most 0.0029.
Values may be sent and summed in bfloat16 or wider, within the bound.
No kernel may reach another device: no remote copies, remote signals or barrier semaphores. Data moves between devices by JAX's collectives and lax.ppermute only.
A program may use at most 192 MiB of HBM per device.

v0:
```python
import jax
import jax.numpy as jnp
from jax import lax
from jax.sharding import PartitionSpec as P

highest = lax.Precision.HIGHEST
denominator = 64.0


def curvature(before_act):
    sigma = jax.nn.sigmoid(before_act)
    return sigma * (1.0 - sigma) * (2.0 + before_act * (1.0 - 2.0 * sigma))


def expert_piece(rows_in, up_piece, down_piece):
    contract = (((1,), (1,)), ((), ()))
    before_act = lax.dot_general(rows_in[0], up_piece, contract, preferred_element_type=jnp.float32)
    lifted = lax.dot_general(rows_in[1], up_piece, contract, preferred_element_type=jnp.float32)
    pulled = lax.dot_general(rows_in[2], down_piece, contract, preferred_element_type=jnp.float32)
    inner = (pulled * curvature(before_act) * lifted).astype(jnp.bfloat16)
    return jnp.dot(inner, up_piece, preferred_element_type=jnp.float32)


def slot_layout(route_rows, experts, capacity):
    tok_total, top_count = route_rows.shape
    flat_ids = route_rows.reshape(tok_total * top_count)
    onehot = (flat_ids[:, None] == jnp.arange(experts, dtype=jnp.int32)[None, :]).astype(jnp.int32)
    before = jnp.cumsum(onehot, axis=0) - onehot
    position = jnp.sum(before * onehot, axis=1)
    slot_ids = flat_ids * capacity + position
    assign = (slot_ids[:, None] == jnp.arange(experts * capacity, dtype=jnp.int32)[None, :]).astype(
        jnp.int32
    )
    owners = jnp.arange(tok_total * top_count, dtype=jnp.int32) // top_count
    sources = jnp.sum(assign * owners[:, None], axis=0)
    filled = jnp.sum(assign, axis=0)
    return (sources, filled, slot_ids.reshape(tok_total, top_count))


def local(tokens, tangent, cotangent, routes, gate_num, w_up, w_down):
    tok_total = tokens.shape[0]
    experts = lax.axis_size("expert") * w_up.shape[0]
    capacity = max(2, 3 * tok_total // experts)
    sources, filled, slot_ids = slot_layout(routes, experts, capacity)
    stacked = jnp.stack([tokens, tangent, cotangent])
    send_rows = jnp.take(stacked, sources, axis=1) * filled.astype(jnp.bfloat16)[None, :, None]
    arrived = lax.all_to_all(send_rows, "expert", split_axis=1, concat_axis=1, tiled=True)
    up_whole, down_whole = (
        lax.all_gather(w_up[0], "dp", axis=0, tiled=True),
        lax.all_gather(w_down[0], "dp", axis=0, tiled=True),
    )
    own_rows = expert_piece(arrived, up_whole, down_whole)
    returned = lax.all_to_all(own_rows, "expert", split_axis=0, concat_axis=0, tiled=True)
    gates = gate_num.astype(jnp.float32) / denominator
    selector = (
        slot_ids[:, :, None] == jnp.arange(experts * capacity, dtype=jnp.int32)[None, None, :]
    ).astype(jnp.float32)
    mixing = jnp.sum(selector * gates[:, :, None], axis=1)
    return jnp.dot(mixing, returned, precision=highest, preferred_element_type=jnp.float32)


def solution(mesh):
    in_specs = (
        P(("dp", "expert"), None),
        P(("dp", "expert"), None),
        P(("dp", "expert"), None),
        P(("dp", "expert"), None),
        P(("dp", "expert"), None),
        P("expert", "dp", None),
        P("expert", "dp", None),
    )
    out_specs = P(("dp", "expert"), None)
    return jax.shard_map(local, mesh=mesh, in_specs=in_specs, out_specs=out_specs, check_vma=False)
```

profile of v0, /device:TPU:1, one launch (start us, length us, event | category | flops | bytes accessed | tf_op | source)
XLA Modules:
  0.0 183.2 jit_solution(11616003569399993482)
XLA Ops:
  6.5 0.0 all-gather.7.cloned.1.call-start
  6.5 0.7 all-gather.7.cloned.1.call-update
  7.3 0.0 all-gather.5.cloned.1.call-start
  7.3 0.7 all-gather.5.cloned.1.call-update
  8.0 0.8 copy.34
  8.8 0.1 eq.55
  8.9 0.1 eq.51
  9.1 0.6 reduce-window.6
  9.7 0.2 slice_reduce_fusion
  9.9 1.4 copy.38
  11.3 1.4 copy.39
  12.6 1.4 copy.40
  14.0 0.1 fusion.27
  14.1 0.1 convert_reduce_fusion
  14.3 1.8 pad_maximum_fusion
  16.1 15.2 %gather_fusion = bf16[384,3,1024]{2,1,0:T(4,128)(2,1)} fusion(bf16[3,128,1024]{2,0,1:T(4,128)(2,1)S(1)} %pad_maximum_fusion, s32[1024]{0:T(1024)S(1)} %pad_clamp_fusion), kind=kCustom, calls=%fused_computation | custom fusion | bytes 4720128 | tf_op jit(solution)/shard_map/jit(_take)/gather | solution.py:46
  31.3 4.1 %multiply_bitcast_fusion = bf16[3,384,1024]{2,0,1:T(4,128)(2,1)S(1)} fusion(bf16[384,3,1024]{2,1,0:T(4,128)(2,1)} %gather_fusion, pred[384]{0:T(512)(128)(4,1)S(1)} %compare_and_fusion, bf16[384]{0:T(512)(128)(2,1)S(1)} %convert_element_type.28), kind=kLoop, calls=%fused_computation.14 | loop fusion | flops 2359296 | bytes 4719744 | tf_op jit(solution)/shard_map/mul | solution.py:46
  35.5 46.0 %all_to_all.17 = bf16[3,384,1024]{2,0,1:T(4,128)(2,1)S(1)} all-to-all(bf16[3,384,1024]{2,0,1:T(4,128)(2,1)S(1)} %multiply_bitcast_fusion), channel_id=1, replica_groups=mesh['dp'=16,'expert'=16] {'expert'}, dimensions={1} | all-to-all | bytes 4718592 | tf_op jit(solution)/shard_map/all_to_all | solution.py:47
  81.4 4.1 %fusion.32 = (bf16[1,384,1024]{2,0,1:T(2,128)(2,1)S(1)}, bf16[1,384,1024]{2,0,1:T(2,128)(2,1)S(1)}, bf16[1,384,1024]{2,0,1:T(2,128)(2,1)}) fusion(bf16[3,384,1024]{2,0,1:T(4,128)(2,1)S(1)} %all_to_all.17), kind=kLoop, calls=%fused_computation.51 | loop fusion | bytes 4718592 | tf_op jit(solution)/shard_map/slice | solution.py:19
  85.5 0.0 all-gather.7.cloned.1.call-done
  85.5 0.0 copy-start.2
  85.5 10.3 %fusion.4 = f32[384,4096]{1,0:T(8,128)} fusion(bf16[1,4096,1024]{2,1,0:T(8,128)(2,1)} %all-gather.7.cloned.1.call-done, bf16[1,384,1024]{2,0,1:T(2,128)(2,1)} %get-tuple-element.9), kind=kOutput, calls=%fused_computation.6 | convolution fusion | flops 3221225472 | bytes 15466496 | tf_op jit(solution)/shard_map/dot_general | solution.py:17
  95.8 0.0 copy-done.2
  95.8 5.3 %fusion.2 = f32[384,4096]{1,0:T(8,128)} fusion(bf16[1,4096,1024]{2,1,0:T(8,128)(2,1)S(1)} %copy-done.2, bf16[1,384,1024]{2,0,1:T(2,128)(2,1)S(1)} %get-tuple-element.8), kind=kOutput, calls=%fused_computation.4 | convolution fusion | flops 3221225472 | bytes 15466496 | tf_op jit(solution)/shard_map/dot_general | solution.py:18
  101.1 24.5 %all-gather.5.cloned.1.call-done = bf16[1,4096,1024]{2,1,0:T(8,128)(2,1)} async-done(((bf16[1,256,1024]{2,1,0:T(8,128)(2,1)}), bf16[1,4096,1024]{2,1,0:T(8,128)(2,1)}) %all-gather.5.cloned.1.call-update) | async-done | bytes 8388624 | tf_op jit(solution)/shard_map/all_gather | solution.py:50
  125.7 0.0 copy-start.1
  125.7 0.0 copy-start
  125.7 17.7 %fusion = f32[384,1024]{1,0:T(8,128)} fusion(bf16[1,4096,1024]{2,1,0:T(8,128)(2,1)} %all-gather.7.cloned.1.call-done, f32[384,4096]{1,0:T(8,128)} %fusion.2, f32[384,4096]{1,0:T(8,128)} %fusion.4, bf16[1,4096,1024]{2,1,0:T(8,128)(2,1)} %all-gather.5.cloned.1.call-done, bf16[1,384,1024]{2,0,1:T(2,128)(2,1)S(1)} %get-tuple-element.7), kind=kOutput, calls=%fused_computation.2 | convolution fusion | flops 6462898176 | bytes 31719424 | tf_op jit(solution)/shard_map/dot_general | solution.py:21
  143.3 6.5 %all-to-all-start.1 = ((f32[16,24,1024]{2,1,0:T(8,128)}), f32[16,24,1024]{2,1,0:T(8,128)S(1)}, u32[]{:S(2)}, u32[]{:S(2)}) async-start(f32[16,24,1024]{2,1,0:T(8,128)} %bitcast.7), calls=%async_computation.1 | async-start | bytes 3145728 | tf_op jit(solution)/shard_map/all_to_all | solution.py:53
  149.9 0.1 reduce_sum.41
  150.0 0.1 copy.37
  150.1 0.0 copy-done.1
  150.1 0.0 copy-done
  150.1 0.1 select_reduce_fusion.1
  150.3 24.2 %all-to-all-done.1 = f32[16,24,1024]{2,1,0:T(8,128)S(1)} async-done(((f32[16,24,1024]{2,1,0:T(8,128)}), f32[16,24,1024]{2,1,0:T(8,128)S(1)}, u32[]{:S(2)}, u32[]{:S(2)}) %all-to-all-start.1) | async-done | bytes 1572896 | tf_op jit(solution)/shard_map/all_to_all | solution.py:53
  174.5 1.9 %fusion.33 = f32[128,1024]{1,0:T(8,128)} fusion(f32[128,384]{1,0:T(8,128)S(1)} %select_reduce_fusion.1, f32[384,1024]{1,0:T(8,128)S(1)} %bitcast.52), kind=kOutput, calls=%fused_computation.52 | convolution fusion | flops 603979776 | bytes 2293760 | tf_op jit(solution)/shard_map/dot_general | solution.py:59
  (10 shorter events, 0.1 us)
Async XLA Ops:
  6.5 79.0 %all-gather.7.cloned.1.call-start = ((), (), s32[]{:S(2)}) async-start(), calls=%async_computation.3 | async-start | bytes 8912896 | tf_op jit(solution)/shard_map/all_gather | solution.py:49
  7.3 118.4 %all-gather.5.cloned.1.call-start = ((), (), s32[]{:S(2)}) async-start(), calls=%async_computation.2 | async-start | bytes 8912896 | tf_op jit(solution)/shard_map/all_gather | solution.py:50
  85.5 10.3 %copy-start.2 = (bf16[1,4096,1024]{2,1,0:T(8,128)(2,1)S(1)}, bf16[1,4096,1024]{2,1,0:T(8,128)(2,1)}, u32[]{:S(2)}) copy-start(bf16[1,4096,1024]{2,1,0:T(8,128)(2,1)} %all-gather.7.cloned.1.call-done) | copy-start | bytes 25165828
  125.7 24.4 %copy-start.1 = (s32[128,2]{0,1:T(2,128)S(1)}, s32[128,2]{0,1:T(2,128)}, u32[]{:S(2)}) copy-start(s32[128,2]{0,1:T(2,128)} %param.11) | copy-start | bytes 3076
  125.7 24.4 %copy-start = (s32[128,2]{0,1:T(2,128)S(1)}, s32[128,2]{0,1:T(2,128)}, u32[]{:S(2)}) copy-start(s32[128,2]{0,1:T(2,128)} %param.10) | copy-start | bytes 3076
  143.3 31.1 %all-to-all-start.1 = ((f32[16,24,1024]{2,1,0:T(8,128)}), f32[16,24,1024]{2,1,0:T(8,128)S(1)}, u32[]{:S(2)}, u32[]{:S(2)}) async-start(f32[16,24,1024]{2,1,0:T(8,128)} %bitcast.7), calls=%async_computation.1 | async-start | bytes 3145728 | tf_op jit(solution)/shard_map/all_to_all | solution.py:53
Sparse Core Ops, SparseCore 0:
  9.2 60.1 all-gather.6
  71.2 54.4 all-gather.4
where the time goes:
time: 184 us; the launch traced here: 183 us
  waiting for transfers between devices  50.1 us (27%)
  blocking collectives  46 us (25%)
  matrix products  35.2 us (19%)
  local copies, waits for them, and re-layouts  24.8 us (13%)
  between operations  13.5 us (7%)
  other arithmetic  7.02 us (4%)
  starting transfers between devices  6.57 us (4%)
    all_to_all x1, blocking collectives, local(): lax.all_to_all(send_rows, 'expert', split_axis=1, concat_axis=1, tiled=True)  46 us
    all_gather x1, waiting for transfers between devices, local(): lax.all_gather(w_down[0], 'dp', axis=0, tiled=True)  24.5 us
    all_to_all x1, waiting for transfers between devices, local(): lax.all_to_all(own_rows, 'expert', split_axis=0, concat_axis=0, tiled=True)  24.2 us
    dot_general x1, matrix products, expert_piece(): return jnp.dot(inner, up_piece, preferred_element_type=jnp.float32)  17.7 us
    gather x1, local copies, waits for them, and re-layouts, local(): jnp.take(stacked, sources, axis=1)  15.2 us
    dot_general x1, matrix products, expert_piece(): lax.dot_general(rows_in[0], up_piece, contract, preferred_element_type=jn...  10.3 us
    all_to_all x1, starting transfers between devices, local(): lax.all_to_all(own_rows, 'expert', split_axis=0, concat_axis=0, tiled=True)  6.53 us
    dot_general x1, matrix products, expert_piece(): lax.dot_general(rows_in[1], up_piece, contract, preferred_element_type=jn...  5.34 us
  transfers between devices with their start and end apart: 3, of which 2 were waited for; matrix products, arithmetic and copies ran while one was open for 26% of the time, Pallas kernels for 0%

commit v1 on v0

v1 whole, which is shorter than its diff:
```python
import functools

import jax
import jax.numpy as jnp
from jax import lax
from jax.experimental import pallas as pl
from jax.experimental.pallas import tpu as pltpu
from jax.sharding import PartitionSpec as P

f32, bf16 = jnp.float32, jnp.bfloat16
CAP = 24
NT = (((1,), (1,)), ((), ()))
VMEM = pl.BlockSpec(memory_space=pltpu.VMEM)


def params(mib):
    return pltpu.CompilerParams(vmem_limit_bytes=mib << 20)


def curvature(x):
    s = jax.nn.sigmoid(x)
    return s * (1.0 - s) * (2.0 + x * (1.0 - 2.0 * s))


def prepare_kernel(slots, routes_ref, routes_t_ref, gates_ref, x_ref, t_ref, c_ref, send_ref, mix_ref):
    n = x_ref.shape[0]
    width = x_ref.shape[1]
    slot = lax.broadcasted_iota(jnp.int32, (slots, n), 0)
    expert = (slot * 2731) >> 16
    place = slot - expert * CAP
    named = (routes_t_ref[0:1, :] == expert) | (routes_t_ref[1:2, :] == expert)
    earlier = lax.broadcasted_iota(jnp.int32, (n, n), 0) < lax.broadcasted_iota(jnp.int32, (n, n), 1)
    named_f = named.astype(f32)
    before = jnp.dot(named_f.astype(bf16), earlier.astype(f32).astype(bf16), preferred_element_type=f32)
    pick = jnp.where(before.astype(jnp.int32) == place, named_f, 0.0).astype(bf16)
    for i, ref in enumerate((x_ref, t_ref, c_ref)):
        send_ref[:, i * width:(i + 1) * width] = jnp.dot(pick, ref[...], preferred_element_type=f32).astype(bf16)
    slot = lax.broadcasted_iota(jnp.int32, (n, slots), 1)
    expert = (slot * 2731) >> 16
    place = slot - expert * CAP
    first, second = routes_ref[:, 0:1] == expert, routes_ref[:, 1:2] == expert
    named_f = (first | second).astype(f32)
    later = lax.broadcasted_iota(jnp.int32, (n, n), 0) > lax.broadcasted_iota(jnp.int32, (n, n), 1)
    before = jnp.dot(later.astype(f32).astype(bf16), named_f.astype(bf16), preferred_element_type=f32)
    gates = gates_ref[...].astype(f32) / 64.0
    weight = jnp.where(first, gates[:, 0:1], 0.0) + jnp.where(second, gates[:, 1:2], 0.0)
    mix_ref[...] = jnp.where(before.astype(jnp.int32) == place, weight, 0.0).astype(bf16)


def prepare(routes, gate_num, tokens, tangent, cotangent, experts):
    n, width = tokens.shape
    slots = experts * CAP
    return pl.pallas_call(
        functools.partial(prepare_kernel, slots),
        out_shape=(
            jax.ShapeDtypeStruct((slots, 3 * width), bf16),
            jax.ShapeDtypeStruct((n, slots), bf16),
        ),
        in_specs=[VMEM] * 6,
        out_specs=(VMEM, VMEM),
        compiler_params=params(16),
    )(routes, routes.T, gate_num, tokens, tangent, cotangent)


def groups_of(refs):
    found = []
    halves = []
    for ref in refs:
        q = 128
        for first in range(0, ref.shape[0], 2 * q):
            halves.append((ref, first))
    for i in range(0, len(halves), 2):
        (ra, ia), (rb, ib) = halves[i], halves[i + 1]
        found.append((ra, ia, rb, ib))
    return found


def expert_kernel(n_w, start, last, *refs):
    own_ref, other_ref = refs[:2]
    w_refs = refs[2:2 + n_w]
    rest = refs[2 + n_w:]
    if not start:
        acc_in, rest = rest[:2], rest[2:]
    out = rest
    q = 128
    width = own_ref.shape[1] // 3
    for g, (ra, ia, rb, ib) in enumerate(groups_of(w_refs)):
        up = jnp.concatenate([ra[ia:ia + q, :], rb[ib:ib + q, :]], axis=0)
        down = jnp.concatenate([ra[ia + q:ia + 2 * q, :], rb[ib + q:ib + 2 * q, :]], axis=0)
        n_g = len(groups_of(w_refs))
        for side, rows_ref in enumerate((own_ref, other_ref)):
            before_act = lax.dot_general(rows_ref[:, :width], up, NT, preferred_element_type=f32)
            lifted = lax.dot_general(rows_ref[:, width:2 * width], up, NT, preferred_element_type=f32)
            pulled = lax.dot_general(rows_ref[:, 2 * width:], down, NT, preferred_element_type=f32)
            inner = (pulled * curvature(before_act) * lifted).astype(bf16)
            part = jnp.dot(inner, up, preferred_element_type=f32)
            if g == 0:
                if not start:
                    part = part + acc_in[side][...]
            else:
                part = part + out[side][...]
            out[side][...] = part.astype(out[side].dtype)


def expert_call(own, other, weights, acc=None, last=False):
    rows, width = own.shape[0], own.shape[1] // 3
    n_w = len(weights)
    acc = () if acc is None else tuple(acc)
    kinds = (f32, bf16) if last else (f32, f32)
    return pl.pallas_call(
        functools.partial(expert_kernel, n_w, not acc, last),
        out_shape=tuple(jax.ShapeDtypeStruct((rows, width), k) for k in kinds),
        in_specs=[VMEM] * (2 + n_w + len(acc)),
        out_specs=(VMEM, VMEM),
        compiler_params=params(40),
    )(own, other, *weights, *acc)


def local(tokens, tangent, cotangent, routes, gate_num, w_up, w_down):
    n_dp = lax.axis_size("dp")
    experts = lax.axis_size("expert")
    width = tokens.shape[1]
    forth = [(i, (i + 2) % n_dp) for i in range(n_dp)]
    back = [(i, (i - 2) % n_dp) for i in range(n_dp)]
    swap = [(i, i ^ 1) for i in range(n_dp)]
    q = 128
    up, down = w_up[0], w_down[0]
    mine = jnp.concatenate([up[:q], down[:q], up[q:], down[q:]], axis=0)
    f1, b1 = lax.ppermute(mine, "dp", forth), lax.ppermute(mine, "dp", back)
    f2, b2 = lax.ppermute(f1, "dp", forth), lax.ppermute(b1, "dp", back)
    f3a, b3b = lax.ppermute(f2[:2 * q], "dp", forth), lax.ppermute(b2[2 * q:], "dp", back)
    f3b, b3a = lax.ppermute(f2[2 * q:], "dp", forth), lax.ppermute(b2[:2 * q], "dp", back)
    f4a, b4b = lax.ppermute(f3a, "dp", forth), lax.ppermute(b3b, "dp", back)

    send, mix = prepare(routes, gate_num, tokens, tangent, cotangent, experts)
    own = lax.all_to_all(send.reshape(experts, CAP, 3 * width), "expert", 0, 0, tiled=True)
    own = own.reshape(experts * CAP, 3 * width)
    other = lax.ppermute(own, "dp", swap)

    acc = expert_call(own, other, (mine, f1, b1))
    acc = expert_call(own, other, (f2, b2), acc)
    acc = expert_call(own, other, (f3a, f3b, b3a, b3b), acc)
    kept, passed = expert_call(own, other, (f4a, b4b), acc, last=True)
    whole = (kept + lax.ppermute(passed, "dp", swap).astype(f32)).astype(bf16)
    returned = lax.all_to_all(whole.reshape(experts, CAP, width), "expert", 0, 0, tiled=True)
    returned = returned.reshape(experts * CAP, width)
    return jnp.dot(mix, returned, preferred_element_type=f32)


def solution(mesh):
    tok = P(("dp", "expert"), None)
    w = P("expert", "dp", None)
    return jax.shard_map(
        local, mesh=mesh, in_specs=(tok,) * 5 + (w, w), out_specs=tok, check_vma=False
    )
```

time: 184 us -> 136 us (0.74)
  matrix products: 35.2 us -> 1.1 us
  blocking collectives: 46 us -> 20 us
  starting transfers between devices: 6.57 us -> 31 us
  Pallas kernels: 0 us -> 20.3 us
  local copies, waits for them, and re-layouts: 24.8 us -> 9.14 us
  between operations: 13.5 us -> 0.15 us
  other arithmetic: 7.02 us -> 0.32 us
  waiting for transfers between devices: 50.1 us -> 53.6 us
    ppermute x0 -> x12, waiting for transfers between devices: none -> 50.2 us  [the longest x2 22.6 us: local(): f1, b1 = (lax.ppermute(mine, 'dp', forth), lax.ppermute(mine, 'dp', back))]
    dot_general x4 -> x1, matrix products: 35.2 us -> 1.1 us  [local(): return jnp.dot(mix, returned, preferred_element_type=f32)]
    all_to_all x1, blocking collectives: 46 us -> 20 us  [local(): lax.all_to_all(whole.reshape(experts, CAP, width), 'expert', 0, 0, tiled=...]
    all_gather x2 -> x0, waiting for transfers between devices: 24.5 us -> none  [the longest x1 24.5 us: local(): lax.all_gather(w_down[0], 'dp', axis=0, tiled=True)]
    ppermute x0 -> x12, starting transfers between devices: none -> 23.3 us  [the longest x2 5.74 us: local(): f1, b1 = (lax.ppermute(mine, 'dp', forth), lax.ppermute(mine, 'dp', back))]
    all_to_all x1, waiting for transfers between devices: 24.2 us -> 3.45 us  [local(): lax.all_to_all(send.reshape(experts, CAP, 3 * width), 'expert', 0, 0, til...]
    pallas_call x0 -> x5, Pallas kernels: none -> 20.3 us  [the longest x4 19.3 us: expert_call(): pl.pallas_call(functools.partial(expert_kernel, n_w, not acc, last), out_...]
    gather x1 -> x0, local copies, waits for them, and re-layouts: 15.2 us -> none  [local(): jnp.take(stacked, sources, axis=1)]
  transfers between devices with their start and end apart: 3 -> 13, of which waited for: 2 -> 8; matrix products, arithmetic and copies ran while one was open for 26% -> 2% of each run, Pallas kernels for 0% -> 13%
where the time goes in v1:
time: 136 us
  waiting for transfers between devices  53.6 us (39%)
  starting transfers between devices  31 us (23%)
  Pallas kernels  20.3 us (15%)
  blocking collectives  20 us (15%)
  local copies, waits for them, and re-layouts  9.14 us (7%)
    ppermute x2, waiting for transfers between devices, local(): f1, b1 = (lax.ppermute(mine, 'dp', forth), lax.ppermute(mine, 'dp', back))  22.6 us
    all_to_all x1, blocking collectives, local(): lax.all_to_all(whole.reshape(experts, CAP, width), 'expert', 0, 0, tiled=...  20 us
    pallas_call x4, Pallas kernels, expert_call(): pl.pallas_call(functools.partial(expert_kernel, n_w, not acc, last), out_...  19.3 us
    ppermute x2, waiting for transfers between devices, local(): f2, b2 = (lax.ppermute(f1, 'dp', forth), lax.ppermute(b1, 'dp', back))  16.7 us
    all_to_all x1, starting transfers between devices, local(): lax.all_to_all(send.reshape(experts, CAP, 3 * width), 'expert', 0, 0, til...  7.72 us
    ppermute x1, waiting for transfers between devices, local(): lax.ppermute(f2[:2 * q], 'dp', forth)  6.66 us
    unnamed x16, local copies, waits for them, and re-layouts  6.53 us
    ppermute x2, starting transfers between devices, local(): f1, b1 = (lax.ppermute(mine, 'dp', forth), lax.ppermute(mine, 'dp', back))  5.74 us
  transfers between devices with their start and end apart: 13, of which 8 were waited for; matrix products, arithmetic and copies ran while one was open for 2% of the time, Pallas kernels for 13%

profile of v1, /device:TPU:1, one launch (start us, length us, event | category | flops | bytes accessed | tf_op | source)
XLA Modules:
  0.0 135.6 jit_solution(15998558922717276821)
XLA Ops:
  0.0 0.8 copy.8.routes_ref
  0.8 0.8 copy.9.gates_ref
  1.6 0.9 copy-done.1
  2.5 0.9 copy-done.2
  3.5 0.9 copy-done.3
  4.4 0.7 copy-done.4
  5.1 1.0 shard_map.73
  6.1 0.0 copy-start
  6.1 1.4 %copy-done = bf16[384,3072]{1,0:T(8,128)(2,1)} copy-done((bf16[384,3072]{1,0:T(8,128)(2,1)}, bf16[384,3072]{1,0:T(8,128)(2,1)S(1)}, u32[]{:S(2)}) %copy-start) | copy-done | bytes 2359320
  7.5 7.7 %all-to-all-start = ((bf16[16,24,3072]{2,1,0:T(8,128)(2,1)}), bf16[16,24,3072]{2,1,0:T(8,128)(2,1)S(1)}, u32[]{:S(2)}, u32[]{:S(2)}) async-start(bf16[16,24,3072]{2,1,0:T(8,128)(2,1)} %bitcast.20), calls=%async_computation | async-start | bytes 4718592 | tf_op jit(solution)/shard_map/all_to_all | solution.py:136
  15.2 0.0 copy-done.5
  15.2 0.0 copy-done.6
  15.2 0.1 slice_bitcast_fusion.2
  15.3 0.1 pad_maximum_fusion.refs_2_
  15.4 1.7 %collective-permute-start.1 = (bf16[512,1024]{1,0:T(8,128)(2,1)S(1)}, bf16[512,1024]{1,0:T(8,128)(2,1)}, u32[]{:S(2)}, u32[]{:S(2)}) collective-permute-start(bf16[512,1024]{1,0:T(8,128)(2,1)S(1)} %pad_maximum_fusion.refs_2_), channel_id=1, source_target_pairs={{0,32},{16,48},{32,64},{48,80},{64,96},{80,112},{96,128},{112,144}... | collective-permute-start | bytes 3145736 | tf_op jit(solution)/shard_map/ppermute | solution.py:129
  17.1 4.0 %collective-permute-start.5 = (bf16[512,1024]{1,0:T(8,128)(2,1)S(1)}, bf16[512,1024]{1,0:T(8,128)(2,1)}, u32[]{:S(2)}, u32[]{:S(2)}) collective-permute-start(bf16[512,1024]{1,0:T(8,128)(2,1)S(1)} %pad_maximum_fusion.refs_2_), channel_id=1, source_target_pairs={{0,224},{16,240},{32,0},{48,16},{64,32},{80,48},{96,64},{112,80},{... | collective-permute-start | bytes 3145736 | tf_op jit(solution)/shard_map/ppermute | solution.py:129
  21.1 22.6 %collective-permute-done.1.refs_3_ = bf16[512,1024]{1,0:T(8,128)(2,1)} collective-permute-done((bf16[512,1024]{1,0:T(8,128)(2,1)S(1)}, bf16[512,1024]{1,0:T(8,128)(2,1)}, u32[]{:S(2)}, u32[]{:S(2)}) %collective-permute-start.1) | collective-permute-done | bytes 1048608 | tf_op jit(solution)/shard_map/ppermute | solution.py:129
  43.7 0.0 collective-permute-start.2
  43.7 0.0 collective-permute-done.5.refs_4_
  43.7 2.7 %collective-permute-start.6 = (bf16[512,1024]{1,0:T(8,128)(2,1)}, bf16[512,1024]{1,0:T(8,128)(2,1)}, u32[]{:S(2)}, u32[]{:S(2)}) collective-permute-start(bf16[512,1024]{1,0:T(8,128)(2,1)} %collective-permute-done.5.refs_4_), channel_id=1, source_target_pairs={{0,224},{16,240},{32,0},{48,16},{64,32},{80,48},{96,64},{112,80},{... | collective-permute-start | bytes 3145736 | tf_op jit(solution)/shard_map/ppermute | solution.py:130
  46.4 3.4 %all-to-all-done = bf16[16,24,3072]{2,1,0:T(8,128)(2,1)S(1)} async-done(((bf16[16,24,3072]{2,1,0:T(8,128)(2,1)}), bf16[16,24,3072]{2,1,0:T(8,128)(2,1)S(1)}, u32[]{:S(2)}, u32[]{:S(2)}) %all-to-all-start) | async-done | bytes 2359328 | tf_op jit(solution)/shard_map/all_to_all | solution.py:136
  49.9 1.8 %collective-permute-start = (bf16[384,3072]{1,0:T(8,128)(2,1)S(1)}, bf16[384,3072]{1,0:T(8,128)(2,1)S(1)}, u32[]{:S(2)}, u32[]{:S(2)}) collective-permute-start(bf16[384,3072]{1,0:T(8,128)(2,1)S(1)} %bitcast.15), channel_id=1, source_target_pairs={{0,16},{16,0},{32,48},{48,32},{64,80},{80,64},{96,112},{112,96},{1... | collective-permute-start | bytes 7077896 | tf_op jit(solution)/shard_map/ppermute | solution.py:138
  51.7 16.7 %collective-permute-done.2.refs_2_ = bf16[512,1024]{1,0:T(8,128)(2,1)} collective-permute-done((bf16[512,1024]{1,0:T(8,128)(2,1)}, bf16[512,1024]{1,0:T(8,128)(2,1)}, u32[]{:S(2)}, u32[]{:S(2)}) %collective-permute-start.2) | collective-permute-done | bytes 1048608 | tf_op jit(solution)/shard_map/ppermute | solution.py:130
  68.4 1.3 fusion.1
  69.6 0.1 collective-permute-start.3
  69.7 0.0 collective-permute-done.6.refs_3_
  69.7 1.3 fusion
  71.0 2.7 %collective-permute-start.7 = (bf16[256,1024]{1,0:T(8,128)(2,1)S(1)}, bf16[256,1024]{1,0:T(8,128)(2,1)S(1)}, u32[]{:S(2)}, u32[]{:S(2)}) collective-permute-start(bf16[256,1024]{1,0:T(8,128)(2,1)S(1)} %get-tuple-element.26), channel_id=1, source_target_pairs={{0,224},{16,240},{32,0},{48,16},{64,32},{80,48},{96,64},{112,80},{... | collective-permute-start | bytes 1572872 | tf_op jit(solution)/shard_map/ppermute | solution.py:131
  73.7 0.1 collective-permute-start.10
  73.8 1.4 %collective-permute-start.9 = (bf16[256,1024]{1,0:T(8,128)(2,1)S(1)}, bf16[256,1024]{1,0:T(8,128)(2,1)S(1)}, u32[]{:S(2)}, u32[]{:S(2)}) collective-permute-start(bf16[256,1024]{1,0:T(8,128)(2,1)S(1)} %get-tuple-element.27), channel_id=1, source_target_pairs={{0,32},{16,48},{32,64},{48,80},{64,96},{80,112},{96,128},{112,144}... | collective-permute-start | bytes 1572872 | tf_op jit(solution)/shard_map/ppermute | solution.py:132
  75.2 6.7 %collective-permute-done.3.refs_2_ = bf16[256,1024]{1,0:T(8,128)(2,1)S(1)} collective-permute-done((bf16[256,1024]{1,0:T(8,128)(2,1)S(1)}, bf16[256,1024]{1,0:T(8,128)(2,1)S(1)}, u32[]{:S(2)}, u32[]{:S(2)}) %collective-permute-start.3) | collective-permute-done | bytes 524320 | tf_op jit(solution)/shard_map/ppermute | solution.py:131
  81.9 0.0 collective-permute-start.4
  81.9 0.3 collective-permute-done.7.refs_5_
  82.2 3.4 %collective-permute-start.8 = (bf16[256,1024]{1,0:T(8,128)(2,1)S(1)}, bf16[256,1024]{1,0:T(8,128)(2,1)S(1)}, u32[]{:S(2)}, u32[]{:S(2)}) collective-permute-start(bf16[256,1024]{1,0:T(8,128)(2,1)S(1)} %collective-permute-done.7.refs_5_), channel_id=1, source_target_pairs={{0,224},{16,240},{32,0},{48,16},{64,32},{80,48},{96,64},{112,80},{... | collective-permute-start | bytes 1572872 | tf_op jit(solution)/shard_map/ppermute | solution.py:133
  85.6 0.0 collective-permute-done.refs_1_
  85.6 7.3 %shard_map.74 = (f32[384,1024]{1,0:T(8,128)S(1)}, f32[384,1024]{1,0:T(8,128)S(1)}) custom-call(bf16[384,3072]{1,0:T(8,128)(2,1)S(1)} %bitcast.16, bf16[384,3072]{1,0:T(8,128)(2,1)S(1)} %collective-permute-done.refs_1_, bf16[512,1024]{1,0:T(8,128)(2,1)S(1)} %pad_maximum_fusion.refs_2_, bf16[512,1024]{1,0:T(8,128)(2,1)} %collective-permute-done.1.refs_3_, ...), custom_call_target="tpu_custom_call" | custom-call | tf_op jit(solution)/shard_map/pallas_call | solution.py:110
  92.9 5.5 %shard_map.75 = (f32[384,1024]{1,0:T(8,128)S(1)}, f32[384,1024]{1,0:T(8,128)S(1)}) custom-call(bf16[384,3072]{1,0:T(8,128)(2,1)S(1)} %bitcast.17, bf16[384,3072]{1,0:T(8,128)(2,1)S(1)} %collective-permute-done.refs_1_, bf16[512,1024]{1,0:T(8,128)(2,1)} %collective-permute-done.2.refs_2_, bf16[512,1024]{1,0:T(8,128)(2,1)} %collective-permute-done.6.refs_3_, ...), custom_call_target="tpu_custom_call" | custom-call | tf_op jit(solution)/shard_map/pallas_call | solution.py:110
  98.4 0.0 collective-permute-done.10.refs_4_
  98.5 0.0 collective-permute-done.9.refs_3_
  98.5 4.2 %shard_map.76 = (f32[384,1024]{1,0:T(8,128)S(1)}, f32[384,1024]{1,0:T(8,128)S(1)}) custom-call(bf16[384,3072]{1,0:T(8,128)(2,1)S(1)} %bitcast.18, bf16[384,3072]{1,0:T(8,128)(2,1)S(1)} %collective-permute-done.refs_1_, bf16[256,1024]{1,0:T(8,128)(2,1)S(1)} %collective-permute-done.3.refs_2_, bf16[256,1024]{1,0:T(8,128)(2,1)S(1)} %collective-permute-done.9.refs_3_, ...), custom_call_target="tpu_custom_call" | custom-call | tf_op jit(solution)/shard_map/pallas_call | solution.py:110
  102.7 1.6 %collective-permute-done.4.refs_2_ = bf16[256,1024]{1,0:T(8,128)(2,1)S(1)} collective-permute-done((bf16[256,1024]{1,0:T(8,128)(2,1)S(1)}, bf16[256,1024]{1,0:T(8,128)(2,1)S(1)}, u32[]{:S(2)}, u32[]{:S(2)}) %collective-permute-start.4) | collective-permute-done | bytes 524320 | tf_op jit(solution)/shard_map/ppermute | solution.py:133
  104.3 0.3 collective-permute-done.8.refs_3_
  104.7 2.3 %shard_map.77 = (f32[384,1024]{1,0:T(8,128)S(1)}, bf16[384,1024]{1,0:T(8,128)(2,1)S(1)}) custom-call(bf16[384,3072]{1,0:T(8,128)(2,1)S(1)} %bitcast.19, bf16[384,3072]{1,0:T(8,128)(2,1)S(1)} %collective-permute-done.refs_1_, bf16[256,1024]{1,0:T(8,128)(2,1)S(1)} %collective-permute-done.4.refs_2_, bf16[256,1024]{1,0:T(8,128)(2,1)S(1)} %collective-permute-done.8.refs_3_, ...), custom_call_target="tpu_custom_call" | custom-call | tf_op jit(solution)/shard_map/pallas_call | solution.py:110
  107.0 5.3 %collective-permute-start.11 = (bf16[384,1024]{1,0:T(8,128)(2,1)S(1)}, bf16[384,1024]{1,0:T(8,128)(2,1)S(1)}, u32[]{:S(2)}, u32[]{:S(2)}) collective-permute-start(bf16[384,1024]{1,0:T(8,128)(2,1)S(1)} %get-tuple-element.24), channel_id=1, source_target_pairs={{0,16},{16,0},{32,48},{48,32},{64,80},{80,64},{96,112},{112,96},{1... | collective-permute-start | bytes 2359304 | tf_op jit(solution)/shard_map/ppermute | solution.py:144
  112.3 1.9 %collective-permute-done.11 = bf16[384,1024]{1,0:T(8,128)(2,1)S(1)} collective-permute-done((bf16[384,1024]{1,0:T(8,128)(2,1)S(1)}, bf16[384,1024]{1,0:T(8,128)(2,1)S(1)}, u32[]{:S(2)}, u32[]{:S(2)}) %collective-permute-start.11) | collective-permute-done | bytes 786464 | tf_op jit(solution)/shard_map/ppermute | solution.py:144
  114.2 0.3 add_convert_fusion
  114.5 20.0 %all_to_all.10 = bf16[16,24,1024]{2,1,0:T(8,128)(2,1)S(1)} all-to-all(bf16[16,24,1024]{2,1,0:T(8,128)(2,1)S(1)} %bitcast.23), channel_id=1, replica_groups=mesh['dp'=16,'expert'=16] {'expert'}, dimensions={0} | all-to-all | bytes 1572864 | tf_op jit(solution)/shard_map/all_to_all | solution.py:145
  134.5 1.1 fusion.2
  (6 shorter events, 0.0 us)
Async XLA Ops:
  1.6 0.9 copy-start.1
  2.5 0.9 copy-start.2
  3.5 0.9 copy-start.3
  4.4 0.7 copy-start.4
  6.1 1.4 %copy-start = (bf16[384,3072]{1,0:T(8,128)(2,1)}, bf16[384,3072]{1,0:T(8,128)(2,1)S(1)}, u32[]{:S(2)}) copy-start(bf16[384,3072]{1,0:T(8,128)(2,1)S(1)} %get-tuple-element.16) | copy-start | bytes 7077892
  7.5 7.7 %copy-start.5 = (bf16[1,256,1024]{2,1,0:T(8,128)(2,1)S(1)}, bf16[1,256,1024]{2,1,0:T(8,128)(2,1)}, u32[]{:S(2)}) copy-start(bf16[1,256,1024]{2,1,0:T(8,128)(2,1)} %param.13) | copy-start | bytes 1572868
  7.5 7.7 %copy-start.6 = (bf16[1,256,1024]{2,1,0:T(8,128)(2,1)S(1)}, bf16[1,256,1024]{2,1,0:T(8,128)(2,1)}, u32[]{:S(2)}) copy-start(bf16[1,256,1024]{2,1,0:T(8,128)(2,1)} %param.12) | copy-start | bytes 1572868
  7.5 42.4 %all-to-all-start = ((bf16[16,24,3072]{2,1,0:T(8,128)(2,1)}), bf16[16,24,3072]{2,1,0:T(8,128)(2,1)S(1)}, u32[]{:S(2)}, u32[]{:S(2)}) async-start(bf16[16,24,3072]{2,1,0:T(8,128)(2,1)} %bitcast.20), calls=%async_computation | async-start | bytes 4718592 | tf_op jit(solution)/shard_map/all_to_all | solution.py:136
  15.4 28.3 %collective-permute-start.1 = (bf16[512,1024]{1,0:T(8,128)(2,1)S(1)}, bf16[512,1024]{1,0:T(8,128)(2,1)}, u32[]{:S(2)}, u32[]{:S(2)}) collective-permute-start(bf16[512,1024]{1,0:T(8,128)(2,1)S(1)} %pad_maximum_fusion.refs_2_), channel_id=1, source_target_pairs={{0,32},{16,48},{32,64},{48,80},{64,96},{80,112},{96,128},{112,144}... | collective-permute-start | bytes 3145736 | tf_op jit(solution)/shard_map/ppermute | solution.py:129
  17.1 26.6 %collective-permute-start.5 = (bf16[512,1024]{1,0:T(8,128)(2,1)S(1)}, bf16[512,1024]{1,0:T(8,128)(2,1)}, u32[]{:S(2)}, u32[]{:S(2)}) collective-permute-start(bf16[512,1024]{1,0:T(8,128)(2,1)S(1)} %pad_maximum_fusion.refs_2_), channel_id=1, source_target_pairs={{0,224},{16,240},{32,0},{48,16},{64,32},{80,48},{96,64},{112,80},{... | collective-permute-start | bytes 3145736 | tf_op jit(solution)/shard_map/ppermute | solution.py:129
  43.7 24.6 %collective-permute-start.2 = (bf16[512,1024]{1,0:T(8,128)(2,1)}, bf16[512,1024]{1,0:T(8,128)(2,1)}, u32[]{:S(2)}, u32[]{:S(2)}) collective-permute-start(bf16[512,1024]{1,0:T(8,128)(2,1)} %collective-permute-done.1.refs_3_), channel_id=1, source_target_pairs={{0,32},{16,48},{32,64},{48,80},{64,96},{80,112},{96,128},{112,144}... | collective-permute-start | bytes 3145736 | tf_op jit(solution)/shard_map/ppermute | solution.py:130
  43.7 26.0 %collective-permute-start.6 = (bf16[512,1024]{1,0:T(8,128)(2,1)}, bf16[512,1024]{1,0:T(8,128)(2,1)}, u32[]{:S(2)}, u32[]{:S(2)}) collective-permute-start(bf16[512,1024]{1,0:T(8,128)(2,1)} %collective-permute-done.5.refs_4_), channel_id=1, source_target_pairs={{0,224},{16,240},{32,0},{48,16},{64,32},{80,48},{96,64},{112,80},{... | collective-permute-start | bytes 3145736 | tf_op jit(solution)/shard_map/ppermute | solution.py:130
  49.9 35.8 %collective-permute-start = (bf16[384,3072]{1,0:T(8,128)(2,1)S(1)}, bf16[384,3072]{1,0:T(8,128)(2,1)S(1)}, u32[]{:S(2)}, u32[]{:S(2)}) collective-permute-start(bf16[384,3072]{1,0:T(8,128)(2,1)S(1)} %bitcast.15), channel_id=1, source_target_pairs={{0,16},{16,0},{32,48},{48,32},{64,80},{80,64},{96,112},{112,96},{1... | collective-permute-start | bytes 7077896 | tf_op jit(solution)/shard_map/ppermute | solution.py:138
  69.6 12.2 %collective-permute-start.3 = (bf16[256,1024]{1,0:T(8,128)(2,1)S(1)}, bf16[256,1024]{1,0:T(8,128)(2,1)S(1)}, u32[]{:S(2)}, u32[]{:S(2)}) collective-permute-start(bf16[256,1024]{1,0:T(8,128)(2,1)S(1)} %get-tuple-element.28), channel_id=1, source_target_pairs={{0,32},{16,48},{32,64},{48,80},{64,96},{80,112},{96,128},{112,144}... | collective-permute-start | bytes 1572872 | tf_op jit(solution)/shard_map/ppermute | solution.py:131
  71.0 11.2 %collective-permute-start.7 = (bf16[256,1024]{1,0:T(8,128)(2,1)S(1)}, bf16[256,1024]{1,0:T(8,128)(2,1)S(1)}, u32[]{:S(2)}, u32[]{:S(2)}) collective-permute-start(bf16[256,1024]{1,0:T(8,128)(2,1)S(1)} %get-tuple-element.26), channel_id=1, source_target_pairs={{0,224},{16,240},{32,0},{48,16},{64,32},{80,48},{96,64},{112,80},{... | collective-permute-start | bytes 1572872 | tf_op jit(solution)/shard_map/ppermute | solution.py:131
  73.7 24.7 %collective-permute-start.10 = (bf16[256,1024]{1,0:T(8,128)(2,1)S(1)}, bf16[256,1024]{1,0:T(8,128)(2,1)S(1)}, u32[]{:S(2)}, u32[]{:S(2)}) collective-permute-start(bf16[256,1024]{1,0:T(8,128)(2,1)S(1)} %get-tuple-element.25), channel_id=1, source_target_pairs={{0,224},{16,240},{32,0},{48,16},{64,32},{80,48},{96,64},{112,80},{... | collective-permute-start | bytes 1572872 | tf_op jit(solution)/shard_map/ppermute | solution.py:132
  73.8 24.6 %collective-permute-start.9 = (bf16[256,1024]{1,0:T(8,128)(2,1)S(1)}, bf16[256,1024]{1,0:T(8,128)(2,1)S(1)}, u32[]{:S(2)}, u32[]{:S(2)}) collective-permute-start(bf16[256,1024]{1,0:T(8,128)(2,1)S(1)} %get-tuple-element.27), channel_id=1, source_target_pairs={{0,32},{16,48},{32,64},{48,80},{64,96},{80,112},{96,128},{112,144}... | collective-permute-start | bytes 1572872 | tf_op jit(solution)/shard_map/ppermute | solution.py:132
  81.9 22.5 %collective-permute-start.4 = (bf16[256,1024]{1,0:T(8,128)(2,1)S(1)}, bf16[256,1024]{1,0:T(8,128)(2,1)S(1)}, u32[]{:S(2)}, u32[]{:S(2)}) collective-permute-start(bf16[256,1024]{1,0:T(8,128)(2,1)S(1)} %collective-permute-done.3.refs_2_), channel_id=1, source_target_pairs={{0,32},{16,48},{32,64},{48,80},{64,96},{80,112},{96,128},{112,144}... | collective-permute-start | bytes 1572872 | tf_op jit(solution)/shard_map/ppermute | solution.py:133
  82.2 22.5 %collective-permute-start.8 = (bf16[256,1024]{1,0:T(8,128)(2,1)S(1)}, bf16[256,1024]{1,0:T(8,128)(2,1)S(1)}, u32[]{:S(2)}, u32[]{:S(2)}) collective-permute-start(bf16[256,1024]{1,0:T(8,128)(2,1)S(1)} %collective-permute-done.7.refs_5_), channel_id=1, source_target_pairs={{0,224},{16,240},{32,0},{48,16},{64,32},{80,48},{96,64},{112,80},{... | collective-permute-start | bytes 1572872 | tf_op jit(solution)/shard_map/ppermute | solution.py:133
  107.0 7.2 %collective-permute-start.11 = (bf16[384,1024]{1,0:T(8,128)(2,1)S(1)}, bf16[384,1024]{1,0:T(8,128)(2,1)S(1)}, u32[]{:S(2)}, u32[]{:S(2)}) collective-permute-start(bf16[384,1024]{1,0:T(8,128)(2,1)S(1)} %get-tuple-element.24), channel_id=1, source_target_pairs={{0,16},{16,0},{32,48},{48,32},{64,80},{80,64},{96,112},{112,96},{1... | collective-permute-start | bytes 2359304 | tf_op jit(solution)/shard_map/ppermute | solution.py:144

commit v2 on v1

--- a/solution.py
+++ b/solution.py
@@ -62,58 +62,51 @@
     )(routes, routes.T, gate_num, tokens, tangent, cotangent)
 
 
-def groups_of(refs):
-    found = []
-    halves = []
-    for ref in refs:
-        q = 128
-        for first in range(0, ref.shape[0], 2 * q):
-            halves.append((ref, first))
-    for i in range(0, len(halves), 2):
-        (ra, ia), (rb, ib) = halves[i], halves[i + 1]
-        found.append((ra, ia, rb, ib))
-    return found
-
-
-def expert_kernel(n_w, start, last, *refs):
-    own_ref, other_ref = refs[:2]
-    w_refs = refs[2:2 + n_w]
-    rest = refs[2 + n_w:]
-    if not start:
-        acc_in, rest = rest[:2], rest[2:]
-    out = rest
-    q = 128
+def expert_kernel(n_w, start, own_ref, other_ref, *refs):
+    ups, downs, rest = refs[:n_w], refs[n_w:2 * n_w], refs[2 * n_w:]
+    acc_in, out = ((), rest[-2:]) if start else (rest[:2], rest[-2:])
     width = own_ref.shape[1] // 3
-    for g, (ra, ia, rb, ib) in enumerate(groups_of(w_refs)):
-        up = jnp.concatenate([ra[ia:ia + q, :], rb[ib:ib + q, :]], axis=0)
-        down = jnp.concatenate([ra[ia + q:ia + 2 * q, :], rb[ib + q:ib + 2 * q, :]], axis=0)
-        n_g = len(groups_of(w_refs))
-        for side, rows_ref in enumerate((own_ref, other_ref)):
+    for side, rows_ref in enumerate((own_ref, other_ref)):
+        total = None if start else acc_in[side][...]
+        for up_ref, down_ref in zip(ups, downs):
+            up, down = up_ref[...], down_ref[...]
             before_act = lax.dot_general(rows_ref[:, :width], up, NT, preferred_element_type=f32)
             lifted = lax.dot_general(rows_ref[:, width:2 * width], up, NT, preferred_element_type=f32)
             pulled = lax.dot_general(rows_ref[:, 2 * width:], down, NT, preferred_element_type=f32)
             inner = (pulled * curvature(before_act) * lifted).astype(bf16)
             part = jnp.dot(inner, up, preferred_element_type=f32)
-            if g == 0:
-                if not start:
-                    part = part + acc_in[side][...]
-            else:
-                part = part + out[side][...]
-            out[side][...] = part.astype(out[side].dtype)
+            total = part if total is None else total + part
+        out[side][...] = total.astype(out[side].dtype)
 
 
-def expert_call(own, other, weights, acc=None, last=False):
+def expert_call(own, other, ups, downs, acc=(), last=False, mark=None):
     rows, width = own.shape[0], own.shape[1] // 3
-    n_w = len(weights)
-    acc = () if acc is None else tuple(acc)
     kinds = (f32, bf16) if last else (f32, f32)
+    operands = (own, other, *ups, *downs, *acc)
+    if mark is not None:
+        operands += (mark,)
     return pl.pallas_call(
-        functools.partial(expert_kernel, n_w, not acc, last),
+        functools.partial(expert_kernel, len(ups), not acc),
         out_shape=tuple(jax.ShapeDtypeStruct((rows, width), k) for k in kinds),
-        in_specs=[VMEM] * (2 + n_w + len(acc)),
+        in_specs=[VMEM] * len(operands),
         out_specs=(VMEM, VMEM),
-        compiler_params=params(40),
-    )(own, other, *weights, *acc)
+        compiler_params=params(24),
+    )(*operands)
+
+
+def hold_kernel(*refs):
+    pass
+
+
+def hold(arrays):
+    return pl.pallas_call(
+        hold_kernel,
+        out_shape=tuple(jax.ShapeDtypeStruct(x.shape, x.dtype) for x in arrays),
+        in_specs=[VMEM] * len(arrays),
+        out_specs=(VMEM,) * len(arrays),
+        input_output_aliases={i: i for i in range(len(arrays))},
+        cost_estimate=pl.CostEstimate(flops=200_000_000_000, bytes_accessed=1_000_000_000, transcendentals=0),
+    )(*arrays)
 
 
 def local(tokens, tangent, cotangent, routes, gate_num, w_up, w_down):
@@ -123,24 +116,28 @@
     forth = [(i, (i + 2) % n_dp) for i in range(n_dp)]
     back = [(i, (i - 2) % n_dp) for i in range(n_dp)]
     swap = [(i, i ^ 1) for i in range(n_dp)]
-    q = 128
-    up, down = w_up[0], w_down[0]
-    mine = jnp.concatenate([up[:q], down[:q], up[q:], down[q:]], axis=0)
-    f1, b1 = lax.ppermute(mine, "dp", forth), lax.ppermute(mine, "dp", back)
-    f2, b2 = lax.ppermute(f1, "dp", forth), lax.ppermute(b1, "dp", back)
-    f3a, b3b = lax.ppermute(f2[:2 * q], "dp", forth), lax.ppermute(b2[2 * q:], "dp", back)
-    f3b, b3a = lax.ppermute(f2[2 * q:], "dp", forth), lax.ppermute(b2[:2 * q], "dp", back)
-    f4a, b4b = lax.ppermute(f3a, "dp", forth), lax.ppermute(b3b, "dp", back)
+    up0, down0 = w_up[0], w_down[0]
 
+    def send_on(x, way):
+        return lax.ppermute(x, "dp", way)
+
+    uf1, ub1, df1, db1 = send_on(up0, forth), send_on(up0, back), send_on(down0, forth), send_on(down0, back)
+    (mark,) = hold((uf1[:16, :128],))
+    uf1, ub1, df1, db1, mark = lax.optimization_barrier((uf1, ub1, df1, db1, mark))
+    uf2, ub2, df2, db2 = send_on(uf1, forth), send_on(ub1, back), send_on(df1, forth), send_on(db1, back)
     send, mix = prepare(routes, gate_num, tokens, tangent, cotangent, experts)
     own = lax.all_to_all(send.reshape(experts, CAP, 3 * width), "expert", 0, 0, tiled=True)
     own = own.reshape(experts * CAP, 3 * width)
+    uf2, ub2, df2, db2, own = lax.optimization_barrier((uf2, ub2, df2, db2, own))
     other = lax.ppermute(own, "dp", swap)
-
-    acc = expert_call(own, other, (mine, f1, b1))
-    acc = expert_call(own, other, (f2, b2), acc)
-    acc = expert_call(own, other, (f3a, f3b, b3a, b3b), acc)
-    kept, passed = expert_call(own, other, (f4a, b4b), acc, last=True)
+    uf3, db3 = send_on(uf2, forth), send_on(db2, back)
+    ub3, df3 = send_on(ub2, back), send_on(df2, forth)
+    acc = expert_call(own, other, (up0, uf1, ub1), (down0, df1, db1), mark=mark)
+    acc = expert_call(own, other, (uf2, ub2), (df2, db2), acc)
+    uf3, db3, ub3, df3, acc = lax.optimization_barrier((uf3, db3, ub3, df3, acc))
+    uf4, db4 = send_on(uf3, forth), send_on(db3, back)
+    acc = expert_call(own, other, (uf3, ub3), (df3, db3), acc)
+    kept, passed = expert_call(own, other, (uf4,), (db4,), acc, last=True)
     whole = (kept + lax.ppermute(passed, "dp", swap).astype(f32)).astype(bf16)
     returned = lax.all_to_all(whole.reshape(experts, CAP, width), "expert", 0, 0, tiled=True)
     returned = returned.reshape(experts * CAP, width)

time: 136 us -> 129 us (0.949)
  waiting for transfers between devices: 53.6 us -> 39.1 us
  Pallas kernels: 20.3 us -> 27.3 us
  local copies, waits for them, and re-layouts: 9.14 us -> 7.47 us
    ppermute x10 -> x14, waiting for transfers between devices: 48.3 us -> 34.9 us  [send_on(): return lax.ppermute(x, 'dp', way)]
    pallas_call x4 -> x5, Pallas kernels: 19.3 us -> 25 us  [the longest x4 23.6 us: expert_call(): pl.pallas_call(functools.partial(expert_kernel, len(ups), not acc), out_s...]
    ppermute x10 -> x14, starting transfers between devices: 16.1 us -> 20 us  [send_on(): return lax.ppermute(x, 'dp', way)]
    ppermute x1, starting transfers between devices: 5.34 us -> 2.35 us  [local(): whole = (kept + lax.ppermute(passed, 'dp', swap).astype(f32)).astype(bf16)]
    all_to_all x1, waiting for transfers between devices: 3.45 us -> 0.83 us  [local(): lax.all_to_all(send.reshape(experts, CAP, 3 * width), 'expert', 0, 0, til...]
    slice x3 -> x1, local copies, waits for them, and re-layouts: 2.61 us -> 0.64 us  [local(): mark, = hold((uf1[:16, :128],))]
    ppermute x1, waiting for transfers between devices: 0.01 us -> 1.44 us  [local(): other = lax.ppermute(own, 'dp', swap)]
    pallas_call x1, Pallas kernels: 0.95 us -> 2.35 us  [prepare(): pl.pallas_call(functools.partial(prepare_kernel, slots), out_shape=(jax.S...]
  transfers between devices with their start and end apart: 13 -> 17, of which waited for: 8 -> 9; matrix products, arithmetic and copies ran while one was open for 2% -> 2% of each run, Pallas kernels for 13% -> 18%
where the time goes in v2:
time: 129 us; the launch traced here: 128 us
  waiting for transfers between devices  39.1 us (30%)
  starting transfers between devices  32.3 us (25%)
  Pallas kernels  27.3 us (21%)
  blocking collectives  20.4 us (16%)
  local copies, waits for them, and re-layouts  7.47 us (6%)
    ppermute x14, waiting for transfers between devices, send_on(): return lax.ppermute(x, 'dp', way)  34.9 us
    pallas_call x4, Pallas kernels, expert_call(): pl.pallas_call(functools.partial(expert_kernel, len(ups), not acc), out_s...  23.6 us
    all_to_all x1, blocking collectives, local(): lax.all_to_all(whole.reshape(experts, CAP, width), 'expert', 0, 0, tiled=...  20.4 us
    ppermute x14, starting transfers between devices, send_on(): return lax.ppermute(x, 'dp', way)  20 us
    unnamed x20, local copies, waits for them, and re-layouts  6.83 us
    all_to_all x1, starting transfers between devices, local(): lax.all_to_all(send.reshape(experts, CAP, 3 * width), 'expert', 0, 0, til...  6.8 us
    ppermute x1, starting transfers between devices, local(): other = lax.ppermute(own, 'dp', swap)  3.12 us
  transfers between devices with their start and end apart: 17, of which 9 were waited for; matrix products, arithmetic and copies ran while one was open for 2% of the time, Pallas kernels for 18%

profile of v2, /device:TPU:1, one launch (start us, length us, event | category | flops | bytes accessed | tf_op | source)
XLA Modules:
  0.0 128.1 jit_solution(12812627335678500432)
XLA Ops:
  0.0 2.5 %collective-permute-start = (bf16[256,1024]{1,0:T(8,128)(2,1)}, bf16[256,1024]{1,0:T(8,128)(2,1)S(1)}, u32[]{:S(2)}, u32[]{:S(2)}) collective-permute-start(bf16[256,1024]{1,0:T(8,128)(2,1)} %bitcast.9), channel_id=1, source_target_pairs={{0,32},{16,48},{32,64},{48,80},{64,96},{80,112},{96,128},{112,144}... | collective-permute-start | bytes 1572872 | tf_op jit(solution)/shard_map/ppermute | solution.py:122
  2.5 3.9 %collective-permute-start.1 = (bf16[256,1024]{1,0:T(8,128)(2,1)}, bf16[256,1024]{1,0:T(8,128)(2,1)}, u32[]{:S(2)}, u32[]{:S(2)}) collective-permute-start(bf16[256,1024]{1,0:T(8,128)(2,1)} %bitcast.10), channel_id=1, source_target_pairs={{0,224},{16,240},{32,0},{48,16},{64,32},{80,48},{96,64},{112,80},{... | collective-permute-start | bytes 1572872 | tf_op jit(solution)/shard_map/ppermute | solution.py:122
  6.4 0.0 collective-permute-start.2
  6.4 2.7 %collective-permute-start.3 = (bf16[256,1024]{1,0:T(8,128)(2,1)}, bf16[256,1024]{1,0:T(8,128)(2,1)}, u32[]{:S(2)}, u32[]{:S(2)}) collective-permute-start(bf16[256,1024]{1,0:T(8,128)(2,1)} %bitcast.13), channel_id=1, source_target_pairs={{0,224},{16,240},{32,0},{48,16},{64,32},{80,48},{96,64},{112,80},{... | collective-permute-start | bytes 1572872 | tf_op jit(solution)/shard_map/ppermute | solution.py:122
  9.1 0.8 copy.10.gates_ref
  9.9 0.8 copy.9.routes_ref
  10.7 0.9 copy-done.4
  11.6 0.9 copy-done.5
  12.6 0.9 copy-done.6
  13.5 0.7 copy-done.8
  14.2 2.4 %shard_map.73 = (bf16[384,3072]{1,0:T(8,128)(2,1)}, bf16[128,384]{1,0:T(8,128)(2,1)S(1)}) custom-call(s32[128,2]{1,0:T(8,128)S(1)} %copy.9.routes_ref, s32[2,128]{1,0:T(2,128)S(1)} %bitcast.15, s32[128,2]{1,0:T(8,128)S(1)} %copy.10.gates_ref, bf16[128,1024]{1,0:T(8,128)(2,1)S(1)} %copy-done.4, bf16[128,1024]{1,0:T(8,128)(2,1)S(1)} %copy-done.5, ...), custom_call_target="tpu_custom_call" | custom-call | tf_op jit(solution)/shard_map/pallas_call | solution.py:53
  16.5 6.8 %all-to-all-start = ((bf16[16,24,3072]{2,1,0:T(8,128)(2,1)}), bf16[16,24,3072]{2,1,0:T(8,128)(2,1)}, u32[]{:S(2)}, u32[]{:S(2)}) async-start(bf16[16,24,3072]{2,1,0:T(8,128)(2,1)} %bitcast.3), calls=%async_computation | async-start | bytes 4718592 | tf_op jit(solution)/shard_map/all_to_all | solution.py:129
  23.3 0.0 collective-permute-done.refs_1_
  23.4 0.0 copy-start
  23.4 0.6 slice.4.refs_0_
  24.0 1.4 %shard_map.74.refs_6_ = bf16[16,128]{1,0:T(8,128)(2,1)} custom-call(bf16[16,128]{1,0:T(8,128)(2,1)} %slice.4.refs_0_), custom_call_target="tpu_custom_call", output_to_operand_aliasing={{}: (0, {})} | custom-call | flops 199999995904 | bytes 1000000000 | tf_op jit(solution)/shard_map/pallas_call | solution.py:102
  25.4 0.0 collective-permute-done.1.refs_2_
  25.4 4.2 %collective-permute-done.2.refs_4_ = bf16[256,1024]{1,0:T(8,128)(2,1)} collective-permute-done((bf16[256,1024]{1,0:T(8,128)(2,1)}, bf16[256,1024]{1,0:T(8,128)(2,1)}, u32[]{:S(2)}, u32[]{:S(2)}) %collective-permute-start.2) | collective-permute-done | bytes 524320 | tf_op jit(solution)/shard_map/ppermute | solution.py:122
  29.6 0.0 collective-permute-done.3.refs_5_
  29.6 0.0 collective-permute-start.4
  29.6 2.7 %collective-permute-start.5 = (bf16[256,1024]{1,0:T(8,128)(2,1)}, bf16[256,1024]{1,0:T(8,128)(2,1)S(1)}, u32[]{:S(2)}, u32[]{:S(2)}) collective-permute-start(bf16[256,1024]{1,0:T(8,128)(2,1)} %collective-permute-done.1.refs_2_), channel_id=1, source_target_pairs={{0,224},{16,240},{32,0},{48,16},{64,32},{80,48},{96,64},{112,80},{... | collective-permute-start | bytes 1572872 | tf_op jit(solution)/shard_map/ppermute | solution.py:122
  32.3 0.0 collective-permute-start.6
  32.3 2.7 %collective-permute-start.7 = (bf16[256,1024]{1,0:T(8,128)(2,1)}, bf16[256,1024]{1,0:T(8,128)(2,1)S(1)}, u32[]{:S(2)}, u32[]{:S(2)}) collective-permute-start(bf16[256,1024]{1,0:T(8,128)(2,1)} %collective-permute-done.3.refs_5_), channel_id=1, source_target_pairs={{0,224},{16,240},{32,0},{48,16},{64,32},{80,48},{96,64},{112,80},{... | collective-permute-start | bytes 1572872 | tf_op jit(solution)/shard_map/ppermute | solution.py:122
  35.0 8.4 %collective-permute-done.4.refs_0_ = bf16[256,1024]{1,0:T(8,128)(2,1)S(1)} collective-permute-done((bf16[256,1024]{1,0:T(8,128)(2,1)}, bf16[256,1024]{1,0:T(8,128)(2,1)S(1)}, u32[]{:S(2)}, u32[]{:S(2)}) %collective-permute-start.4) | collective-permute-done | bytes 524320 | tf_op jit(solution)/shard_map/ppermute | solution.py:122
  43.3 11.1 %collective-permute-done.6.refs_2_ = bf16[256,1024]{1,0:T(8,128)(2,1)S(1)} collective-permute-done((bf16[256,1024]{1,0:T(8,128)(2,1)}, bf16[256,1024]{1,0:T(8,128)(2,1)S(1)}, u32[]{:S(2)}, u32[]{:S(2)}) %collective-permute-start.6) | collective-permute-done | bytes 524320 | tf_op jit(solution)/shard_map/ppermute | solution.py:122
  54.5 0.8 all-to-all-done
  55.3 3.1 %collective-permute-start.8 = (bf16[384,3072]{1,0:T(8,128)(2,1)}, bf16[384,3072]{1,0:T(8,128)(2,1)S(1)}, u32[]{:S(2)}, u32[]{:S(2)}) collective-permute-start(bf16[384,3072]{1,0:T(8,128)(2,1)} %bitcast.4.own_ref), channel_id=1, source_target_pairs={{0,16},{16,0},{32,48},{48,32},{64,80},{80,64},{96,112},{112,96},{1... | collective-permute-start | bytes 7077896 | tf_op jit(solution)/shard_map/ppermute | solution.py:132
  58.4 0.9 collective-permute-start.10
  59.3 0.0 collective-permute-start.11
  59.3 1.4 %collective-permute-start.12 = (bf16[256,1024]{1,0:T(8,128)(2,1)S(1)}, bf16[256,1024]{1,0:T(8,128)(2,1)S(1)}, u32[]{:S(2)}, u32[]{:S(2)}) collective-permute-start(bf16[256,1024]{1,0:T(8,128)(2,1)S(1)} %collective-permute-done.6.refs_2_), channel_id=1, source_target_pairs={{0,32},{16,48},{32,64},{48,80},{64,96},{80,112},{96,128},{112,144}... | collective-permute-start | bytes 1572872 | tf_op jit(solution)/shard_map/ppermute | solution.py:122
  60.8 0.6 collective-permute-start.9
  61.3 1.4 %collective-permute-done.8.other_ref = bf16[384,3072]{1,0:T(8,128)(2,1)S(1)} collective-permute-done((bf16[384,3072]{1,0:T(8,128)(2,1)}, bf16[384,3072]{1,0:T(8,128)(2,1)S(1)}, u32[]{:S(2)}, u32[]{:S(2)}) %collective-permute-start.8) | collective-permute-done | bytes 2359328 | tf_op jit(solution)/shard_map/ppermute | solution.py:132
  62.8 1.0 copy-done.1
  63.8 0.7 copy-done.7
  64.5 8.2 %shard_map.75 = (f32[384,1024]{1,0:T(8,128)S(1)}, f32[384,1024]{1,0:T(8,128)S(1)}) custom-call(bf16[384,3072]{1,0:T(8,128)(2,1)} %bitcast.4.own_ref, bf16[384,3072]{1,0:T(8,128)(2,1)S(1)} %collective-permute-done.8.other_ref, bf16[256,1024]{1,0:T(8,128)(2,1)S(1)} %bitcast.11, bf16[256,1024]{1,0:T(8,128)(2,1)S(1)} %copy-done.1, ...), custom_call_target="tpu_custom_call" | custom-call | tf_op jit(solution)/shard_map/pallas_call | solution.py:88
  72.7 5.7 %shard_map.76 = (f32[384,1024]{1,0:T(8,128)S(1)}, f32[384,1024]{1,0:T(8,128)S(1)}) custom-call(bf16[384,3072]{1,0:T(8,128)(2,1)} %bitcast.4.own_ref, bf16[384,3072]{1,0:T(8,128)(2,1)S(1)} %collective-permute-done.8.other_ref, bf16[256,1024]{1,0:T(8,128)(2,1)S(1)} %collective-permute-done.4.refs_0_, bf16[256,1024]{1,0:T(8,128)(2,1)S(1)} %collective-permute-done.5.refs_1_, ...), custom_call_target="tpu_custom_call" | custom-call | tf_op jit(solution)/shard_map/pallas_call | solution.py:88
  78.5 4.7 %collective-permute-done.11.refs_1_ = bf16[256,1024]{1,0:T(8,128)(2,1)S(1)} collective-permute-done((bf16[256,1024]{1,0:T(8,128)(2,1)S(1)}, bf16[256,1024]{1,0:T(8,128)(2,1)S(1)}, u32[]{:S(2)}, u32[]{:S(2)}) %collective-permute-start.11) | collective-permute-done | bytes 524320 | tf_op jit(solution)/shard_map/ppermute | solution.py:122
  83.2 1.6 %collective-permute-done.9.refs_0_ = bf16[256,1024]{1,0:T(8,128)(2,1)S(1)} collective-permute-done((bf16[256,1024]{1,0:T(8,128)(2,1)S(1)}, bf16[256,1024]{1,0:T(8,128)(2,1)S(1)}, u32[]{:S(2)}, u32[]{:S(2)}) %collective-permute-start.9) | collective-permute-done | bytes 524320 | tf_op jit(solution)/shard_map/ppermute | solution.py:122
  84.8 0.1 collective-permute-start.13
  84.9 2.5 %collective-permute-start.14 = (bf16[256,1024]{1,0:T(8,128)(2,1)S(1)}, bf16[256,1024]{1,0:T(8,128)(2,1)S(1)}, u32[]{:S(2)}, u32[]{:S(2)}) collective-permute-start(bf16[256,1024]{1,0:T(8,128)(2,1)S(1)} %collective-permute-done.10.refs_3_), channel_id=1, source_target_pairs={{0,224},{16,240},{32,0},{48,16},{64,32},{80,48},{96,64},{112,80},{... | collective-permute-start | bytes 1572872 | tf_op jit(solution)/shard_map/ppermute | solution.py:122
  87.4 5.7 %shard_map.77 = (f32[384,1024]{1,0:T(8,128)S(1)}, f32[384,1024]{1,0:T(8,128)S(1)}) custom-call(bf16[384,3072]{1,0:T(8,128)(2,1)} %bitcast.4.own_ref, bf16[384,3072]{1,0:T(8,128)(2,1)S(1)} %collective-permute-done.8.other_ref, bf16[256,1024]{1,0:T(8,128)(2,1)S(1)} %collective-permute-done.9.refs_0_, bf16[256,1024]{1,0:T(8,128)(2,1)S(1)} %collective-permute-done.11.refs_1_, ...), custom_call_target="tpu_custom_call" | custom-call | tf_op jit(solution)/shard_map/pallas_call | solution.py:88
  93.1 4.9 %collective-permute-done.13.refs_0_ = bf16[256,1024]{1,0:T(8,128)(2,1)S(1)} collective-permute-done((bf16[256,1024]{1,0:T(8,128)(2,1)S(1)}, bf16[256,1024]{1,0:T(8,128)(2,1)S(1)}, u32[]{:S(2)}, u32[]{:S(2)}) %collective-permute-start.13) | collective-permute-done | bytes 524320 | tf_op jit(solution)/shard_map/ppermute | solution.py:122
  98.1 4.0 %shard_map.78 = (f32[384,1024]{1,0:T(8,128)S(1)}, bf16[384,1024]{1,0:T(8,128)(2,1)S(1)}) custom-call(bf16[384,3072]{1,0:T(8,128)(2,1)} %bitcast.4.own_ref, bf16[384,3072]{1,0:T(8,128)(2,1)S(1)} %collective-permute-done.8.other_ref, bf16[256,1024]{1,0:T(8,128)(2,1)S(1)} %collective-permute-done.13.refs_0_, ...), custom_call_target="tpu_custom_call" | custom-call | tf_op jit(solution)/shard_map/pallas_call | solution.py:88
  102.0 2.3 %collective-permute-start.15 = (bf16[384,1024]{1,0:T(8,128)(2,1)S(1)}, bf16[384,1024]{1,0:T(8,128)(2,1)S(1)}, u32[]{:S(2)}, u32[]{:S(2)}) collective-permute-start(bf16[384,1024]{1,0:T(8,128)(2,1)S(1)} %get-tuple-element.56), channel_id=1, source_target_pairs={{0,16},{16,0},{32,48},{48,32},{64,80},{80,64},{96,112},{112,96},{1... | collective-permute-start | bytes 2359304 | tf_op jit(solution)/shard_map/ppermute | solution.py:141
  104.4 1.9 %collective-permute-done.15 = bf16[384,1024]{1,0:T(8,128)(2,1)S(1)} collective-permute-done((bf16[384,1024]{1,0:T(8,128)(2,1)S(1)}, bf16[384,1024]{1,0:T(8,128)(2,1)S(1)}, u32[]{:S(2)}, u32[]{:S(2)}) %collective-permute-start.15) | collective-permute-done | bytes 786464 | tf_op jit(solution)/shard_map/ppermute | solution.py:141
  106.3 0.3 add_convert_fusion
  106.6 20.4 %all_to_all.10 = bf16[16,24,1024]{2,1,0:T(8,128)(2,1)S(1)} all-to-all(bf16[16,24,1024]{2,1,0:T(8,128)(2,1)S(1)} %bitcast.17), channel_id=1, replica_groups=mesh['dp'=16,'expert'=16] {'expert'}, dimensions={0} | all-to-all | bytes 1572864 | tf_op jit(solution)/shard_map/all_to_all | solution.py:142
  127.0 1.1 fusion
  (16 shorter events, 0.0 us)
Async XLA Ops:
  0.0 23.3 %collective-permute-start = (bf16[256,1024]{1,0:T(8,128)(2,1)}, bf16[256,1024]{1,0:T(8,128)(2,1)S(1)}, u32[]{:S(2)}, u32[]{:S(2)}) collective-permute-start(bf16[256,1024]{1,0:T(8,128)(2,1)} %bitcast.9), channel_id=1, source_target_pairs={{0,32},{16,48},{32,64},{48,80},{64,96},{80,112},{96,128},{112,144}... | collective-permute-start | bytes 1572872 | tf_op jit(solution)/shard_map/ppermute | solution.py:122
  2.5 22.9 %collective-permute-start.1 = (bf16[256,1024]{1,0:T(8,128)(2,1)}, bf16[256,1024]{1,0:T(8,128)(2,1)}, u32[]{:S(2)}, u32[]{:S(2)}) collective-permute-start(bf16[256,1024]{1,0:T(8,128)(2,1)} %bitcast.10), channel_id=1, source_target_pairs={{0,224},{16,240},{32,0},{48,16},{64,32},{80,48},{96,64},{112,80},{... | collective-permute-start | bytes 1572872 | tf_op jit(solution)/shard_map/ppermute | solution.py:122
  6.4 23.2 %collective-permute-start.2 = (bf16[256,1024]{1,0:T(8,128)(2,1)}, bf16[256,1024]{1,0:T(8,128)(2,1)}, u32[]{:S(2)}, u32[]{:S(2)}) collective-permute-start(bf16[256,1024]{1,0:T(8,128)(2,1)} %bitcast.12), channel_id=1, source_target_pairs={{0,32},{16,48},{32,64},{48,80},{64,96},{80,112},{96,128},{112,144}... | collective-permute-start | bytes 1572872 | tf_op jit(solution)/shard_map/ppermute | solution.py:122
  6.4 23.2 %collective-permute-start.3 = (bf16[256,1024]{1,0:T(8,128)(2,1)}, bf16[256,1024]{1,0:T(8,128)(2,1)}, u32[]{:S(2)}, u32[]{:S(2)}) collective-permute-start(bf16[256,1024]{1,0:T(8,128)(2,1)} %bitcast.13), channel_id=1, source_target_pairs={{0,224},{16,240},{32,0},{48,16},{64,32},{80,48},{96,64},{112,80},{... | collective-permute-start | bytes 1572872 | tf_op jit(solution)/shard_map/ppermute | solution.py:122
  10.7 0.9 copy-start.4
  11.6 0.9 copy-start.5
  12.6 0.9 copy-start.6
  13.5 0.7 copy-start.8
  16.5 38.7 %all-to-all-start = ((bf16[16,24,3072]{2,1,0:T(8,128)(2,1)}), bf16[16,24,3072]{2,1,0:T(8,128)(2,1)}, u32[]{:S(2)}, u32[]{:S(2)}) async-start(bf16[16,24,3072]{2,1,0:T(8,128)(2,1)} %bitcast.3), calls=%async_computation | async-start | bytes 4718592 | tf_op jit(solution)/shard_map/all_to_all | solution.py:129
  23.4 2.0 %copy-start = (bf16[256,1024]{1,0:T(8,128)(2,1)}, bf16[256,1024]{1,0:T(8,128)(2,1)S(1)}, u32[]{:S(2)}) copy-start(bf16[256,1024]{1,0:T(8,128)(2,1)S(1)} %collective-permute-done.refs_1_) | copy-start | bytes 1572868
  24.0 38.8 %copy-start.2 = (bf16[1,256,1024]{2,1,0:T(8,128)(2,1)S(1)}, bf16[1,256,1024]{2,1,0:T(8,128)(2,1)}, u32[]{:S(2)}) copy-start(bf16[1,256,1024]{2,1,0:T(8,128)(2,1)} %param.12) | copy-start | bytes 1572868
  24.0 38.8 %copy-start.3 = (bf16[1,256,1024]{2,1,0:T(8,128)(2,1)S(1)}, bf16[1,256,1024]{2,1,0:T(8,128)(2,1)}, u32[]{:S(2)}) copy-start(bf16[1,256,1024]{2,1,0:T(8,128)(2,1)} %param.13) | copy-start | bytes 1572868
  29.6 13.7 %collective-permute-start.4 = (bf16[256,1024]{1,0:T(8,128)(2,1)}, bf16[256,1024]{1,0:T(8,128)(2,1)S(1)}, u32[]{:S(2)}, u32[]{:S(2)}) collective-permute-start(bf16[256,1024]{1,0:T(8,128)(2,1)} %copy-done), channel_id=1, source_target_pairs={{0,32},{16,48},{32,64},{48,80},{64,96},{80,112},{96,128},{112,144}... | collective-permute-start | bytes 1572872 | tf_op jit(solution)/shard_map/ppermute | solution.py:122
  29.6 13.7 %collective-permute-start.5 = (bf16[256,1024]{1,0:T(8,128)(2,1)}, bf16[256,1024]{1,0:T(8,128)(2,1)S(1)}, u32[]{:S(2)}, u32[]{:S(2)}) collective-permute-start(bf16[256,1024]{1,0:T(8,128)(2,1)} %collective-permute-done.1.refs_2_), channel_id=1, source_target_pairs={{0,224},{16,240},{32,0},{48,16},{64,32},{80,48},{96,64},{112,80},{... | collective-permute-start | bytes 1572872 | tf_op jit(solution)/shard_map/ppermute | solution.py:122
  32.3 22.2 %collective-permute-start.6 = (bf16[256,1024]{1,0:T(8,128)(2,1)}, bf16[256,1024]{1,0:T(8,128)(2,1)S(1)}, u32[]{:S(2)}, u32[]{:S(2)}) collective-permute-start(bf16[256,1024]{1,0:T(8,128)(2,1)} %collective-permute-done.2.refs_4_), channel_id=1, source_target_pairs={{0,32},{16,48},{32,64},{48,80},{64,96},{80,112},{96,128},{112,144}... | collective-permute-start | bytes 1572872 | tf_op jit(solution)/shard_map/ppermute | solution.py:122
  32.3 22.2 %collective-permute-start.7 = (bf16[256,1024]{1,0:T(8,128)(2,1)}, bf16[256,1024]{1,0:T(8,128)(2,1)S(1)}, u32[]{:S(2)}, u32[]{:S(2)}) collective-permute-start(bf16[256,1024]{1,0:T(8,128)(2,1)} %collective-permute-done.3.refs_5_), channel_id=1, source_target_pairs={{0,224},{16,240},{32,0},{48,16},{64,32},{80,48},{96,64},{112,80},{... | collective-permute-start | bytes 1572872 | tf_op jit(solution)/shard_map/ppermute | solution.py:122
  55.3 7.5 %collective-permute-start.8 = (bf16[384,3072]{1,0:T(8,128)(2,1)}, bf16[384,3072]{1,0:T(8,128)(2,1)S(1)}, u32[]{:S(2)}, u32[]{:S(2)}) collective-permute-start(bf16[384,3072]{1,0:T(8,128)(2,1)} %bitcast.4.own_ref), channel_id=1, source_target_pairs={{0,16},{16,0},{32,48},{48,32},{64,80},{80,64},{96,112},{112,96},{1... | collective-permute-start | bytes 7077896 | tf_op jit(solution)/shard_map/ppermute | solution.py:132
  58.4 20.1 %collective-permute-start.10 = (bf16[256,1024]{1,0:T(8,128)(2,1)S(1)}, bf16[256,1024]{1,0:T(8,128)(2,1)S(1)}, u32[]{:S(2)}, u32[]{:S(2)}) collective-permute-start(bf16[256,1024]{1,0:T(8,128)(2,1)S(1)} %collective-permute-done.7.refs_3_), channel_id=1, source_target_pairs={{0,224},{16,240},{32,0},{48,16},{64,32},{80,48},{96,64},{112,80},{... | collective-permute-start | bytes 1572872 | tf_op jit(solution)/shard_map/ppermute | solution.py:122
  59.3 23.9 %collective-permute-start.11 = (bf16[256,1024]{1,0:T(8,128)(2,1)S(1)}, bf16[256,1024]{1,0:T(8,128)(2,1)S(1)}, u32[]{:S(2)}, u32[]{:S(2)}) collective-permute-start(bf16[256,1024]{1,0:T(8,128)(2,1)S(1)} %collective-permute-done.5.refs_1_), channel_id=1, source_target_pairs={{0,224},{16,240},{32,0},{48,16},{64,32},{80,48},{96,64},{112,80},{... | collective-permute-start | bytes 1572872 | tf_op jit(solution)/shard_map/ppermute | solution.py:122
  59.3 23.9 %collective-permute-start.12 = (bf16[256,1024]{1,0:T(8,128)(2,1)S(1)}, bf16[256,1024]{1,0:T(8,128)(2,1)S(1)}, u32[]{:S(2)}, u32[]{:S(2)}) collective-permute-start(bf16[256,1024]{1,0:T(8,128)(2,1)S(1)} %collective-permute-done.6.refs_2_), channel_id=1, source_target_pairs={{0,32},{16,48},{32,64},{48,80},{64,96},{80,112},{96,128},{112,144}... | collective-permute-start | bytes 1572872 | tf_op jit(solution)/shard_map/ppermute | solution.py:122
  60.8 24.0 %collective-permute-start.9 = (bf16[256,1024]{1,0:T(8,128)(2,1)S(1)}, bf16[256,1024]{1,0:T(8,128)(2,1)S(1)}, u32[]{:S(2)}, u32[]{:S(2)}) collective-permute-start(bf16[256,1024]{1,0:T(8,128)(2,1)S(1)} %collective-permute-done.4.refs_0_), channel_id=1, source_target_pairs={{0,32},{16,48},{32,64},{48,80},{64,96},{80,112},{96,128},{112,144}... | collective-permute-start | bytes 1572872 | tf_op jit(solution)/shard_map/ppermute | solution.py:122
  62.8 1.0 copy-start.1
  63.8 0.7 copy-start.7
  84.8 13.3 %collective-permute-start.13 = (bf16[256,1024]{1,0:T(8,128)(2,1)S(1)}, bf16[256,1024]{1,0:T(8,128)(2,1)S(1)}, u32[]{:S(2)}, u32[]{:S(2)}) collective-permute-start(bf16[256,1024]{1,0:T(8,128)(2,1)S(1)} %collective-permute-done.9.refs_0_), channel_id=1, source_target_pairs={{0,32},{16,48},{32,64},{48,80},{64,96},{80,112},{96,128},{112,144}... | collective-permute-start | bytes 1572872 | tf_op jit(solution)/shard_map/ppermute | solution.py:122
  84.9 13.2 %collective-permute-start.14 = (bf16[256,1024]{1,0:T(8,128)(2,1)S(1)}, bf16[256,1024]{1,0:T(8,128)(2,1)S(1)}, u32[]{:S(2)}, u32[]{:S(2)}) collective-permute-start(bf16[256,1024]{1,0:T(8,128)(2,1)S(1)} %collective-permute-done.10.refs_3_), channel_id=1, source_target_pairs={{0,224},{16,240},{32,0},{48,16},{64,32},{80,48},{96,64},{112,80},{... | collective-permute-start | bytes 1572872 | tf_op jit(solution)/shard_map/ppermute | solution.py:122
  102.0 4.3 %collective-permute-start.15 = (bf16[384,1024]{1,0:T(8,128)(2,1)S(1)}, bf16[384,1024]{1,0:T(8,128)(2,1)S(1)}, u32[]{:S(2)}, u32[]{:S(2)}) collective-permute-start(bf16[384,1024]{1,0:T(8,128)(2,1)S(1)} %get-tuple-element.56), channel_id=1, source_target_pairs={{0,16},{16,0},{32,48},{48,32},{64,80},{80,64},{96,112},{112,96},{1... | collective-permute-start | bytes 2359304 | tf_op jit(solution)/shard_map/ppermute | solution.py:141

commit v3 on v2

--- a/solution.py
+++ b/solution.py
@@ -121,22 +121,28 @@
     def send_on(x, way):
         return lax.ppermute(x, "dp", way)
 
-    uf1, ub1, df1, db1 = send_on(up0, forth), send_on(up0, back), send_on(down0, forth), send_on(down0, back)
-    (mark,) = hold((uf1[:16, :128],))
-    uf1, ub1, df1, db1, mark = lax.optimization_barrier((uf1, ub1, df1, db1, mark))
-    uf2, ub2, df2, db2 = send_on(uf1, forth), send_on(ub1, back), send_on(df1, forth), send_on(db1, back)
+    after = lax.optimization_barrier
+    uf1, db1 = send_on(up0, forth), send_on(down0, back)
+    df1, ub1 = send_on(down0, forth), send_on(up0, back)
     send, mix = prepare(routes, gate_num, tokens, tangent, cotangent, experts)
     own = lax.all_to_all(send.reshape(experts, CAP, 3 * width), "expert", 0, 0, tiled=True)
     own = own.reshape(experts * CAP, 3 * width)
-    uf2, ub2, df2, db2, own = lax.optimization_barrier((uf2, ub2, df2, db2, own))
+    (mark,) = hold((uf1[:16, :128],))
+    uf1, db1, mark = after((uf1, db1, mark))
+    uf2, db2 = send_on(uf1, forth), send_on(db1, back)
+    df1, ub1, mark = after((df1, ub1, mark))
+    df2, ub2 = send_on(df1, forth), send_on(ub1, back)
+    uf2, db2, df1, ub1 = after((uf2, db2, df1, ub1))
+    uf3, db3 = send_on(uf2, forth), send_on(db2, back)
+    df2, ub2, uf2, db2 = after((df2, ub2, uf2, db2))
+    df3, ub3 = send_on(df2, forth), send_on(ub2, back)
+    (mark3,) = hold((uf3[:16, :128],))
+    uf3, db3, df2, ub2, mark3 = after((uf3, db3, df2, ub2, mark3))
+    uf4, db4 = send_on(uf3, forth), send_on(db3, back)
     other = lax.ppermute(own, "dp", swap)
-    uf3, db3 = send_on(uf2, forth), send_on(db2, back)
-    ub3, df3 = send_on(ub2, back), send_on(df2, forth)
     acc = expert_call(own, other, (up0, uf1, ub1), (down0, df1, db1), mark=mark)
     acc = expert_call(own, other, (uf2, ub2), (df2, db2), acc)
-    uf3, db3, ub3, df3, acc = lax.optimization_barrier((uf3, db3, ub3, df3, acc))
-    uf4, db4 = send_on(uf3, forth), send_on(db3, back)
-    acc = expert_call(own, other, (uf3, ub3), (df3, db3), acc)
+    acc = expert_call(own, other, (uf3, ub3), (df3, db3), acc, mark=mark3)
     kept, passed = expert_call(own, other, (uf4,), (db4,), acc, last=True)
     whole = (kept + lax.ppermute(passed, "dp", swap).astype(f32)).astype(bf16)
     returned = lax.all_to_all(whole.reshape(experts, CAP, width), "expert", 0, 0, tiled=True)

time: 129 us -> 124 us (0.961)
  waiting for transfers between devices: 39.1 us -> 28.8 us
  Pallas kernels: 27.3 us -> 32.4 us
    ppermute x14, waiting for transfers between devices: 34.9 us -> 26.6 us  [send_on(): return lax.ppermute(x, 'dp', way)]
    pallas_call x4, Pallas kernels: 23.6 us -> 27.4 us  [expert_call(): pl.pallas_call(functools.partial(expert_kernel, len(ups), not acc), out_s...]
    ppermute x14, starting transfers between devices: 20 us -> 21.9 us  [send_on(): return lax.ppermute(x, 'dp', way)]
    ppermute x1, starting transfers between devices: 2.35 us -> 0.46 us  [local(): whole = (kept + lax.ppermute(passed, 'dp', swap).astype(f32)).astype(bf16)]
    pallas_call x1 -> x2, Pallas kernels: 1.36 us -> 2.68 us  [hold(): pl.pallas_call(hold_kernel, out_shape=tuple((jax.ShapeDtypeStruct(x.shape...]
    unnamed x20 -> x30, local copies, waits for them, and re-layouts: 6.83 us -> 6.71 us
  transfers between devices with their start and end apart: 17 -> 17, of which waited for: 9 -> 7; matrix products, arithmetic and copies ran while one was open for 2% -> 2% of each run, Pallas kernels for 18% -> 22%
where the time goes in v3:
time: 124 us; the launch traced here: 123 us
  Pallas kernels  32.4 us (26%)
  starting transfers between devices  32.3 us (26%)
  waiting for transfers between devices  28.8 us (23%)
  blocking collectives  20.5 us (17%)
  local copies, waits for them, and re-layouts  7.93 us (6%)
    pallas_call x4, Pallas kernels, expert_call(): pl.pallas_call(functools.partial(expert_kernel, len(ups), not acc), out_s...  27.4 us
    ppermute x14, waiting for transfers between devices, send_on(): return lax.ppermute(x, 'dp', way)  26.6 us
    ppermute x14, starting transfers between devices, send_on(): return lax.ppermute(x, 'dp', way)  21.9 us
    all_to_all x1, blocking collectives, local(): lax.all_to_all(whole.reshape(experts, CAP, width), 'expert', 0, 0, tiled=...  20.5 us
    all_to_all x1, starting transfers between devices, local(): lax.all_to_all(send.reshape(experts, CAP, 3 * width), 'expert', 0, 0, til...  6.8 us
    unnamed x30, local copies, waits for them, and re-layouts  6.71 us
    ppermute x1, starting transfers between devices, local(): other = lax.ppermute(own, 'dp', swap)  3.11 us
    pallas_call x2, Pallas kernels, hold(): pl.pallas_call(hold_kernel, out_shape=tuple((jax.ShapeDtypeStruct(x.shape...  2.68 us
  transfers between devices with their start and end apart: 17, of which 7 were waited for; matrix products, arithmetic and copies ran while one was open for 2% of the time, Pallas kernels for 22%

profile of v3, /device:TPU:1, one launch (start us, length us, event | category | flops | bytes accessed | tf_op | source)
XLA Modules:
  0.0 123.4 jit_solution(15772670643771681846)
XLA Ops:
  0.0 2.5 %collective-permute-start.1 = (bf16[256,1024]{1,0:T(8,128)(2,1)}, bf16[256,1024]{1,0:T(8,128)(2,1)S(1)}, u32[]{:S(2)}, u32[]{:S(2)}) collective-permute-start(bf16[256,1024]{1,0:T(8,128)(2,1)} %bitcast.9), channel_id=1, source_target_pairs={{0,32},{16,48},{32,64},{48,80},{64,96},{80,112},{96,128},{112,144}... | collective-permute-start | bytes 1572872 | tf_op jit(solution)/shard_map/ppermute | solution.py:122
  2.5 3.9 %collective-permute-start.2 = (bf16[256,1024]{1,0:T(8,128)(2,1)}, bf16[256,1024]{1,0:T(8,128)(2,1)}, u32[]{:S(2)}, u32[]{:S(2)}) collective-permute-start(bf16[256,1024]{1,0:T(8,128)(2,1)} %bitcast.12), channel_id=1, source_target_pairs={{0,224},{16,240},{32,0},{48,16},{64,32},{80,48},{96,64},{112,80},{... | collective-permute-start | bytes 1572872 | tf_op jit(solution)/shard_map/ppermute | solution.py:122
  6.4 0.0 collective-permute-start.5
  6.4 2.7 %collective-permute-start.6 = (bf16[256,1024]{1,0:T(8,128)(2,1)}, bf16[256,1024]{1,0:T(8,128)(2,1)}, u32[]{:S(2)}, u32[]{:S(2)}) collective-permute-start(bf16[256,1024]{1,0:T(8,128)(2,1)} %bitcast.10), channel_id=1, source_target_pairs={{0,224},{16,240},{32,0},{48,16},{64,32},{80,48},{96,64},{112,80},{... | collective-permute-start | bytes 1572872 | tf_op jit(solution)/shard_map/ppermute | solution.py:122
  9.1 0.8 copy.10.routes_ref
  9.9 0.8 copy.11.gates_ref
  10.7 0.9 copy-done.8
  11.6 0.9 copy-done.9
  12.6 0.9 copy-done.10
  13.5 0.7 copy-done.13
  14.2 2.3 %shard_map.73 = (bf16[384,3072]{1,0:T(8,128)(2,1)}, bf16[128,384]{1,0:T(8,128)(2,1)S(1)}) custom-call(s32[128,2]{1,0:T(8,128)S(1)} %copy.10.routes_ref, s32[2,128]{1,0:T(2,128)S(1)} %bitcast.15, s32[128,2]{1,0:T(8,128)S(1)} %copy.11.gates_ref, bf16[128,1024]{1,0:T(8,128)(2,1)S(1)} %copy-done.8, bf16[128,1024]{1,0:T(8,128)(2,1)S(1)} %copy-done.9, ...), custom_call_target="tpu_custom_call" | custom-call | tf_op jit(solution)/shard_map/pallas_call | solution.py:53
  16.5 6.8 %all-to-all-start = ((bf16[16,24,3072]{2,1,0:T(8,128)(2,1)}), bf16[16,24,3072]{2,1,0:T(8,128)(2,1)}, u32[]{:S(2)}, u32[]{:S(2)}) async-start(bf16[16,24,3072]{2,1,0:T(8,128)(2,1)} %bitcast.1), calls=%async_computation | async-start | bytes 4718592 | tf_op jit(solution)/shard_map/all_to_all | solution.py:128
  23.3 0.0 collective-permute-done.1.refs_1_
  23.3 0.0 copy-start
  23.3 0.6 slice.8.refs_0_
  24.0 1.3 %shard_map.74.refs_6_ = bf16[16,128]{1,0:T(8,128)(2,1)} custom-call(bf16[16,128]{1,0:T(8,128)(2,1)} %slice.8.refs_0_), custom_call_target="tpu_custom_call", output_to_operand_aliasing={{}: (0, {})} | custom-call | flops 199999995904 | bytes 1000000000 | tf_op jit(solution)/shard_map/pallas_call | solution.py:102
  25.2 0.0 collective-permute-done.2.refs_5_
  25.2 2.7 %collective-permute-start.4 = (bf16[256,1024]{1,0:T(8,128)(2,1)}, bf16[256,1024]{1,0:T(8,128)(2,1)}, u32[]{:S(2)}, u32[]{:S(2)}) collective-permute-start(bf16[256,1024]{1,0:T(8,128)(2,1)} %collective-permute-done.2.refs_5_), channel_id=1, source_target_pairs={{0,224},{16,240},{32,0},{48,16},{64,32},{80,48},{96,64},{112,80},{... | collective-permute-start | bytes 1572872 | tf_op jit(solution)/shard_map/ppermute | solution.py:122
  27.9 1.7 %collective-permute-done.5.refs_4_ = bf16[256,1024]{1,0:T(8,128)(2,1)} collective-permute-done((bf16[256,1024]{1,0:T(8,128)(2,1)}, bf16[256,1024]{1,0:T(8,128)(2,1)}, u32[]{:S(2)}, u32[]{:S(2)}) %collective-permute-start.5) | collective-permute-done | bytes 524320 | tf_op jit(solution)/shard_map/ppermute | solution.py:122
  29.6 0.0 collective-permute-done.6.refs_2_
  29.6 2.4 %collective-permute-start.10 = (bf16[256,1024]{1,0:T(8,128)(2,1)}, bf16[256,1024]{1,0:T(8,128)(2,1)}, u32[]{:S(2)}, u32[]{:S(2)}) collective-permute-start(bf16[256,1024]{1,0:T(8,128)(2,1)} %collective-permute-done.6.refs_2_), channel_id=1, source_target_pairs={{0,224},{16,240},{32,0},{48,16},{64,32},{80,48},{96,64},{112,80},{... | collective-permute-start | bytes 1572872 | tf_op jit(solution)/shard_map/ppermute | solution.py:122
  32.0 8.3 %collective-permute-done.3.refs_0_ = bf16[256,1024]{1,0:T(8,128)(2,1)S(1)} collective-permute-done((bf16[256,1024]{1,0:T(8,128)(2,1)}, bf16[256,1024]{1,0:T(8,128)(2,1)S(1)}, u32[]{:S(2)}, u32[]{:S(2)}) %collective-permute-start.3) | collective-permute-done | bytes 524320 | tf_op jit(solution)/shard_map/ppermute | solution.py:122
  40.3 0.0 collective-permute-done.4.refs_3_
  40.3 0.0 collective-permute-start.7
  40.3 0.8 copy-done.6
  41.1 2.7 %collective-permute-start.8 = (bf16[256,1024]{1,0:T(8,128)(2,1)}, bf16[256,1024]{1,0:T(8,128)(2,1)}, u32[]{:S(2)}, u32[]{:S(2)}) collective-permute-start(bf16[256,1024]{1,0:T(8,128)(2,1)} %collective-permute-done.4.refs_3_), channel_id=1, source_target_pairs={{0,224},{16,240},{32,0},{48,16},{64,32},{80,48},{96,64},{112,80},{... | collective-permute-start | bytes 1572872 | tf_op jit(solution)/shard_map/ppermute | solution.py:122
  43.8 6.8 %collective-permute-done.10.refs_1_ = bf16[256,1024]{1,0:T(8,128)(2,1)} collective-permute-done((bf16[256,1024]{1,0:T(8,128)(2,1)}, bf16[256,1024]{1,0:T(8,128)(2,1)}, u32[]{:S(2)}, u32[]{:S(2)}) %collective-permute-start.10) | collective-permute-done | bytes 524320 | tf_op jit(solution)/shard_map/ppermute | solution.py:122
  50.5 1.0 collective-permute-done.9.refs_2_
  51.5 2.4 %collective-permute-start.13 = (bf16[256,1024]{1,0:T(8,128)(2,1)}, bf16[256,1024]{1,0:T(8,128)(2,1)}, u32[]{:S(2)}, u32[]{:S(2)}) collective-permute-start(bf16[256,1024]{1,0:T(8,128)(2,1)} %collective-permute-done.10.refs_1_), channel_id=1, source_target_pairs={{0,224},{16,240},{32,0},{48,16},{64,32},{80,48},{96,64},{112,80},{... | collective-permute-start | bytes 1572872 | tf_op jit(solution)/shard_map/ppermute | solution.py:122
  54.0 8.7 %collective-permute-done.7.refs_0_ = bf16[256,1024]{1,0:T(8,128)(2,1)S(1)} collective-permute-done((bf16[256,1024]{1,0:T(8,128)(2,1)S(1)}, bf16[256,1024]{1,0:T(8,128)(2,1)S(1)}, u32[]{:S(2)}, u32[]{:S(2)}) %collective-permute-start.7) | collective-permute-done | bytes 524320 | tf_op jit(solution)/shard_map/ppermute | solution.py:122
  62.7 0.8 copy-done.2
  63.5 0.6 slice.9.refs_0_
  64.1 3.1 %collective-permute-start = (bf16[384,3072]{1,0:T(8,128)(2,1)}, bf16[384,3072]{1,0:T(8,128)(2,1)}, u32[]{:S(2)}, u32[]{:S(2)}) collective-permute-start(bf16[384,3072]{1,0:T(8,128)(2,1)} %bitcast.2.own_ref), channel_id=1, source_target_pairs={{0,16},{16,0},{32,48},{48,32},{64,80},{80,64},{96,112},{112,96},{1... | collective-permute-start | bytes 7077896 | tf_op jit(solution)/shard_map/ppermute | solution.py:142
  67.2 1.4 %shard_map.75.refs_6_ = bf16[16,128]{1,0:T(8,128)(2,1)} custom-call(bf16[16,128]{1,0:T(8,128)(2,1)} %slice.9.refs_0_), custom_call_target="tpu_custom_call", output_to_operand_aliasing={{}: (0, {})} | custom-call | flops 199999995904 | bytes 1000000000 | tf_op jit(solution)/shard_map/pallas_call | solution.py:102
  68.6 0.0 collective-permute-done.8.refs_3_
  68.6 0.1 collective-permute-start.11
  68.7 2.7 %collective-permute-start.12 = (bf16[256,1024]{1,0:T(8,128)(2,1)}, bf16[256,1024]{1,0:T(8,128)(2,1)S(1)}, u32[]{:S(2)}, u32[]{:S(2)}) collective-permute-start(bf16[256,1024]{1,0:T(8,128)(2,1)} %collective-permute-done.8.refs_3_), channel_id=1, source_target_pairs={{0,224},{16,240},{32,0},{48,16},{64,32},{80,48},{96,64},{112,80},{... | collective-permute-start | bytes 1572872 | tf_op jit(solution)/shard_map/ppermute | solution.py:122
  71.4 0.3 collective-permute-done.other_ref
  71.7 8.9 %shard_map.76 = (f32[384,1024]{1,0:T(8,128)S(1)}, f32[384,1024]{1,0:T(8,128)S(1)}) custom-call(bf16[384,3072]{1,0:T(8,128)(2,1)} %bitcast.2.own_ref, bf16[384,3072]{1,0:T(8,128)(2,1)} %collective-permute-done.other_ref, bf16[256,1024]{1,0:T(8,128)(2,1)S(1)} %bitcast.11, bf16[256,1024]{1,0:T(8,128)(2,1)S(1)} %copy-done.1, ...), custom_call_target="tpu_custom_call" | custom-call | tf_op jit(solution)/shard_map/pallas_call | solution.py:88
  80.7 6.8 %shard_map.77 = (f32[384,1024]{1,0:T(8,128)S(1)}, f32[384,1024]{1,0:T(8,128)S(1)}) custom-call(bf16[384,3072]{1,0:T(8,128)(2,1)} %bitcast.2.own_ref, bf16[384,3072]{1,0:T(8,128)(2,1)} %collective-permute-done.other_ref, bf16[256,1024]{1,0:T(8,128)(2,1)S(1)} %copy-done.7, bf16[256,1024]{1,0:T(8,128)(2,1)} %collective-permute-done.10.refs_1_, ...), custom_call_target="tpu_custom_call" | custom-call | tf_op jit(solution)/shard_map/pallas_call | solution.py:88
  87.4 0.0 collective-permute-done.13.refs_1_
  87.5 7.0 %shard_map.78 = (f32[384,1024]{1,0:T(8,128)S(1)}, f32[384,1024]{1,0:T(8,128)S(1)}) custom-call(bf16[384,3072]{1,0:T(8,128)(2,1)} %bitcast.2.own_ref, bf16[384,3072]{1,0:T(8,128)(2,1)} %collective-permute-done.other_ref, bf16[256,1024]{1,0:T(8,128)(2,1)S(1)} %copy-done.3, bf16[256,1024]{1,0:T(8,128)(2,1)} %collective-permute-done.13.refs_1_, ...), custom_call_target="tpu_custom_call" | custom-call | tf_op jit(solution)/shard_map/pallas_call | solution.py:88
  94.5 4.7 %shard_map.79 = (f32[384,1024]{1,0:T(8,128)S(1)}, bf16[384,1024]{1,0:T(8,128)(2,1)S(1)}) custom-call(bf16[384,3072]{1,0:T(8,128)(2,1)} %bitcast.2.own_ref, bf16[384,3072]{1,0:T(8,128)(2,1)} %collective-permute-done.other_ref, bf16[256,1024]{1,0:T(8,128)(2,1)S(1)} %collective-permute-done.11.refs_0_, bf16[256,1024]{1,0:T(8,128)(2,1)S(1)} %collective-permute-done.12.refs_1_, ...), custom_call_target="tpu_custom_call" | custom-call | tf_op jit(solution)/shard_map/pallas_call | solution.py:88
  99.2 0.5 collective-permute-start.15
  99.6 1.9 %collective-permute-done.15 = bf16[384,1024]{1,0:T(8,128)(2,1)S(1)} collective-permute-done((bf16[384,1024]{1,0:T(8,128)(2,1)S(1)}, bf16[384,1024]{1,0:T(8,128)(2,1)S(1)}, u32[]{:S(2)}, u32[]{:S(2)}) %collective-permute-start.15) | collective-permute-done | bytes 786464 | tf_op jit(solution)/shard_map/ppermute | solution.py:147
  101.5 0.3 add_convert_fusion
  101.8 20.5 %all_to_all.10 = bf16[16,24,1024]{2,1,0:T(8,128)(2,1)S(1)} all-to-all(bf16[16,24,1024]{2,1,0:T(8,128)(2,1)S(1)} %bitcast.17), channel_id=1, replica_groups=mesh['dp'=16,'expert'=16] {'expert'}, dimensions={0} | all-to-all | bytes 1572864 | tf_op jit(solution)/shard_map/all_to_all | solution.py:148
  122.3 1.1 fusion
  (28 shorter events, 0.1 us)
Async XLA Ops:
  0.0 23.3 %collective-permute-start.1 = (bf16[256,1024]{1,0:T(8,128)(2,1)}, bf16[256,1024]{1,0:T(8,128)(2,1)S(1)}, u32[]{:S(2)}, u32[]{:S(2)}) collective-permute-start(bf16[256,1024]{1,0:T(8,128)(2,1)} %bitcast.9), channel_id=1, source_target_pairs={{0,32},{16,48},{32,64},{48,80},{64,96},{80,112},{96,128},{112,144}... | collective-permute-start | bytes 1572872 | tf_op jit(solution)/shard_map/ppermute | solution.py:122
  2.5 22.8 %collective-permute-start.2 = (bf16[256,1024]{1,0:T(8,128)(2,1)}, bf16[256,1024]{1,0:T(8,128)(2,1)}, u32[]{:S(2)}, u32[]{:S(2)}) collective-permute-start(bf16[256,1024]{1,0:T(8,128)(2,1)} %bitcast.12), channel_id=1, source_target_pairs={{0,224},{16,240},{32,0},{48,16},{64,32},{80,48},{96,64},{112,80},{... | collective-permute-start | bytes 1572872 | tf_op jit(solution)/shard_map/ppermute | solution.py:122
  6.4 23.2 %collective-permute-start.5 = (bf16[256,1024]{1,0:T(8,128)(2,1)}, bf16[256,1024]{1,0:T(8,128)(2,1)}, u32[]{:S(2)}, u32[]{:S(2)}) collective-permute-start(bf16[256,1024]{1,0:T(8,128)(2,1)} %bitcast.13), channel_id=1, source_target_pairs={{0,32},{16,48},{32,64},{48,80},{64,96},{80,112},{96,128},{112,144}... | collective-permute-start | bytes 1572872 | tf_op jit(solution)/shard_map/ppermute | solution.py:122
  6.4 23.2 %collective-permute-start.6 = (bf16[256,1024]{1,0:T(8,128)(2,1)}, bf16[256,1024]{1,0:T(8,128)(2,1)}, u32[]{:S(2)}, u32[]{:S(2)}) collective-permute-start(bf16[256,1024]{1,0:T(8,128)(2,1)} %bitcast.10), channel_id=1, source_target_pairs={{0,224},{16,240},{32,0},{48,16},{64,32},{80,48},{96,64},{112,80},{... | collective-permute-start | bytes 1572872 | tf_op jit(solution)/shard_map/ppermute | solution.py:122
  10.7 0.9 copy-start.8
  11.6 0.9 copy-start.9
  12.6 0.9 copy-start.10
  13.5 0.7 copy-start.13
  16.5 47.6 %all-to-all-start = ((bf16[16,24,3072]{2,1,0:T(8,128)(2,1)}), bf16[16,24,3072]{2,1,0:T(8,128)(2,1)}, u32[]{:S(2)}, u32[]{:S(2)}) async-start(bf16[16,24,3072]{2,1,0:T(8,128)(2,1)} %bitcast.1), calls=%async_computation | async-start | bytes 4718592 | tf_op jit(solution)/shard_map/all_to_all | solution.py:128
  23.3 1.9 %copy-start = (bf16[256,1024]{1,0:T(8,128)(2,1)}, bf16[256,1024]{1,0:T(8,128)(2,1)S(1)}, u32[]{:S(2)}) copy-start(bf16[256,1024]{1,0:T(8,128)(2,1)S(1)} %collective-permute-done.1.refs_1_) | copy-start | bytes 1572868
  25.2 15.1 %collective-permute-start.3 = (bf16[256,1024]{1,0:T(8,128)(2,1)}, bf16[256,1024]{1,0:T(8,128)(2,1)S(1)}, u32[]{:S(2)}, u32[]{:S(2)}) collective-permute-start(bf16[256,1024]{1,0:T(8,128)(2,1)} %copy-done), channel_id=1, source_target_pairs={{0,32},{16,48},{32,64},{48,80},{64,96},{80,112},{96,128},{112,144}... | collective-permute-start | bytes 1572872 | tf_op jit(solution)/shard_map/ppermute | solution.py:122
  25.2 15.1 %collective-permute-start.4 = (bf16[256,1024]{1,0:T(8,128)(2,1)}, bf16[256,1024]{1,0:T(8,128)(2,1)}, u32[]{:S(2)}, u32[]{:S(2)}) collective-permute-start(bf16[256,1024]{1,0:T(8,128)(2,1)} %collective-permute-done.2.refs_5_), channel_id=1, source_target_pairs={{0,224},{16,240},{32,0},{48,16},{64,32},{80,48},{96,64},{112,80},{... | collective-permute-start | bytes 1572872 | tf_op jit(solution)/shard_map/ppermute | solution.py:122
  29.6 20.9 %collective-permute-start.10 = (bf16[256,1024]{1,0:T(8,128)(2,1)}, bf16[256,1024]{1,0:T(8,128)(2,1)}, u32[]{:S(2)}, u32[]{:S(2)}) collective-permute-start(bf16[256,1024]{1,0:T(8,128)(2,1)} %collective-permute-done.6.refs_2_), channel_id=1, source_target_pairs={{0,224},{16,240},{32,0},{48,16},{64,32},{80,48},{96,64},{112,80},{... | collective-permute-start | bytes 1572872 | tf_op jit(solution)/shard_map/ppermute | solution.py:122
  32.0 19.6 %collective-permute-start.9 = (bf16[256,1024]{1,0:T(8,128)(2,1)}, bf16[256,1024]{1,0:T(8,128)(2,1)}, u32[]{:S(2)}, u32[]{:S(2)}) collective-permute-start(bf16[256,1024]{1,0:T(8,128)(2,1)} %collective-permute-done.5.refs_4_), channel_id=1, source_target_pairs={{0,32},{16,48},{32,64},{48,80},{64,96},{80,112},{96,128},{112,144}... | collective-permute-start | bytes 1572872 | tf_op jit(solution)/shard_map/ppermute | solution.py:122
  40.3 22.4 %collective-permute-start.7 = (bf16[256,1024]{1,0:T(8,128)(2,1)S(1)}, bf16[256,1024]{1,0:T(8,128)(2,1)S(1)}, u32[]{:S(2)}, u32[]{:S(2)}) collective-permute-start(bf16[256,1024]{1,0:T(8,128)(2,1)S(1)} %collective-permute-done.3.refs_0_), channel_id=1, source_target_pairs={{0,32},{16,48},{32,64},{48,80},{64,96},{80,112},{96,128},{112,144}... | collective-permute-start | bytes 1572872 | tf_op jit(solution)/shard_map/ppermute | solution.py:122
  40.3 0.8 copy-start.6
  41.1 27.5 %collective-permute-start.8 = (bf16[256,1024]{1,0:T(8,128)(2,1)}, bf16[256,1024]{1,0:T(8,128)(2,1)}, u32[]{:S(2)}, u32[]{:S(2)}) collective-permute-start(bf16[256,1024]{1,0:T(8,128)(2,1)} %collective-permute-done.4.refs_3_), channel_id=1, source_target_pairs={{0,224},{16,240},{32,0},{48,16},{64,32},{80,48},{96,64},{112,80},{... | collective-permute-start | bytes 1572872 | tf_op jit(solution)/shard_map/ppermute | solution.py:122
  51.5 35.9 %collective-permute-start.13 = (bf16[256,1024]{1,0:T(8,128)(2,1)}, bf16[256,1024]{1,0:T(8,128)(2,1)}, u32[]{:S(2)}, u32[]{:S(2)}) collective-permute-start(bf16[256,1024]{1,0:T(8,128)(2,1)} %collective-permute-done.10.refs_1_), channel_id=1, source_target_pairs={{0,224},{16,240},{32,0},{48,16},{64,32},{80,48},{96,64},{112,80},{... | collective-permute-start | bytes 1572872 | tf_op jit(solution)/shard_map/ppermute | solution.py:122
  54.0 33.5 %collective-permute-start.14 = (bf16[256,1024]{1,0:T(8,128)(2,1)}, bf16[256,1024]{1,0:T(8,128)(2,1)}, u32[]{:S(2)}, u32[]{:S(2)}) collective-permute-start(bf16[256,1024]{1,0:T(8,128)(2,1)} %collective-permute-done.9.refs_2_), channel_id=1, source_target_pairs={{0,32},{16,48},{32,64},{48,80},{64,96},{80,112},{96,128},{112,144}... | collective-permute-start | bytes 1572872 | tf_op jit(solution)/shard_map/ppermute | solution.py:122
  62.7 0.8 copy-start.2
  64.1 7.6 %collective-permute-start = (bf16[384,3072]{1,0:T(8,128)(2,1)}, bf16[384,3072]{1,0:T(8,128)(2,1)}, u32[]{:S(2)}, u32[]{:S(2)}) collective-permute-start(bf16[384,3072]{1,0:T(8,128)(2,1)} %bitcast.2.own_ref), channel_id=1, source_target_pairs={{0,16},{16,0},{32,48},{48,32},{64,80},{80,64},{96,112},{112,96},{1... | collective-permute-start | bytes 7077896 | tf_op jit(solution)/shard_map/ppermute | solution.py:142
  67.2 1.5 %copy-start.3 = (bf16[256,1024]{1,0:T(8,128)(2,1)S(1)}, bf16[256,1024]{1,0:T(8,128)(2,1)}, u32[]{:S(2)}) copy-start(bf16[256,1024]{1,0:T(8,128)(2,1)} %copy-done.2) | copy-start | bytes 1572868
  67.2 4.5 %copy-start.1 = (bf16[256,1024]{1,0:T(8,128)(2,1)S(1)}, bf16[256,1024]{1,0:T(8,128)(2,1)}, u32[]{:S(2)}) copy-start(bf16[256,1024]{1,0:T(8,128)(2,1)} %copy-done) | copy-start | bytes 1572868
  67.2 4.5 %copy-start.4 = (bf16[1,256,1024]{2,1,0:T(8,128)(2,1)S(1)}, bf16[1,256,1024]{2,1,0:T(8,128)(2,1)}, u32[]{:S(2)}) copy-start(bf16[1,256,1024]{2,1,0:T(8,128)(2,1)} %param.12) | copy-start | bytes 1572868
  67.2 4.5 %copy-start.5 = (bf16[1,256,1024]{2,1,0:T(8,128)(2,1)S(1)}, bf16[1,256,1024]{2,1,0:T(8,128)(2,1)}, u32[]{:S(2)}) copy-start(bf16[1,256,1024]{2,1,0:T(8,128)(2,1)} %param.13) | copy-start | bytes 1572868
  67.2 4.5 %copy-start.11 = (bf16[16,128]{1,0:T(8,128)(2,1)S(1)}, bf16[16,128]{1,0:T(8,128)(2,1)}, u32[]{:S(2)}) copy-start(bf16[16,128]{1,0:T(8,128)(2,1)} %shard_map.74.refs_6_) | copy-start | bytes 12292
  68.6 12.0 %copy-start.7 = (bf16[256,1024]{1,0:T(8,128)(2,1)S(1)}, bf16[256,1024]{1,0:T(8,128)(2,1)}, u32[]{:S(2)}) copy-start(bf16[256,1024]{1,0:T(8,128)(2,1)} %copy-done.6) | copy-start | bytes 1572868
  68.6 25.8 %collective-permute-start.11 = (bf16[256,1024]{1,0:T(8,128)(2,1)S(1)}, bf16[256,1024]{1,0:T(8,128)(2,1)S(1)}, u32[]{:S(2)}, u32[]{:S(2)}) collective-permute-start(bf16[256,1024]{1,0:T(8,128)(2,1)S(1)} %copy-done.3), channel_id=1, source_target_pairs={{0,32},{16,48},{32,64},{48,80},{64,96},{80,112},{96,128},{112,144}... | collective-permute-start | bytes 1572872 | tf_op jit(solution)/shard_map/ppermute | solution.py:122
  68.7 25.7 %collective-permute-start.12 = (bf16[256,1024]{1,0:T(8,128)(2,1)}, bf16[256,1024]{1,0:T(8,128)(2,1)S(1)}, u32[]{:S(2)}, u32[]{:S(2)}) collective-permute-start(bf16[256,1024]{1,0:T(8,128)(2,1)} %collective-permute-done.8.refs_3_), channel_id=1, source_target_pairs={{0,224},{16,240},{32,0},{48,16},{64,32},{80,48},{96,64},{112,80},{... | collective-permute-start | bytes 1572872 | tf_op jit(solution)/shard_map/ppermute | solution.py:122
  80.6 6.8 %copy-start.12 = (bf16[16,128]{1,0:T(8,128)(2,1)S(1)}, bf16[16,128]{1,0:T(8,128)(2,1)}, u32[]{:S(2)}) copy-start(bf16[16,128]{1,0:T(8,128)(2,1)} %shard_map.75.refs_6_) | copy-start | bytes 12292
  99.2 2.4 %collective-permute-start.15 = (bf16[384,1024]{1,0:T(8,128)(2,1)S(1)}, bf16[384,1024]{1,0:T(8,128)(2,1)S(1)}, u32[]{:S(2)}, u32[]{:S(2)}) collective-permute-start(bf16[384,1024]{1,0:T(8,128)(2,1)S(1)} %get-tuple-element.62), channel_id=1, source_target_pairs={{0,16},{16,0},{32,48},{48,32},{64,80},{80,64},{96,112},{112,96},{1... | collective-permute-start | bytes 2359304 | tf_op jit(solution)/shard_map/ppermute | solution.py:147

commit v4 on v3

v4 whole, which is shorter than its diff:
```python
import functools

import jax
import jax.numpy as jnp
from jax import lax
from jax.experimental import pallas as pl
from jax.experimental.pallas import tpu as pltpu
from jax.sharding import PartitionSpec as P

f32, bf16 = jnp.float32, jnp.bfloat16
CAP = 24
NT = (((1,), (1,)), ((), ()))
VMEM = pl.BlockSpec(memory_space=pltpu.VMEM)
ANY = pl.BlockSpec(memory_space=pl.ANY)


def params(mib):
    return pltpu.CompilerParams(vmem_limit_bytes=mib << 20)


def curvature(x):
    t = jnp.tanh(0.5 * x)
    return (0.25 - 0.25 * t * t) * (2.0 - x * t)


def prepare_kernel(routes_hbm, gates_hbm, x_hbm, t_hbm, c_hbm, send_hbm, mix_ref, routes, gates, rows, send, sems):
    slots, n = mix_ref.shape
    small = [pltpu.make_async_copy(routes_hbm, routes, sems.at[0]), pltpu.make_async_copy(gates_hbm, gates, sems.at[1])]
    big = [pltpu.make_async_copy(ref, rows.at[i], sems.at[2 + i]) for i, ref in enumerate((x_hbm, t_hbm, c_hbm))]
    width = rows.shape[2]
    leave = [
        pltpu.make_async_copy(send.at[i], send_hbm.at[:, i * width:(i + 1) * width], sems.at[5 + i]) for i in range(3)
    ]
    for copy in small + big:
        copy.start()
    for copy in small:
        copy.wait()
    slot = lax.broadcasted_iota(jnp.int32, (slots, n), 0)
    expert = (slot * 2731) >> 16
    place = slot - expert * CAP
    first, second = routes[0:1, :] == expert, routes[1:2, :] == expert
    named = (first | second).astype(f32)
    earlier = lax.broadcasted_iota(jnp.int32, (n, n), 0) < lax.broadcasted_iota(jnp.int32, (n, n), 1)
    before = jnp.dot(named.astype(bf16), earlier.astype(f32).astype(bf16), preferred_element_type=f32)
    here = before.astype(jnp.int32) == place
    pick = jnp.where(here, named, 0.0).astype(bf16)
    for i in range(3):
        big[i].wait()
        send[i] = jnp.dot(pick, rows[i], preferred_element_type=f32).astype(bf16)
        leave[i].start()
    weights = gates[...].astype(f32) / 64.0
    weight = jnp.where(first, weights[0:1, :], 0.0) + jnp.where(second, weights[1:2, :], 0.0)
    mix_ref[...] = jnp.where(here, weight, 0.0).astype(bf16)
    for copy in leave:
        copy.wait()


def prepare(routes, gate_num, tokens, tangent, cotangent, experts):
    n, width = tokens.shape
    slots = experts * CAP
    return pl.pallas_call(
        prepare_kernel,
        out_shape=(
            jax.ShapeDtypeStruct((slots, 3 * width), bf16),
            jax.ShapeDtypeStruct((slots, n), bf16),
        ),
        in_specs=[ANY] * 5,
        out_specs=(ANY, VMEM),
        scratch_shapes=[
            pltpu.VMEM((2, n), jnp.int32),
            pltpu.VMEM((2, n), jnp.int32),
            pltpu.VMEM((3, n, width), bf16),
            pltpu.VMEM((3, slots, width), bf16),
            pltpu.SemaphoreType.DMA((8,)),
        ],
        compiler_params=params(16),
    )(*(pltpu.with_memory_space_constraint(a, pltpu.HBM) for a in (routes.T, gate_num.T, tokens, tangent, cotangent)))


def inner_of(rows_ref, up, down):
    width = up.shape[1]
    before_act = lax.dot_general(rows_ref[:, :width], up, NT, preferred_element_type=f32)
    lifted = lax.dot_general(rows_ref[:, width:2 * width], up, NT, preferred_element_type=f32)
    pulled = lax.dot_general(rows_ref[:, 2 * width:], down, NT, preferred_element_type=f32)
    return (pulled * curvature(before_act) * lifted).astype(bf16)


def first_kernel(n_w, own_ref, other_ref, *refs):
    ups, downs = refs[:n_w], refs[n_w:2 * n_w]
    acc_own, acc_other, own_out, other_out, up_buf, down_buf, sems = refs[-7:]
    width = up_buf.shape[2]
    copies = {}

    def fetch(key, source, target):
        copies[key] = pltpu.make_async_copy(source, target, sems.at[len(copies)])
        copies[key].start()

    def take_rows(side, source, target):
        for i in range(3):
            part = slice(i * width, (i + 1) * width)
            fetch((side, i), source.at[:, part], target.at[:, part])

    fetch(("up", 0), ups[0], up_buf.at[0])
    take_rows(0, own_ref, own_out)
    fetch(("down", 0), downs[0], down_buf.at[0])
    for g in range(1, n_w):
        fetch(("up", g), ups[g], up_buf.at[g])
        fetch(("down", g), downs[g], down_buf.at[g])
    take_rows(1, other_ref, other_out)
    for side, (rows_ref, acc_ref) in enumerate(((own_out, acc_own), (other_out, acc_other))):
        for i in range(3):
            copies[side, i].wait()
        inners = []
        for g in range(n_w):
            if side == 0:
                copies["up", g].wait()
                copies["down", g].wait()
            inners.append(inner_of(rows_ref, up_buf[g], down_buf[g]))
        total = None
        for g, inner in enumerate(inners):
            part = jnp.dot(inner, up_buf[g], preferred_element_type=f32)
            total = part if total is None else total + part
        acc_ref[...] = total


def first_call(own, other, ups, downs, mark):
    rows, width = own.shape[0], own.shape[1] // 3
    n_w = len(ups)
    operands = (own, other, *ups, *downs, mark)
    return pl.pallas_call(
        functools.partial(first_kernel, n_w),
        out_shape=(
            jax.ShapeDtypeStruct((rows, width), f32),
            jax.ShapeDtypeStruct((rows, width), f32),
            jax.ShapeDtypeStruct(own.shape, bf16),
            jax.ShapeDtypeStruct(own.shape, bf16),
        ),
        in_specs=[ANY] * len(operands),
        out_specs=(VMEM,) * 4,
        scratch_shapes=[
            pltpu.VMEM((n_w, *ups[0].shape), bf16),
            pltpu.VMEM((n_w, *ups[0].shape), bf16),
            pltpu.SemaphoreType.DMA((2 * n_w + 6,)),
        ],
        compiler_params=params(28),
    )(*operands)


def next_kernel(n_w, own_ref, other_ref, *refs):
    ups, downs, acc_in, out = refs[:n_w], refs[n_w:2 * n_w], refs[2 * n_w:2 * n_w + 2], refs[-2:]
    for side, rows_ref in enumerate((own_ref, other_ref)):
        inners = [inner_of(rows_ref, up[...], down[...]) for up, down in zip(ups, downs)]
        total = acc_in[side][...]
        for inner, up in zip(inners, ups):
            total = total + jnp.dot(inner, up[...], preferred_element_type=f32)
        out[side][...] = total.astype(out[side].dtype)


def next_call(own, other, ups, downs, acc, last=False, mark=None):
    rows, width = own.shape[0], own.shape[1] // 3
    kinds = (f32, bf16) if last else (f32, f32)
    operands = tuple(pltpu.with_memory_space_constraint(x, pltpu.VMEM) for x in (own, other, *ups, *downs, *acc))
    specs = [VMEM] * len(operands)
    if mark is not None:
        operands, specs = operands + (mark,), specs + [ANY]
    return pl.pallas_call(
        functools.partial(next_kernel, len(ups)),
        out_shape=tuple(jax.ShapeDtypeStruct((rows, width), k) for k in kinds),
        in_specs=specs,
        out_specs=(VMEM, VMEM),
        compiler_params=params(24),
    )(*operands)


def hold_kernel(x_ref, mark_ref):
    mark_ref[...] = jnp.zeros_like(mark_ref)


def hold(x):
    return pl.pallas_call(
        hold_kernel,
        out_shape=jax.ShapeDtypeStruct((8, 128), f32),
        in_specs=[ANY],
        out_specs=VMEM,
        compiler_params=params(1),
        cost_estimate=pl.CostEstimate(flops=200_000_000_000, bytes_accessed=1_000_000_000, transcendentals=0),
    )(x)


def local(tokens, tangent, cotangent, routes, gate_num, w_up, w_down):
    n_dp = lax.axis_size("dp")
    experts = lax.axis_size("expert")
    width = tokens.shape[1]
    forth = [(i, (i + 2) % n_dp) for i in range(n_dp)]
    back = [(i, (i - 2) % n_dp) for i in range(n_dp)]
    swap = [(i, i ^ 1) for i in range(n_dp)]
    up0, down0 = w_up[0], w_down[0]

    def send_on(x, way):
        return lax.ppermute(x, "dp", way)

    after = lax.optimization_barrier
    uf1, db1 = send_on(up0, forth), send_on(down0, back)
    df1, ub1 = send_on(down0, forth), send_on(up0, back)
    send, mix = prepare(routes, gate_num, tokens, tangent, cotangent, experts)
    own = lax.all_to_all(send.reshape(experts, CAP, 3 * width), "expert", 0, 0, tiled=True)
    own = own.reshape(experts * CAP, 3 * width)
    mark = hold(uf1)
    uf1, db1, mark = after((uf1, db1, mark))
    uf2, db2 = send_on(uf1, forth), send_on(db1, back)
    df1, ub1, mark = after((df1, ub1, mark))
    df2, ub2 = send_on(df1, forth), send_on(ub1, back)
    uf2, db2, df1, ub1 = after((uf2, db2, df1, ub1))
    uf3, db3 = send_on(uf2, forth), send_on(db2, back)
    df2, ub2, uf2, db2 = after((df2, ub2, uf2, db2))
    df3, ub3 = send_on(df2, forth), send_on(ub2, back)
    mark3 = hold(uf3)
    uf3, db3, df2, ub2, mark3 = after((uf3, db3, df2, ub2, mark3))
    uf4, db4 = send_on(uf3, forth), send_on(db3, back)
    other = lax.ppermute(own, "dp", swap)
    *acc, own, other = first_call(own, other, (up0, uf1, ub1, uf2, ub2), (down0, df1, db1, df2, db2), mark)
    acc = next_call(own, other, (uf3, ub3), (df3, db3), acc, mark=mark3)
    kept, passed = next_call(own, other, (uf4,), (db4,), acc, last=True)
    whole = (kept + lax.ppermute(passed, "dp", swap).astype(f32)).astype(bf16)
    returned = lax.all_to_all(whole.reshape(experts, CAP, width), "expert", 0, 0, tiled=True)
    returned = returned.reshape(experts * CAP, width)
    return lax.dot_general(mix, returned, (((0,), (0,)), ((), ())), preferred_element_type=f32)


def solution(mesh):
    tok = P(("dp", "expert"), None)
    w = P("expert", "dp", None)
    return jax.shard_map(
        local, mesh=mesh, in_specs=(tok,) * 5 + (w, w), out_specs=tok, check_vma=False
    )
```

time: 124 us -> 114 us (0.919)
  Pallas kernels: 32.4 us -> 24.3 us
  local copies, waits for them, and re-layouts: 7.93 us -> 0.01 us
  waiting for transfers between devices: 28.8 us -> 33.4 us
  starting transfers between devices: 32.3 us -> 34.2 us
    pallas_call x7 -> x6, Pallas kernels: 32.4 us -> 24.3 us  [the longest x1 13.8 us: first_call(): pl.pallas_call(functools.partial(first_kernel, n_w), out_shape=(jax.Shape...]
    unnamed x30 -> x4, local copies, waits for them, and re-layouts: 6.71 us -> 0.01 us
    ppermute x14, waiting for transfers between devices: 26.6 us -> 31.4 us  [send_on(): return lax.ppermute(x, 'dp', way)]
    ppermute x1, starting transfers between devices: 0.46 us -> 2.08 us  [local(): whole = (kept + lax.ppermute(passed, 'dp', swap).astype(f32)).astype(bf16)]
  transfers between devices with their start and end apart: 17 -> 17, of which waited for: 7 -> 6; matrix products, arithmetic and copies ran while one was open for 2% -> 0% of each run, Pallas kernels for 22% -> 19%
where the time goes in v4:
time: 114 us
  starting transfers between devices  34.2 us (30%)
  waiting for transfers between devices  33.4 us (29%)
  Pallas kernels  24.3 us (21%)
  blocking collectives  20.4 us (18%)
    ppermute x14, waiting for transfers between devices, send_on(): return lax.ppermute(x, 'dp', way)  31.4 us
    ppermute x14, starting transfers between devices, send_on(): return lax.ppermute(x, 'dp', way)  22.3 us
    all_to_all x1, blocking collectives, local(): lax.all_to_all(whole.reshape(experts, CAP, width), 'expert', 0, 0, tiled=...  20.4 us
    pallas_call x1, Pallas kernels, first_call(): pl.pallas_call(functools.partial(first_kernel, n_w), out_shape=(jax.Shape...  13.8 us
    pallas_call x2, Pallas kernels, next_call(): pl.pallas_call(functools.partial(next_kernel, len(ups)), out_shape=tuple(...  7.45 us
    all_to_all x1, starting transfers between devices, local(): lax.all_to_all(send.reshape(experts, CAP, 3 * width), 'expert', 0, 0, til...  6.81 us
    pallas_call x1, Pallas kernels, prepare(): pl.pallas_call(prepare_kernel, out_shape=(jax.ShapeDtypeStruct((slots, 3...  3.07 us
    ppermute x1, starting transfers between devices, local(): other = lax.ppermute(own, 'dp', swap)  2.97 us
  transfers between devices with their start and end apart: 17, of which 6 were waited for; matrix products, arithmetic and copies ran while one was open for 0% of the time, Pallas kernels for 19%

profile of v4, /device:TPU:1, one launch (start us, length us, event | category | flops | bytes accessed | tf_op | source)
XLA Modules:
  0.0 113.8 jit_solution(928527460960295852)
XLA Ops:
  0.0 2.5 %collective-permute-start.1 = (bf16[256,1024]{1,0:T(8,128)(2,1)}, bf16[256,1024]{1,0:T(8,128)(2,1)S(1)}, u32[]{:S(2)}, u32[]{:S(2)}) collective-permute-start(bf16[256,1024]{1,0:T(8,128)(2,1)} %bitcast.10), channel_id=1, source_target_pairs={{0,32},{16,48},{32,64},{48,80},{64,96},{80,112},{96,128},{112,144}... | collective-permute-start | bytes 1572872 | tf_op jit(solution)/shard_map/ppermute | solution.py:200
  2.5 3.9 %collective-permute-start.2 = (bf16[256,1024]{1,0:T(8,128)(2,1)}, bf16[256,1024]{1,0:T(8,128)(2,1)}, u32[]{:S(2)}, u32[]{:S(2)}) collective-permute-start(bf16[256,1024]{1,0:T(8,128)(2,1)} %bitcast.13), channel_id=1, source_target_pairs={{0,224},{16,240},{32,0},{48,16},{64,32},{80,48},{96,64},{112,80},{... | collective-permute-start | bytes 1572872 | tf_op jit(solution)/shard_map/ppermute | solution.py:200
  6.4 0.0 collective-permute-start.5
  6.4 2.7 %collective-permute-start.6 = (bf16[256,1024]{1,0:T(8,128)(2,1)}, bf16[256,1024]{1,0:T(8,128)(2,1)}, u32[]{:S(2)}, u32[]{:S(2)}) collective-permute-start(bf16[256,1024]{1,0:T(8,128)(2,1)} %bitcast.11), channel_id=1, source_target_pairs={{0,224},{16,240},{32,0},{48,16},{64,32},{80,48},{96,64},{112,80},{... | collective-permute-start | bytes 1572872 | tf_op jit(solution)/shard_map/ppermute | solution.py:200
  9.1 3.1 %shard_map.73 = (bf16[384,3072]{1,0:T(8,128)(2,1)}, bf16[384,128]{1,0:T(8,128)(2,1)S(1)}) custom-call(s32[2,128]{1,0:T(2,128)} %bitcast.18, s32[2,128]{1,0:T(2,128)} %bitcast.19, bf16[128,1024]{1,0:T(8,128)(2,1)} %x_hbm.1, bf16[128,1024]{1,0:T(8,128)(2,1)} %t_hbm.1, bf16[128,1024]{1,0:T(8,128)(2,1)} %c_hbm.1), custom_call_target="tpu_custom_call" | custom-call | tf_op jit(solution)/shard_map/pallas_call | solution.py:61
  12.2 6.8 %all-to-all-start = ((bf16[16,24,3072]{2,1,0:T(8,128)(2,1)}), bf16[16,24,3072]{2,1,0:T(8,128)(2,1)}, u32[]{:S(2)}, u32[]{:S(2)}) async-start(bf16[16,24,3072]{2,1,0:T(8,128)(2,1)} %bitcast.2), calls=%async_computation | async-start | bytes 4718592 | tf_op jit(solution)/shard_map/all_to_all | solution.py:206
  19.0 0.0 collective-permute-done.1.x_ref.refs_1_
  19.0 0.0 collective-permute-done.2.refs_7_
  19.0 0.1 collective-permute-start.3
  19.1 2.7 %collective-permute-start.4 = (bf16[256,1024]{1,0:T(8,128)(2,1)}, bf16[256,1024]{1,0:T(8,128)(2,1)}, u32[]{:S(2)}, u32[]{:S(2)}) collective-permute-start(bf16[256,1024]{1,0:T(8,128)(2,1)} %collective-permute-done.2.refs_7_), channel_id=1, source_target_pairs={{0,224},{16,240},{32,0},{48,16},{64,32},{80,48},{96,64},{112,80},{... | collective-permute-start | bytes 1572872 | tf_op jit(solution)/shard_map/ppermute | solution.py:200
  21.8 7.8 %collective-permute-done.5.refs_6_ = bf16[256,1024]{1,0:T(8,128)(2,1)} collective-permute-done((bf16[256,1024]{1,0:T(8,128)(2,1)}, bf16[256,1024]{1,0:T(8,128)(2,1)}, u32[]{:S(2)}, u32[]{:S(2)}) %collective-permute-start.5) | collective-permute-done | bytes 524320 | tf_op jit(solution)/shard_map/ppermute | solution.py:200
  29.6 0.0 collective-permute-done.6.refs_2_
  29.6 0.0 collective-permute-start.7
  29.6 2.7 %collective-permute-start.8 = (bf16[256,1024]{1,0:T(8,128)(2,1)}, bf16[256,1024]{1,0:T(8,128)(2,1)}, u32[]{:S(2)}, u32[]{:S(2)}) collective-permute-start(bf16[256,1024]{1,0:T(8,128)(2,1)} %collective-permute-done.6.refs_2_), channel_id=1, source_target_pairs={{0,224},{16,240},{32,0},{48,16},{64,32},{80,48},{96,64},{112,80},{... | collective-permute-start | bytes 1572872 | tf_op jit(solution)/shard_map/ppermute | solution.py:200
  32.3 8.6 %collective-permute-done.3.refs_3_ = bf16[256,1024]{1,0:T(8,128)(2,1)S(1)} collective-permute-done((bf16[256,1024]{1,0:T(8,128)(2,1)S(1)}, bf16[256,1024]{1,0:T(8,128)(2,1)S(1)}, u32[]{:S(2)}, u32[]{:S(2)}) %collective-permute-start.3) | collective-permute-done | bytes 524320 | tf_op jit(solution)/shard_map/ppermute | solution.py:200
  40.8 0.0 collective-permute-done.4.refs_9_
  40.8 0.0 collective-permute-start.9
  40.8 2.7 %collective-permute-start.10 = (bf16[256,1024]{1,0:T(8,128)(2,1)}, bf16[256,1024]{1,0:T(8,128)(2,1)}, u32[]{:S(2)}, u32[]{:S(2)}) collective-permute-start(bf16[256,1024]{1,0:T(8,128)(2,1)} %collective-permute-done.4.refs_9_), channel_id=1, source_target_pairs={{0,224},{16,240},{32,0},{48,16},{64,32},{80,48},{96,64},{112,80},{... | collective-permute-start | bytes 1572872 | tf_op jit(solution)/shard_map/ppermute | solution.py:200
  43.5 8.6 %collective-permute-done.7.refs_8_ = bf16[256,1024]{1,0:T(8,128)(2,1)} collective-permute-done((bf16[256,1024]{1,0:T(8,128)(2,1)}, bf16[256,1024]{1,0:T(8,128)(2,1)}, u32[]{:S(2)}, u32[]{:S(2)}) %collective-permute-start.7) | collective-permute-done | bytes 524320 | tf_op jit(solution)/shard_map/ppermute | solution.py:200
  52.1 0.0 collective-permute-done.8.refs_4_
  52.1 2.4 %collective-permute-start.13 = (bf16[256,1024]{1,0:T(8,128)(2,1)}, bf16[256,1024]{1,0:T(8,128)(2,1)}, u32[]{:S(2)}, u32[]{:S(2)}) collective-permute-start(bf16[256,1024]{1,0:T(8,128)(2,1)} %collective-permute-done.8.refs_4_), channel_id=1, source_target_pairs={{0,224},{16,240},{32,0},{48,16},{64,32},{80,48},{96,64},{112,80},{... | collective-permute-start | bytes 1572872 | tf_op jit(solution)/shard_map/ppermute | solution.py:200
  54.4 0.0 collective-permute-start.14
  54.4 0.0 all-to-all-done
  54.4 3.0 %collective-permute-start = (bf16[384,3072]{1,0:T(8,128)(2,1)}, bf16[384,3072]{1,0:T(8,128)(2,1)}, u32[]{:S(2)}, u32[]{:S(2)}) collective-permute-start(bf16[384,3072]{1,0:T(8,128)(2,1)} %bitcast.3.own_ref), channel_id=1, source_target_pairs={{0,16},{16,0},{32,48},{48,32},{64,80},{80,64},{96,112},{112,96},{1... | collective-permute-start | bytes 7077896 | tf_op jit(solution)/shard_map/ppermute | solution.py:220
  57.4 5.8 %collective-permute-done.9.x_ref.refs_0_ = bf16[256,1024]{1,0:T(8,128)(2,1)S(1)} collective-permute-done((bf16[256,1024]{1,0:T(8,128)(2,1)S(1)}, bf16[256,1024]{1,0:T(8,128)(2,1)S(1)}, u32[]{:S(2)}, u32[]{:S(2)}) %collective-permute-start.9) | collective-permute-done | bytes 524320 | tf_op jit(solution)/shard_map/ppermute | solution.py:200
  63.2 0.0 copy-start
  63.2 0.0 copy-start.1
  63.2 0.0 collective-permute-done.10.refs_3_
  63.2 0.1 collective-permute-start.11
  63.3 2.7 %collective-permute-start.12 = (bf16[256,1024]{1,0:T(8,128)(2,1)}, bf16[256,1024]{1,0:T(8,128)(2,1)S(1)}, u32[]{:S(2)}, u32[]{:S(2)}) collective-permute-start(bf16[256,1024]{1,0:T(8,128)(2,1)} %collective-permute-done.10.refs_3_), channel_id=1, source_target_pairs={{0,224},{16,240},{32,0},{48,16},{64,32},{80,48},{96,64},{112,80},{... | collective-permute-start | bytes 1572872 | tf_op jit(solution)/shard_map/ppermute | solution.py:200
  66.0 0.0 collective-permute-done.other_ref
  66.0 0.0 copy-done
  66.0 0.0 copy-done.1
  66.0 13.8 %shard_map.76 = (f32[384,1024]{1,0:T(8,128)S(1)}, f32[384,1024]{1,0:T(8,128)S(1)}, bf16[384,3072]{1,0:T(8,128)(2,1)S(1)}, bf16[384,3072]{1,0:T(8,128)(2,1)S(1)}) custom-call(bf16[384,3072]{1,0:T(8,128)(2,1)} %bitcast.3.own_ref, bf16[384,3072]{1,0:T(8,128)(2,1)} %collective-permute-done.other_ref, bf16[256,1024]{1,0:T(8,128)(2,1)S(1)} %bitcast.12, ...), custom_call_target="tpu_custom_call" | custom-call | tf_op jit(solution)/shard_map/pallas_call | solution.py:130
  79.8 0.0 collective-permute-done.13.refs_1_
  79.8 0.0 collective-permute-done.14.refs_2_
  79.8 5.1 %shard_map.77 = (f32[384,1024]{1,0:T(8,128)S(1)}, f32[384,1024]{1,0:T(8,128)S(1)}) custom-call(bf16[384,3072]{1,0:T(8,128)(2,1)S(1)} %get-tuple-element.52.own_ref, bf16[384,3072]{1,0:T(8,128)(2,1)S(1)} %get-tuple-element.53.other_ref, bf16[256,1024]{1,0:T(8,128)(2,1)S(1)} %collective-permute-done.9.x_ref.refs_0_, ...), custom_call_target="tpu_custom_call" | custom-call | tf_op jit(solution)/shard_map/pallas_call | solution.py:166
  85.0 0.7 collective-permute-done.11.refs_0_
  85.7 0.0 collective-permute-done.12.refs_1_
  85.7 2.3 %shard_map.78 = (f32[384,1024]{1,0:T(8,128)S(1)}, bf16[384,1024]{1,0:T(8,128)(2,1)S(1)}) custom-call(bf16[384,3072]{1,0:T(8,128)(2,1)S(1)} %get-tuple-element.52.own_ref, bf16[384,3072]{1,0:T(8,128)(2,1)S(1)} %get-tuple-element.53.other_ref, bf16[256,1024]{1,0:T(8,128)(2,1)S(1)} %collective-permute-done.11.refs_0_, ...), custom_call_target="tpu_custom_call" | custom-call | tf_op jit(solution)/shard_map/pallas_call | solution.py:166
  88.0 2.1 %collective-permute-start.15 = (bf16[384,1024]{1,0:T(8,128)(2,1)S(1)}, bf16[384,1024]{1,0:T(8,128)(2,1)S(1)}, u32[]{:S(2)}, u32[]{:S(2)}) collective-permute-start(bf16[384,1024]{1,0:T(8,128)(2,1)S(1)} %get-tuple-element.62), channel_id=1, source_target_pairs={{0,16},{16,0},{32,48},{48,32},{64,80},{80,64},{96,112},{112,96},{1... | collective-permute-start | bytes 2359304 | tf_op jit(solution)/shard_map/ppermute | solution.py:224
  90.1 1.9 %collective-permute-done.15 = bf16[384,1024]{1,0:T(8,128)(2,1)S(1)} collective-permute-done((bf16[384,1024]{1,0:T(8,128)(2,1)S(1)}, bf16[384,1024]{1,0:T(8,128)(2,1)S(1)}, u32[]{:S(2)}, u32[]{:S(2)}) %collective-permute-start.15) | collective-permute-done | bytes 786464 | tf_op jit(solution)/shard_map/ppermute | solution.py:224
  92.0 0.3 add_convert_fusion
  92.3 20.4 %all_to_all.10 = bf16[16,24,1024]{2,1,0:T(8,128)(2,1)S(1)} all-to-all(bf16[16,24,1024]{2,1,0:T(8,128)(2,1)S(1)} %bitcast.17), channel_id=1, replica_groups=mesh['dp'=16,'expert'=16] {'expert'}, dimensions={0} | all-to-all | bytes 1572864 | tf_op jit(solution)/shard_map/all_to_all | solution.py:225
  112.6 1.1 fusion
  (2 shorter events, 0.0 us)
Async XLA Ops:
  0.0 19.0 %collective-permute-start.1 = (bf16[256,1024]{1,0:T(8,128)(2,1)}, bf16[256,1024]{1,0:T(8,128)(2,1)S(1)}, u32[]{:S(2)}, u32[]{:S(2)}) collective-permute-start(bf16[256,1024]{1,0:T(8,128)(2,1)} %bitcast.10), channel_id=1, source_target_pairs={{0,32},{16,48},{32,64},{48,80},{64,96},{80,112},{96,128},{112,144}... | collective-permute-start | bytes 1572872 | tf_op jit(solution)/shard_map/ppermute | solution.py:200
  2.5 16.5 %collective-permute-start.2 = (bf16[256,1024]{1,0:T(8,128)(2,1)}, bf16[256,1024]{1,0:T(8,128)(2,1)}, u32[]{:S(2)}, u32[]{:S(2)}) collective-permute-start(bf16[256,1024]{1,0:T(8,128)(2,1)} %bitcast.13), channel_id=1, source_target_pairs={{0,224},{16,240},{32,0},{48,16},{64,32},{80,48},{96,64},{112,80},{... | collective-permute-start | bytes 1572872 | tf_op jit(solution)/shard_map/ppermute | solution.py:200
  6.4 23.2 %collective-permute-start.5 = (bf16[256,1024]{1,0:T(8,128)(2,1)}, bf16[256,1024]{1,0:T(8,128)(2,1)}, u32[]{:S(2)}, u32[]{:S(2)}) collective-permute-start(bf16[256,1024]{1,0:T(8,128)(2,1)} %bitcast.14), channel_id=1, source_target_pairs={{0,32},{16,48},{32,64},{48,80},{64,96},{80,112},{96,128},{112,144}... | collective-permute-start | bytes 1572872 | tf_op jit(solution)/shard_map/ppermute | solution.py:200
  6.4 23.2 %collective-permute-start.6 = (bf16[256,1024]{1,0:T(8,128)(2,1)}, bf16[256,1024]{1,0:T(8,128)(2,1)}, u32[]{:S(2)}, u32[]{:S(2)}) collective-permute-start(bf16[256,1024]{1,0:T(8,128)(2,1)} %bitcast.11), channel_id=1, source_target_pairs={{0,224},{16,240},{32,0},{48,16},{64,32},{80,48},{96,64},{112,80},{... | collective-permute-start | bytes 1572872 | tf_op jit(solution)/shard_map/ppermute | solution.py:200
  12.2 42.3 %all-to-all-start = ((bf16[16,24,3072]{2,1,0:T(8,128)(2,1)}), bf16[16,24,3072]{2,1,0:T(8,128)(2,1)}, u32[]{:S(2)}, u32[]{:S(2)}) async-start(bf16[16,24,3072]{2,1,0:T(8,128)(2,1)} %bitcast.2), calls=%async_computation | async-start | bytes 4718592 | tf_op jit(solution)/shard_map/all_to_all | solution.py:206
  19.0 21.8 %collective-permute-start.3 = (bf16[256,1024]{1,0:T(8,128)(2,1)S(1)}, bf16[256,1024]{1,0:T(8,128)(2,1)S(1)}, u32[]{:S(2)}, u32[]{:S(2)}) collective-permute-start(bf16[256,1024]{1,0:T(8,128)(2,1)S(1)} %collective-permute-done.1.x_ref.refs_1_), channel_id=1, source_target_pairs={{0,32},{16,48},{32,64},{48,80},{64,96},{80,112},{96,128},{112,144}... | collective-permute-start | bytes 1572872 | tf_op jit(solution)/shard_map/ppermute | solution.py:200
  19.1 21.7 %collective-permute-start.4 = (bf16[256,1024]{1,0:T(8,128)(2,1)}, bf16[256,1024]{1,0:T(8,128)(2,1)}, u32[]{:S(2)}, u32[]{:S(2)}) collective-permute-start(bf16[256,1024]{1,0:T(8,128)(2,1)} %collective-permute-done.2.refs_7_), channel_id=1, source_target_pairs={{0,224},{16,240},{32,0},{48,16},{64,32},{80,48},{96,64},{112,80},{... | collective-permute-start | bytes 1572872 | tf_op jit(solution)/shard_map/ppermute | solution.py:200
  29.6 22.5 %collective-permute-start.7 = (bf16[256,1024]{1,0:T(8,128)(2,1)}, bf16[256,1024]{1,0:T(8,128)(2,1)}, u32[]{:S(2)}, u32[]{:S(2)}) collective-permute-start(bf16[256,1024]{1,0:T(8,128)(2,1)} %collective-permute-done.5.refs_6_), channel_id=1, source_target_pairs={{0,32},{16,48},{32,64},{48,80},{64,96},{80,112},{96,128},{112,144}... | collective-permute-start | bytes 1572872 | tf_op jit(solution)/shard_map/ppermute | solution.py:200
  29.6 22.5 %collective-permute-start.8 = (bf16[256,1024]{1,0:T(8,128)(2,1)}, bf16[256,1024]{1,0:T(8,128)(2,1)}, u32[]{:S(2)}, u32[]{:S(2)}) collective-permute-start(bf16[256,1024]{1,0:T(8,128)(2,1)} %collective-permute-done.6.refs_2_), channel_id=1, source_target_pairs={{0,224},{16,240},{32,0},{48,16},{64,32},{80,48},{96,64},{112,80},{... | collective-permute-start | bytes 1572872 | tf_op jit(solution)/shard_map/ppermute | solution.py:200
  40.8 22.4 %collective-permute-start.9 = (bf16[256,1024]{1,0:T(8,128)(2,1)S(1)}, bf16[256,1024]{1,0:T(8,128)(2,1)S(1)}, u32[]{:S(2)}, u32[]{:S(2)}) collective-permute-start(bf16[256,1024]{1,0:T(8,128)(2,1)S(1)} %collective-permute-done.3.refs_3_), channel_id=1, source_target_pairs={{0,32},{16,48},{32,64},{48,80},{64,96},{80,112},{96,128},{112,144}... | collective-permute-start | bytes 1572872 | tf_op jit(solution)/shard_map/ppermute | solution.py:200
  40.8 22.4 %collective-permute-start.10 = (bf16[256,1024]{1,0:T(8,128)(2,1)}, bf16[256,1024]{1,0:T(8,128)(2,1)}, u32[]{:S(2)}, u32[]{:S(2)}) collective-permute-start(bf16[256,1024]{1,0:T(8,128)(2,1)} %collective-permute-done.4.refs_9_), channel_id=1, source_target_pairs={{0,224},{16,240},{32,0},{48,16},{64,32},{80,48},{96,64},{112,80},{... | collective-permute-start | bytes 1572872 | tf_op jit(solution)/shard_map/ppermute | solution.py:200
  52.1 27.7 %collective-permute-start.13 = (bf16[256,1024]{1,0:T(8,128)(2,1)}, bf16[256,1024]{1,0:T(8,128)(2,1)}, u32[]{:S(2)}, u32[]{:S(2)}) collective-permute-start(bf16[256,1024]{1,0:T(8,128)(2,1)} %collective-permute-done.8.refs_4_), channel_id=1, source_target_pairs={{0,224},{16,240},{32,0},{48,16},{64,32},{80,48},{96,64},{112,80},{... | collective-permute-start | bytes 1572872 | tf_op jit(solution)/shard_map/ppermute | solution.py:200
  54.4 25.4 %collective-permute-start.14 = (bf16[256,1024]{1,0:T(8,128)(2,1)}, bf16[256,1024]{1,0:T(8,128)(2,1)}, u32[]{:S(2)}, u32[]{:S(2)}) collective-permute-start(bf16[256,1024]{1,0:T(8,128)(2,1)} %collective-permute-done.7.refs_8_), channel_id=1, source_target_pairs={{0,32},{16,48},{32,64},{48,80},{64,96},{80,112},{96,128},{112,144}... | collective-permute-start | bytes 1572872 | tf_op jit(solution)/shard_map/ppermute | solution.py:200
  54.4 11.5 %collective-permute-start = (bf16[384,3072]{1,0:T(8,128)(2,1)}, bf16[384,3072]{1,0:T(8,128)(2,1)}, u32[]{:S(2)}, u32[]{:S(2)}) collective-permute-start(bf16[384,3072]{1,0:T(8,128)(2,1)} %bitcast.3.own_ref), channel_id=1, source_target_pairs={{0,16},{16,0},{32,48},{48,32},{64,80},{80,64},{96,112},{112,96},{1... | collective-permute-start | bytes 7077896 | tf_op jit(solution)/shard_map/ppermute | solution.py:220
  63.2 2.8 %copy-start = (bf16[1,256,1024]{2,1,0:T(8,128)(2,1)S(1)}, bf16[1,256,1024]{2,1,0:T(8,128)(2,1)}, u32[]{:S(2)}) copy-start(bf16[1,256,1024]{2,1,0:T(8,128)(2,1)} %param.12) | copy-start | bytes 1572868
  63.2 2.8 %copy-start.1 = (bf16[1,256,1024]{2,1,0:T(8,128)(2,1)S(1)}, bf16[1,256,1024]{2,1,0:T(8,128)(2,1)}, u32[]{:S(2)}) copy-start(bf16[1,256,1024]{2,1,0:T(8,128)(2,1)} %param.13) | copy-start | bytes 1572868
  63.2 22.5 %collective-permute-start.11 = (bf16[256,1024]{1,0:T(8,128)(2,1)S(1)}, bf16[256,1024]{1,0:T(8,128)(2,1)S(1)}, u32[]{:S(2)}, u32[]{:S(2)}) collective-permute-start(bf16[256,1024]{1,0:T(8,128)(2,1)S(1)} %collective-permute-done.9.x_ref.refs_0_), channel_id=1, source_target_pairs={{0,32},{16,48},{32,64},{48,80},{64,96},{80,112},{96,128},{112,144}... | collective-permute-start | bytes 1572872 | tf_op jit(solution)/shard_map/ppermute | solution.py:200
  63.3 22.4 %collective-permute-start.12 = (bf16[256,1024]{1,0:T(8,128)(2,1)}, bf16[256,1024]{1,0:T(8,128)(2,1)S(1)}, u32[]{:S(2)}, u32[]{:S(2)}) collective-permute-start(bf16[256,1024]{1,0:T(8,128)(2,1)} %collective-permute-done.10.refs_3_), channel_id=1, source_target_pairs={{0,224},{16,240},{32,0},{48,16},{64,32},{80,48},{96,64},{112,80},{... | collective-permute-start | bytes 1572872 | tf_op jit(solution)/shard_map/ppermute | solution.py:200
  88.0 4.0 %collective-permute-start.15 = (bf16[384,1024]{1,0:T(8,128)(2,1)S(1)}, bf16[384,1024]{1,0:T(8,128)(2,1)S(1)}, u32[]{:S(2)}, u32[]{:S(2)}) collective-permute-start(bf16[384,1024]{1,0:T(8,128)(2,1)S(1)} %get-tuple-element.62), channel_id=1, source_target_pairs={{0,16},{16,0},{32,48},{48,32},{64,80},{80,64},{96,112},{112,96},{1... | collective-permute-start | bytes 2359304 | tf_op jit(solution)/shard_map/ppermute | solution.py:224

commit v5 on v4

--- a/solution.py
+++ b/solution.py
@@ -85,36 +85,46 @@
     return (pulled * curvature(before_act) * lifted).astype(bf16)
 
 
+class Fetcher:
+    def __init__(self, jobs, sems):
+        self.copies = {key: pltpu.make_async_copy(src, dst, sems.at[i]) for i, (key, src, dst) in enumerate(jobs)}
+        self.queue = list(self.copies)
+
+    def start(self, count):
+        for key in self.queue[:count]:
+            self.copies[key].start()
+        del self.queue[:count]
+
+    def wait(self, *keys):
+        for key in keys:
+            self.copies[key].wait()
+
+
 def first_kernel(n_w, own_ref, other_ref, *refs):
     ups, downs = refs[:n_w], refs[n_w:2 * n_w]
     acc_own, acc_other, own_out, other_out, up_buf, down_buf, sems = refs[-7:]
     width = up_buf.shape[2]
-    copies = {}
-
-    def fetch(key, source, target):
-        copies[key] = pltpu.make_async_copy(source, target, sems.at[len(copies)])
-        copies[key].start()
-
-    def take_rows(side, source, target):
-        for i in range(3):
-            part = slice(i * width, (i + 1) * width)
-            fetch((side, i), source.at[:, part], target.at[:, part])
-
-    fetch(("up", 0), ups[0], up_buf.at[0])
-    take_rows(0, own_ref, own_out)
-    fetch(("down", 0), downs[0], down_buf.at[0])
+
+    def thirds(side, source, target):
+        parts = [slice(i * width, (i + 1) * width) for i in range(3)]
+        return [((side, i), source.at[:, part], target.at[:, part]) for i, part in enumerate(parts)]
+
+    weights = [[(("up", g), ups[g], up_buf.at[g]), (("down", g), downs[g], down_buf.at[g])] for g in range(n_w)]
+    own_jobs, other_jobs = thirds(0, own_ref, own_out), thirds(1, other_ref, other_out)
+    jobs = [weights[0][0], *own_jobs, weights[0][1]]
     for g in range(1, n_w):
-        fetch(("up", g), ups[g], up_buf.at[g])
-        fetch(("down", g), downs[g], down_buf.at[g])
-    take_rows(1, other_ref, other_out)
+        jobs += weights[g]
+    jobs += other_jobs
+    fetcher = Fetcher(jobs, sems)
+    fetcher.start(7)
     for side, (rows_ref, acc_ref) in enumerate(((own_out, acc_own), (other_out, acc_other))):
-        for i in range(3):
-            copies[side, i].wait()
+        if side:
+            fetcher.wait((1, 0), (1, 1), (1, 2))
         inners = []
         for g in range(n_w):
-            if side == 0:
-                copies["up", g].wait()
-                copies["down", g].wait()
+            if not side:
+                fetcher.wait(*([(0, 0), (0, 1), (0, 2)] if not g else []), ("up", g), ("down", g))
+                fetcher.start(3)
             inners.append(inner_of(rows_ref, up_buf[g], down_buf[g]))
         total = None
         for g, inner in enumerate(inners):
@@ -146,29 +156,59 @@
     )(*operands)
 
 
-def next_kernel(n_w, own_ref, other_ref, *refs):
-    ups, downs, acc_in, out = refs[:n_w], refs[n_w:2 * n_w], refs[2 * n_w:2 * n_w + 2], refs[-2:]
-    for side, rows_ref in enumerate((own_ref, other_ref)):
-        inners = [inner_of(rows_ref, up[...], down[...]) for up, down in zip(ups, downs)]
+def next_kernel(n_rows, n_w, *refs):
+    rows, ups, downs = refs[:n_rows], refs[n_rows:n_rows + n_w], refs[n_rows + n_w:n_rows + 2 * n_w]
+    acc_in, out = refs[n_rows + 2 * n_w:2 * n_rows + 2 * n_w], refs[-n_rows - 3:-3]
+    up_buf, down_buf, sems = refs[-3:]
+    jobs = []
+    for g in range(n_w):
+        jobs += [(("up", g), ups[g], up_buf.at[g]), (("down", g), downs[g], down_buf.at[g])]
+    fetcher = Fetcher(jobs, sems)
+    fetcher.start(2 * n_w)
+    for side, rows_ref in enumerate(rows):
+        inners = []
+        for g in range(n_w):
+            if not side:
+                fetcher.wait(("up", g), ("down", g))
+            inners.append(inner_of(rows_ref, up_buf[g], down_buf[g]))
         total = acc_in[side][...]
-        for inner, up in zip(inners, ups):
-            total = total + jnp.dot(inner, up[...], preferred_element_type=f32)
+        for g, inner in enumerate(inners):
+            total = total + jnp.dot(inner, up_buf[g], preferred_element_type=f32)
         out[side][...] = total.astype(out[side].dtype)
 
 
-def next_call(own, other, ups, downs, acc, last=False, mark=None):
-    rows, width = own.shape[0], own.shape[1] // 3
-    kinds = (f32, bf16) if last else (f32, f32)
-    operands = tuple(pltpu.with_memory_space_constraint(x, pltpu.VMEM) for x in (own, other, *ups, *downs, *acc))
-    specs = [VMEM] * len(operands)
-    if mark is not None:
-        operands, specs = operands + (mark,), specs + [ANY]
-    return pl.pallas_call(
-        functools.partial(next_kernel, len(ups)),
-        out_shape=tuple(jax.ShapeDtypeStruct((rows, width), k) for k in kinds),
-        in_specs=specs,
-        out_specs=(VMEM, VMEM),
+def next_call(rows, ups, downs, acc, mark):
+    n_w = len(ups)
+    inside = [pltpu.with_memory_space_constraint(x, pltpu.VMEM) for x in (*rows, *acc)]
+    operands = (*inside[:len(rows)], *ups, *downs, *inside[len(rows):], mark)
+    return pl.pallas_call(
+        functools.partial(next_kernel, len(rows), n_w),
+        out_shape=tuple(jax.ShapeDtypeStruct(x.shape, f32) for x in acc),
+        in_specs=[VMEM] * len(rows) + [ANY] * (2 * n_w) + [VMEM] * len(acc) + [ANY],
+        out_specs=(VMEM,) * len(acc),
+        scratch_shapes=[
+            pltpu.VMEM((n_w, *ups[0].shape), bf16),
+            pltpu.VMEM((n_w, *ups[0].shape), bf16),
+            pltpu.SemaphoreType.DMA((2 * n_w,)),
+        ],
         compiler_params=params(24),
+    )(*operands)
+
+
+def last_kernel(rows_ref, up_ref, down_ref, acc_ref, out_ref):
+    inner = inner_of(rows_ref, up_ref[...], down_ref[...])
+    total = acc_ref[...] + jnp.dot(inner, up_ref[...], preferred_element_type=f32)
+    out_ref[...] = total.astype(out_ref.dtype)
+
+
+def last_call(rows, up, down, acc, kind):
+    operands = tuple(pltpu.with_memory_space_constraint(x, pltpu.VMEM) for x in (rows, up, down, acc))
+    return pl.pallas_call(
+        last_kernel,
+        out_shape=jax.ShapeDtypeStruct(acc.shape, kind),
+        in_specs=[VMEM] * 4,
+        out_specs=VMEM,
+        compiler_params=params(16),
     )(*operands)
 
 
@@ -219,9 +259,10 @@
     uf4, db4 = send_on(uf3, forth), send_on(db3, back)
     other = lax.ppermute(own, "dp", swap)
     *acc, own, other = first_call(own, other, (up0, uf1, ub1, uf2, ub2), (down0, df1, db1, df2, db2), mark)
-    acc = next_call(own, other, (uf3, ub3), (df3, db3), acc, mark=mark3)
-    kept, passed = next_call(own, other, (uf4,), (db4,), acc, last=True)
-    whole = (kept + lax.ppermute(passed, "dp", swap).astype(f32)).astype(bf16)
+    mine, theirs = next_call((own, other), (uf3, ub3), (df3, db3), acc, mark3)
+    passed = lax.ppermute(last_call(other, uf4, db4, theirs, bf16), "dp", swap)
+    kept = last_call(own, uf4, db4, mine, f32)
+    whole = (kept + passed.astype(f32)).astype(bf16)
     returned = lax.all_to_all(whole.reshape(experts, CAP, width), "expert", 0, 0, tiled=True)
     returned = returned.reshape(experts * CAP, width)
     return lax.dot_general(mix, returned, (((0,), (0,)), ((), ())), preferred_element_type=f32)

time: 114 us -> 114 us (level)
  waiting for transfers between devices: 33.4 us -> 31.5 us
    ppermute x1, waiting for transfers between devices: 1.91 us -> 0.48 us  [local(): passed = lax.ppermute(last_call(other, uf4, db4, theirs, bf16), 'dp', swap)]
    pallas_call x2 -> x3, Pallas kernels: 7.45 us -> 8.34 us  [the longest x1 5.48 us: next_call(): pl.pallas_call(functools.partial(next_kernel, len(rows), n_w), out_shape=...]
  transfers between devices with their start and end apart: 17 -> 17, of which waited for: 6 -> 6; matrix products, arithmetic and copies ran while one was open for 0% -> 0% of each run, Pallas kernels for 19% -> 21%
where the time goes in v5:
time: 114 us; the launch traced here: 113 us
  starting transfers between devices  34.5 us (30%)
  waiting for transfers between devices  31.5 us (28%)
  Pallas kernels  25.3 us (22%)
  blocking collectives  20.4 us (18%)
    ppermute x14, waiting for transfers between devices, send_on(): return lax.ppermute(x, 'dp', way)  31 us
    ppermute x14, starting transfers between devices, send_on(): return lax.ppermute(x, 'dp', way)  22.3 us
    all_to_all x1, blocking collectives, local(): lax.all_to_all(whole.reshape(experts, CAP, width), 'expert', 0, 0, tiled=...  20.4 us
    pallas_call x1, Pallas kernels, first_call(): pl.pallas_call(functools.partial(first_kernel, n_w), out_shape=(jax.Shape...  13.9 us
    all_to_all x1, starting transfers between devices, local(): lax.all_to_all(send.reshape(experts, CAP, 3 * width), 'expert', 0, 0, til...  6.81 us
    pallas_call x1, Pallas kernels, next_call(): pl.pallas_call(functools.partial(next_kernel, len(rows), n_w), out_shape=...  5.48 us
    pallas_call x1, Pallas kernels, prepare(): pl.pallas_call(prepare_kernel, out_shape=(jax.ShapeDtypeStruct((slots, 3...  3.12 us
    ppermute x1, starting transfers between devices, local(): other = lax.ppermute(own, 'dp', swap)  2.97 us
  transfers between devices with their start and end apart: 17, of which 6 were waited for; matrix products, arithmetic and copies ran while one was open for 0% of the time, Pallas kernels for 21%

profile of v5, /device:TPU:1, one launch (start us, length us, event | category | flops | bytes accessed | tf_op | source)
XLA Modules:
  0.0 113.3 jit_solution(12286154629889766706)
XLA Ops:
  0.0 2.5 %collective-permute-start.1 = (bf16[256,1024]{1,0:T(8,128)(2,1)}, bf16[256,1024]{1,0:T(8,128)(2,1)S(1)}, u32[]{:S(2)}, u32[]{:S(2)}) collective-permute-start(bf16[256,1024]{1,0:T(8,128)(2,1)} %bitcast.10), channel_id=1, source_target_pairs={{0,32},{16,48},{32,64},{48,80},{64,96},{80,112},{96,128},{112,144}... | collective-permute-start | bytes 1572872 | tf_op jit(solution)/shard_map/ppermute | solution.py:240
  2.5 3.9 %collective-permute-start.2 = (bf16[256,1024]{1,0:T(8,128)(2,1)}, bf16[256,1024]{1,0:T(8,128)(2,1)}, u32[]{:S(2)}, u32[]{:S(2)}) collective-permute-start(bf16[256,1024]{1,0:T(8,128)(2,1)} %bitcast.13), channel_id=1, source_target_pairs={{0,224},{16,240},{32,0},{48,16},{64,32},{80,48},{96,64},{112,80},{... | collective-permute-start | bytes 1572872 | tf_op jit(solution)/shard_map/ppermute | solution.py:240
  6.4 0.0 collective-permute-start.5
  6.4 2.7 %collective-permute-start.6 = (bf16[256,1024]{1,0:T(8,128)(2,1)}, bf16[256,1024]{1,0:T(8,128)(2,1)}, u32[]{:S(2)}, u32[]{:S(2)}) collective-permute-start(bf16[256,1024]{1,0:T(8,128)(2,1)} %bitcast.11), channel_id=1, source_target_pairs={{0,224},{16,240},{32,0},{48,16},{64,32},{80,48},{96,64},{112,80},{... | collective-permute-start | bytes 1572872 | tf_op jit(solution)/shard_map/ppermute | solution.py:240
  9.1 3.1 %shard_map.73 = (bf16[384,3072]{1,0:T(8,128)(2,1)}, bf16[384,128]{1,0:T(8,128)(2,1)S(1)}) custom-call(s32[2,128]{1,0:T(2,128)} %bitcast.18, s32[2,128]{1,0:T(2,128)} %bitcast.19, bf16[128,1024]{1,0:T(8,128)(2,1)} %x_hbm.1, bf16[128,1024]{1,0:T(8,128)(2,1)} %t_hbm.1, bf16[128,1024]{1,0:T(8,128)(2,1)} %c_hbm.1), custom_call_target="tpu_custom_call" | custom-call | tf_op jit(solution)/shard_map/pallas_call | solution.py:61
  12.2 6.8 %all-to-all-start = ((bf16[16,24,3072]{2,1,0:T(8,128)(2,1)}), bf16[16,24,3072]{2,1,0:T(8,128)(2,1)}, u32[]{:S(2)}, u32[]{:S(2)}) async-start(bf16[16,24,3072]{2,1,0:T(8,128)(2,1)} %bitcast.2), calls=%async_computation | async-start | bytes 4718592 | tf_op jit(solution)/shard_map/all_to_all | solution.py:246
  19.0 0.0 collective-permute-done.1.x_ref.refs_1_
  19.1 0.0 collective-permute-done.2.refs_7_
  19.1 0.1 collective-permute-start.3
  19.2 2.7 %collective-permute-start.4 = (bf16[256,1024]{1,0:T(8,128)(2,1)}, bf16[256,1024]{1,0:T(8,128)(2,1)}, u32[]{:S(2)}, u32[]{:S(2)}) collective-permute-start(bf16[256,1024]{1,0:T(8,128)(2,1)} %collective-permute-done.2.refs_7_), channel_id=1, source_target_pairs={{0,224},{16,240},{32,0},{48,16},{64,32},{80,48},{96,64},{112,80},{... | collective-permute-start | bytes 1572872 | tf_op jit(solution)/shard_map/ppermute | solution.py:240
  21.8 7.8 %collective-permute-done.5.refs_6_ = bf16[256,1024]{1,0:T(8,128)(2,1)} collective-permute-done((bf16[256,1024]{1,0:T(8,128)(2,1)}, bf16[256,1024]{1,0:T(8,128)(2,1)}, u32[]{:S(2)}, u32[]{:S(2)}) %collective-permute-start.5) | collective-permute-done | bytes 524320 | tf_op jit(solution)/shard_map/ppermute | solution.py:240
  29.6 0.0 collective-permute-done.6.refs_2_
  29.6 0.0 collective-permute-start.7
  29.6 2.7 %collective-permute-start.8 = (bf16[256,1024]{1,0:T(8,128)(2,1)}, bf16[256,1024]{1,0:T(8,128)(2,1)}, u32[]{:S(2)}, u32[]{:S(2)}) collective-permute-start(bf16[256,1024]{1,0:T(8,128)(2,1)} %collective-permute-done.6.refs_2_), channel_id=1, source_target_pairs={{0,224},{16,240},{32,0},{48,16},{64,32},{80,48},{96,64},{112,80},{... | collective-permute-start | bytes 1572872 | tf_op jit(solution)/shard_map/ppermute | solution.py:240
  32.3 8.6 %collective-permute-done.3.refs_3_ = bf16[256,1024]{1,0:T(8,128)(2,1)S(1)} collective-permute-done((bf16[256,1024]{1,0:T(8,128)(2,1)S(1)}, bf16[256,1024]{1,0:T(8,128)(2,1)S(1)}, u32[]{:S(2)}, u32[]{:S(2)}) %collective-permute-start.3) | collective-permute-done | bytes 524320 | tf_op jit(solution)/shard_map/ppermute | solution.py:240
  40.8 0.0 collective-permute-done.4.refs_9_
  40.8 0.0 collective-permute-start.9
  40.8 2.7 %collective-permute-start.10 = (bf16[256,1024]{1,0:T(8,128)(2,1)}, bf16[256,1024]{1,0:T(8,128)(2,1)}, u32[]{:S(2)}, u32[]{:S(2)}) collective-permute-start(bf16[256,1024]{1,0:T(8,128)(2,1)} %collective-permute-done.4.refs_9_), channel_id=1, source_target_pairs={{0,224},{16,240},{32,0},{48,16},{64,32},{80,48},{96,64},{112,80},{... | collective-permute-start | bytes 1572872 | tf_op jit(solution)/shard_map/ppermute | solution.py:240
  43.5 8.6 %collective-permute-done.7.refs_8_ = bf16[256,1024]{1,0:T(8,128)(2,1)} collective-permute-done((bf16[256,1024]{1,0:T(8,128)(2,1)}, bf16[256,1024]{1,0:T(8,128)(2,1)}, u32[]{:S(2)}, u32[]{:S(2)}) %collective-permute-start.7) | collective-permute-done | bytes 524320 | tf_op jit(solution)/shard_map/ppermute | solution.py:240
  52.1 0.0 collective-permute-done.8.refs_4_
  52.1 2.4 %collective-permute-start.13 = (bf16[256,1024]{1,0:T(8,128)(2,1)}, bf16[256,1024]{1,0:T(8,128)(2,1)}, u32[]{:S(2)}, u32[]{:S(2)}) collective-permute-start(bf16[256,1024]{1,0:T(8,128)(2,1)} %collective-permute-done.8.refs_4_), channel_id=1, source_target_pairs={{0,224},{16,240},{32,0},{48,16},{64,32},{80,48},{96,64},{112,80},{... | collective-permute-start | bytes 1572872 | tf_op jit(solution)/shard_map/ppermute | solution.py:240
  54.4 0.0 collective-permute-start.14
  54.4 0.0 all-to-all-done
  54.4 3.0 %collective-permute-start = (bf16[384,3072]{1,0:T(8,128)(2,1)}, bf16[384,3072]{1,0:T(8,128)(2,1)}, u32[]{:S(2)}, u32[]{:S(2)}) collective-permute-start(bf16[384,3072]{1,0:T(8,128)(2,1)} %bitcast.3.own_ref), channel_id=1, source_target_pairs={{0,16},{16,0},{32,48},{48,32},{64,80},{80,64},{96,112},{112,96},{1... | collective-permute-start | bytes 7077896 | tf_op jit(solution)/shard_map/ppermute | solution.py:260
  57.4 5.8 %collective-permute-done.9.x_ref.refs_2_ = bf16[256,1024]{1,0:T(8,128)(2,1)S(1)} collective-permute-done((bf16[256,1024]{1,0:T(8,128)(2,1)S(1)}, bf16[256,1024]{1,0:T(8,128)(2,1)S(1)}, u32[]{:S(2)}, u32[]{:S(2)}) %collective-permute-start.9) | collective-permute-done | bytes 524320 | tf_op jit(solution)/shard_map/ppermute | solution.py:240
  63.2 0.0 copy-start
  63.2 0.0 copy-start.1
  63.2 0.0 collective-permute-done.10.refs_5_
  63.2 0.1 collective-permute-start.11
  63.3 2.7 %collective-permute-start.12 = (bf16[256,1024]{1,0:T(8,128)(2,1)}, bf16[256,1024]{1,0:T(8,128)(2,1)S(1)}, u32[]{:S(2)}, u32[]{:S(2)}) collective-permute-start(bf16[256,1024]{1,0:T(8,128)(2,1)} %collective-permute-done.10.refs_5_), channel_id=1, source_target_pairs={{0,224},{16,240},{32,0},{48,16},{64,32},{80,48},{96,64},{112,80},{... | collective-permute-start | bytes 1572872 | tf_op jit(solution)/shard_map/ppermute | solution.py:240
  66.0 0.0 collective-permute-done.other_ref
  66.0 0.0 copy-done
  66.0 0.0 copy-done.1
  66.0 13.9 %shard_map.76 = (f32[384,1024]{1,0:T(8,128)S(1)}, f32[384,1024]{1,0:T(8,128)S(1)}, bf16[384,3072]{1,0:T(8,128)(2,1)S(1)}, bf16[384,3072]{1,0:T(8,128)(2,1)S(1)}) custom-call(bf16[384,3072]{1,0:T(8,128)(2,1)} %bitcast.3.own_ref, bf16[384,3072]{1,0:T(8,128)(2,1)} %collective-permute-done.other_ref, bf16[256,1024]{1,0:T(8,128)(2,1)S(1)} %bitcast.12, ...), custom_call_target="tpu_custom_call" | custom-call | tf_op jit(solution)/shard_map/pallas_call | solution.py:140
  79.9 0.0 collective-permute-done.13.refs_3_
  79.9 0.0 collective-permute-done.14.refs_4_
  79.9 5.5 %shard_map.77 = (f32[384,1024]{1,0:T(8,128)S(1)}, f32[384,1024]{1,0:T(8,128)S(1)}) custom-call(bf16[384,3072]{1,0:T(8,128)(2,1)S(1)} %get-tuple-element.50.refs_0_.rows_ref, bf16[384,3072]{1,0:T(8,128)(2,1)S(1)} %get-tuple-element.53.refs_1_.rows_ref, bf16[256,1024]{1,0:T(8,128)(2,1)S(1)} %collective-permute-done.9.x_ref.refs_2_, ...), custom_call_target="tpu_custom_call" | custom-call | tf_op jit(solution)/shard_map/pallas_call | solution.py:184
  85.4 0.3 collective-permute-done.11.up_ref
  85.7 0.0 collective-permute-done.12.down_ref
  85.7 1.4 %shard_map.79 = bf16[384,1024]{1,0:T(8,128)(2,1)S(1)} custom-call(bf16[384,3072]{1,0:T(8,128)(2,1)S(1)} %get-tuple-element.53.refs_1_.rows_ref, bf16[256,1024]{1,0:T(8,128)(2,1)S(1)} %collective-permute-done.11.up_ref, bf16[256,1024]{1,0:T(8,128)(2,1)S(1)} %collective-permute-done.12.down_ref, f32[384,1024]{1,0:T(8,128)S(1)} %get-tuple-element.58.acc_ref), custom_call_target="tpu_custom_call" | custom-call | tf_op jit(solution)/shard_map/pallas_call | solution.py:206
  87.1 2.5 %collective-permute-start.15 = (bf16[384,1024]{1,0:T(8,128)(2,1)S(1)}, bf16[384,1024]{1,0:T(8,128)(2,1)S(1)}, u32[]{:S(2)}, u32[]{:S(2)}) collective-permute-start(bf16[384,1024]{1,0:T(8,128)(2,1)S(1)} %shard_map.79), channel_id=1, source_target_pairs={{0,16},{16,0},{32,48},{48,32},{64,80},{80,64},{96,112},{112,96},{1... | collective-permute-start | bytes 2359304 | tf_op jit(solution)/shard_map/ppermute | solution.py:263
  89.6 1.4 %shard_map.78 = f32[384,1024]{1,0:T(8,128)S(1)} custom-call(bf16[384,3072]{1,0:T(8,128)(2,1)S(1)} %get-tuple-element.50.refs_0_.rows_ref, bf16[256,1024]{1,0:T(8,128)(2,1)S(1)} %collective-permute-done.11.up_ref, bf16[256,1024]{1,0:T(8,128)(2,1)S(1)} %collective-permute-done.12.down_ref, f32[384,1024]{1,0:T(8,128)S(1)} %get-tuple-element.57.acc_ref), custom_call_target="tpu_custom_call" | custom-call | tf_op jit(solution)/shard_map/pallas_call | solution.py:206
  91.0 0.5 collective-permute-done.15
  91.5 0.3 add_convert_fusion
  91.8 20.4 %all_to_all.10 = bf16[16,24,1024]{2,1,0:T(8,128)(2,1)S(1)} all-to-all(bf16[16,24,1024]{2,1,0:T(8,128)(2,1)S(1)} %bitcast.17), channel_id=1, replica_groups=mesh['dp'=16,'expert'=16] {'expert'}, dimensions={0} | all-to-all | bytes 1572864 | tf_op jit(solution)/shard_map/all_to_all | solution.py:266
  112.2 1.1 fusion
  (2 shorter events, 0.0 us)
Async XLA Ops:
  0.0 19.0 %collective-permute-start.1 = (bf16[256,1024]{1,0:T(8,128)(2,1)}, bf16[256,1024]{1,0:T(8,128)(2,1)S(1)}, u32[]{:S(2)}, u32[]{:S(2)}) collective-permute-start(bf16[256,1024]{1,0:T(8,128)(2,1)} %bitcast.10), channel_id=1, source_target_pairs={{0,32},{16,48},{32,64},{48,80},{64,96},{80,112},{96,128},{112,144}... | collective-permute-start | bytes 1572872 | tf_op jit(solution)/shard_map/ppermute | solution.py:240
  2.5 16.6 %collective-permute-start.2 = (bf16[256,1024]{1,0:T(8,128)(2,1)}, bf16[256,1024]{1,0:T(8,128)(2,1)}, u32[]{:S(2)}, u32[]{:S(2)}) collective-permute-start(bf16[256,1024]{1,0:T(8,128)(2,1)} %bitcast.13), channel_id=1, source_target_pairs={{0,224},{16,240},{32,0},{48,16},{64,32},{80,48},{96,64},{112,80},{... | collective-permute-start | bytes 1572872 | tf_op jit(solution)/shard_map/ppermute | solution.py:240
  6.4 23.2 %collective-permute-start.5 = (bf16[256,1024]{1,0:T(8,128)(2,1)}, bf16[256,1024]{1,0:T(8,128)(2,1)}, u32[]{:S(2)}, u32[]{:S(2)}) collective-permute-start(bf16[256,1024]{1,0:T(8,128)(2,1)} %bitcast.14), channel_id=1, source_target_pairs={{0,32},{16,48},{32,64},{48,80},{64,96},{80,112},{96,128},{112,144}... | collective-permute-start | bytes 1572872 | tf_op jit(solution)/shard_map/ppermute | solution.py:240
  6.4 23.2 %collective-permute-start.6 = (bf16[256,1024]{1,0:T(8,128)(2,1)}, bf16[256,1024]{1,0:T(8,128)(2,1)}, u32[]{:S(2)}, u32[]{:S(2)}) collective-permute-start(bf16[256,1024]{1,0:T(8,128)(2,1)} %bitcast.11), channel_id=1, source_target_pairs={{0,224},{16,240},{32,0},{48,16},{64,32},{80,48},{96,64},{112,80},{... | collective-permute-start | bytes 1572872 | tf_op jit(solution)/shard_map/ppermute | solution.py:240
  12.2 42.2 %all-to-all-start = ((bf16[16,24,3072]{2,1,0:T(8,128)(2,1)}), bf16[16,24,3072]{2,1,0:T(8,128)(2,1)}, u32[]{:S(2)}, u32[]{:S(2)}) async-start(bf16[16,24,3072]{2,1,0:T(8,128)(2,1)} %bitcast.2), calls=%async_computation | async-start | bytes 4718592 | tf_op jit(solution)/shard_map/all_to_all | solution.py:246
  19.1 21.8 %collective-permute-start.3 = (bf16[256,1024]{1,0:T(8,128)(2,1)S(1)}, bf16[256,1024]{1,0:T(8,128)(2,1)S(1)}, u32[]{:S(2)}, u32[]{:S(2)}) collective-permute-start(bf16[256,1024]{1,0:T(8,128)(2,1)S(1)} %collective-permute-done.1.x_ref.refs_1_), channel_id=1, source_target_pairs={{0,32},{16,48},{32,64},{48,80},{64,96},{80,112},{96,128},{112,144}... | collective-permute-start | bytes 1572872 | tf_op jit(solution)/shard_map/ppermute | solution.py:240
  19.2 21.7 %collective-permute-start.4 = (bf16[256,1024]{1,0:T(8,128)(2,1)}, bf16[256,1024]{1,0:T(8,128)(2,1)}, u32[]{:S(2)}, u32[]{:S(2)}) collective-permute-start(bf16[256,1024]{1,0:T(8,128)(2,1)} %collective-permute-done.2.refs_7_), channel_id=1, source_target_pairs={{0,224},{16,240},{32,0},{48,16},{64,32},{80,48},{96,64},{112,80},{... | collective-permute-start | bytes 1572872 | tf_op jit(solution)/shard_map/ppermute | solution.py:240
  29.6 22.5 %collective-permute-start.7 = (bf16[256,1024]{1,0:T(8,128)(2,1)}, bf16[256,1024]{1,0:T(8,128)(2,1)}, u32[]{:S(2)}, u32[]{:S(2)}) collective-permute-start(bf16[256,1024]{1,0:T(8,128)(2,1)} %collective-permute-done.5.refs_6_), channel_id=1, source_target_pairs={{0,32},{16,48},{32,64},{48,80},{64,96},{80,112},{96,128},{112,144}... | collective-permute-start | bytes 1572872 | tf_op jit(solution)/shard_map/ppermute | solution.py:240
  29.6 22.5 %collective-permute-start.8 = (bf16[256,1024]{1,0:T(8,128)(2,1)}, bf16[256,1024]{1,0:T(8,128)(2,1)}, u32[]{:S(2)}, u32[]{:S(2)}) collective-permute-start(bf16[256,1024]{1,0:T(8,128)(2,1)} %collective-permute-done.6.refs_2_), channel_id=1, source_target_pairs={{0,224},{16,240},{32,0},{48,16},{64,32},{80,48},{96,64},{112,80},{... | collective-permute-start | bytes 1572872 | tf_op jit(solution)/shard_map/ppermute | solution.py:240
  40.8 22.4 %collective-permute-start.9 = (bf16[256,1024]{1,0:T(8,128)(2,1)S(1)}, bf16[256,1024]{1,0:T(8,128)(2,1)S(1)}, u32[]{:S(2)}, u32[]{:S(2)}) collective-permute-start(bf16[256,1024]{1,0:T(8,128)(2,1)S(1)} %collective-permute-done.3.refs_3_), channel_id=1, source_target_pairs={{0,32},{16,48},{32,64},{48,80},{64,96},{80,112},{96,128},{112,144}... | collective-permute-start | bytes 1572872 | tf_op jit(solution)/shard_map/ppermute | solution.py:240
  40.8 22.4 %collective-permute-start.10 = (bf16[256,1024]{1,0:T(8,128)(2,1)}, bf16[256,1024]{1,0:T(8,128)(2,1)}, u32[]{:S(2)}, u32[]{:S(2)}) collective-permute-start(bf16[256,1024]{1,0:T(8,128)(2,1)} %collective-permute-done.4.refs_9_), channel_id=1, source_target_pairs={{0,224},{16,240},{32,0},{48,16},{64,32},{80,48},{96,64},{112,80},{... | collective-permute-start | bytes 1572872 | tf_op jit(solution)/shard_map/ppermute | solution.py:240
  52.1 27.8 %collective-permute-start.13 = (bf16[256,1024]{1,0:T(8,128)(2,1)}, bf16[256,1024]{1,0:T(8,128)(2,1)}, u32[]{:S(2)}, u32[]{:S(2)}) collective-permute-start(bf16[256,1024]{1,0:T(8,128)(2,1)} %collective-permute-done.8.refs_4_), channel_id=1, source_target_pairs={{0,224},{16,240},{32,0},{48,16},{64,32},{80,48},{96,64},{112,80},{... | collective-permute-start | bytes 1572872 | tf_op jit(solution)/shard_map/ppermute | solution.py:240
  54.4 25.4 %collective-permute-start.14 = (bf16[256,1024]{1,0:T(8,128)(2,1)}, bf16[256,1024]{1,0:T(8,128)(2,1)}, u32[]{:S(2)}, u32[]{:S(2)}) collective-permute-start(bf16[256,1024]{1,0:T(8,128)(2,1)} %collective-permute-done.7.refs_8_), channel_id=1, source_target_pairs={{0,32},{16,48},{32,64},{48,80},{64,96},{80,112},{96,128},{112,144}... | collective-permute-start | bytes 1572872 | tf_op jit(solution)/shard_map/ppermute | solution.py:240
  54.4 11.5 %collective-permute-start = (bf16[384,3072]{1,0:T(8,128)(2,1)}, bf16[384,3072]{1,0:T(8,128)(2,1)}, u32[]{:S(2)}, u32[]{:S(2)}) collective-permute-start(bf16[384,3072]{1,0:T(8,128)(2,1)} %bitcast.3.own_ref), channel_id=1, source_target_pairs={{0,16},{16,0},{32,48},{48,32},{64,80},{80,64},{96,112},{112,96},{1... | collective-permute-start | bytes 7077896 | tf_op jit(solution)/shard_map/ppermute | solution.py:260
  63.2 2.8 %copy-start = (bf16[1,256,1024]{2,1,0:T(8,128)(2,1)S(1)}, bf16[1,256,1024]{2,1,0:T(8,128)(2,1)}, u32[]{:S(2)}) copy-start(bf16[1,256,1024]{2,1,0:T(8,128)(2,1)} %param.12) | copy-start | bytes 1572868
  63.2 2.8 %copy-start.1 = (bf16[1,256,1024]{2,1,0:T(8,128)(2,1)S(1)}, bf16[1,256,1024]{2,1,0:T(8,128)(2,1)}, u32[]{:S(2)}) copy-start(bf16[1,256,1024]{2,1,0:T(8,128)(2,1)} %param.13) | copy-start | bytes 1572868
  63.2 22.5 %collective-permute-start.11 = (bf16[256,1024]{1,0:T(8,128)(2,1)S(1)}, bf16[256,1024]{1,0:T(8,128)(2,1)S(1)}, u32[]{:S(2)}, u32[]{:S(2)}) collective-permute-start(bf16[256,1024]{1,0:T(8,128)(2,1)S(1)} %collective-permute-done.9.x_ref.refs_2_), channel_id=1, source_target_pairs={{0,32},{16,48},{32,64},{48,80},{64,96},{80,112},{96,128},{112,144}... | collective-permute-start | bytes 1572872 | tf_op jit(solution)/shard_map/ppermute | solution.py:240
  63.3 22.4 %collective-permute-start.12 = (bf16[256,1024]{1,0:T(8,128)(2,1)}, bf16[256,1024]{1,0:T(8,128)(2,1)S(1)}, u32[]{:S(2)}, u32[]{:S(2)}) collective-permute-start(bf16[256,1024]{1,0:T(8,128)(2,1)} %collective-permute-done.10.refs_5_), channel_id=1, source_target_pairs={{0,224},{16,240},{32,0},{48,16},{64,32},{80,48},{96,64},{112,80},{... | collective-permute-start | bytes 1572872 | tf_op jit(solution)/shard_map/ppermute | solution.py:240
  87.1 4.4 %collective-permute-start.15 = (bf16[384,1024]{1,0:T(8,128)(2,1)S(1)}, bf16[384,1024]{1,0:T(8,128)(2,1)S(1)}, u32[]{:S(2)}, u32[]{:S(2)}) collective-permute-start(bf16[384,1024]{1,0:T(8,128)(2,1)S(1)} %shard_map.79), channel_id=1, source_target_pairs={{0,16},{16,0},{32,48},{48,32},{64,80},{80,64},{96,112},{112,96},{1... | collective-permute-start | bytes 2359304 | tf_op jit(solution)/shard_map/ppermute | solution.py:263

commit v6 on v5

--- a/solution.py
+++ b/solution.py
@@ -85,120 +85,106 @@
     return (pulled * curvature(before_act) * lifted).astype(bf16)
 
 
-class Fetcher:
-    def __init__(self, jobs, sems):
-        self.copies = {key: pltpu.make_async_copy(src, dst, sems.at[i]) for i, (key, src, dst) in enumerate(jobs)}
-        self.queue = list(self.copies)
-
-    def start(self, count):
-        for key in self.queue[:count]:
-            self.copies[key].start()
-        del self.queue[:count]
-
-    def wait(self, *keys):
-        for key in keys:
-            self.copies[key].wait()
-
-
-def first_kernel(n_w, own_ref, other_ref, *refs):
+def accumulate(rows_ref, ups, downs, total=None):
+    inners = [inner_of(rows_ref, up[...], down[...]) for up, down in zip(ups, downs)]
+    for inner, up in zip(inners, ups):
+        part = jnp.dot(inner, up[...], preferred_element_type=f32)
+        total = part if total is None else total + part
+    return total
+
+
+def own_kernel(n_w, own_ref, *refs):
     ups, downs = refs[:n_w], refs[n_w:2 * n_w]
-    acc_own, acc_other, own_out, other_out, up_buf, down_buf, sems = refs[-7:]
-    width = up_buf.shape[2]
-
-    def thirds(side, source, target):
-        parts = [slice(i * width, (i + 1) * width) for i in range(3)]
-        return [((side, i), source.at[:, part], target.at[:, part]) for i, part in enumerate(parts)]
-
-    weights = [[(("up", g), ups[g], up_buf.at[g]), (("down", g), downs[g], down_buf.at[g])] for g in range(n_w)]
-    own_jobs, other_jobs = thirds(0, own_ref, own_out), thirds(1, other_ref, other_out)
-    jobs = [weights[0][0], *own_jobs, weights[0][1]]
-    for g in range(1, n_w):
-        jobs += weights[g]
-    jobs += other_jobs
-    fetcher = Fetcher(jobs, sems)
-    fetcher.start(7)
-    for side, (rows_ref, acc_ref) in enumerate(((own_out, acc_own), (other_out, acc_other))):
-        if side:
-            fetcher.wait((1, 0), (1, 1), (1, 2))
-        inners = []
-        for g in range(n_w):
-            if not side:
-                fetcher.wait(*([(0, 0), (0, 1), (0, 2)] if not g else []), ("up", g), ("down", g))
-                fetcher.start(3)
-            inners.append(inner_of(rows_ref, up_buf[g], down_buf[g]))
-        total = None
-        for g, inner in enumerate(inners):
-            part = jnp.dot(inner, up_buf[g], preferred_element_type=f32)
-            total = part if total is None else total + part
-        acc_ref[...] = total
-
-
-def first_call(own, other, ups, downs, mark):
+    acc_ref, own_out, up_out, down_out, sems = refs[-5:]
+    own_copy = pltpu.make_async_copy(own_ref, own_out, sems.at[0])
+    copies = []
+    for g in range(n_w):
+        copies.append(pltpu.make_async_copy(ups[g], up_out.at[g], sems.at[1 + 2 * g]))
+        copies.append(pltpu.make_async_copy(downs[g], down_out.at[g], sems.at[2 + 2 * g]))
+    for copy in (own_copy, *copies[:4]):
+        copy.start()
+    for copy in (own_copy, *copies[:2]):
+        copy.wait()
+    for copy in copies[4:]:
+        copy.start()
+    total = accumulate(own_out, [up_out.at[0]], [down_out.at[0]])
+    for copy in copies[2:]:
+        copy.wait()
+    rest = range(1, n_w)
+    acc_ref[...] = accumulate(own_out, [up_out.at[g] for g in rest], [down_out.at[g] for g in rest], total)
+
+
+def own_call(own, ups, downs, mark):
     rows, width = own.shape[0], own.shape[1] // 3
     n_w = len(ups)
-    operands = (own, other, *ups, *downs, mark)
-    return pl.pallas_call(
-        functools.partial(first_kernel, n_w),
-        out_shape=(
-            jax.ShapeDtypeStruct((rows, width), f32),
-            jax.ShapeDtypeStruct((rows, width), f32),
-            jax.ShapeDtypeStruct(own.shape, bf16),
-            jax.ShapeDtypeStruct(own.shape, bf16),
-        ),
+    stack = jax.ShapeDtypeStruct((n_w, *ups[0].shape), bf16)
+    operands = (own, *ups, *downs, mark)
+    return pl.pallas_call(
+        functools.partial(own_kernel, n_w),
+        out_shape=(jax.ShapeDtypeStruct((rows, width), f32), jax.ShapeDtypeStruct(own.shape, bf16), stack, stack),
         in_specs=[ANY] * len(operands),
         out_specs=(VMEM,) * 4,
-        scratch_shapes=[
-            pltpu.VMEM((n_w, *ups[0].shape), bf16),
-            pltpu.VMEM((n_w, *ups[0].shape), bf16),
-            pltpu.SemaphoreType.DMA((2 * n_w + 6,)),
-        ],
-        compiler_params=params(28),
+        scratch_shapes=[pltpu.SemaphoreType.DMA((2 * n_w + 1,))],
+        compiler_params=params(16),
     )(*operands)
 
 
-def next_kernel(n_rows, n_w, *refs):
-    rows, ups, downs = refs[:n_rows], refs[n_rows:n_rows + n_w], refs[n_rows + n_w:n_rows + 2 * n_w]
-    acc_in, out = refs[n_rows + 2 * n_w:2 * n_rows + 2 * n_w], refs[-n_rows - 3:-3]
-    up_buf, down_buf, sems = refs[-3:]
-    jobs = []
+def other_kernel(other_ref, up_ref, down_ref, acc_ref, other_out, sem):
+    copy = pltpu.make_async_copy(other_ref, other_out, sem)
+    copy.start()
+    copy.wait()
+    blocks = range(up_ref.shape[0])
+    acc_ref[...] = accumulate(other_out, [up_ref.at[g] for g in blocks], [down_ref.at[g] for g in blocks])
+
+
+def other_call(other, up_stack, down_stack):
+    rows, width = other.shape[0], other.shape[1] // 3
+    stacks = [pltpu.with_memory_space_constraint(x, pltpu.VMEM) for x in (up_stack, down_stack)]
+    return pl.pallas_call(
+        other_kernel,
+        out_shape=(jax.ShapeDtypeStruct((rows, width), f32), jax.ShapeDtypeStruct(other.shape, bf16)),
+        in_specs=[ANY, VMEM, VMEM],
+        out_specs=(VMEM, VMEM),
+        scratch_shapes=[pltpu.SemaphoreType.DMA],
+        compiler_params=params(16),
+    )(other, *stacks)
+
+
+def next_kernel(n_w, own_ref, other_ref, *refs):
+    ups, downs, accs = refs[:n_w], refs[n_w:2 * n_w], refs[2 * n_w:2 * n_w + 2]
+    outs, up_buf, down_buf, sems = refs[-5:-3], *refs[-3:]
+    copies = []
     for g in range(n_w):
-        jobs += [(("up", g), ups[g], up_buf.at[g]), (("down", g), downs[g], down_buf.at[g])]
-    fetcher = Fetcher(jobs, sems)
-    fetcher.start(2 * n_w)
-    for side, rows_ref in enumerate(rows):
-        inners = []
-        for g in range(n_w):
-            if not side:
-                fetcher.wait(("up", g), ("down", g))
-            inners.append(inner_of(rows_ref, up_buf[g], down_buf[g]))
-        total = acc_in[side][...]
-        for g, inner in enumerate(inners):
-            total = total + jnp.dot(inner, up_buf[g], preferred_element_type=f32)
-        out[side][...] = total.astype(out[side].dtype)
+        copies.append(pltpu.make_async_copy(ups[g], up_buf.at[g], sems.at[2 * g]))
+        copies.append(pltpu.make_async_copy(downs[g], down_buf.at[g], sems.at[2 * g + 1]))
+    for copy in copies:
+        copy.start()
+    for copy in copies:
+        copy.wait()
+    blocks = range(n_w)
+    for rows_ref, acc_ref, out_ref in zip((own_ref, other_ref), accs, outs):
+        out_ref[...] = accumulate(rows_ref, [up_buf.at[g] for g in blocks], [down_buf.at[g] for g in blocks], acc_ref[...])
 
 
 def next_call(rows, ups, downs, acc, mark):
     n_w = len(ups)
     inside = [pltpu.with_memory_space_constraint(x, pltpu.VMEM) for x in (*rows, *acc)]
-    operands = (*inside[:len(rows)], *ups, *downs, *inside[len(rows):], mark)
-    return pl.pallas_call(
-        functools.partial(next_kernel, len(rows), n_w),
+    return pl.pallas_call(
+        functools.partial(next_kernel, n_w),
         out_shape=tuple(jax.ShapeDtypeStruct(x.shape, f32) for x in acc),
-        in_specs=[VMEM] * len(rows) + [ANY] * (2 * n_w) + [VMEM] * len(acc) + [ANY],
-        out_specs=(VMEM,) * len(acc),
+        in_specs=[VMEM] * 2 + [ANY] * (2 * n_w) + [VMEM] * 2 + [ANY],
+        out_specs=(VMEM,) * 2,
         scratch_shapes=[
             pltpu.VMEM((n_w, *ups[0].shape), bf16),
             pltpu.VMEM((n_w, *ups[0].shape), bf16),
             pltpu.SemaphoreType.DMA((2 * n_w,)),
         ],
-        compiler_params=params(24),
-    )(*operands)
+        compiler_params=params(20),
+    )(*inside[:2], *ups, *downs, *inside[2:], mark)
 
 
 def last_kernel(rows_ref, up_ref, down_ref, acc_ref, out_ref):
-    inner = inner_of(rows_ref, up_ref[...], down_ref[...])
-    total = acc_ref[...] + jnp.dot(inner, up_ref[...], preferred_element_type=f32)
-    out_ref[...] = total.astype(out_ref.dtype)
+    out_ref[...] = accumulate(rows_ref, [up_ref], [down_ref], acc_ref[...]).astype(out_ref.dtype)
 
 
 def last_call(rows, up, down, acc, kind):
@@ -212,19 +198,19 @@
     )(*operands)
 
 
-def hold_kernel(x_ref, mark_ref):
-    mark_ref[...] = jnp.zeros_like(mark_ref)
-
-
-def hold(x):
+def hold_kernel(*refs):
+    refs[-1][...] = jnp.zeros_like(refs[-1])
+
+
+def hold(*arrays):
     return pl.pallas_call(
         hold_kernel,
         out_shape=jax.ShapeDtypeStruct((8, 128), f32),
-        in_specs=[ANY],
+        in_specs=[ANY] * len(arrays),
         out_specs=VMEM,
         compiler_params=params(1),
         cost_estimate=pl.CostEstimate(flops=200_000_000_000, bytes_accessed=1_000_000_000, transcendentals=0),
-    )(x)
+    )(*arrays)
 
 
 def local(tokens, tangent, cotangent, routes, gate_num, w_up, w_down):
@@ -254,14 +240,15 @@
     uf3, db3 = send_on(uf2, forth), send_on(db2, back)
     df2, ub2, uf2, db2 = after((df2, ub2, uf2, db2))
     df3, ub3 = send_on(df2, forth), send_on(ub2, back)
-    mark3 = hold(uf3)
+    mine, kept_own, up_stack, down_stack = own_call(own, (up0, uf1, ub1, uf2, ub2), (down0, df1, db1, df2, db2), mark)
+    mark3 = hold(uf3, kept_own)
     uf3, db3, df2, ub2, mark3 = after((uf3, db3, df2, ub2, mark3))
     uf4, db4 = send_on(uf3, forth), send_on(db3, back)
     other = lax.ppermute(own, "dp", swap)
-    *acc, own, other = first_call(own, other, (up0, uf1, ub1, uf2, ub2), (down0, df1, db1, df2, db2), mark)
-    mine, theirs = next_call((own, other), (uf3, ub3), (df3, db3), acc, mark3)
-    passed = lax.ppermute(last_call(other, uf4, db4, theirs, bf16), "dp", swap)
-    kept = last_call(own, uf4, db4, mine, f32)
+    theirs, kept_other = other_call(other, up_stack, down_stack)
+    mine, theirs = next_call((kept_own, kept_other), (uf3, ub3), (df3, db3), (mine, theirs), mark3)
+    passed = lax.ppermute(last_call(kept_other, uf4, db4, theirs, bf16), "dp", swap)
+    kept = last_call(kept_own, uf4, db4, mine, f32)
     whole = (kept + passed.astype(f32)).astype(bf16)
     returned = lax.all_to_all(whole.reshape(experts, CAP, width), "expert", 0, 0, tiled=True)
     returned = returned.reshape(experts * CAP, width)

time: 114 us -> 112 us (0.982)
    ppermute x1, starting transfers between devices: 2.47 us -> 1.32 us  [local(): lax.ppermute(last_call(kept_other, uf4, db4, theirs, bf16), 'dp', swap)]
    pallas_call x2 -> x3, Pallas kernels: 19.3 us -> 19.2 us  [the longest x1 7.81 us: own_call(): pl.pallas_call(functools.partial(own_kernel, n_w), out_shape=(jax.ShapeDt...]
  transfers between devices with their start and end apart: 17 -> 17, of which waited for: 6 -> 5; matrix products, arithmetic and copies ran while one was open for 0% -> 0% of each run, Pallas kernels for 21% -> 21%
where the time goes in v6:
time: 112 us
  starting transfers between devices  33.8 us (30%)
  waiting for transfers between devices  31.3 us (28%)
  Pallas kernels  25.1 us (22%)
  blocking collectives  20.4 us (18%)
  matrix products  1.12 us (1%)
    ppermute x14, waiting for transfers between devices, send_on(): return lax.ppermute(x, 'dp', way)  30.8 us
    ppermute x14, starting transfers between devices, send_on(): return lax.ppermute(x, 'dp', way)  22.7 us
    all_to_all x1, blocking collectives, local(): lax.all_to_all(whole.reshape(experts, CAP, width), 'expert', 0, 0, tiled=...  20.4 us
    pallas_call x1, Pallas kernels, own_call(): pl.pallas_call(functools.partial(own_kernel, n_w), out_shape=(jax.ShapeDt...  7.81 us
    all_to_all x1, starting transfers between devices, local(): lax.all_to_all(send.reshape(experts, CAP, 3 * width), 'expert', 0, 0, til...  6.81 us
    pallas_call x1, Pallas kernels, other_call(): pl.pallas_call(other_kernel, out_shape=(jax.ShapeDtypeStruct((rows, width...  6.43 us
    pallas_call x1, Pallas kernels, next_call(): pl.pallas_call(functools.partial(next_kernel, n_w), out_shape=tuple((jax....  4.97 us
    pallas_call x1, Pallas kernels, prepare(): pl.pallas_call(prepare_kernel, out_shape=(jax.ShapeDtypeStruct((slots, 3...  3.07 us
  transfers between devices with their start and end apart: 17, of which 5 were waited for; matrix products, arithmetic and copies ran while one was open for 0% of the time, Pallas kernels for 21%

profile of v6, /device:TPU:1, one launch (start us, length us, event | category | flops | bytes accessed | tf_op | source)
XLA Modules:
  0.0 112.1 jit_solution(12802144692636587145)
XLA Ops:
  0.0 2.5 %collective-permute-start = (bf16[256,1024]{1,0:T(8,128)(2,1)}, bf16[256,1024]{1,0:T(8,128)(2,1)S(1)}, u32[]{:S(2)}, u32[]{:S(2)}) collective-permute-start(bf16[256,1024]{1,0:T(8,128)(2,1)} %bitcast.10), channel_id=1, source_target_pairs={{0,32},{16,48},{32,64},{48,80},{64,96},{80,112},{96,128},{112,144}... | collective-permute-start | bytes 1572872 | tf_op jit(solution)/shard_map/ppermute | solution.py:226
  2.5 3.9 %collective-permute-start.1 = (bf16[256,1024]{1,0:T(8,128)(2,1)}, bf16[256,1024]{1,0:T(8,128)(2,1)}, u32[]{:S(2)}, u32[]{:S(2)}) collective-permute-start(bf16[256,1024]{1,0:T(8,128)(2,1)} %bitcast.13), channel_id=1, source_target_pairs={{0,224},{16,240},{32,0},{48,16},{64,32},{80,48},{96,64},{112,80},{... | collective-permute-start | bytes 1572872 | tf_op jit(solution)/shard_map/ppermute | solution.py:226
  6.4 0.0 collective-permute-start.4
  6.4 2.7 %collective-permute-start.5 = (bf16[256,1024]{1,0:T(8,128)(2,1)}, bf16[256,1024]{1,0:T(8,128)(2,1)}, u32[]{:S(2)}, u32[]{:S(2)}) collective-permute-start(bf16[256,1024]{1,0:T(8,128)(2,1)} %bitcast.11), channel_id=1, source_target_pairs={{0,224},{16,240},{32,0},{48,16},{64,32},{80,48},{96,64},{112,80},{... | collective-permute-start | bytes 1572872 | tf_op jit(solution)/shard_map/ppermute | solution.py:226
  9.1 3.1 %shard_map.73 = (bf16[384,3072]{1,0:T(8,128)(2,1)}, bf16[384,128]{1,0:T(8,128)(2,1)S(1)}) custom-call(s32[2,128]{1,0:T(2,128)} %bitcast.18, s32[2,128]{1,0:T(2,128)} %bitcast.19, bf16[128,1024]{1,0:T(8,128)(2,1)} %x_hbm.1, bf16[128,1024]{1,0:T(8,128)(2,1)} %t_hbm.1, bf16[128,1024]{1,0:T(8,128)(2,1)} %c_hbm.1), custom_call_target="tpu_custom_call" | custom-call | tf_op jit(solution)/shard_map/pallas_call | solution.py:61
  12.2 6.8 %all-to-all-start = ((bf16[16,24,3072]{2,1,0:T(8,128)(2,1)}), bf16[16,24,3072]{2,1,0:T(8,128)(2,1)}, u32[]{:S(2)}, u32[]{:S(2)}) async-start(bf16[16,24,3072]{2,1,0:T(8,128)(2,1)} %bitcast.2), calls=%async_computation | async-start | bytes 4718592 | tf_op jit(solution)/shard_map/all_to_all | solution.py:232
  19.0 0.0 collective-permute-done.refs_0_.refs_1_
  19.0 0.0 copy-start
  19.0 0.0 copy-start.1
  19.0 0.0 collective-permute-done.1.refs_7_
  19.0 0.1 collective-permute-start.2
  19.1 2.7 %collective-permute-start.3 = (bf16[256,1024]{1,0:T(8,128)(2,1)}, bf16[256,1024]{1,0:T(8,128)(2,1)}, u32[]{:S(2)}, u32[]{:S(2)}) collective-permute-start(bf16[256,1024]{1,0:T(8,128)(2,1)} %collective-permute-done.1.refs_7_), channel_id=1, source_target_pairs={{0,224},{16,240},{32,0},{48,16},{64,32},{80,48},{96,64},{112,80},{... | collective-permute-start | bytes 1572872 | tf_op jit(solution)/shard_map/ppermute | solution.py:226
  21.8 7.8 %collective-permute-done.4.refs_6_ = bf16[256,1024]{1,0:T(8,128)(2,1)} collective-permute-done((bf16[256,1024]{1,0:T(8,128)(2,1)}, bf16[256,1024]{1,0:T(8,128)(2,1)}, u32[]{:S(2)}, u32[]{:S(2)}) %collective-permute-start.4) | collective-permute-done | bytes 524320 | tf_op jit(solution)/shard_map/ppermute | solution.py:226
  29.6 0.0 collective-permute-done.5.refs_2_
  29.6 0.0 collective-permute-start.6
  29.6 2.7 %collective-permute-start.7 = (bf16[256,1024]{1,0:T(8,128)(2,1)}, bf16[256,1024]{1,0:T(8,128)(2,1)}, u32[]{:S(2)}, u32[]{:S(2)}) collective-permute-start(bf16[256,1024]{1,0:T(8,128)(2,1)} %collective-permute-done.5.refs_2_), channel_id=1, source_target_pairs={{0,224},{16,240},{32,0},{48,16},{64,32},{80,48},{96,64},{112,80},{... | collective-permute-start | bytes 1572872 | tf_op jit(solution)/shard_map/ppermute | solution.py:226
  32.3 8.6 %collective-permute-done.2.refs_3_ = bf16[256,1024]{1,0:T(8,128)(2,1)S(1)} collective-permute-done((bf16[256,1024]{1,0:T(8,128)(2,1)S(1)}, bf16[256,1024]{1,0:T(8,128)(2,1)S(1)}, u32[]{:S(2)}, u32[]{:S(2)}) %collective-permute-start.2) | collective-permute-done | bytes 524320 | tf_op jit(solution)/shard_map/ppermute | solution.py:226
  40.8 0.0 collective-permute-done.3.refs_9_
  40.8 0.0 collective-permute-start.8
  40.8 2.7 %collective-permute-start.9 = (bf16[256,1024]{1,0:T(8,128)(2,1)}, bf16[256,1024]{1,0:T(8,128)(2,1)}, u32[]{:S(2)}, u32[]{:S(2)}) collective-permute-start(bf16[256,1024]{1,0:T(8,128)(2,1)} %collective-permute-done.3.refs_9_), channel_id=1, source_target_pairs={{0,224},{16,240},{32,0},{48,16},{64,32},{80,48},{96,64},{112,80},{... | collective-permute-start | bytes 1572872 | tf_op jit(solution)/shard_map/ppermute | solution.py:226
  43.5 8.6 %collective-permute-done.6.refs_8_ = bf16[256,1024]{1,0:T(8,128)(2,1)} collective-permute-done((bf16[256,1024]{1,0:T(8,128)(2,1)}, bf16[256,1024]{1,0:T(8,128)(2,1)}, u32[]{:S(2)}, u32[]{:S(2)}) %collective-permute-start.6) | collective-permute-done | bytes 524320 | tf_op jit(solution)/shard_map/ppermute | solution.py:226
  52.1 0.0 collective-permute-done.7.refs_4_
  52.1 2.4 %collective-permute-start.13 = (bf16[256,1024]{1,0:T(8,128)(2,1)}, bf16[256,1024]{1,0:T(8,128)(2,1)}, u32[]{:S(2)}, u32[]{:S(2)}) collective-permute-start(bf16[256,1024]{1,0:T(8,128)(2,1)} %collective-permute-done.7.refs_4_), channel_id=1, source_target_pairs={{0,224},{16,240},{32,0},{48,16},{64,32},{80,48},{96,64},{112,80},{... | collective-permute-start | bytes 1572872 | tf_op jit(solution)/shard_map/ppermute | solution.py:226
  54.4 0.0 collective-permute-start.14
  54.4 0.0 all-to-all-done
  54.4 3.0 %collective-permute-start.12 = (bf16[384,3072]{1,0:T(8,128)(2,1)}, bf16[384,3072]{1,0:T(8,128)(2,1)}, u32[]{:S(2)}, u32[]{:S(2)}) collective-permute-start(bf16[384,3072]{1,0:T(8,128)(2,1)} %bitcast.3.own_ref), channel_id=1, source_target_pairs={{0,16},{16,0},{32,48},{48,32},{64,80},{80,64},{96,112},{112,96},{1... | collective-permute-start | bytes 7077896 | tf_op jit(solution)/shard_map/ppermute | solution.py:247
  57.4 0.0 copy-done
  57.4 0.0 copy-done.1
  57.4 7.8 %shard_map.75 = (f32[384,1024]{1,0:T(8,128)S(1)}, bf16[384,3072]{1,0:T(8,128)(2,1)S(1)}, bf16[5,256,1024]{2,1,0:T(8,128)(2,1)S(1)}, bf16[5,256,1024]{2,1,0:T(8,128)(2,1)S(1)}) custom-call(bf16[384,3072]{1,0:T(8,128)(2,1)} %bitcast.3.own_ref, bf16[256,1024]{1,0:T(8,128)(2,1)S(1)} %bitcast.12, bf16[256,1024]{1,0:T(8,128)(2,1)S(1)} %collective-permute-done.refs_0_.refs_1_, ...), custom_call_target="tpu_custom_call" | custom-call | tf_op jit(solution)/shard_map/pallas_call | solution.py:122
  65.2 0.0 collective-permute-done.8.refs_0_
  65.3 0.0 collective-permute-done.9.refs_3_
  65.3 0.1 collective-permute-start.10
  65.4 3.0 %collective-permute-start.11 = (bf16[256,1024]{1,0:T(8,128)(2,1)}, bf16[256,1024]{1,0:T(8,128)(2,1)S(1)}, u32[]{:S(2)}, u32[]{:S(2)}) collective-permute-start(bf16[256,1024]{1,0:T(8,128)(2,1)} %collective-permute-done.9.refs_3_), channel_id=1, source_target_pairs={{0,224},{16,240},{32,0},{48,16},{64,32},{80,48},{96,64},{112,80},{... | collective-permute-start | bytes 1572872 | tf_op jit(solution)/shard_map/ppermute | solution.py:226
  68.4 0.0 collective-permute-done.12.other_ref
  68.4 6.4 %shard_map.77 = (f32[384,1024]{1,0:T(8,128)S(1)}, bf16[384,3072]{1,0:T(8,128)(2,1)S(1)}) custom-call(bf16[384,3072]{1,0:T(8,128)(2,1)} %collective-permute-done.12.other_ref, bf16[5,256,1024]{2,1,0:T(8,128)(2,1)S(1)} %get-tuple-element.51.up_ref, bf16[5,256,1024]{2,1,0:T(8,128)(2,1)S(1)} %get-tuple-element.52.down_ref), custom_call_target="tpu_custom_call" | custom-call | tf_op jit(solution)/shard_map/pallas_call | solution.py:143
  74.8 0.0 collective-permute-done.13.refs_1_
  74.8 0.0 collective-permute-done.14.refs_2_
  74.8 5.0 %shard_map.78 = (f32[384,1024]{1,0:T(8,128)S(1)}, f32[384,1024]{1,0:T(8,128)S(1)}) custom-call(bf16[384,3072]{1,0:T(8,128)(2,1)S(1)} %get-tuple-element.48.refs_1_.own_ref.rows_ref, bf16[384,3072]{1,0:T(8,128)(2,1)S(1)} %get-tuple-element.53.other_ref.rows_ref, bf16[256,1024]{1,0:T(8,128)(2,1)S(1)} %collective-permute-done.8.refs_0_, ...), custom_call_target="tpu_custom_call" | custom-call | tf_op jit(solution)/shard_map/pallas_call | solution.py:172
  79.8 5.8 %collective-permute-done.10.up_ref = bf16[256,1024]{1,0:T(8,128)(2,1)S(1)} collective-permute-done((bf16[256,1024]{1,0:T(8,128)(2,1)S(1)}, bf16[256,1024]{1,0:T(8,128)(2,1)S(1)}, u32[]{:S(2)}, u32[]{:S(2)}) %collective-permute-start.10) | collective-permute-done | bytes 524320 | tf_op jit(solution)/shard_map/ppermute | solution.py:226
  85.7 0.0 collective-permute-done.11.down_ref
  85.7 1.4 %shard_map.80 = bf16[384,1024]{1,0:T(8,128)(2,1)S(1)} custom-call(bf16[384,3072]{1,0:T(8,128)(2,1)S(1)} %get-tuple-element.53.other_ref.rows_ref, bf16[256,1024]{1,0:T(8,128)(2,1)S(1)} %collective-permute-done.10.up_ref, bf16[256,1024]{1,0:T(8,128)(2,1)S(1)} %collective-permute-done.11.down_ref, f32[384,1024]{1,0:T(8,128)S(1)} %get-tuple-element.58.acc_ref), custom_call_target="tpu_custom_call" | custom-call | tf_op jit(solution)/shard_map/pallas_call | solution.py:192
  87.1 1.3 %collective-permute-start.15 = (bf16[384,1024]{1,0:T(8,128)(2,1)S(1)}, bf16[384,1024]{1,0:T(8,128)(2,1)S(1)}, u32[]{:S(2)}, u32[]{:S(2)}) collective-permute-start(bf16[384,1024]{1,0:T(8,128)(2,1)S(1)} %shard_map.80), channel_id=1, source_target_pairs={{0,16},{16,0},{32,48},{48,32},{64,80},{80,64},{96,112},{112,96},{1... | collective-permute-start | bytes 2359304 | tf_op jit(solution)/shard_map/ppermute | solution.py:250
  88.4 1.4 %shard_map.79 = f32[384,1024]{1,0:T(8,128)S(1)} custom-call(bf16[384,3072]{1,0:T(8,128)(2,1)S(1)} %get-tuple-element.48.refs_1_.own_ref.rows_ref, bf16[256,1024]{1,0:T(8,128)(2,1)S(1)} %collective-permute-done.10.up_ref, bf16[256,1024]{1,0:T(8,128)(2,1)S(1)} %collective-permute-done.11.down_ref, f32[384,1024]{1,0:T(8,128)S(1)} %get-tuple-element.57.acc_ref), custom_call_target="tpu_custom_call" | custom-call | tf_op jit(solution)/shard_map/pallas_call | solution.py:192
  89.9 0.5 collective-permute-done.15
  90.3 0.3 add_convert_fusion
  90.6 20.4 %all_to_all.10 = bf16[16,24,1024]{2,1,0:T(8,128)(2,1)S(1)} all-to-all(bf16[16,24,1024]{2,1,0:T(8,128)(2,1)S(1)} %bitcast.17), channel_id=1, replica_groups=mesh['dp'=16,'expert'=16] {'expert'}, dimensions={0} | all-to-all | bytes 1572864 | tf_op jit(solution)/shard_map/all_to_all | solution.py:253
  111.0 1.1 fusion
  (2 shorter events, 0.0 us)
Async XLA Ops:
  0.0 19.0 %collective-permute-start = (bf16[256,1024]{1,0:T(8,128)(2,1)}, bf16[256,1024]{1,0:T(8,128)(2,1)S(1)}, u32[]{:S(2)}, u32[]{:S(2)}) collective-permute-start(bf16[256,1024]{1,0:T(8,128)(2,1)} %bitcast.10), channel_id=1, source_target_pairs={{0,32},{16,48},{32,64},{48,80},{64,96},{80,112},{96,128},{112,144}... | collective-permute-start | bytes 1572872 | tf_op jit(solution)/shard_map/ppermute | solution.py:226
  2.5 16.6 %collective-permute-start.1 = (bf16[256,1024]{1,0:T(8,128)(2,1)}, bf16[256,1024]{1,0:T(8,128)(2,1)}, u32[]{:S(2)}, u32[]{:S(2)}) collective-permute-start(bf16[256,1024]{1,0:T(8,128)(2,1)} %bitcast.13), channel_id=1, source_target_pairs={{0,224},{16,240},{32,0},{48,16},{64,32},{80,48},{96,64},{112,80},{... | collective-permute-start | bytes 1572872 | tf_op jit(solution)/shard_map/ppermute | solution.py:226
  6.4 23.2 %collective-permute-start.4 = (bf16[256,1024]{1,0:T(8,128)(2,1)}, bf16[256,1024]{1,0:T(8,128)(2,1)}, u32[]{:S(2)}, u32[]{:S(2)}) collective-permute-start(bf16[256,1024]{1,0:T(8,128)(2,1)} %bitcast.14), channel_id=1, source_target_pairs={{0,32},{16,48},{32,64},{48,80},{64,96},{80,112},{96,128},{112,144}... | collective-permute-start | bytes 1572872 | tf_op jit(solution)/shard_map/ppermute | solution.py:226
  6.4 23.2 %collective-permute-start.5 = (bf16[256,1024]{1,0:T(8,128)(2,1)}, bf16[256,1024]{1,0:T(8,128)(2,1)}, u32[]{:S(2)}, u32[]{:S(2)}) collective-permute-start(bf16[256,1024]{1,0:T(8,128)(2,1)} %bitcast.11), channel_id=1, source_target_pairs={{0,224},{16,240},{32,0},{48,16},{64,32},{80,48},{96,64},{112,80},{... | collective-permute-start | bytes 1572872 | tf_op jit(solution)/shard_map/ppermute | solution.py:226
  12.2 42.3 %all-to-all-start = ((bf16[16,24,3072]{2,1,0:T(8,128)(2,1)}), bf16[16,24,3072]{2,1,0:T(8,128)(2,1)}, u32[]{:S(2)}, u32[]{:S(2)}) async-start(bf16[16,24,3072]{2,1,0:T(8,128)(2,1)} %bitcast.2), calls=%async_computation | async-start | bytes 4718592 | tf_op jit(solution)/shard_map/all_to_all | solution.py:232
  19.0 38.4 %copy-start = (bf16[1,256,1024]{2,1,0:T(8,128)(2,1)S(1)}, bf16[1,256,1024]{2,1,0:T(8,128)(2,1)}, u32[]{:S(2)}) copy-start(bf16[1,256,1024]{2,1,0:T(8,128)(2,1)} %param.12) | copy-start | bytes 1572868
  19.0 38.4 %copy-start.1 = (bf16[1,256,1024]{2,1,0:T(8,128)(2,1)S(1)}, bf16[1,256,1024]{2,1,0:T(8,128)(2,1)}, u32[]{:S(2)}) copy-start(bf16[1,256,1024]{2,1,0:T(8,128)(2,1)} %param.13) | copy-start | bytes 1572868
  19.0 21.8 %collective-permute-start.2 = (bf16[256,1024]{1,0:T(8,128)(2,1)S(1)}, bf16[256,1024]{1,0:T(8,128)(2,1)S(1)}, u32[]{:S(2)}, u32[]{:S(2)}) collective-permute-start(bf16[256,1024]{1,0:T(8,128)(2,1)S(1)} %collective-permute-done.refs_0_.refs_1_), channel_id=1, source_target_pairs={{0,32},{16,48},{32,64},{48,80},{64,96},{80,112},{96,128},{112,144}... | collective-permute-start | bytes 1572872 | tf_op jit(solution)/shard_map/ppermute | solution.py:226
  19.1 21.7 %collective-permute-start.3 = (bf16[256,1024]{1,0:T(8,128)(2,1)}, bf16[256,1024]{1,0:T(8,128)(2,1)}, u32[]{:S(2)}, u32[]{:S(2)}) collective-permute-start(bf16[256,1024]{1,0:T(8,128)(2,1)} %collective-permute-done.1.refs_7_), channel_id=1, source_target_pairs={{0,224},{16,240},{32,0},{48,16},{64,32},{80,48},{96,64},{112,80},{... | collective-permute-start | bytes 1572872 | tf_op jit(solution)/shard_map/ppermute | solution.py:226
  29.6 22.5 %collective-permute-start.6 = (bf16[256,1024]{1,0:T(8,128)(2,1)}, bf16[256,1024]{1,0:T(8,128)(2,1)}, u32[]{:S(2)}, u32[]{:S(2)}) collective-permute-start(bf16[256,1024]{1,0:T(8,128)(2,1)} %collective-permute-done.4.refs_6_), channel_id=1, source_target_pairs={{0,32},{16,48},{32,64},{48,80},{64,96},{80,112},{96,128},{112,144}... | collective-permute-start | bytes 1572872 | tf_op jit(solution)/shard_map/ppermute | solution.py:226
  29.6 22.5 %collective-permute-start.7 = (bf16[256,1024]{1,0:T(8,128)(2,1)}, bf16[256,1024]{1,0:T(8,128)(2,1)}, u32[]{:S(2)}, u32[]{:S(2)}) collective-permute-start(bf16[256,1024]{1,0:T(8,128)(2,1)} %collective-permute-done.5.refs_2_), channel_id=1, source_target_pairs={{0,224},{16,240},{32,0},{48,16},{64,32},{80,48},{96,64},{112,80},{... | collective-permute-start | bytes 1572872 | tf_op jit(solution)/shard_map/ppermute | solution.py:226
  40.8 24.4 %collective-permute-start.8 = (bf16[256,1024]{1,0:T(8,128)(2,1)S(1)}, bf16[256,1024]{1,0:T(8,128)(2,1)S(1)}, u32[]{:S(2)}, u32[]{:S(2)}) collective-permute-start(bf16[256,1024]{1,0:T(8,128)(2,1)S(1)} %collective-permute-done.2.refs_3_), channel_id=1, source_target_pairs={{0,32},{16,48},{32,64},{48,80},{64,96},{80,112},{96,128},{112,144}... | collective-permute-start | bytes 1572872 | tf_op jit(solution)/shard_map/ppermute | solution.py:226
  40.8 24.4 %collective-permute-start.9 = (bf16[256,1024]{1,0:T(8,128)(2,1)}, bf16[256,1024]{1,0:T(8,128)(2,1)}, u32[]{:S(2)}, u32[]{:S(2)}) collective-permute-start(bf16[256,1024]{1,0:T(8,128)(2,1)} %collective-permute-done.3.refs_9_), channel_id=1, source_target_pairs={{0,224},{16,240},{32,0},{48,16},{64,32},{80,48},{96,64},{112,80},{... | collective-permute-start | bytes 1572872 | tf_op jit(solution)/shard_map/ppermute | solution.py:226
  52.1 22.8 %collective-permute-start.13 = (bf16[256,1024]{1,0:T(8,128)(2,1)}, bf16[256,1024]{1,0:T(8,128)(2,1)}, u32[]{:S(2)}, u32[]{:S(2)}) collective-permute-start(bf16[256,1024]{1,0:T(8,128)(2,1)} %collective-permute-done.7.refs_4_), channel_id=1, source_target_pairs={{0,224},{16,240},{32,0},{48,16},{64,32},{80,48},{96,64},{112,80},{... | collective-permute-start | bytes 1572872 | tf_op jit(solution)/shard_map/ppermute | solution.py:226
  54.4 20.4 %collective-permute-start.14 = (bf16[256,1024]{1,0:T(8,128)(2,1)}, bf16[256,1024]{1,0:T(8,128)(2,1)}, u32[]{:S(2)}, u32[]{:S(2)}) collective-permute-start(bf16[256,1024]{1,0:T(8,128)(2,1)} %collective-permute-done.6.refs_8_), channel_id=1, source_target_pairs={{0,32},{16,48},{32,64},{48,80},{64,96},{80,112},{96,128},{112,144}... | collective-permute-start | bytes 1572872 | tf_op jit(solution)/shard_map/ppermute | solution.py:226
  54.4 14.0 %collective-permute-start.12 = (bf16[384,3072]{1,0:T(8,128)(2,1)}, bf16[384,3072]{1,0:T(8,128)(2,1)}, u32[]{:S(2)}, u32[]{:S(2)}) collective-permute-start(bf16[384,3072]{1,0:T(8,128)(2,1)} %bitcast.3.own_ref), channel_id=1, source_target_pairs={{0,16},{16,0},{32,48},{48,32},{64,80},{80,64},{96,112},{112,96},{1... | collective-permute-start | bytes 7077896 | tf_op jit(solution)/shard_map/ppermute | solution.py:247
  65.3 20.4 %collective-permute-start.10 = (bf16[256,1024]{1,0:T(8,128)(2,1)S(1)}, bf16[256,1024]{1,0:T(8,128)(2,1)S(1)}, u32[]{:S(2)}, u32[]{:S(2)}) collective-permute-start(bf16[256,1024]{1,0:T(8,128)(2,1)S(1)} %collective-permute-done.8.refs_0_), channel_id=1, source_target_pairs={{0,32},{16,48},{32,64},{48,80},{64,96},{80,112},{96,128},{112,144}... | collective-permute-start | bytes 1572872 | tf_op jit(solution)/shard_map/ppermute | solution.py:226
  65.4 20.3 %collective-permute-start.11 = (bf16[256,1024]{1,0:T(8,128)(2,1)}, bf16[256,1024]{1,0:T(8,128)(2,1)S(1)}, u32[]{:S(2)}, u32[]{:S(2)}) collective-permute-start(bf16[256,1024]{1,0:T(8,128)(2,1)} %collective-permute-done.9.refs_3_), channel_id=1, source_target_pairs={{0,224},{16,240},{32,0},{48,16},{64,32},{80,48},{96,64},{112,80},{... | collective-permute-start | bytes 1572872 | tf_op jit(solution)/shard_map/ppermute | solution.py:226
  87.1 3.2 %collective-permute-start.15 = (bf16[384,1024]{1,0:T(8,128)(2,1)S(1)}, bf16[384,1024]{1,0:T(8,128)(2,1)S(1)}, u32[]{:S(2)}, u32[]{:S(2)}) collective-permute-start(bf16[384,1024]{1,0:T(8,128)(2,1)S(1)} %shard_map.80), channel_id=1, source_target_pairs={{0,16},{16,0},{32,48},{48,32},{64,80},{80,64},{96,112},{112,96},{1... | collective-permute-start | bytes 2359304 | tf_op jit(solution)/shard_map/ppermute | solution.py:250

commit v7 on v6

--- a/solution.py
+++ b/solution.py
@@ -183,18 +183,33 @@
     )(*inside[:2], *ups, *downs, *inside[2:], mark)
 
 
-def last_kernel(rows_ref, up_ref, down_ref, acc_ref, out_ref):
-    out_ref[...] = accumulate(rows_ref, [up_ref], [down_ref], acc_ref[...]).astype(out_ref.dtype)
-
-
-def last_call(rows, up, down, acc, kind):
-    operands = tuple(pltpu.with_memory_space_constraint(x, pltpu.VMEM) for x in (rows, up, down, acc))
-    return pl.pallas_call(
-        last_kernel,
-        out_shape=jax.ShapeDtypeStruct(acc.shape, kind),
-        in_specs=[VMEM] * 4,
+def factor_kernel(rows_ref, up_ref, factor_ref):
+    width = up_ref.shape[1]
+    before_act = lax.dot_general(rows_ref[:, :width], up_ref[...], NT, preferred_element_type=f32)
+    lifted = lax.dot_general(rows_ref[:, width:2 * width], up_ref[...], NT, preferred_element_type=f32)
+    factor_ref[...] = curvature(before_act) * lifted
+
+
+def last_other_kernel(rows_ref, factor_ref, up_ref, down_ref, acc_ref, out_ref):
+    width = up_ref.shape[1]
+    pulled = lax.dot_general(rows_ref[:, 2 * width:], down_ref[...], NT, preferred_element_type=f32)
+    inner = (pulled * factor_ref[...]).astype(bf16)
+    total = acc_ref[...] + jnp.dot(inner, up_ref[...], preferred_element_type=f32)
+    out_ref[...] = total.astype(out_ref.dtype)
+
+
+def last_own_kernel(rows_ref, up_ref, down_ref, acc_ref, out_ref):
+    out_ref[...] = accumulate(rows_ref, [up_ref], [down_ref], acc_ref[...])
+
+
+def last_call(kernel, shape, kind, *operands):
+    operands = tuple(pltpu.with_memory_space_constraint(x, pltpu.VMEM) for x in operands)
+    return pl.pallas_call(
+        kernel,
+        out_shape=jax.ShapeDtypeStruct(shape, kind),
+        in_specs=[VMEM] * len(operands),
         out_specs=VMEM,
-        compiler_params=params(16),
+        compiler_params=params(12),
     )(*operands)
 
 
@@ -247,8 +262,11 @@
     other = lax.ppermute(own, "dp", swap)
     theirs, kept_other = other_call(other, up_stack, down_stack)
     mine, theirs = next_call((kept_own, kept_other), (uf3, ub3), (df3, db3), (mine, theirs), mark3)
-    passed = lax.ppermute(last_call(kept_other, uf4, db4, theirs, bf16), "dp", swap)
-    kept = last_call(kept_own, uf4, db4, mine, f32)
+    uf4, theirs = after((uf4, theirs))
+    factor = last_call(factor_kernel, (other.shape[0], uf4.shape[0]), f32, kept_other, uf4)
+    passed = last_call(last_other_kernel, theirs.shape, bf16, kept_other, factor, uf4, db4, theirs)
+    passed = send_on(passed, swap)
+    kept = last_call(last_own_kernel, mine.shape, f32, kept_own, uf4, db4, mine)
     whole = (kept + passed.astype(f32)).astype(bf16)
     returned = lax.all_to_all(whole.reshape(experts, CAP, width), "expert", 0, 0, tiled=True)
     returned = returned.reshape(experts * CAP, width)

time: 112 us -> 113 us (level)
    ppermute x1 -> x0, starting transfers between devices: 1.32 us -> none  [local(): lax.ppermute(last_call(kept_other, uf4, db4, theirs, bf16), 'dp', swap)]
    ppermute x14 -> x15, starting transfers between devices: 22.7 us -> 24 us  [send_on(): return lax.ppermute(x, 'dp', way)]
    ppermute x14 -> x15, waiting for transfers between devices: 30.8 us -> 31.3 us  [send_on(): return lax.ppermute(x, 'dp', way)]
    pallas_call x2 -> x3, Pallas kernels: 2.86 us -> 3.09 us  [last_call(): pl.pallas_call(kernel, out_shape=jax.ShapeDtypeStruct(shape, kind), in_sp...]
  transfers between devices with their start and end apart: 17 -> 17, of which waited for: 5 -> 5; matrix products, arithmetic and copies ran while one was open for 0% -> 0% of each run, Pallas kernels for 21% -> 22%
where the time goes in v7:
time: 113 us; the launch traced here: 112 us
  starting transfers between devices  33.8 us (30%)
  waiting for transfers between devices  31.3 us (28%)
  Pallas kernels  25.4 us (22%)
  blocking collectives  20.4 us (18%)
    ppermute x15, waiting for transfers between devices, send_on(): return lax.ppermute(x, 'dp', way)  31.3 us
    ppermute x15, starting transfers between devices, send_on(): return lax.ppermute(x, 'dp', way)  24 us
    all_to_all x1, blocking collectives, local(): lax.all_to_all(whole.reshape(experts, CAP, width), 'expert', 0, 0, tiled=...  20.4 us
    pallas_call x1, Pallas kernels, own_call(): pl.pallas_call(functools.partial(own_kernel, n_w), out_shape=(jax.ShapeDt...  7.81 us
    all_to_all x1, starting transfers between devices, local(): lax.all_to_all(send.reshape(experts, CAP, 3 * width), 'expert', 0, 0, til...  6.81 us
    pallas_call x1, Pallas kernels, other_call(): pl.pallas_call(other_kernel, out_shape=(jax.ShapeDtypeStruct((rows, width...  6.43 us
    pallas_call x1, Pallas kernels, next_call(): pl.pallas_call(functools.partial(next_kernel, n_w), out_shape=tuple((jax....  4.97 us
    pallas_call x3, Pallas kernels, last_call(): pl.pallas_call(kernel, out_shape=jax.ShapeDtypeStruct(shape, kind), in_sp...  3.09 us
  transfers between devices with their start and end apart: 17, of which 5 were waited for; matrix products, arithmetic and copies ran while one was open for 0% of the time, Pallas kernels for 22%

profile of v7, /device:TPU:1, one launch (start us, length us, event | category | flops | bytes accessed | tf_op | source)
XLA Modules:
  0.0 112.3 jit_solution(13167174143032171085)
XLA Ops:
  0.0 2.5 %collective-permute-start = (bf16[256,1024]{1,0:T(8,128)(2,1)}, bf16[256,1024]{1,0:T(8,128)(2,1)S(1)}, u32[]{:S(2)}, u32[]{:S(2)}) collective-permute-start(bf16[256,1024]{1,0:T(8,128)(2,1)} %bitcast.10), channel_id=1, source_target_pairs={{0,32},{16,48},{32,64},{48,80},{64,96},{80,112},{96,128},{112,144}... | collective-permute-start | bytes 1572872 | tf_op jit(solution)/shard_map/ppermute | solution.py:241
  2.5 3.9 %collective-permute-start.1 = (bf16[256,1024]{1,0:T(8,128)(2,1)}, bf16[256,1024]{1,0:T(8,128)(2,1)}, u32[]{:S(2)}, u32[]{:S(2)}) collective-permute-start(bf16[256,1024]{1,0:T(8,128)(2,1)} %bitcast.13), channel_id=1, source_target_pairs={{0,224},{16,240},{32,0},{48,16},{64,32},{80,48},{96,64},{112,80},{... | collective-permute-start | bytes 1572872 | tf_op jit(solution)/shard_map/ppermute | solution.py:241
  6.4 0.0 collective-permute-start.4
  6.4 2.7 %collective-permute-start.5 = (bf16[256,1024]{1,0:T(8,128)(2,1)}, bf16[256,1024]{1,0:T(8,128)(2,1)}, u32[]{:S(2)}, u32[]{:S(2)}) collective-permute-start(bf16[256,1024]{1,0:T(8,128)(2,1)} %bitcast.11), channel_id=1, source_target_pairs={{0,224},{16,240},{32,0},{48,16},{64,32},{80,48},{96,64},{112,80},{... | collective-permute-start | bytes 1572872 | tf_op jit(solution)/shard_map/ppermute | solution.py:241
  9.1 3.1 %shard_map.73 = (bf16[384,3072]{1,0:T(8,128)(2,1)}, bf16[384,128]{1,0:T(8,128)(2,1)S(1)}) custom-call(s32[2,128]{1,0:T(2,128)} %bitcast.18, s32[2,128]{1,0:T(2,128)} %bitcast.19, bf16[128,1024]{1,0:T(8,128)(2,1)} %x_hbm.1, bf16[128,1024]{1,0:T(8,128)(2,1)} %t_hbm.1, bf16[128,1024]{1,0:T(8,128)(2,1)} %c_hbm.1), custom_call_target="tpu_custom_call" | custom-call | tf_op jit(solution)/shard_map/pallas_call | solution.py:61
  12.2 6.8 %all-to-all-start = ((bf16[16,24,3072]{2,1,0:T(8,128)(2,1)}), bf16[16,24,3072]{2,1,0:T(8,128)(2,1)}, u32[]{:S(2)}, u32[]{:S(2)}) async-start(bf16[16,24,3072]{2,1,0:T(8,128)(2,1)} %bitcast.2), calls=%async_computation | async-start | bytes 4718592 | tf_op jit(solution)/shard_map/all_to_all | solution.py:247
  19.0 0.0 collective-permute-done.refs_0_.refs_1_
  19.0 0.0 copy-start
  19.0 0.0 copy-start.1
  19.0 0.0 collective-permute-done.1.refs_7_
  19.0 0.1 collective-permute-start.2
  19.1 2.7 %collective-permute-start.3 = (bf16[256,1024]{1,0:T(8,128)(2,1)}, bf16[256,1024]{1,0:T(8,128)(2,1)}, u32[]{:S(2)}, u32[]{:S(2)}) collective-permute-start(bf16[256,1024]{1,0:T(8,128)(2,1)} %collective-permute-done.1.refs_7_), channel_id=1, source_target_pairs={{0,224},{16,240},{32,0},{48,16},{64,32},{80,48},{96,64},{112,80},{... | collective-permute-start | bytes 1572872 | tf_op jit(solution)/shard_map/ppermute | solution.py:241
  21.8 7.8 %collective-permute-done.4.refs_6_ = bf16[256,1024]{1,0:T(8,128)(2,1)} collective-permute-done((bf16[256,1024]{1,0:T(8,128)(2,1)}, bf16[256,1024]{1,0:T(8,128)(2,1)}, u32[]{:S(2)}, u32[]{:S(2)}) %collective-permute-start.4) | collective-permute-done | bytes 524320 | tf_op jit(solution)/shard_map/ppermute | solution.py:241
  29.6 0.0 collective-permute-done.5.refs_2_
  29.6 0.0 collective-permute-start.6
  29.6 2.7 %collective-permute-start.7 = (bf16[256,1024]{1,0:T(8,128)(2,1)}, bf16[256,1024]{1,0:T(8,128)(2,1)}, u32[]{:S(2)}, u32[]{:S(2)}) collective-permute-start(bf16[256,1024]{1,0:T(8,128)(2,1)} %collective-permute-done.5.refs_2_), channel_id=1, source_target_pairs={{0,224},{16,240},{32,0},{48,16},{64,32},{80,48},{96,64},{112,80},{... | collective-permute-start | bytes 1572872 | tf_op jit(solution)/shard_map/ppermute | solution.py:241
  32.3 8.6 %collective-permute-done.2.refs_3_ = bf16[256,1024]{1,0:T(8,128)(2,1)S(1)} collective-permute-done((bf16[256,1024]{1,0:T(8,128)(2,1)S(1)}, bf16[256,1024]{1,0:T(8,128)(2,1)S(1)}, u32[]{:S(2)}, u32[]{:S(2)}) %collective-permute-start.2) | collective-permute-done | bytes 524320 | tf_op jit(solution)/shard_map/ppermute | solution.py:241
  40.8 0.0 collective-permute-done.3.refs_9_
  40.8 0.0 collective-permute-start.8
  40.8 2.7 %collective-permute-start.9 = (bf16[256,1024]{1,0:T(8,128)(2,1)}, bf16[256,1024]{1,0:T(8,128)(2,1)}, u32[]{:S(2)}, u32[]{:S(2)}) collective-permute-start(bf16[256,1024]{1,0:T(8,128)(2,1)} %collective-permute-done.3.refs_9_), channel_id=1, source_target_pairs={{0,224},{16,240},{32,0},{48,16},{64,32},{80,48},{96,64},{112,80},{... | collective-permute-start | bytes 1572872 | tf_op jit(solution)/shard_map/ppermute | solution.py:241
  43.5 8.6 %collective-permute-done.6.refs_8_ = bf16[256,1024]{1,0:T(8,128)(2,1)} collective-permute-done((bf16[256,1024]{1,0:T(8,128)(2,1)}, bf16[256,1024]{1,0:T(8,128)(2,1)}, u32[]{:S(2)}, u32[]{:S(2)}) %collective-permute-start.6) | collective-permute-done | bytes 524320 | tf_op jit(solution)/shard_map/ppermute | solution.py:241
  52.1 0.0 collective-permute-done.7.refs_4_
  52.1 2.4 %collective-permute-start.12 = (bf16[256,1024]{1,0:T(8,128)(2,1)}, bf16[256,1024]{1,0:T(8,128)(2,1)}, u32[]{:S(2)}, u32[]{:S(2)}) collective-permute-start(bf16[256,1024]{1,0:T(8,128)(2,1)} %collective-permute-done.7.refs_4_), channel_id=1, source_target_pairs={{0,224},{16,240},{32,0},{48,16},{64,32},{80,48},{96,64},{112,80},{... | collective-permute-start | bytes 1572872 | tf_op jit(solution)/shard_map/ppermute | solution.py:241
  54.4 0.0 collective-permute-start.13
  54.4 0.0 all-to-all-done
  54.4 3.0 %collective-permute-start.11 = (bf16[384,3072]{1,0:T(8,128)(2,1)}, bf16[384,3072]{1,0:T(8,128)(2,1)}, u32[]{:S(2)}, u32[]{:S(2)}) collective-permute-start(bf16[384,3072]{1,0:T(8,128)(2,1)} %bitcast.3.own_ref), channel_id=1, source_target_pairs={{0,16},{16,0},{32,48},{48,32},{64,80},{80,64},{96,112},{112,96},{1... | collective-permute-start | bytes 7077896 | tf_op jit(solution)/shard_map/ppermute | solution.py:262
  57.4 0.0 copy-done
  57.4 0.0 copy-done.1
  57.4 7.8 %shard_map.75 = (f32[384,1024]{1,0:T(8,128)S(1)}, bf16[384,3072]{1,0:T(8,128)(2,1)S(1)}, bf16[5,256,1024]{2,1,0:T(8,128)(2,1)S(1)}, bf16[5,256,1024]{2,1,0:T(8,128)(2,1)S(1)}) custom-call(bf16[384,3072]{1,0:T(8,128)(2,1)} %bitcast.3.own_ref, bf16[256,1024]{1,0:T(8,128)(2,1)S(1)} %bitcast.12, bf16[256,1024]{1,0:T(8,128)(2,1)S(1)} %collective-permute-done.refs_0_.refs_1_, ...), custom_call_target="tpu_custom_call" | custom-call | tf_op jit(solution)/shard_map/pallas_call | solution.py:122
  65.2 0.0 collective-permute-done.8.refs_0_
  65.3 0.0 collective-permute-done.9.refs_3_
  65.3 0.1 collective-permute-start.10
  65.4 3.0 %collective-permute-start.14 = (bf16[256,1024]{1,0:T(8,128)(2,1)}, bf16[256,1024]{1,0:T(8,128)(2,1)S(1)}, u32[]{:S(2)}, u32[]{:S(2)}) collective-permute-start(bf16[256,1024]{1,0:T(8,128)(2,1)} %collective-permute-done.9.refs_3_), channel_id=1, source_target_pairs={{0,224},{16,240},{32,0},{48,16},{64,32},{80,48},{96,64},{112,80},{... | collective-permute-start | bytes 1572872 | tf_op jit(solution)/shard_map/ppermute | solution.py:241
  68.4 0.0 collective-permute-done.11.other_ref
  68.4 6.4 %shard_map.77 = (f32[384,1024]{1,0:T(8,128)S(1)}, bf16[384,3072]{1,0:T(8,128)(2,1)S(1)}) custom-call(bf16[384,3072]{1,0:T(8,128)(2,1)} %collective-permute-done.11.other_ref, bf16[5,256,1024]{2,1,0:T(8,128)(2,1)S(1)} %get-tuple-element.52.up_ref, bf16[5,256,1024]{2,1,0:T(8,128)(2,1)S(1)} %get-tuple-element.53.down_ref), custom_call_target="tpu_custom_call" | custom-call | tf_op jit(solution)/shard_map/pallas_call | solution.py:143
  74.8 0.0 collective-permute-done.12.refs_1_
  74.8 0.0 collective-permute-done.13.refs_2_
  74.8 5.0 %shard_map.78 = (f32[384,1024]{1,0:T(8,128)S(1)}, f32[384,1024]{1,0:T(8,128)S(1)}) custom-call(bf16[384,3072]{1,0:T(8,128)(2,1)S(1)} %get-tuple-element.50.refs_1_.own_ref.rows_ref, bf16[384,3072]{1,0:T(8,128)(2,1)S(1)} %get-tuple-element.54.other_ref.rows_ref, bf16[256,1024]{1,0:T(8,128)(2,1)S(1)} %collective-permute-done.8.refs_0_, ...), custom_call_target="tpu_custom_call" | custom-call | tf_op jit(solution)/shard_map/pallas_call | solution.py:172
  79.8 5.8 %collective-permute-done.10.up_ref = bf16[256,1024]{1,0:T(8,128)(2,1)S(1)} collective-permute-done((bf16[256,1024]{1,0:T(8,128)(2,1)S(1)}, bf16[256,1024]{1,0:T(8,128)(2,1)S(1)}, u32[]{:S(2)}, u32[]{:S(2)}) %collective-permute-start.10) | collective-permute-done | bytes 524320 | tf_op jit(solution)/shard_map/ppermute | solution.py:241
  85.7 0.6 shard_map.80.factor_ref
  86.3 0.0 collective-permute-done.14.down_ref
  86.3 1.0 shard_map.81
  87.4 1.3 %collective-permute-start.15 = (bf16[384,1024]{1,0:T(8,128)(2,1)S(1)}, bf16[384,1024]{1,0:T(8,128)(2,1)S(1)}, u32[]{:S(2)}, u32[]{:S(2)}) collective-permute-start(bf16[384,1024]{1,0:T(8,128)(2,1)S(1)} %shard_map.81), channel_id=1, source_target_pairs={{0,16},{16,0},{32,48},{48,32},{64,80},{80,64},{96,112},{112,96},{1... | collective-permute-start | bytes 2359304 | tf_op jit(solution)/shard_map/ppermute | solution.py:241
  88.7 1.4 %shard_map.79 = f32[384,1024]{1,0:T(8,128)S(1)} custom-call(bf16[384,3072]{1,0:T(8,128)(2,1)S(1)} %get-tuple-element.50.refs_1_.own_ref.rows_ref, bf16[256,1024]{1,0:T(8,128)(2,1)S(1)} %collective-permute-done.10.up_ref, bf16[256,1024]{1,0:T(8,128)(2,1)S(1)} %collective-permute-done.14.down_ref, f32[384,1024]{1,0:T(8,128)S(1)} %get-tuple-element.61.acc_ref), custom_call_target="tpu_custom_call" | custom-call | tf_op jit(solution)/shard_map/pallas_call | solution.py:207
  90.1 0.5 collective-permute-done.15
  90.6 0.3 add_convert_fusion
  90.8 20.4 %all_to_all.10 = bf16[16,24,1024]{2,1,0:T(8,128)(2,1)S(1)} all-to-all(bf16[16,24,1024]{2,1,0:T(8,128)(2,1)S(1)} %bitcast.17), channel_id=1, replica_groups=mesh['dp'=16,'expert'=16] {'expert'}, dimensions={0} | all-to-all | bytes 1572864 | tf_op jit(solution)/shard_map/all_to_all | solution.py:271
  111.2 1.1 fusion
  (2 shorter events, 0.0 us)
Async XLA Ops:
  0.0 19.0 %collective-permute-start = (bf16[256,1024]{1,0:T(8,128)(2,1)}, bf16[256,1024]{1,0:T(8,128)(2,1)S(1)}, u32[]{:S(2)}, u32[]{:S(2)}) collective-permute-start(bf16[256,1024]{1,0:T(8,128)(2,1)} %bitcast.10), channel_id=1, source_target_pairs={{0,32},{16,48},{32,64},{48,80},{64,96},{80,112},{96,128},{112,144}... | collective-permute-start | bytes 1572872 | tf_op jit(solution)/shard_map/ppermute | solution.py:241
  2.5 16.6 %collective-permute-start.1 = (bf16[256,1024]{1,0:T(8,128)(2,1)}, bf16[256,1024]{1,0:T(8,128)(2,1)}, u32[]{:S(2)}, u32[]{:S(2)}) collective-permute-start(bf16[256,1024]{1,0:T(8,128)(2,1)} %bitcast.13), channel_id=1, source_target_pairs={{0,224},{16,240},{32,0},{48,16},{64,32},{80,48},{96,64},{112,80},{... | collective-permute-start | bytes 1572872 | tf_op jit(solution)/shard_map/ppermute | solution.py:241
  6.4 23.2 %collective-permute-start.4 = (bf16[256,1024]{1,0:T(8,128)(2,1)}, bf16[256,1024]{1,0:T(8,128)(2,1)}, u32[]{:S(2)}, u32[]{:S(2)}) collective-permute-start(bf16[256,1024]{1,0:T(8,128)(2,1)} %bitcast.14), channel_id=1, source_target_pairs={{0,32},{16,48},{32,64},{48,80},{64,96},{80,112},{96,128},{112,144}... | collective-permute-start | bytes 1572872 | tf_op jit(solution)/shard_map/ppermute | solution.py:241
  6.4 23.2 %collective-permute-start.5 = (bf16[256,1024]{1,0:T(8,128)(2,1)}, bf16[256,1024]{1,0:T(8,128)(2,1)}, u32[]{:S(2)}, u32[]{:S(2)}) collective-permute-start(bf16[256,1024]{1,0:T(8,128)(2,1)} %bitcast.11), channel_id=1, source_target_pairs={{0,224},{16,240},{32,0},{48,16},{64,32},{80,48},{96,64},{112,80},{... | collective-permute-start | bytes 1572872 | tf_op jit(solution)/shard_map/ppermute | solution.py:241
  12.2 42.3 %all-to-all-start = ((bf16[16,24,3072]{2,1,0:T(8,128)(2,1)}), bf16[16,24,3072]{2,1,0:T(8,128)(2,1)}, u32[]{:S(2)}, u32[]{:S(2)}) async-start(bf16[16,24,3072]{2,1,0:T(8,128)(2,1)} %bitcast.2), calls=%async_computation | async-start | bytes 4718592 | tf_op jit(solution)/shard_map/all_to_all | solution.py:247
  19.0 38.4 %copy-start = (bf16[1,256,1024]{2,1,0:T(8,128)(2,1)S(1)}, bf16[1,256,1024]{2,1,0:T(8,128)(2,1)}, u32[]{:S(2)}) copy-start(bf16[1,256,1024]{2,1,0:T(8,128)(2,1)} %param.12) | copy-start | bytes 1572868
  19.0 38.4 %copy-start.1 = (bf16[1,256,1024]{2,1,0:T(8,128)(2,1)S(1)}, bf16[1,256,1024]{2,1,0:T(8,128)(2,1)}, u32[]{:S(2)}) copy-start(bf16[1,256,1024]{2,1,0:T(8,128)(2,1)} %param.13) | copy-start | bytes 1572868
  19.0 21.8 %collective-permute-start.2 = (bf16[256,1024]{1,0:T(8,128)(2,1)S(1)}, bf16[256,1024]{1,0:T(8,128)(2,1)S(1)}, u32[]{:S(2)}, u32[]{:S(2)}) collective-permute-start(bf16[256,1024]{1,0:T(8,128)(2,1)S(1)} %collective-permute-done.refs_0_.refs_1_), channel_id=1, source_target_pairs={{0,32},{16,48},{32,64},{48,80},{64,96},{80,112},{96,128},{112,144}... | collective-permute-start | bytes 1572872 | tf_op jit(solution)/shard_map/ppermute | solution.py:241
  19.1 21.7 %collective-permute-start.3 = (bf16[256,1024]{1,0:T(8,128)(2,1)}, bf16[256,1024]{1,0:T(8,128)(2,1)}, u32[]{:S(2)}, u32[]{:S(2)}) collective-permute-start(bf16[256,1024]{1,0:T(8,128)(2,1)} %collective-permute-done.1.refs_7_), channel_id=1, source_target_pairs={{0,224},{16,240},{32,0},{48,16},{64,32},{80,48},{96,64},{112,80},{... | collective-permute-start | bytes 1572872 | tf_op jit(solution)/shard_map/ppermute | solution.py:241
  29.6 22.5 %collective-permute-start.6 = (bf16[256,1024]{1,0:T(8,128)(2,1)}, bf16[256,1024]{1,0:T(8,128)(2,1)}, u32[]{:S(2)}, u32[]{:S(2)}) collective-permute-start(bf16[256,1024]{1,0:T(8,128)(2,1)} %collective-permute-done.4.refs_6_), channel_id=1, source_target_pairs={{0,32},{16,48},{32,64},{48,80},{64,96},{80,112},{96,128},{112,144}... | collective-permute-start | bytes 1572872 | tf_op jit(solution)/shard_map/ppermute | solution.py:241
  29.6 22.5 %collective-permute-start.7 = (bf16[256,1024]{1,0:T(8,128)(2,1)}, bf16[256,1024]{1,0:T(8,128)(2,1)}, u32[]{:S(2)}, u32[]{:S(2)}) collective-permute-start(bf16[256,1024]{1,0:T(8,128)(2,1)} %collective-permute-done.5.refs_2_), channel_id=1, source_target_pairs={{0,224},{16,240},{32,0},{48,16},{64,32},{80,48},{96,64},{112,80},{... | collective-permute-start | bytes 1572872 | tf_op jit(solution)/shard_map/ppermute | solution.py:241
  40.8 24.4 %collective-permute-start.8 = (bf16[256,1024]{1,0:T(8,128)(2,1)S(1)}, bf16[256,1024]{1,0:T(8,128)(2,1)S(1)}, u32[]{:S(2)}, u32[]{:S(2)}) collective-permute-start(bf16[256,1024]{1,0:T(8,128)(2,1)S(1)} %collective-permute-done.2.refs_3_), channel_id=1, source_target_pairs={{0,32},{16,48},{32,64},{48,80},{64,96},{80,112},{96,128},{112,144}... | collective-permute-start | bytes 1572872 | tf_op jit(solution)/shard_map/ppermute | solution.py:241
  40.8 24.4 %collective-permute-start.9 = (bf16[256,1024]{1,0:T(8,128)(2,1)}, bf16[256,1024]{1,0:T(8,128)(2,1)}, u32[]{:S(2)}, u32[]{:S(2)}) collective-permute-start(bf16[256,1024]{1,0:T(8,128)(2,1)} %collective-permute-done.3.refs_9_), channel_id=1, source_target_pairs={{0,224},{16,240},{32,0},{48,16},{64,32},{80,48},{96,64},{112,80},{... | collective-permute-start | bytes 1572872 | tf_op jit(solution)/shard_map/ppermute | solution.py:241
  52.1 22.8 %collective-permute-start.12 = (bf16[256,1024]{1,0:T(8,128)(2,1)}, bf16[256,1024]{1,0:T(8,128)(2,1)}, u32[]{:S(2)}, u32[]{:S(2)}) collective-permute-start(bf16[256,1024]{1,0:T(8,128)(2,1)} %collective-permute-done.7.refs_4_), channel_id=1, source_target_pairs={{0,224},{16,240},{32,0},{48,16},{64,32},{80,48},{96,64},{112,80},{... | collective-permute-start | bytes 1572872 | tf_op jit(solution)/shard_map/ppermute | solution.py:241
  54.4 20.4 %collective-permute-start.13 = (bf16[256,1024]{1,0:T(8,128)(2,1)}, bf16[256,1024]{1,0:T(8,128)(2,1)}, u32[]{:S(2)}, u32[]{:S(2)}) collective-permute-start(bf16[256,1024]{1,0:T(8,128)(2,1)} %collective-permute-done.6.refs_8_), channel_id=1, source_target_pairs={{0,32},{16,48},{32,64},{48,80},{64,96},{80,112},{96,128},{112,144}... | collective-permute-start | bytes 1572872 | tf_op jit(solution)/shard_map/ppermute | solution.py:241
  54.4 14.0 %collective-permute-start.11 = (bf16[384,3072]{1,0:T(8,128)(2,1)}, bf16[384,3072]{1,0:T(8,128)(2,1)}, u32[]{:S(2)}, u32[]{:S(2)}) collective-permute-start(bf16[384,3072]{1,0:T(8,128)(2,1)} %bitcast.3.own_ref), channel_id=1, source_target_pairs={{0,16},{16,0},{32,48},{48,32},{64,80},{80,64},{96,112},{112,96},{1... | collective-permute-start | bytes 7077896 | tf_op jit(solution)/shard_map/ppermute | solution.py:262
  65.3 20.4 %collective-permute-start.10 = (bf16[256,1024]{1,0:T(8,128)(2,1)S(1)}, bf16[256,1024]{1,0:T(8,128)(2,1)S(1)}, u32[]{:S(2)}, u32[]{:S(2)}) collective-permute-start(bf16[256,1024]{1,0:T(8,128)(2,1)S(1)} %collective-permute-done.8.refs_0_), channel_id=1, source_target_pairs={{0,32},{16,48},{32,64},{48,80},{64,96},{80,112},{96,128},{112,144}... | collective-permute-start | bytes 1572872 | tf_op jit(solution)/shard_map/ppermute | solution.py:241
  65.4 21.0 %collective-permute-start.14 = (bf16[256,1024]{1,0:T(8,128)(2,1)}, bf16[256,1024]{1,0:T(8,128)(2,1)S(1)}, u32[]{:S(2)}, u32[]{:S(2)}) collective-permute-start(bf16[256,1024]{1,0:T(8,128)(2,1)} %collective-permute-done.9.refs_3_), channel_id=1, source_target_pairs={{0,224},{16,240},{32,0},{48,16},{64,32},{80,48},{96,64},{112,80},{... | collective-permute-start | bytes 1572872 | tf_op jit(solution)/shard_map/ppermute | solution.py:241
  87.4 3.2 %collective-permute-start.15 = (bf16[384,1024]{1,0:T(8,128)(2,1)S(1)}, bf16[384,1024]{1,0:T(8,128)(2,1)S(1)}, u32[]{:S(2)}, u32[]{:S(2)}) collective-permute-start(bf16[384,1024]{1,0:T(8,128)(2,1)S(1)} %shard_map.81), channel_id=1, source_target_pairs={{0,16},{16,0},{32,48},{48,32},{64,80},{80,64},{96,112},{112,96},{1... | collective-permute-start | bytes 2359304 | tf_op jit(solution)/shard_map/ppermute | solution.py:241

commit v8 on v7

--- a/solution.py
+++ b/solution.py
@@ -163,7 +163,8 @@
         copy.wait()
     blocks = range(n_w)
     for rows_ref, acc_ref, out_ref in zip((own_ref, other_ref), accs, outs):
-        out_ref[...] = accumulate(rows_ref, [up_buf.at[g] for g in blocks], [down_buf.at[g] for g in blocks], acc_ref[...])
+        total = accumulate(rows_ref, [up_buf.at[g] for g in blocks], [down_buf.at[g] for g in blocks], acc_ref[...])
+        out_ref[...] = total.astype(out_ref.dtype)
 
 
 def next_call(rows, ups, downs, acc, mark):
@@ -171,7 +172,7 @@
     inside = [pltpu.with_memory_space_constraint(x, pltpu.VMEM) for x in (*rows, *acc)]
     return pl.pallas_call(
         functools.partial(next_kernel, n_w),
-        out_shape=tuple(jax.ShapeDtypeStruct(x.shape, f32) for x in acc),
+        out_shape=tuple(jax.ShapeDtypeStruct(x.shape, kind) for x, kind in zip(acc, (f32, bf16))),
         in_specs=[VMEM] * 2 + [ANY] * (2 * n_w) + [VMEM] * 2 + [ANY],
         out_specs=(VMEM,) * 2,
         scratch_shapes=[
@@ -190,16 +191,16 @@
     factor_ref[...] = curvature(before_act) * lifted
 
 
-def last_other_kernel(rows_ref, factor_ref, up_ref, down_ref, acc_ref, out_ref):
+def last_own_kernel(rows_ref, up_ref, down_ref, acc_ref, out_ref):
+    out_ref[...] = accumulate(rows_ref, [up_ref], [down_ref], acc_ref[...])
+
+
+def last_far_kernel(rows_ref, factor_ref, up_ref, down_ref, acc_ref, passed_ref, out_ref):
     width = up_ref.shape[1]
     pulled = lax.dot_general(rows_ref[:, 2 * width:], down_ref[...], NT, preferred_element_type=f32)
     inner = (pulled * factor_ref[...]).astype(bf16)
-    total = acc_ref[...] + jnp.dot(inner, up_ref[...], preferred_element_type=f32)
-    out_ref[...] = total.astype(out_ref.dtype)
-
-
-def last_own_kernel(rows_ref, up_ref, down_ref, acc_ref, out_ref):
-    out_ref[...] = accumulate(rows_ref, [up_ref], [down_ref], acc_ref[...])
+    total = acc_ref[...] + passed_ref[...].astype(f32)
+    out_ref[...] = (total + jnp.dot(inner, up_ref[...], preferred_element_type=f32)).astype(out_ref.dtype)
 
 
 def last_call(kernel, shape, kind, *operands):
@@ -262,12 +263,12 @@
     other = lax.ppermute(own, "dp", swap)
     theirs, kept_other = other_call(other, up_stack, down_stack)
     mine, theirs = next_call((kept_own, kept_other), (uf3, ub3), (df3, db3), (mine, theirs), mark3)
-    uf4, theirs = after((uf4, theirs))
-    factor = last_call(factor_kernel, (other.shape[0], uf4.shape[0]), f32, kept_other, uf4)
-    passed = last_call(last_other_kernel, theirs.shape, bf16, kept_other, factor, uf4, db4, theirs)
-    passed = send_on(passed, swap)
-    kept = last_call(last_own_kernel, mine.shape, f32, kept_own, uf4, db4, mine)
-    whole = (kept + passed.astype(f32)).astype(bf16)
+    passed = send_on(theirs, swap)
+    far_up, far_down = send_on(uf4, swap), send_on(db4, swap)
+    part = last_call(last_own_kernel, mine.shape, f32, kept_own, uf4, db4, mine)
+    far_up, part = after((far_up, part))
+    factor = last_call(factor_kernel, (own.shape[0], far_up.shape[0]), f32, kept_own, far_up)
+    whole = last_call(last_far_kernel, mine.shape, bf16, kept_own, factor, far_up, far_down, part, passed)
     returned = lax.all_to_all(whole.reshape(experts, CAP, width), "expert", 0, 0, tiled=True)
     returned = returned.reshape(experts * CAP, width)
     return lax.dot_general(mix, returned, (((0,), (0,)), ((), ())), preferred_element_type=f32)

time: 113 us -> 112 us (level)
  waiting for transfers between devices: 31.3 us -> 29 us
  starting transfers between devices: 33.8 us -> 35.5 us
    ppermute x15 -> x17, waiting for transfers between devices: 31.3 us -> 29 us  [send_on(): return lax.ppermute(x, 'dp', way)]
    ppermute x15 -> x17, starting transfers between devices: 24 us -> 25.7 us  [send_on(): return lax.ppermute(x, 'dp', way)]
  transfers between devices with their start and end apart: 17 -> 19, of which waited for: 5 -> 6; matrix products, arithmetic and copies ran while one was open for 0% -> 0% of each run, Pallas kernels for 22% -> 22%
where the time goes in v8:
time: 112 us
  starting transfers between devices  35.5 us (32%)
  waiting for transfers between devices  29 us (26%)
  Pallas kernels  25.5 us (23%)
  blocking collectives  20.4 us (18%)
  matrix products  1.12 us (1%)
    ppermute x17, waiting for transfers between devices, send_on(): return lax.ppermute(x, 'dp', way)  29 us
    ppermute x17, starting transfers between devices, send_on(): return lax.ppermute(x, 'dp', way)  25.7 us
    all_to_all x1, blocking collectives, local(): lax.all_to_all(whole.reshape(experts, CAP, width), 'expert', 0, 0, tiled=...  20.4 us
    pallas_call x1, Pallas kernels, own_call(): pl.pallas_call(functools.partial(own_kernel, n_w), out_shape=(jax.ShapeDt...  7.81 us
    all_to_all x1, starting transfers between devices, local(): lax.all_to_all(send.reshape(experts, CAP, 3 * width), 'expert', 0, 0, til...  6.81 us
    pallas_call x1, Pallas kernels, other_call(): pl.pallas_call(other_kernel, out_shape=(jax.ShapeDtypeStruct((rows, width...  6.47 us
    pallas_call x1, Pallas kernels, next_call(): pl.pallas_call(functools.partial(next_kernel, n_w), out_shape=tuple((jax....  5.02 us
    pallas_call x1, Pallas kernels, prepare(): pl.pallas_call(prepare_kernel, out_shape=(jax.ShapeDtypeStruct((slots, 3...  3.13 us
  transfers between devices with their start and end apart: 19, of which 6 were waited for; matrix products, arithmetic and copies ran while one was open for 0% of the time, Pallas kernels for 22%

profile of v8, /device:TPU:1, one launch (start us, length us, event | category | flops | bytes accessed | tf_op | source)
XLA Modules:
  0.0 111.7 jit_solution(10610026552482140934)
XLA Ops:
  0.0 2.5 %collective-permute-start = (bf16[256,1024]{1,0:T(8,128)(2,1)}, bf16[256,1024]{1,0:T(8,128)(2,1)S(1)}, u32[]{:S(2)}, u32[]{:S(2)}) collective-permute-start(bf16[256,1024]{1,0:T(8,128)(2,1)} %bitcast.11), channel_id=1, source_target_pairs={{0,32},{16,48},{32,64},{48,80},{64,96},{80,112},{96,128},{112,144}... | collective-permute-start | bytes 1572872 | tf_op jit(solution)/shard_map/ppermute | solution.py:242
  2.5 3.9 %collective-permute-start.1 = (bf16[256,1024]{1,0:T(8,128)(2,1)}, bf16[256,1024]{1,0:T(8,128)(2,1)}, u32[]{:S(2)}, u32[]{:S(2)}) collective-permute-start(bf16[256,1024]{1,0:T(8,128)(2,1)} %bitcast.14), channel_id=1, source_target_pairs={{0,224},{16,240},{32,0},{48,16},{64,32},{80,48},{96,64},{112,80},{... | collective-permute-start | bytes 1572872 | tf_op jit(solution)/shard_map/ppermute | solution.py:242
  6.4 0.0 collective-permute-start.4
  6.4 2.7 %collective-permute-start.5 = (bf16[256,1024]{1,0:T(8,128)(2,1)}, bf16[256,1024]{1,0:T(8,128)(2,1)}, u32[]{:S(2)}, u32[]{:S(2)}) collective-permute-start(bf16[256,1024]{1,0:T(8,128)(2,1)} %bitcast.12), channel_id=1, source_target_pairs={{0,224},{16,240},{32,0},{48,16},{64,32},{80,48},{96,64},{112,80},{... | collective-permute-start | bytes 1572872 | tf_op jit(solution)/shard_map/ppermute | solution.py:242
  9.1 3.1 %shard_map.73 = (bf16[384,3072]{1,0:T(8,128)(2,1)}, bf16[384,128]{1,0:T(8,128)(2,1)S(1)}) custom-call(s32[2,128]{1,0:T(2,128)} %bitcast.18, s32[2,128]{1,0:T(2,128)} %bitcast.19, bf16[128,1024]{1,0:T(8,128)(2,1)} %x_hbm.1, bf16[128,1024]{1,0:T(8,128)(2,1)} %t_hbm.1, bf16[128,1024]{1,0:T(8,128)(2,1)} %c_hbm.1), custom_call_target="tpu_custom_call" | custom-call | tf_op jit(solution)/shard_map/pallas_call | solution.py:61
  12.2 6.8 %all-to-all-start = ((bf16[16,24,3072]{2,1,0:T(8,128)(2,1)}), bf16[16,24,3072]{2,1,0:T(8,128)(2,1)}, u32[]{:S(2)}, u32[]{:S(2)}) async-start(bf16[16,24,3072]{2,1,0:T(8,128)(2,1)} %bitcast.2), calls=%async_computation | async-start | bytes 4718592 | tf_op jit(solution)/shard_map/all_to_all | solution.py:248
  19.0 0.0 collective-permute-done.refs_0_.refs_1_
  19.1 0.0 copy-start
  19.1 0.0 copy-start.1
  19.1 0.0 collective-permute-done.1.refs_7_
  19.1 0.1 collective-permute-start.2
  19.2 2.7 %collective-permute-start.3 = (bf16[256,1024]{1,0:T(8,128)(2,1)}, bf16[256,1024]{1,0:T(8,128)(2,1)}, u32[]{:S(2)}, u32[]{:S(2)}) collective-permute-start(bf16[256,1024]{1,0:T(8,128)(2,1)} %collective-permute-done.1.refs_7_), channel_id=1, source_target_pairs={{0,224},{16,240},{32,0},{48,16},{64,32},{80,48},{96,64},{112,80},{... | collective-permute-start | bytes 1572872 | tf_op jit(solution)/shard_map/ppermute | solution.py:242
  21.9 7.8 %collective-permute-done.4.refs_6_ = bf16[256,1024]{1,0:T(8,128)(2,1)} collective-permute-done((bf16[256,1024]{1,0:T(8,128)(2,1)}, bf16[256,1024]{1,0:T(8,128)(2,1)}, u32[]{:S(2)}, u32[]{:S(2)}) %collective-permute-start.4) | collective-permute-done | bytes 524320 | tf_op jit(solution)/shard_map/ppermute | solution.py:242
  29.6 0.0 collective-permute-done.5.refs_2_
  29.6 0.0 collective-permute-start.6
  29.6 2.7 %collective-permute-start.7 = (bf16[256,1024]{1,0:T(8,128)(2,1)}, bf16[256,1024]{1,0:T(8,128)(2,1)}, u32[]{:S(2)}, u32[]{:S(2)}) collective-permute-start(bf16[256,1024]{1,0:T(8,128)(2,1)} %collective-permute-done.5.refs_2_), channel_id=1, source_target_pairs={{0,224},{16,240},{32,0},{48,16},{64,32},{80,48},{96,64},{112,80},{... | collective-permute-start | bytes 1572872 | tf_op jit(solution)/shard_map/ppermute | solution.py:242
  32.3 8.6 %collective-permute-done.2.refs_3_ = bf16[256,1024]{1,0:T(8,128)(2,1)S(1)} collective-permute-done((bf16[256,1024]{1,0:T(8,128)(2,1)S(1)}, bf16[256,1024]{1,0:T(8,128)(2,1)S(1)}, u32[]{:S(2)}, u32[]{:S(2)}) %collective-permute-start.2) | collective-permute-done | bytes 524320 | tf_op jit(solution)/shard_map/ppermute | solution.py:242
  40.8 0.0 collective-permute-done.3.refs_9_
  40.8 0.0 collective-permute-start.8
  40.8 2.7 %collective-permute-start.9 = (bf16[256,1024]{1,0:T(8,128)(2,1)}, bf16[256,1024]{1,0:T(8,128)(2,1)}, u32[]{:S(2)}, u32[]{:S(2)}) collective-permute-start(bf16[256,1024]{1,0:T(8,128)(2,1)} %collective-permute-done.3.refs_9_), channel_id=1, source_target_pairs={{0,224},{16,240},{32,0},{48,16},{64,32},{80,48},{96,64},{112,80},{... | collective-permute-start | bytes 1572872 | tf_op jit(solution)/shard_map/ppermute | solution.py:242
  43.5 8.6 %collective-permute-done.6.refs_8_ = bf16[256,1024]{1,0:T(8,128)(2,1)} collective-permute-done((bf16[256,1024]{1,0:T(8,128)(2,1)}, bf16[256,1024]{1,0:T(8,128)(2,1)}, u32[]{:S(2)}, u32[]{:S(2)}) %collective-permute-start.6) | collective-permute-done | bytes 524320 | tf_op jit(solution)/shard_map/ppermute | solution.py:242
  52.1 0.0 collective-permute-done.7.refs_4_
  52.1 2.4 %collective-permute-start.14 = (bf16[256,1024]{1,0:T(8,128)(2,1)}, bf16[256,1024]{1,0:T(8,128)(2,1)}, u32[]{:S(2)}, u32[]{:S(2)}) collective-permute-start(bf16[256,1024]{1,0:T(8,128)(2,1)} %collective-permute-done.7.refs_4_), channel_id=1, source_target_pairs={{0,224},{16,240},{32,0},{48,16},{64,32},{80,48},{96,64},{112,80},{... | collective-permute-start | bytes 1572872 | tf_op jit(solution)/shard_map/ppermute | solution.py:242
  54.4 0.0 collective-permute-start.15
  54.4 0.0 all-to-all-done
  54.4 3.0 %collective-permute-start.13 = (bf16[384,3072]{1,0:T(8,128)(2,1)}, bf16[384,3072]{1,0:T(8,128)(2,1)}, u32[]{:S(2)}, u32[]{:S(2)}) collective-permute-start(bf16[384,3072]{1,0:T(8,128)(2,1)} %bitcast.3.own_ref), channel_id=1, source_target_pairs={{0,16},{16,0},{32,48},{48,32},{64,80},{80,64},{96,112},{112,96},{1... | collective-permute-start | bytes 7077896 | tf_op jit(solution)/shard_map/ppermute | solution.py:263
  57.4 7.8 %shard_map.75 = (f32[384,1024]{1,0:T(8,128)S(1)}, bf16[384,3072]{1,0:T(8,128)(2,1)S(1)}, bf16[5,256,1024]{2,1,0:T(8,128)(2,1)S(1)}, bf16[5,256,1024]{2,1,0:T(8,128)(2,1)S(1)}) custom-call(bf16[384,3072]{1,0:T(8,128)(2,1)} %bitcast.3.own_ref, bf16[256,1024]{1,0:T(8,128)(2,1)S(1)} %bitcast.13, bf16[256,1024]{1,0:T(8,128)(2,1)S(1)} %collective-permute-done.refs_0_.refs_1_, ...), custom_call_target="tpu_custom_call" | custom-call | tf_op jit(solution)/shard_map/pallas_call | solution.py:122
  65.2 0.0 collective-permute-done.8.refs_0_
  65.3 0.0 collective-permute-done.9.refs_3_
  65.3 0.1 collective-permute-start.10
  65.4 3.0 %collective-permute-start.12 = (bf16[256,1024]{1,0:T(8,128)(2,1)}, bf16[256,1024]{1,0:T(8,128)(2,1)S(1)}, u32[]{:S(2)}, u32[]{:S(2)}) collective-permute-start(bf16[256,1024]{1,0:T(8,128)(2,1)} %collective-permute-done.9.refs_3_), channel_id=1, source_target_pairs={{0,224},{16,240},{32,0},{48,16},{64,32},{80,48},{96,64},{112,80},{... | collective-permute-start | bytes 1572872 | tf_op jit(solution)/shard_map/ppermute | solution.py:242
  68.4 6.5 %shard_map.77 = (f32[384,1024]{1,0:T(8,128)S(1)}, bf16[384,3072]{1,0:T(8,128)(2,1)S(1)}) custom-call(bf16[384,3072]{1,0:T(8,128)(2,1)} %collective-permute-done.13.other_ref, bf16[5,256,1024]{2,1,0:T(8,128)(2,1)S(1)} %get-tuple-element.53.up_ref, bf16[5,256,1024]{2,1,0:T(8,128)(2,1)S(1)} %get-tuple-element.54.down_ref), custom_call_target="tpu_custom_call" | custom-call | tf_op jit(solution)/shard_map/pallas_call | solution.py:143
  74.9 0.0 collective-permute-done.14.refs_1_
  74.9 0.0 collective-permute-done.15.refs_2_
  74.9 5.0 %shard_map.78 = (f32[384,1024]{1,0:T(8,128)S(1)}, bf16[384,1024]{1,0:T(8,128)(2,1)S(1)}) custom-call(bf16[384,3072]{1,0:T(8,128)(2,1)S(1)} %get-tuple-element.50.refs_1_.own_ref.rows_ref, bf16[384,3072]{1,0:T(8,128)(2,1)S(1)} %get-tuple-element.55.other_ref, bf16[256,1024]{1,0:T(8,128)(2,1)S(1)} %collective-permute-done.8.refs_0_, ...), custom_call_target="tpu_custom_call" | custom-call | tf_op jit(solution)/shard_map/pallas_call | solution.py:173
  79.9 1.8 %collective-permute-start.17 = (bf16[384,1024]{1,0:T(8,128)(2,1)S(1)}, bf16[384,1024]{1,0:T(8,128)(2,1)S(1)}, u32[]{:S(2)}, u32[]{:S(2)}) collective-permute-start(bf16[384,1024]{1,0:T(8,128)(2,1)S(1)} %get-tuple-element.62), channel_id=1, source_target_pairs={{0,16},{16,0},{32,48},{48,32},{64,80},{80,64},{96,112},{112,96},{1... | collective-permute-start | bytes 2359304 | tf_op jit(solution)/shard_map/ppermute | solution.py:242
  81.7 4.0 %collective-permute-done.10.up_ref = bf16[256,1024]{1,0:T(8,128)(2,1)S(1)} collective-permute-done((bf16[256,1024]{1,0:T(8,128)(2,1)S(1)}, bf16[256,1024]{1,0:T(8,128)(2,1)S(1)}, u32[]{:S(2)}, u32[]{:S(2)}) %collective-permute-start.10) | collective-permute-done | bytes 524320 | tf_op jit(solution)/shard_map/ppermute | solution.py:242
  85.7 1.2 %collective-permute-start.11 = (bf16[256,1024]{1,0:T(8,128)(2,1)S(1)}, bf16[256,1024]{1,0:T(8,128)(2,1)S(1)}, u32[]{:S(2)}, u32[]{:S(2)}) collective-permute-start(bf16[256,1024]{1,0:T(8,128)(2,1)S(1)} %collective-permute-done.10.up_ref), channel_id=1, source_target_pairs={{0,16},{16,0},{32,48},{48,32},{64,80},{80,64},{96,112},{112,96},{1... | collective-permute-start | bytes 1572872 | tf_op jit(solution)/shard_map/ppermute | solution.py:242
  86.9 0.0 collective-permute-done.12.down_ref
  86.9 0.0 collective-permute-start.16
  86.9 1.4 %shard_map.79.acc_ref = f32[384,1024]{1,0:T(8,128)S(1)} custom-call(bf16[384,3072]{1,0:T(8,128)(2,1)S(1)} %get-tuple-element.50.refs_1_.own_ref.rows_ref, bf16[256,1024]{1,0:T(8,128)(2,1)S(1)} %collective-permute-done.10.up_ref, bf16[256,1024]{1,0:T(8,128)(2,1)S(1)} %collective-permute-done.12.down_ref, f32[384,1024]{1,0:T(8,128)S(1)} %get-tuple-element.59.acc_ref), custom_call_target="tpu_custom_call" | custom-call | tf_op jit(solution)/shard_map/pallas_call | solution.py:208
  88.4 0.1 collective-permute-done.11.up_ref
  88.4 0.6 shard_map.80.factor_ref
  89.1 0.1 collective-permute-done.16.down_ref
  89.2 0.0 collective-permute-done.17.passed_ref
  89.2 1.0 shard_map.81
  90.2 20.4 %all_to_all.10 = bf16[16,24,1024]{2,1,0:T(8,128)(2,1)S(1)} all-to-all(bf16[16,24,1024]{2,1,0:T(8,128)(2,1)S(1)} %bitcast.10), channel_id=1, replica_groups=mesh['dp'=16,'expert'=16] {'expert'}, dimensions={0} | all-to-all | bytes 1572864 | tf_op jit(solution)/shard_map/all_to_all | solution.py:272
  110.6 1.1 %fusion = f32[128,1024]{1,0:T(8,128)} fusion(bf16[384,128]{1,0:T(8,128)(2,1)S(1)} %get-tuple-element.34, bf16[384,1024]{1,0:T(8,128)(2,1)S(1)} %bitcast.17), kind=kOutput, calls=%fused_computation | convolution fusion | flops 100663296 | bytes 1409024 | tf_op jit(solution)/shard_map/dot_general | solution.py:274
  (5 shorter events, 0.0 us)
Async XLA Ops:
  0.0 19.0 %collective-permute-start = (bf16[256,1024]{1,0:T(8,128)(2,1)}, bf16[256,1024]{1,0:T(8,128)(2,1)S(1)}, u32[]{:S(2)}, u32[]{:S(2)}) collective-permute-start(bf16[256,1024]{1,0:T(8,128)(2,1)} %bitcast.11), channel_id=1, source_target_pairs={{0,32},{16,48},{32,64},{48,80},{64,96},{80,112},{96,128},{112,144}... | collective-permute-start | bytes 1572872 | tf_op jit(solution)/shard_map/ppermute | solution.py:242
  2.5 16.6 %collective-permute-start.1 = (bf16[256,1024]{1,0:T(8,128)(2,1)}, bf16[256,1024]{1,0:T(8,128)(2,1)}, u32[]{:S(2)}, u32[]{:S(2)}) collective-permute-start(bf16[256,1024]{1,0:T(8,128)(2,1)} %bitcast.14), channel_id=1, source_target_pairs={{0,224},{16,240},{32,0},{48,16},{64,32},{80,48},{96,64},{112,80},{... | collective-permute-start | bytes 1572872 | tf_op jit(solution)/shard_map/ppermute | solution.py:242
  6.4 23.2 %collective-permute-start.4 = (bf16[256,1024]{1,0:T(8,128)(2,1)}, bf16[256,1024]{1,0:T(8,128)(2,1)}, u32[]{:S(2)}, u32[]{:S(2)}) collective-permute-start(bf16[256,1024]{1,0:T(8,128)(2,1)} %bitcast.15), channel_id=1, source_target_pairs={{0,32},{16,48},{32,64},{48,80},{64,96},{80,112},{96,128},{112,144}... | collective-permute-start | bytes 1572872 | tf_op jit(solution)/shard_map/ppermute | solution.py:242
  6.4 23.2 %collective-permute-start.5 = (bf16[256,1024]{1,0:T(8,128)(2,1)}, bf16[256,1024]{1,0:T(8,128)(2,1)}, u32[]{:S(2)}, u32[]{:S(2)}) collective-permute-start(bf16[256,1024]{1,0:T(8,128)(2,1)} %bitcast.12), channel_id=1, source_target_pairs={{0,224},{16,240},{32,0},{48,16},{64,32},{80,48},{96,64},{112,80},{... | collective-permute-start | bytes 1572872 | tf_op jit(solution)/shard_map/ppermute | solution.py:242
  12.2 42.2 %all-to-all-start = ((bf16[16,24,3072]{2,1,0:T(8,128)(2,1)}), bf16[16,24,3072]{2,1,0:T(8,128)(2,1)}, u32[]{:S(2)}, u32[]{:S(2)}) async-start(bf16[16,24,3072]{2,1,0:T(8,128)(2,1)} %bitcast.2), calls=%async_computation | async-start | bytes 4718592 | tf_op jit(solution)/shard_map/all_to_all | solution.py:248
  19.1 38.4 %copy-start = (bf16[1,256,1024]{2,1,0:T(8,128)(2,1)S(1)}, bf16[1,256,1024]{2,1,0:T(8,128)(2,1)}, u32[]{:S(2)}) copy-start(bf16[1,256,1024]{2,1,0:T(8,128)(2,1)} %param.12) | copy-start | bytes 1572868
  19.1 38.4 %copy-start.1 = (bf16[1,256,1024]{2,1,0:T(8,128)(2,1)S(1)}, bf16[1,256,1024]{2,1,0:T(8,128)(2,1)}, u32[]{:S(2)}) copy-start(bf16[1,256,1024]{2,1,0:T(8,128)(2,1)} %param.13) | copy-start | bytes 1572868
  19.1 21.7 %collective-permute-start.2 = (bf16[256,1024]{1,0:T(8,128)(2,1)S(1)}, bf16[256,1024]{1,0:T(8,128)(2,1)S(1)}, u32[]{:S(2)}, u32[]{:S(2)}) collective-permute-start(bf16[256,1024]{1,0:T(8,128)(2,1)S(1)} %collective-permute-done.refs_0_.refs_1_), channel_id=1, source_target_pairs={{0,32},{16,48},{32,64},{48,80},{64,96},{80,112},{96,128},{112,144}... | collective-permute-start | bytes 1572872 | tf_op jit(solution)/shard_map/ppermute | solution.py:242
  19.2 21.7 %collective-permute-start.3 = (bf16[256,1024]{1,0:T(8,128)(2,1)}, bf16[256,1024]{1,0:T(8,128)(2,1)}, u32[]{:S(2)}, u32[]{:S(2)}) collective-permute-start(bf16[256,1024]{1,0:T(8,128)(2,1)} %collective-permute-done.1.refs_7_), channel_id=1, source_target_pairs={{0,224},{16,240},{32,0},{48,16},{64,32},{80,48},{96,64},{112,80},{... | collective-permute-start | bytes 1572872 | tf_op jit(solution)/shard_map/ppermute | solution.py:242
  29.6 22.5 %collective-permute-start.6 = (bf16[256,1024]{1,0:T(8,128)(2,1)}, bf16[256,1024]{1,0:T(8,128)(2,1)}, u32[]{:S(2)}, u32[]{:S(2)}) collective-permute-start(bf16[256,1024]{1,0:T(8,128)(2,1)} %collective-permute-done.4.refs_6_), channel_id=1, source_target_pairs={{0,32},{16,48},{32,64},{48,80},{64,96},{80,112},{96,128},{112,144}... | collective-permute-start | bytes 1572872 | tf_op jit(solution)/shard_map/ppermute | solution.py:242
  29.6 22.5 %collective-permute-start.7 = (bf16[256,1024]{1,0:T(8,128)(2,1)}, bf16[256,1024]{1,0:T(8,128)(2,1)}, u32[]{:S(2)}, u32[]{:S(2)}) collective-permute-start(bf16[256,1024]{1,0:T(8,128)(2,1)} %collective-permute-done.5.refs_2_), channel_id=1, source_target_pairs={{0,224},{16,240},{32,0},{48,16},{64,32},{80,48},{96,64},{112,80},{... | collective-permute-start | bytes 1572872 | tf_op jit(solution)/shard_map/ppermute | solution.py:242
  40.8 24.4 %collective-permute-start.8 = (bf16[256,1024]{1,0:T(8,128)(2,1)S(1)}, bf16[256,1024]{1,0:T(8,128)(2,1)S(1)}, u32[]{:S(2)}, u32[]{:S(2)}) collective-permute-start(bf16[256,1024]{1,0:T(8,128)(2,1)S(1)} %collective-permute-done.2.refs_3_), channel_id=1, source_target_pairs={{0,32},{16,48},{32,64},{48,80},{64,96},{80,112},{96,128},{112,144}... | collective-permute-start | bytes 1572872 | tf_op jit(solution)/shard_map/ppermute | solution.py:242
  40.8 24.4 %collective-permute-start.9 = (bf16[256,1024]{1,0:T(8,128)(2,1)}, bf16[256,1024]{1,0:T(8,128)(2,1)}, u32[]{:S(2)}, u32[]{:S(2)}) collective-permute-start(bf16[256,1024]{1,0:T(8,128)(2,1)} %collective-permute-done.3.refs_9_), channel_id=1, source_target_pairs={{0,224},{16,240},{32,0},{48,16},{64,32},{80,48},{96,64},{112,80},{... | collective-permute-start | bytes 1572872 | tf_op jit(solution)/shard_map/ppermute | solution.py:242
  52.1 22.8 %collective-permute-start.14 = (bf16[256,1024]{1,0:T(8,128)(2,1)}, bf16[256,1024]{1,0:T(8,128)(2,1)}, u32[]{:S(2)}, u32[]{:S(2)}) collective-permute-start(bf16[256,1024]{1,0:T(8,128)(2,1)} %collective-permute-done.7.refs_4_), channel_id=1, source_target_pairs={{0,224},{16,240},{32,0},{48,16},{64,32},{80,48},{96,64},{112,80},{... | collective-permute-start | bytes 1572872 | tf_op jit(solution)/shard_map/ppermute | solution.py:242
  54.4 20.4 %collective-permute-start.15 = (bf16[256,1024]{1,0:T(8,128)(2,1)}, bf16[256,1024]{1,0:T(8,128)(2,1)}, u32[]{:S(2)}, u32[]{:S(2)}) collective-permute-start(bf16[256,1024]{1,0:T(8,128)(2,1)} %collective-permute-done.6.refs_8_), channel_id=1, source_target_pairs={{0,32},{16,48},{32,64},{48,80},{64,96},{80,112},{96,128},{112,144}... | collective-permute-start | bytes 1572872 | tf_op jit(solution)/shard_map/ppermute | solution.py:242
  54.4 13.9 %collective-permute-start.13 = (bf16[384,3072]{1,0:T(8,128)(2,1)}, bf16[384,3072]{1,0:T(8,128)(2,1)}, u32[]{:S(2)}, u32[]{:S(2)}) collective-permute-start(bf16[384,3072]{1,0:T(8,128)(2,1)} %bitcast.3.own_ref), channel_id=1, source_target_pairs={{0,16},{16,0},{32,48},{48,32},{64,80},{80,64},{96,112},{112,96},{1... | collective-permute-start | bytes 7077896 | tf_op jit(solution)/shard_map/ppermute | solution.py:263
  65.3 20.4 %collective-permute-start.10 = (bf16[256,1024]{1,0:T(8,128)(2,1)S(1)}, bf16[256,1024]{1,0:T(8,128)(2,1)S(1)}, u32[]{:S(2)}, u32[]{:S(2)}) collective-permute-start(bf16[256,1024]{1,0:T(8,128)(2,1)S(1)} %collective-permute-done.8.refs_0_), channel_id=1, source_target_pairs={{0,32},{16,48},{32,64},{48,80},{64,96},{80,112},{96,128},{112,144}... | collective-permute-start | bytes 1572872 | tf_op jit(solution)/shard_map/ppermute | solution.py:242
  65.4 21.5 %collective-permute-start.12 = (bf16[256,1024]{1,0:T(8,128)(2,1)}, bf16[256,1024]{1,0:T(8,128)(2,1)S(1)}, u32[]{:S(2)}, u32[]{:S(2)}) collective-permute-start(bf16[256,1024]{1,0:T(8,128)(2,1)} %collective-permute-done.9.refs_3_), channel_id=1, source_target_pairs={{0,224},{16,240},{32,0},{48,16},{64,32},{80,48},{96,64},{112,80},{... | collective-permute-start | bytes 1572872 | tf_op jit(solution)/shard_map/ppermute | solution.py:242
  79.9 9.3 %collective-permute-start.17 = (bf16[384,1024]{1,0:T(8,128)(2,1)S(1)}, bf16[384,1024]{1,0:T(8,128)(2,1)S(1)}, u32[]{:S(2)}, u32[]{:S(2)}) collective-permute-start(bf16[384,1024]{1,0:T(8,128)(2,1)S(1)} %get-tuple-element.62), channel_id=1, source_target_pairs={{0,16},{16,0},{32,48},{48,32},{64,80},{80,64},{96,112},{112,96},{1... | collective-permute-start | bytes 2359304 | tf_op jit(solution)/shard_map/ppermute | solution.py:242
  85.7 2.8 %collective-permute-start.11 = (bf16[256,1024]{1,0:T(8,128)(2,1)S(1)}, bf16[256,1024]{1,0:T(8,128)(2,1)S(1)}, u32[]{:S(2)}, u32[]{:S(2)}) collective-permute-start(bf16[256,1024]{1,0:T(8,128)(2,1)S(1)} %collective-permute-done.10.up_ref), channel_id=1, source_target_pairs={{0,16},{16,0},{32,48},{48,32},{64,80},{80,64},{96,112},{112,96},{1... | collective-permute-start | bytes 1572872 | tf_op jit(solution)/shard_map/ppermute | solution.py:242
  86.9 2.3 %collective-permute-start.16 = (bf16[256,1024]{1,0:T(8,128)(2,1)S(1)}, bf16[256,1024]{1,0:T(8,128)(2,1)S(1)}, u32[]{:S(2)}, u32[]{:S(2)}) collective-permute-start(bf16[256,1024]{1,0:T(8,128)(2,1)S(1)} %collective-permute-done.12.down_ref), channel_id=1, source_target_pairs={{0,16},{16,0},{32,48},{48,32},{64,80},{80,64},{96,112},{112,96},{1... | collective-permute-start | bytes 1572872 | tf_op jit(solution)/shard_map/ppermute | solution.py:242

commit v9 on v8

--- a/solution.py
+++ b/solution.py
@@ -191,16 +191,15 @@
     factor_ref[...] = curvature(before_act) * lifted
 
 
-def last_own_kernel(rows_ref, up_ref, down_ref, acc_ref, out_ref):
-    out_ref[...] = accumulate(rows_ref, [up_ref], [down_ref], acc_ref[...])
-
-
-def last_far_kernel(rows_ref, factor_ref, up_ref, down_ref, acc_ref, passed_ref, out_ref):
+def last_kernel(rows_ref, factor_ref, up_ref, down_ref, *refs):
+    totals, out_ref = refs[:-1], refs[-1]
     width = up_ref.shape[1]
     pulled = lax.dot_general(rows_ref[:, 2 * width:], down_ref[...], NT, preferred_element_type=f32)
     inner = (pulled * factor_ref[...]).astype(bf16)
-    total = acc_ref[...] + passed_ref[...].astype(f32)
-    out_ref[...] = (total + jnp.dot(inner, up_ref[...], preferred_element_type=f32)).astype(out_ref.dtype)
+    total = jnp.dot(inner, up_ref[...], preferred_element_type=f32)
+    for ref in totals:
+        total = total + ref[...].astype(f32)
+    out_ref[...] = total.astype(out_ref.dtype)
 
 
 def last_call(kernel, shape, kind, *operands):
@@ -264,11 +263,16 @@
     theirs, kept_other = other_call(other, up_stack, down_stack)
     mine, theirs = next_call((kept_own, kept_other), (uf3, ub3), (df3, db3), (mine, theirs), mark3)
     passed = send_on(theirs, swap)
-    far_up, far_down = send_on(uf4, swap), send_on(db4, swap)
-    part = last_call(last_own_kernel, mine.shape, f32, kept_own, uf4, db4, mine)
+    far_up = send_on(uf4, swap)
+    uf4, mine = after((uf4, mine))
+    shape = (own.shape[0], uf4.shape[0])
+    factor = last_call(factor_kernel, shape, f32, kept_own, uf4)
+    db4, factor = after((db4, factor))
+    far_down = send_on(db4, swap)
+    part = last_call(last_kernel, mine.shape, f32, kept_own, factor, uf4, db4, mine)
     far_up, part = after((far_up, part))
-    factor = last_call(factor_kernel, (own.shape[0], far_up.shape[0]), f32, kept_own, far_up)
-    whole = last_call(last_far_kernel, mine.shape, bf16, kept_own, factor, far_up, far_down, part, passed)
+    factor = last_call(factor_kernel, shape, f32, kept_own, far_up)
+    whole = last_call(last_kernel, mine.shape, bf16, kept_own, factor, far_up, far_down, part, passed)
     returned = lax.all_to_all(whole.reshape(experts, CAP, width), "expert", 0, 0, tiled=True)
     returned = returned.reshape(experts * CAP, width)
     return lax.dot_general(mix, returned, (((0,), (0,)), ((), ())), preferred_element_type=f32)

time: 112 us -> 112 us (level)
    pallas_call x3 -> x4, Pallas kernels: 3.11 us -> 3.33 us  [last_call(): pl.pallas_call(kernel, out_shape=jax.ShapeDtypeStruct(shape, kind), in_sp...]
  transfers between devices with their start and end apart: 19 -> 19, of which waited for: 6 -> 5; matrix products, arithmetic and copies ran while one was open for 0% -> 0% of each run, Pallas kernels for 22% -> 22%
where the time goes in v9:
time: 112 us
  starting transfers between devices  35.6 us (32%)
  waiting for transfers between devices  29.1 us (26%)
  Pallas kernels  25.7 us (23%)
  blocking collectives  20.5 us (18%)
  matrix products  1.12 us (1%)
    ppermute x17, waiting for transfers between devices, send_on(): return lax.ppermute(x, 'dp', way)  29.1 us
    ppermute x17, starting transfers between devices, send_on(): return lax.ppermute(x, 'dp', way)  25.8 us
    all_to_all x1, blocking collectives, local(): lax.all_to_all(whole.reshape(experts, CAP, width), 'expert', 0, 0, tiled=...  20.5 us
    pallas_call x1, Pallas kernels, own_call(): pl.pallas_call(functools.partial(own_kernel, n_w), out_shape=(jax.ShapeDt...  7.81 us
    all_to_all x1, starting transfers between devices, local(): lax.all_to_all(send.reshape(experts, CAP, 3 * width), 'expert', 0, 0, til...  6.81 us
    pallas_call x1, Pallas kernels, other_call(): pl.pallas_call(other_kernel, out_shape=(jax.ShapeDtypeStruct((rows, width...  6.47 us
    pallas_call x1, Pallas kernels, next_call(): pl.pallas_call(functools.partial(next_kernel, n_w), out_shape=tuple((jax....  5 us
    pallas_call x4, Pallas kernels, last_call(): pl.pallas_call(kernel, out_shape=jax.ShapeDtypeStruct(shape, kind), in_sp...  3.33 us
  transfers between devices with their start and end apart: 19, of which 5 were waited for; matrix products, arithmetic and copies ran while one was open for 0% of the time, Pallas kernels for 22%

profile of v9, /device:TPU:1, one launch (start us, length us, event | category | flops | bytes accessed | tf_op | source)
XLA Modules:
  0.0 112.2 jit_solution(4023298413340327418)
XLA Ops:
  0.0 2.5 %collective-permute-start = (bf16[256,1024]{1,0:T(8,128)(2,1)}, bf16[256,1024]{1,0:T(8,128)(2,1)S(1)}, u32[]{:S(2)}, u32[]{:S(2)}) collective-permute-start(bf16[256,1024]{1,0:T(8,128)(2,1)} %bitcast.11), channel_id=1, source_target_pairs={{0,32},{16,48},{32,64},{48,80},{64,96},{80,112},{96,128},{112,144}... | collective-permute-start | bytes 1572872 | tf_op jit(solution)/shard_map/ppermute | solution.py:241
  2.5 3.9 %collective-permute-start.1 = (bf16[256,1024]{1,0:T(8,128)(2,1)}, bf16[256,1024]{1,0:T(8,128)(2,1)}, u32[]{:S(2)}, u32[]{:S(2)}) collective-permute-start(bf16[256,1024]{1,0:T(8,128)(2,1)} %bitcast.14), channel_id=1, source_target_pairs={{0,224},{16,240},{32,0},{48,16},{64,32},{80,48},{96,64},{112,80},{... | collective-permute-start | bytes 1572872 | tf_op jit(solution)/shard_map/ppermute | solution.py:241
  6.4 0.0 collective-permute-start.4
  6.4 2.7 %collective-permute-start.5 = (bf16[256,1024]{1,0:T(8,128)(2,1)}, bf16[256,1024]{1,0:T(8,128)(2,1)}, u32[]{:S(2)}, u32[]{:S(2)}) collective-permute-start(bf16[256,1024]{1,0:T(8,128)(2,1)} %bitcast.12), channel_id=1, source_target_pairs={{0,224},{16,240},{32,0},{48,16},{64,32},{80,48},{96,64},{112,80},{... | collective-permute-start | bytes 1572872 | tf_op jit(solution)/shard_map/ppermute | solution.py:241
  9.1 3.1 %shard_map.73 = (bf16[384,3072]{1,0:T(8,128)(2,1)}, bf16[384,128]{1,0:T(8,128)(2,1)S(1)}) custom-call(s32[2,128]{1,0:T(2,128)} %bitcast.18, s32[2,128]{1,0:T(2,128)} %bitcast.19, bf16[128,1024]{1,0:T(8,128)(2,1)} %x_hbm.1, bf16[128,1024]{1,0:T(8,128)(2,1)} %t_hbm.1, bf16[128,1024]{1,0:T(8,128)(2,1)} %c_hbm.1), custom_call_target="tpu_custom_call" | custom-call | tf_op jit(solution)/shard_map/pallas_call | solution.py:61
  12.2 6.8 %all-to-all-start = ((bf16[16,24,3072]{2,1,0:T(8,128)(2,1)}), bf16[16,24,3072]{2,1,0:T(8,128)(2,1)}, u32[]{:S(2)}, u32[]{:S(2)}) async-start(bf16[16,24,3072]{2,1,0:T(8,128)(2,1)} %bitcast.2), calls=%async_computation | async-start | bytes 4718592 | tf_op jit(solution)/shard_map/all_to_all | solution.py:247
  19.0 0.0 collective-permute-done.refs_0_.refs_1_
  19.1 0.0 copy-start
  19.1 0.0 copy-start.1
  19.1 0.0 collective-permute-done.1.refs_7_
  19.1 0.1 collective-permute-start.2
  19.2 2.7 %collective-permute-start.3 = (bf16[256,1024]{1,0:T(8,128)(2,1)}, bf16[256,1024]{1,0:T(8,128)(2,1)}, u32[]{:S(2)}, u32[]{:S(2)}) collective-permute-start(bf16[256,1024]{1,0:T(8,128)(2,1)} %collective-permute-done.1.refs_7_), channel_id=1, source_target_pairs={{0,224},{16,240},{32,0},{48,16},{64,32},{80,48},{96,64},{112,80},{... | collective-permute-start | bytes 1572872 | tf_op jit(solution)/shard_map/ppermute | solution.py:241
  21.9 7.8 %collective-permute-done.4.refs_6_ = bf16[256,1024]{1,0:T(8,128)(2,1)} collective-permute-done((bf16[256,1024]{1,0:T(8,128)(2,1)}, bf16[256,1024]{1,0:T(8,128)(2,1)}, u32[]{:S(2)}, u32[]{:S(2)}) %collective-permute-start.4) | collective-permute-done | bytes 524320 | tf_op jit(solution)/shard_map/ppermute | solution.py:241
  29.6 0.0 collective-permute-done.5.refs_2_
  29.6 0.0 collective-permute-start.6
  29.6 2.7 %collective-permute-start.7 = (bf16[256,1024]{1,0:T(8,128)(2,1)}, bf16[256,1024]{1,0:T(8,128)(2,1)}, u32[]{:S(2)}, u32[]{:S(2)}) collective-permute-start(bf16[256,1024]{1,0:T(8,128)(2,1)} %collective-permute-done.5.refs_2_), channel_id=1, source_target_pairs={{0,224},{16,240},{32,0},{48,16},{64,32},{80,48},{96,64},{112,80},{... | collective-permute-start | bytes 1572872 | tf_op jit(solution)/shard_map/ppermute | solution.py:241
  32.3 8.6 %collective-permute-done.2.refs_3_ = bf16[256,1024]{1,0:T(8,128)(2,1)S(1)} collective-permute-done((bf16[256,1024]{1,0:T(8,128)(2,1)S(1)}, bf16[256,1024]{1,0:T(8,128)(2,1)S(1)}, u32[]{:S(2)}, u32[]{:S(2)}) %collective-permute-start.2) | collective-permute-done | bytes 524320 | tf_op jit(solution)/shard_map/ppermute | solution.py:241
  40.8 0.0 collective-permute-done.3.refs_9_
  40.8 0.0 collective-permute-start.8
  40.8 2.7 %collective-permute-start.9 = (bf16[256,1024]{1,0:T(8,128)(2,1)}, bf16[256,1024]{1,0:T(8,128)(2,1)}, u32[]{:S(2)}, u32[]{:S(2)}) collective-permute-start(bf16[256,1024]{1,0:T(8,128)(2,1)} %collective-permute-done.3.refs_9_), channel_id=1, source_target_pairs={{0,224},{16,240},{32,0},{48,16},{64,32},{80,48},{96,64},{112,80},{... | collective-permute-start | bytes 1572872 | tf_op jit(solution)/shard_map/ppermute | solution.py:241
  43.5 8.6 %collective-permute-done.6.refs_8_ = bf16[256,1024]{1,0:T(8,128)(2,1)} collective-permute-done((bf16[256,1024]{1,0:T(8,128)(2,1)}, bf16[256,1024]{1,0:T(8,128)(2,1)}, u32[]{:S(2)}, u32[]{:S(2)}) %collective-permute-start.6) | collective-permute-done | bytes 524320 | tf_op jit(solution)/shard_map/ppermute | solution.py:241
  52.1 0.0 collective-permute-done.7.refs_4_
  52.1 2.4 %collective-permute-start.14 = (bf16[256,1024]{1,0:T(8,128)(2,1)}, bf16[256,1024]{1,0:T(8,128)(2,1)}, u32[]{:S(2)}, u32[]{:S(2)}) collective-permute-start(bf16[256,1024]{1,0:T(8,128)(2,1)} %collective-permute-done.7.refs_4_), channel_id=1, source_target_pairs={{0,224},{16,240},{32,0},{48,16},{64,32},{80,48},{96,64},{112,80},{... | collective-permute-start | bytes 1572872 | tf_op jit(solution)/shard_map/ppermute | solution.py:241
  54.4 0.0 collective-permute-start.15
  54.4 0.0 all-to-all-done
  54.4 3.0 %collective-permute-start.13 = (bf16[384,3072]{1,0:T(8,128)(2,1)}, bf16[384,3072]{1,0:T(8,128)(2,1)}, u32[]{:S(2)}, u32[]{:S(2)}) collective-permute-start(bf16[384,3072]{1,0:T(8,128)(2,1)} %bitcast.3.own_ref), channel_id=1, source_target_pairs={{0,16},{16,0},{32,48},{48,32},{64,80},{80,64},{96,112},{112,96},{1... | collective-permute-start | bytes 7077896 | tf_op jit(solution)/shard_map/ppermute | solution.py:262
  57.4 7.8 %shard_map.75 = (f32[384,1024]{1,0:T(8,128)S(1)}, bf16[384,3072]{1,0:T(8,128)(2,1)S(1)}, bf16[5,256,1024]{2,1,0:T(8,128)(2,1)S(1)}, bf16[5,256,1024]{2,1,0:T(8,128)(2,1)S(1)}) custom-call(bf16[384,3072]{1,0:T(8,128)(2,1)} %bitcast.3.own_ref, bf16[256,1024]{1,0:T(8,128)(2,1)S(1)} %bitcast.13, bf16[256,1024]{1,0:T(8,128)(2,1)S(1)} %collective-permute-done.refs_0_.refs_1_, ...), custom_call_target="tpu_custom_call" | custom-call | tf_op jit(solution)/shard_map/pallas_call | solution.py:122
  65.2 0.0 collective-permute-done.8.refs_0_
  65.3 0.0 collective-permute-done.9.refs_3_
  65.3 0.1 collective-permute-start.10
  65.4 3.0 %collective-permute-start.12 = (bf16[256,1024]{1,0:T(8,128)(2,1)}, bf16[256,1024]{1,0:T(8,128)(2,1)S(1)}, u32[]{:S(2)}, u32[]{:S(2)}) collective-permute-start(bf16[256,1024]{1,0:T(8,128)(2,1)} %collective-permute-done.9.refs_3_), channel_id=1, source_target_pairs={{0,224},{16,240},{32,0},{48,16},{64,32},{80,48},{96,64},{112,80},{... | collective-permute-start | bytes 1572872 | tf_op jit(solution)/shard_map/ppermute | solution.py:241
  68.4 0.0 collective-permute-done.13.other_ref
  68.4 6.5 %shard_map.77 = (f32[384,1024]{1,0:T(8,128)S(1)}, bf16[384,3072]{1,0:T(8,128)(2,1)S(1)}) custom-call(bf16[384,3072]{1,0:T(8,128)(2,1)} %collective-permute-done.13.other_ref, bf16[5,256,1024]{2,1,0:T(8,128)(2,1)S(1)} %get-tuple-element.57.up_ref, bf16[5,256,1024]{2,1,0:T(8,128)(2,1)S(1)} %get-tuple-element.58.down_ref), custom_call_target="tpu_custom_call" | custom-call | tf_op jit(solution)/shard_map/pallas_call | solution.py:143
  74.9 0.0 collective-permute-done.14.refs_1_
  74.9 0.0 collective-permute-done.15.refs_2_
  74.9 5.0 %shard_map.78 = (f32[384,1024]{1,0:T(8,128)S(1)}, bf16[384,1024]{1,0:T(8,128)(2,1)S(1)}) custom-call(bf16[384,3072]{1,0:T(8,128)(2,1)S(1)} %get-tuple-element.54.refs_1_.own_ref.rows_ref, bf16[384,3072]{1,0:T(8,128)(2,1)S(1)} %get-tuple-element.59.other_ref, bf16[256,1024]{1,0:T(8,128)(2,1)S(1)} %collective-permute-done.8.refs_0_, ...), custom_call_target="tpu_custom_call" | custom-call | tf_op jit(solution)/shard_map/pallas_call | solution.py:173
  79.9 1.8 %collective-permute-start.17 = (bf16[384,1024]{1,0:T(8,128)(2,1)S(1)}, bf16[384,1024]{1,0:T(8,128)(2,1)S(1)}, u32[]{:S(2)}, u32[]{:S(2)}) collective-permute-start(bf16[384,1024]{1,0:T(8,128)(2,1)S(1)} %get-tuple-element.70), channel_id=1, source_target_pairs={{0,16},{16,0},{32,48},{48,32},{64,80},{80,64},{96,112},{112,96},{1... | collective-permute-start | bytes 2359304 | tf_op jit(solution)/shard_map/ppermute | solution.py:241
  81.7 4.0 %collective-permute-done.10.up_ref = bf16[256,1024]{1,0:T(8,128)(2,1)S(1)} collective-permute-done((bf16[256,1024]{1,0:T(8,128)(2,1)S(1)}, bf16[256,1024]{1,0:T(8,128)(2,1)S(1)}, u32[]{:S(2)}, u32[]{:S(2)}) %collective-permute-start.10) | collective-permute-done | bytes 524320 | tf_op jit(solution)/shard_map/ppermute | solution.py:241
  85.7 1.2 %collective-permute-start.11 = (bf16[256,1024]{1,0:T(8,128)(2,1)S(1)}, bf16[256,1024]{1,0:T(8,128)(2,1)S(1)}, u32[]{:S(2)}, u32[]{:S(2)}) collective-permute-start(bf16[256,1024]{1,0:T(8,128)(2,1)S(1)} %collective-permute-done.10.up_ref), channel_id=1, source_target_pairs={{0,16},{16,0},{32,48},{48,32},{64,80},{80,64},{96,112},{112,96},{1... | collective-permute-start | bytes 1572872 | tf_op jit(solution)/shard_map/ppermute | solution.py:241
  86.9 0.6 shard_map.79.factor_ref
  87.6 0.1 collective-permute-start.16
  87.7 1.0 shard_map.80.refs_0_
  88.7 0.0 collective-permute-done.11.up_ref
  88.7 0.6 shard_map.81.factor_ref
  89.4 0.2 collective-permute-done.16.down_ref
  89.6 1.0 shard_map.82
  90.6 20.5 %all_to_all.10 = bf16[16,24,1024]{2,1,0:T(8,128)(2,1)S(1)} all-to-all(bf16[16,24,1024]{2,1,0:T(8,128)(2,1)S(1)} %bitcast.10), channel_id=1, replica_groups=mesh['dp'=16,'expert'=16] {'expert'}, dimensions={0} | all-to-all | bytes 1572864 | tf_op jit(solution)/shard_map/all_to_all | solution.py:276
  111.0 1.1 fusion
  (6 shorter events, 0.0 us)
Async XLA Ops:
  0.0 19.0 %collective-permute-start = (bf16[256,1024]{1,0:T(8,128)(2,1)}, bf16[256,1024]{1,0:T(8,128)(2,1)S(1)}, u32[]{:S(2)}, u32[]{:S(2)}) collective-permute-start(bf16[256,1024]{1,0:T(8,128)(2,1)} %bitcast.11), channel_id=1, source_target_pairs={{0,32},{16,48},{32,64},{48,80},{64,96},{80,112},{96,128},{112,144}... | collective-permute-start | bytes 1572872 | tf_op jit(solution)/shard_map/ppermute | solution.py:241
  2.5 16.6 %collective-permute-start.1 = (bf16[256,1024]{1,0:T(8,128)(2,1)}, bf16[256,1024]{1,0:T(8,128)(2,1)}, u32[]{:S(2)}, u32[]{:S(2)}) collective-permute-start(bf16[256,1024]{1,0:T(8,128)(2,1)} %bitcast.14), channel_id=1, source_target_pairs={{0,224},{16,240},{32,0},{48,16},{64,32},{80,48},{96,64},{112,80},{... | collective-permute-start | bytes 1572872 | tf_op jit(solution)/shard_map/ppermute | solution.py:241
  6.4 23.2 %collective-permute-start.4 = (bf16[256,1024]{1,0:T(8,128)(2,1)}, bf16[256,1024]{1,0:T(8,128)(2,1)}, u32[]{:S(2)}, u32[]{:S(2)}) collective-permute-start(bf16[256,1024]{1,0:T(8,128)(2,1)} %bitcast.15), channel_id=1, source_target_pairs={{0,32},{16,48},{32,64},{48,80},{64,96},{80,112},{96,128},{112,144}... | collective-permute-start | bytes 1572872 | tf_op jit(solution)/shard_map/ppermute | solution.py:241
  6.4 23.2 %collective-permute-start.5 = (bf16[256,1024]{1,0:T(8,128)(2,1)}, bf16[256,1024]{1,0:T(8,128)(2,1)}, u32[]{:S(2)}, u32[]{:S(2)}) collective-permute-start(bf16[256,1024]{1,0:T(8,128)(2,1)} %bitcast.12), channel_id=1, source_target_pairs={{0,224},{16,240},{32,0},{48,16},{64,32},{80,48},{96,64},{112,80},{... | collective-permute-start | bytes 1572872 | tf_op jit(solution)/shard_map/ppermute | solution.py:241
  12.2 42.2 %all-to-all-start = ((bf16[16,24,3072]{2,1,0:T(8,128)(2,1)}), bf16[16,24,3072]{2,1,0:T(8,128)(2,1)}, u32[]{:S(2)}, u32[]{:S(2)}) async-start(bf16[16,24,3072]{2,1,0:T(8,128)(2,1)} %bitcast.2), calls=%async_computation | async-start | bytes 4718592 | tf_op jit(solution)/shard_map/all_to_all | solution.py:247
  19.1 38.4 %copy-start = (bf16[1,256,1024]{2,1,0:T(8,128)(2,1)S(1)}, bf16[1,256,1024]{2,1,0:T(8,128)(2,1)}, u32[]{:S(2)}) copy-start(bf16[1,256,1024]{2,1,0:T(8,128)(2,1)} %param.12) | copy-start | bytes 1572868
  19.1 38.4 %copy-start.1 = (bf16[1,256,1024]{2,1,0:T(8,128)(2,1)S(1)}, bf16[1,256,1024]{2,1,0:T(8,128)(2,1)}, u32[]{:S(2)}) copy-start(bf16[1,256,1024]{2,1,0:T(8,128)(2,1)} %param.13) | copy-start | bytes 1572868
  19.1 21.7 %collective-permute-start.2 = (bf16[256,1024]{1,0:T(8,128)(2,1)S(1)}, bf16[256,1024]{1,0:T(8,128)(2,1)S(1)}, u32[]{:S(2)}, u32[]{:S(2)}) collective-permute-start(bf16[256,1024]{1,0:T(8,128)(2,1)S(1)} %collective-permute-done.refs_0_.refs_1_), channel_id=1, source_target_pairs={{0,32},{16,48},{32,64},{48,80},{64,96},{80,112},{96,128},{112,144}... | collective-permute-start | bytes 1572872 | tf_op jit(solution)/shard_map/ppermute | solution.py:241
  19.2 21.7 %collective-permute-start.3 = (bf16[256,1024]{1,0:T(8,128)(2,1)}, bf16[256,1024]{1,0:T(8,128)(2,1)}, u32[]{:S(2)}, u32[]{:S(2)}) collective-permute-start(bf16[256,1024]{1,0:T(8,128)(2,1)} %collective-permute-done.1.refs_7_), channel_id=1, source_target_pairs={{0,224},{16,240},{32,0},{48,16},{64,32},{80,48},{96,64},{112,80},{... | collective-permute-start | bytes 1572872 | tf_op jit(solution)/shard_map/ppermute | solution.py:241
  29.6 22.5 %collective-permute-start.6 = (bf16[256,1024]{1,0:T(8,128)(2,1)}, bf16[256,1024]{1,0:T(8,128)(2,1)}, u32[]{:S(2)}, u32[]{:S(2)}) collective-permute-start(bf16[256,1024]{1,0:T(8,128)(2,1)} %collective-permute-done.4.refs_6_), channel_id=1, source_target_pairs={{0,32},{16,48},{32,64},{48,80},{64,96},{80,112},{96,128},{112,144}... | collective-permute-start | bytes 1572872 | tf_op jit(solution)/shard_map/ppermute | solution.py:241
  29.6 22.5 %collective-permute-start.7 = (bf16[256,1024]{1,0:T(8,128)(2,1)}, bf16[256,1024]{1,0:T(8,128)(2,1)}, u32[]{:S(2)}, u32[]{:S(2)}) collective-permute-start(bf16[256,1024]{1,0:T(8,128)(2,1)} %collective-permute-done.5.refs_2_), channel_id=1, source_target_pairs={{0,224},{16,240},{32,0},{48,16},{64,32},{80,48},{96,64},{112,80},{... | collective-permute-start | bytes 1572872 | tf_op jit(solution)/shard_map/ppermute | solution.py:241
  40.8 24.4 %collective-permute-start.8 = (bf16[256,1024]{1,0:T(8,128)(2,1)S(1)}, bf16[256,1024]{1,0:T(8,128)(2,1)S(1)}, u32[]{:S(2)}, u32[]{:S(2)}) collective-permute-start(bf16[256,1024]{1,0:T(8,128)(2,1)S(1)} %collective-permute-done.2.refs_3_), channel_id=1, source_target_pairs={{0,32},{16,48},{32,64},{48,80},{64,96},{80,112},{96,128},{112,144}... | collective-permute-start | bytes 1572872 | tf_op jit(solution)/shard_map/ppermute | solution.py:241
  40.8 24.4 %collective-permute-start.9 = (bf16[256,1024]{1,0:T(8,128)(2,1)}, bf16[256,1024]{1,0:T(8,128)(2,1)}, u32[]{:S(2)}, u32[]{:S(2)}) collective-permute-start(bf16[256,1024]{1,0:T(8,128)(2,1)} %collective-permute-done.3.refs_9_), channel_id=1, source_target_pairs={{0,224},{16,240},{32,0},{48,16},{64,32},{80,48},{96,64},{112,80},{... | collective-permute-start | bytes 1572872 | tf_op jit(solution)/shard_map/ppermute | solution.py:241
  52.1 22.8 %collective-permute-start.14 = (bf16[256,1024]{1,0:T(8,128)(2,1)}, bf16[256,1024]{1,0:T(8,128)(2,1)}, u32[]{:S(2)}, u32[]{:S(2)}) collective-permute-start(bf16[256,1024]{1,0:T(8,128)(2,1)} %collective-permute-done.7.refs_4_), channel_id=1, source_target_pairs={{0,224},{16,240},{32,0},{48,16},{64,32},{80,48},{96,64},{112,80},{... | collective-permute-start | bytes 1572872 | tf_op jit(solution)/shard_map/ppermute | solution.py:241
  54.4 20.4 %collective-permute-start.15 = (bf16[256,1024]{1,0:T(8,128)(2,1)}, bf16[256,1024]{1,0:T(8,128)(2,1)}, u32[]{:S(2)}, u32[]{:S(2)}) collective-permute-start(bf16[256,1024]{1,0:T(8,128)(2,1)} %collective-permute-done.6.refs_8_), channel_id=1, source_target_pairs={{0,32},{16,48},{32,64},{48,80},{64,96},{80,112},{96,128},{112,144}... | collective-permute-start | bytes 1572872 | tf_op jit(solution)/shard_map/ppermute | solution.py:241
  54.4 13.9 %collective-permute-start.13 = (bf16[384,3072]{1,0:T(8,128)(2,1)}, bf16[384,3072]{1,0:T(8,128)(2,1)}, u32[]{:S(2)}, u32[]{:S(2)}) collective-permute-start(bf16[384,3072]{1,0:T(8,128)(2,1)} %bitcast.3.own_ref), channel_id=1, source_target_pairs={{0,16},{16,0},{32,48},{48,32},{64,80},{80,64},{96,112},{112,96},{1... | collective-permute-start | bytes 7077896 | tf_op jit(solution)/shard_map/ppermute | solution.py:262
  65.3 20.4 %collective-permute-start.10 = (bf16[256,1024]{1,0:T(8,128)(2,1)S(1)}, bf16[256,1024]{1,0:T(8,128)(2,1)S(1)}, u32[]{:S(2)}, u32[]{:S(2)}) collective-permute-start(bf16[256,1024]{1,0:T(8,128)(2,1)S(1)} %collective-permute-done.8.refs_0_), channel_id=1, source_target_pairs={{0,32},{16,48},{32,64},{48,80},{64,96},{80,112},{96,128},{112,144}... | collective-permute-start | bytes 1572872 | tf_op jit(solution)/shard_map/ppermute | solution.py:241
  65.4 22.2 %collective-permute-start.12 = (bf16[256,1024]{1,0:T(8,128)(2,1)}, bf16[256,1024]{1,0:T(8,128)(2,1)S(1)}, u32[]{:S(2)}, u32[]{:S(2)}) collective-permute-start(bf16[256,1024]{1,0:T(8,128)(2,1)} %collective-permute-done.9.refs_3_), channel_id=1, source_target_pairs={{0,224},{16,240},{32,0},{48,16},{64,32},{80,48},{96,64},{112,80},{... | collective-permute-start | bytes 1572872 | tf_op jit(solution)/shard_map/ppermute | solution.py:241
  79.9 9.7 %collective-permute-start.17 = (bf16[384,1024]{1,0:T(8,128)(2,1)S(1)}, bf16[384,1024]{1,0:T(8,128)(2,1)S(1)}, u32[]{:S(2)}, u32[]{:S(2)}) collective-permute-start(bf16[384,1024]{1,0:T(8,128)(2,1)S(1)} %get-tuple-element.70), channel_id=1, source_target_pairs={{0,16},{16,0},{32,48},{48,32},{64,80},{80,64},{96,112},{112,96},{1... | collective-permute-start | bytes 2359304 | tf_op jit(solution)/shard_map/ppermute | solution.py:241
  85.7 3.0 %collective-permute-start.11 = (bf16[256,1024]{1,0:T(8,128)(2,1)S(1)}, bf16[256,1024]{1,0:T(8,128)(2,1)S(1)}, u32[]{:S(2)}, u32[]{:S(2)}) collective-permute-start(bf16[256,1024]{1,0:T(8,128)(2,1)S(1)} %collective-permute-done.10.up_ref), channel_id=1, source_target_pairs={{0,16},{16,0},{32,48},{48,32},{64,80},{80,64},{96,112},{112,96},{1... | collective-permute-start | bytes 1572872 | tf_op jit(solution)/shard_map/ppermute | solution.py:241
  87.6 2.0 %collective-permute-start.16 = (bf16[256,1024]{1,0:T(8,128)(2,1)S(1)}, bf16[256,1024]{1,0:T(8,128)(2,1)S(1)}, u32[]{:S(2)}, u32[]{:S(2)}) collective-permute-start(bf16[256,1024]{1,0:T(8,128)(2,1)S(1)} %collective-permute-done.12.down_ref), channel_id=1, source_target_pairs={{0,16},{16,0},{32,48},{48,32},{64,80},{80,64},{96,112},{112,96},{1... | collective-permute-start | bytes 1572872 | tf_op jit(solution)/shard_map/ppermute | solution.py:241

commit v10 on v8

--- a/solution.py
+++ b/solution.py
@@ -184,23 +184,13 @@
     )(*inside[:2], *ups, *downs, *inside[2:], mark)
 
 
-def factor_kernel(rows_ref, up_ref, factor_ref):
-    width = up_ref.shape[1]
-    before_act = lax.dot_general(rows_ref[:, :width], up_ref[...], NT, preferred_element_type=f32)
-    lifted = lax.dot_general(rows_ref[:, width:2 * width], up_ref[...], NT, preferred_element_type=f32)
-    factor_ref[...] = curvature(before_act) * lifted
-
-
 def last_own_kernel(rows_ref, up_ref, down_ref, acc_ref, out_ref):
     out_ref[...] = accumulate(rows_ref, [up_ref], [down_ref], acc_ref[...])
 
 
-def last_far_kernel(rows_ref, factor_ref, up_ref, down_ref, acc_ref, passed_ref, out_ref):
-    width = up_ref.shape[1]
-    pulled = lax.dot_general(rows_ref[:, 2 * width:], down_ref[...], NT, preferred_element_type=f32)
-    inner = (pulled * factor_ref[...]).astype(bf16)
+def last_far_kernel(rows_ref, up_ref, down_ref, acc_ref, passed_ref, out_ref):
     total = acc_ref[...] + passed_ref[...].astype(f32)
-    out_ref[...] = (total + jnp.dot(inner, up_ref[...], preferred_element_type=f32)).astype(out_ref.dtype)
+    out_ref[...] = accumulate(rows_ref, [up_ref], [down_ref], total).astype(out_ref.dtype)
 
 
 def last_call(kernel, shape, kind, *operands):
@@ -266,9 +256,8 @@
     passed = send_on(theirs, swap)
     far_up, far_down = send_on(uf4, swap), send_on(db4, swap)
     part = last_call(last_own_kernel, mine.shape, f32, kept_own, uf4, db4, mine)
-    far_up, part = after((far_up, part))
-    factor = last_call(factor_kernel, (own.shape[0], far_up.shape[0]), f32, kept_own, far_up)
-    whole = last_call(last_far_kernel, mine.shape, bf16, kept_own, factor, far_up, far_down, part, passed)
+    far_up, far_down, part = after((far_up, far_down, part))
+    whole = last_call(last_far_kernel, mine.shape, bf16, kept_own, far_up, far_down, part, passed)
     returned = lax.all_to_all(whole.reshape(experts, CAP, width), "expert", 0, 0, tiled=True)
     returned = returned.reshape(experts * CAP, width)
     return lax.dot_general(mix, returned, (((0,), (0,)), ((), ())), preferred_element_type=f32)

time: 112 us -> 112 us (level)
    pallas_call x3 -> x2, Pallas kernels: 3.11 us -> 2.9 us  [last_call(): pl.pallas_call(kernel, out_shape=jax.ShapeDtypeStruct(shape, kind), in_sp...]
  transfers between devices with their start and end apart: 19 -> 19, of which waited for: 6 -> 6; matrix products, arithmetic and copies ran while one was open for 0% -> 0% of each run, Pallas kernels for 22% -> 21%
where the time goes in v10:
time: 112 us
  starting transfers between devices  35.5 us (32%)
  waiting for transfers between devices  29.7 us (27%)
  Pallas kernels  25.3 us (23%)
  blocking collectives  20.4 us (18%)
  matrix products  1.12 us (1%)
    ppermute x17, waiting for transfers between devices, send_on(): return lax.ppermute(x, 'dp', way)  29.7 us
    ppermute x17, starting transfers between devices, send_on(): return lax.ppermute(x, 'dp', way)  25.7 us
    all_to_all x1, blocking collectives, local(): lax.all_to_all(whole.reshape(experts, CAP, width), 'expert', 0, 0, tiled=...  20.4 us
    pallas_call x1, Pallas kernels, own_call(): pl.pallas_call(functools.partial(own_kernel, n_w), out_shape=(jax.ShapeDt...  7.81 us
    all_to_all x1, starting transfers between devices, local(): lax.all_to_all(send.reshape(experts, CAP, 3 * width), 'expert', 0, 0, til...  6.81 us
    pallas_call x1, Pallas kernels, other_call(): pl.pallas_call(other_kernel, out_shape=(jax.ShapeDtypeStruct((rows, width...  6.47 us
    pallas_call x1, Pallas kernels, next_call(): pl.pallas_call(functools.partial(next_kernel, n_w), out_shape=tuple((jax....  5.02 us
    pallas_call x1, Pallas kernels, prepare(): pl.pallas_call(prepare_kernel, out_shape=(jax.ShapeDtypeStruct((slots, 3...  3.13 us
  transfers between devices with their start and end apart: 19, of which 6 were waited for; matrix products, arithmetic and copies ran while one was open for 0% of the time, Pallas kernels for 21%

profile of v10, /device:TPU:1, one launch (start us, length us, event | category | flops | bytes accessed | tf_op | source)
XLA Modules:
  0.0 112.2 jit_solution(8342722354902987900)
XLA Ops:
  0.0 2.5 %collective-permute-start = (bf16[256,1024]{1,0:T(8,128)(2,1)}, bf16[256,1024]{1,0:T(8,128)(2,1)S(1)}, u32[]{:S(2)}, u32[]{:S(2)}) collective-permute-start(bf16[256,1024]{1,0:T(8,128)(2,1)} %bitcast.11), channel_id=1, source_target_pairs={{0,32},{16,48},{32,64},{48,80},{64,96},{80,112},{96,128},{112,144}... | collective-permute-start | bytes 1572872 | tf_op jit(solution)/shard_map/ppermute | solution.py:232
  2.5 3.9 %collective-permute-start.1 = (bf16[256,1024]{1,0:T(8,128)(2,1)}, bf16[256,1024]{1,0:T(8,128)(2,1)}, u32[]{:S(2)}, u32[]{:S(2)}) collective-permute-start(bf16[256,1024]{1,0:T(8,128)(2,1)} %bitcast.14), channel_id=1, source_target_pairs={{0,224},{16,240},{32,0},{48,16},{64,32},{80,48},{96,64},{112,80},{... | collective-permute-start | bytes 1572872 | tf_op jit(solution)/shard_map/ppermute | solution.py:232
  6.4 0.0 collective-permute-start.4
  6.4 2.7 %collective-permute-start.5 = (bf16[256,1024]{1,0:T(8,128)(2,1)}, bf16[256,1024]{1,0:T(8,128)(2,1)}, u32[]{:S(2)}, u32[]{:S(2)}) collective-permute-start(bf16[256,1024]{1,0:T(8,128)(2,1)} %bitcast.12), channel_id=1, source_target_pairs={{0,224},{16,240},{32,0},{48,16},{64,32},{80,48},{96,64},{112,80},{... | collective-permute-start | bytes 1572872 | tf_op jit(solution)/shard_map/ppermute | solution.py:232
  9.1 3.1 %shard_map.73 = (bf16[384,3072]{1,0:T(8,128)(2,1)}, bf16[384,128]{1,0:T(8,128)(2,1)S(1)}) custom-call(s32[2,128]{1,0:T(2,128)} %bitcast.18, s32[2,128]{1,0:T(2,128)} %bitcast.19, bf16[128,1024]{1,0:T(8,128)(2,1)} %x_hbm.1, bf16[128,1024]{1,0:T(8,128)(2,1)} %t_hbm.1, bf16[128,1024]{1,0:T(8,128)(2,1)} %c_hbm.1), custom_call_target="tpu_custom_call" | custom-call | tf_op jit(solution)/shard_map/pallas_call | solution.py:61
  12.2 6.8 %all-to-all-start = ((bf16[16,24,3072]{2,1,0:T(8,128)(2,1)}), bf16[16,24,3072]{2,1,0:T(8,128)(2,1)}, u32[]{:S(2)}, u32[]{:S(2)}) async-start(bf16[16,24,3072]{2,1,0:T(8,128)(2,1)} %bitcast.2), calls=%async_computation | async-start | bytes 4718592 | tf_op jit(solution)/shard_map/all_to_all | solution.py:238
  19.0 0.0 collective-permute-done.refs_0_.refs_1_
  19.1 0.0 copy-start
  19.1 0.0 copy-start.1
  19.1 0.0 collective-permute-done.1.refs_7_
  19.1 0.1 collective-permute-start.2
  19.2 2.7 %collective-permute-start.3 = (bf16[256,1024]{1,0:T(8,128)(2,1)}, bf16[256,1024]{1,0:T(8,128)(2,1)}, u32[]{:S(2)}, u32[]{:S(2)}) collective-permute-start(bf16[256,1024]{1,0:T(8,128)(2,1)} %collective-permute-done.1.refs_7_), channel_id=1, source_target_pairs={{0,224},{16,240},{32,0},{48,16},{64,32},{80,48},{96,64},{112,80},{... | collective-permute-start | bytes 1572872 | tf_op jit(solution)/shard_map/ppermute | solution.py:232
  21.9 7.8 %collective-permute-done.4.refs_6_ = bf16[256,1024]{1,0:T(8,128)(2,1)} collective-permute-done((bf16[256,1024]{1,0:T(8,128)(2,1)}, bf16[256,1024]{1,0:T(8,128)(2,1)}, u32[]{:S(2)}, u32[]{:S(2)}) %collective-permute-start.4) | collective-permute-done | bytes 524320 | tf_op jit(solution)/shard_map/ppermute | solution.py:232
  29.6 0.0 collective-permute-done.5.refs_2_
  29.6 0.0 collective-permute-start.6
  29.6 2.7 %collective-permute-start.7 = (bf16[256,1024]{1,0:T(8,128)(2,1)}, bf16[256,1024]{1,0:T(8,128)(2,1)}, u32[]{:S(2)}, u32[]{:S(2)}) collective-permute-start(bf16[256,1024]{1,0:T(8,128)(2,1)} %collective-permute-done.5.refs_2_), channel_id=1, source_target_pairs={{0,224},{16,240},{32,0},{48,16},{64,32},{80,48},{96,64},{112,80},{... | collective-permute-start | bytes 1572872 | tf_op jit(solution)/shard_map/ppermute | solution.py:232
  32.3 8.6 %collective-permute-done.2.refs_3_ = bf16[256,1024]{1,0:T(8,128)(2,1)S(1)} collective-permute-done((bf16[256,1024]{1,0:T(8,128)(2,1)S(1)}, bf16[256,1024]{1,0:T(8,128)(2,1)S(1)}, u32[]{:S(2)}, u32[]{:S(2)}) %collective-permute-start.2) | collective-permute-done | bytes 524320 | tf_op jit(solution)/shard_map/ppermute | solution.py:232
  40.8 0.0 collective-permute-done.3.refs_9_
  40.8 0.0 collective-permute-start.8
  40.8 2.7 %collective-permute-start.9 = (bf16[256,1024]{1,0:T(8,128)(2,1)}, bf16[256,1024]{1,0:T(8,128)(2,1)}, u32[]{:S(2)}, u32[]{:S(2)}) collective-permute-start(bf16[256,1024]{1,0:T(8,128)(2,1)} %collective-permute-done.3.refs_9_), channel_id=1, source_target_pairs={{0,224},{16,240},{32,0},{48,16},{64,32},{80,48},{96,64},{112,80},{... | collective-permute-start | bytes 1572872 | tf_op jit(solution)/shard_map/ppermute | solution.py:232
  43.5 8.6 %collective-permute-done.6.refs_8_ = bf16[256,1024]{1,0:T(8,128)(2,1)} collective-permute-done((bf16[256,1024]{1,0:T(8,128)(2,1)}, bf16[256,1024]{1,0:T(8,128)(2,1)}, u32[]{:S(2)}, u32[]{:S(2)}) %collective-permute-start.6) | collective-permute-done | bytes 524320 | tf_op jit(solution)/shard_map/ppermute | solution.py:232
  52.1 0.0 collective-permute-done.7.refs_4_
  52.1 2.4 %collective-permute-start.15 = (bf16[256,1024]{1,0:T(8,128)(2,1)}, bf16[256,1024]{1,0:T(8,128)(2,1)}, u32[]{:S(2)}, u32[]{:S(2)}) collective-permute-start(bf16[256,1024]{1,0:T(8,128)(2,1)} %collective-permute-done.7.refs_4_), channel_id=1, source_target_pairs={{0,224},{16,240},{32,0},{48,16},{64,32},{80,48},{96,64},{112,80},{... | collective-permute-start | bytes 1572872 | tf_op jit(solution)/shard_map/ppermute | solution.py:232
  54.4 0.0 collective-permute-start.16
  54.4 0.0 all-to-all-done
  54.4 3.0 %collective-permute-start.14 = (bf16[384,3072]{1,0:T(8,128)(2,1)}, bf16[384,3072]{1,0:T(8,128)(2,1)}, u32[]{:S(2)}, u32[]{:S(2)}) collective-permute-start(bf16[384,3072]{1,0:T(8,128)(2,1)} %bitcast.3.own_ref), channel_id=1, source_target_pairs={{0,16},{16,0},{32,48},{48,32},{64,80},{80,64},{96,112},{112,96},{1... | collective-permute-start | bytes 7077896 | tf_op jit(solution)/shard_map/ppermute | solution.py:253
  57.4 7.8 %shard_map.75 = (f32[384,1024]{1,0:T(8,128)S(1)}, bf16[384,3072]{1,0:T(8,128)(2,1)S(1)}, bf16[5,256,1024]{2,1,0:T(8,128)(2,1)S(1)}, bf16[5,256,1024]{2,1,0:T(8,128)(2,1)S(1)}) custom-call(bf16[384,3072]{1,0:T(8,128)(2,1)} %bitcast.3.own_ref, bf16[256,1024]{1,0:T(8,128)(2,1)S(1)} %bitcast.13, bf16[256,1024]{1,0:T(8,128)(2,1)S(1)} %collective-permute-done.refs_0_.refs_1_, ...), custom_call_target="tpu_custom_call" | custom-call | tf_op jit(solution)/shard_map/pallas_call | solution.py:122
  65.2 0.0 collective-permute-done.8.refs_0_
  65.3 0.0 collective-permute-done.9.refs_3_
  65.3 0.1 collective-permute-start.10
  65.4 3.0 %collective-permute-start.12 = (bf16[256,1024]{1,0:T(8,128)(2,1)}, bf16[256,1024]{1,0:T(8,128)(2,1)S(1)}, u32[]{:S(2)}, u32[]{:S(2)}) collective-permute-start(bf16[256,1024]{1,0:T(8,128)(2,1)} %collective-permute-done.9.refs_3_), channel_id=1, source_target_pairs={{0,224},{16,240},{32,0},{48,16},{64,32},{80,48},{96,64},{112,80},{... | collective-permute-start | bytes 1572872 | tf_op jit(solution)/shard_map/ppermute | solution.py:232
  68.4 0.0 collective-permute-done.14.other_ref
  68.4 6.5 %shard_map.77 = (f32[384,1024]{1,0:T(8,128)S(1)}, bf16[384,3072]{1,0:T(8,128)(2,1)S(1)}) custom-call(bf16[384,3072]{1,0:T(8,128)(2,1)} %collective-permute-done.14.other_ref, bf16[5,256,1024]{2,1,0:T(8,128)(2,1)S(1)} %get-tuple-element.54.up_ref, bf16[5,256,1024]{2,1,0:T(8,128)(2,1)S(1)} %get-tuple-element.55.down_ref), custom_call_target="tpu_custom_call" | custom-call | tf_op jit(solution)/shard_map/pallas_call | solution.py:143
  74.9 0.0 collective-permute-done.15.refs_1_
  74.9 0.0 collective-permute-done.16.refs_2_
  74.9 5.0 %shard_map.78 = (f32[384,1024]{1,0:T(8,128)S(1)}, bf16[384,1024]{1,0:T(8,128)(2,1)S(1)}) custom-call(bf16[384,3072]{1,0:T(8,128)(2,1)S(1)} %get-tuple-element.51.refs_1_.own_ref.rows_ref, bf16[384,3072]{1,0:T(8,128)(2,1)S(1)} %get-tuple-element.56.other_ref, bf16[256,1024]{1,0:T(8,128)(2,1)S(1)} %collective-permute-done.8.refs_0_, ...), custom_call_target="tpu_custom_call" | custom-call | tf_op jit(solution)/shard_map/pallas_call | solution.py:173
  79.9 1.8 %collective-permute-start.17 = (bf16[384,1024]{1,0:T(8,128)(2,1)S(1)}, bf16[384,1024]{1,0:T(8,128)(2,1)S(1)}, u32[]{:S(2)}, u32[]{:S(2)}) collective-permute-start(bf16[384,1024]{1,0:T(8,128)(2,1)S(1)} %get-tuple-element.64), channel_id=1, source_target_pairs={{0,16},{16,0},{32,48},{48,32},{64,80},{80,64},{96,112},{112,96},{1... | collective-permute-start | bytes 2359304 | tf_op jit(solution)/shard_map/ppermute | solution.py:232
  81.7 4.0 %collective-permute-done.10.up_ref = bf16[256,1024]{1,0:T(8,128)(2,1)S(1)} collective-permute-done((bf16[256,1024]{1,0:T(8,128)(2,1)S(1)}, bf16[256,1024]{1,0:T(8,128)(2,1)S(1)}, u32[]{:S(2)}, u32[]{:S(2)}) %collective-permute-start.10) | collective-permute-done | bytes 524320 | tf_op jit(solution)/shard_map/ppermute | solution.py:232
  85.7 1.2 %collective-permute-start.11 = (bf16[256,1024]{1,0:T(8,128)(2,1)S(1)}, bf16[256,1024]{1,0:T(8,128)(2,1)S(1)}, u32[]{:S(2)}, u32[]{:S(2)}) collective-permute-start(bf16[256,1024]{1,0:T(8,128)(2,1)S(1)} %collective-permute-done.10.up_ref), channel_id=1, source_target_pairs={{0,16},{16,0},{32,48},{48,32},{64,80},{80,64},{96,112},{112,96},{1... | collective-permute-start | bytes 1572872 | tf_op jit(solution)/shard_map/ppermute | solution.py:232
  86.9 0.0 collective-permute-done.12.down_ref
  86.9 0.0 collective-permute-start.13
  86.9 1.4 %shard_map.79.acc_ref = f32[384,1024]{1,0:T(8,128)S(1)} custom-call(bf16[384,3072]{1,0:T(8,128)(2,1)S(1)} %get-tuple-element.51.refs_1_.own_ref.rows_ref, bf16[256,1024]{1,0:T(8,128)(2,1)S(1)} %collective-permute-done.10.up_ref, bf16[256,1024]{1,0:T(8,128)(2,1)S(1)} %collective-permute-done.12.down_ref, f32[384,1024]{1,0:T(8,128)S(1)} %get-tuple-element.60.acc_ref), custom_call_target="tpu_custom_call" | custom-call | tf_op jit(solution)/shard_map/pallas_call | solution.py:198
  88.4 0.1 collective-permute-done.11.up_ref
  88.4 0.7 collective-permute-done.13.down_ref
  89.2 0.0 collective-permute-done.17.passed_ref
  89.2 1.5 %shard_map.80 = bf16[384,1024]{1,0:T(8,128)(2,1)S(1)} custom-call(bf16[384,3072]{1,0:T(8,128)(2,1)S(1)} %get-tuple-element.51.refs_1_.own_ref.rows_ref, bf16[256,1024]{1,0:T(8,128)(2,1)S(1)} %collective-permute-done.11.up_ref, bf16[256,1024]{1,0:T(8,128)(2,1)S(1)} %collective-permute-done.13.down_ref, f32[384,1024]{1,0:T(8,128)S(1)} %shard_map.79.acc_ref, ...), custom_call_target="tpu_custom_call" | custom-call | tf_op jit(solution)/shard_map/pallas_call | solution.py:198
  90.7 20.4 %all_to_all.10 = bf16[16,24,1024]{2,1,0:T(8,128)(2,1)S(1)} all-to-all(bf16[16,24,1024]{2,1,0:T(8,128)(2,1)S(1)} %bitcast.10), channel_id=1, replica_groups=mesh['dp'=16,'expert'=16] {'expert'}, dimensions={0} | all-to-all | bytes 1572864 | tf_op jit(solution)/shard_map/all_to_all | solution.py:261
  111.0 1.1 %fusion = f32[128,1024]{1,0:T(8,128)} fusion(bf16[384,128]{1,0:T(8,128)(2,1)S(1)} %get-tuple-element.35, bf16[384,1024]{1,0:T(8,128)(2,1)S(1)} %bitcast.17), kind=kOutput, calls=%fused_computation | convolution fusion | flops 100663296 | bytes 1409024 | tf_op jit(solution)/shard_map/dot_general | solution.py:263
  (4 shorter events, 0.0 us)
Async XLA Ops:
  0.0 19.0 %collective-permute-start = (bf16[256,1024]{1,0:T(8,128)(2,1)}, bf16[256,1024]{1,0:T(8,128)(2,1)S(1)}, u32[]{:S(2)}, u32[]{:S(2)}) collective-permute-start(bf16[256,1024]{1,0:T(8,128)(2,1)} %bitcast.11), channel_id=1, source_target_pairs={{0,32},{16,48},{32,64},{48,80},{64,96},{80,112},{96,128},{112,144}... | collective-permute-start | bytes 1572872 | tf_op jit(solution)/shard_map/ppermute | solution.py:232
  2.5 16.6 %collective-permute-start.1 = (bf16[256,1024]{1,0:T(8,128)(2,1)}, bf16[256,1024]{1,0:T(8,128)(2,1)}, u32[]{:S(2)}, u32[]{:S(2)}) collective-permute-start(bf16[256,1024]{1,0:T(8,128)(2,1)} %bitcast.14), channel_id=1, source_target_pairs={{0,224},{16,240},{32,0},{48,16},{64,32},{80,48},{96,64},{112,80},{... | collective-permute-start | bytes 1572872 | tf_op jit(solution)/shard_map/ppermute | solution.py:232
  6.4 23.2 %collective-permute-start.4 = (bf16[256,1024]{1,0:T(8,128)(2,1)}, bf16[256,1024]{1,0:T(8,128)(2,1)}, u32[]{:S(2)}, u32[]{:S(2)}) collective-permute-start(bf16[256,1024]{1,0:T(8,128)(2,1)} %bitcast.15), channel_id=1, source_target_pairs={{0,32},{16,48},{32,64},{48,80},{64,96},{80,112},{96,128},{112,144}... | collective-permute-start | bytes 1572872 | tf_op jit(solution)/shard_map/ppermute | solution.py:232
  6.4 23.2 %collective-permute-start.5 = (bf16[256,1024]{1,0:T(8,128)(2,1)}, bf16[256,1024]{1,0:T(8,128)(2,1)}, u32[]{:S(2)}, u32[]{:S(2)}) collective-permute-start(bf16[256,1024]{1,0:T(8,128)(2,1)} %bitcast.12), channel_id=1, source_target_pairs={{0,224},{16,240},{32,0},{48,16},{64,32},{80,48},{96,64},{112,80},{... | collective-permute-start | bytes 1572872 | tf_op jit(solution)/shard_map/ppermute | solution.py:232
  12.2 42.2 %all-to-all-start = ((bf16[16,24,3072]{2,1,0:T(8,128)(2,1)}), bf16[16,24,3072]{2,1,0:T(8,128)(2,1)}, u32[]{:S(2)}, u32[]{:S(2)}) async-start(bf16[16,24,3072]{2,1,0:T(8,128)(2,1)} %bitcast.2), calls=%async_computation | async-start | bytes 4718592 | tf_op jit(solution)/shard_map/all_to_all | solution.py:238
  19.1 38.4 %copy-start = (bf16[1,256,1024]{2,1,0:T(8,128)(2,1)S(1)}, bf16[1,256,1024]{2,1,0:T(8,128)(2,1)}, u32[]{:S(2)}) copy-start(bf16[1,256,1024]{2,1,0:T(8,128)(2,1)} %param.12) | copy-start | bytes 1572868
  19.1 38.4 %copy-start.1 = (bf16[1,256,1024]{2,1,0:T(8,128)(2,1)S(1)}, bf16[1,256,1024]{2,1,0:T(8,128)(2,1)}, u32[]{:S(2)}) copy-start(bf16[1,256,1024]{2,1,0:T(8,128)(2,1)} %param.13) | copy-start | bytes 1572868
  19.1 21.7 %collective-permute-start.2 = (bf16[256,1024]{1,0:T(8,128)(2,1)S(1)}, bf16[256,1024]{1,0:T(8,128)(2,1)S(1)}, u32[]{:S(2)}, u32[]{:S(2)}) collective-permute-start(bf16[256,1024]{1,0:T(8,128)(2,1)S(1)} %collective-permute-done.refs_0_.refs_1_), channel_id=1, source_target_pairs={{0,32},{16,48},{32,64},{48,80},{64,96},{80,112},{96,128},{112,144}... | collective-permute-start | bytes 1572872 | tf_op jit(solution)/shard_map/ppermute | solution.py:232
  19.2 21.7 %collective-permute-start.3 = (bf16[256,1024]{1,0:T(8,128)(2,1)}, bf16[256,1024]{1,0:T(8,128)(2,1)}, u32[]{:S(2)}, u32[]{:S(2)}) collective-permute-start(bf16[256,1024]{1,0:T(8,128)(2,1)} %collective-permute-done.1.refs_7_), channel_id=1, source_target_pairs={{0,224},{16,240},{32,0},{48,16},{64,32},{80,48},{96,64},{112,80},{... | collective-permute-start | bytes 1572872 | tf_op jit(solution)/shard_map/ppermute | solution.py:232
  29.6 22.5 %collective-permute-start.6 = (bf16[256,1024]{1,0:T(8,128)(2,1)}, bf16[256,1024]{1,0:T(8,128)(2,1)}, u32[]{:S(2)}, u32[]{:S(2)}) collective-permute-start(bf16[256,1024]{1,0:T(8,128)(2,1)} %collective-permute-done.4.refs_6_), channel_id=1, source_target_pairs={{0,32},{16,48},{32,64},{48,80},{64,96},{80,112},{96,128},{112,144}... | collective-permute-start | bytes 1572872 | tf_op jit(solution)/shard_map/ppermute | solution.py:232
  29.6 22.5 %collective-permute-start.7 = (bf16[256,1024]{1,0:T(8,128)(2,1)}, bf16[256,1024]{1,0:T(8,128)(2,1)}, u32[]{:S(2)}, u32[]{:S(2)}) collective-permute-start(bf16[256,1024]{1,0:T(8,128)(2,1)} %collective-permute-done.5.refs_2_), channel_id=1, source_target_pairs={{0,224},{16,240},{32,0},{48,16},{64,32},{80,48},{96,64},{112,80},{... | collective-permute-start | bytes 1572872 | tf_op jit(solution)/shard_map/ppermute | solution.py:232
  40.8 24.4 %collective-permute-start.8 = (bf16[256,1024]{1,0:T(8,128)(2,1)S(1)}, bf16[256,1024]{1,0:T(8,128)(2,1)S(1)}, u32[]{:S(2)}, u32[]{:S(2)}) collective-permute-start(bf16[256,1024]{1,0:T(8,128)(2,1)S(1)} %collective-permute-done.2.refs_3_), channel_id=1, source_target_pairs={{0,32},{16,48},{32,64},{48,80},{64,96},{80,112},{96,128},{112,144}... | collective-permute-start | bytes 1572872 | tf_op jit(solution)/shard_map/ppermute | solution.py:232
  40.8 24.4 %collective-permute-start.9 = (bf16[256,1024]{1,0:T(8,128)(2,1)}, bf16[256,1024]{1,0:T(8,128)(2,1)}, u32[]{:S(2)}, u32[]{:S(2)}) collective-permute-start(bf16[256,1024]{1,0:T(8,128)(2,1)} %collective-permute-done.3.refs_9_), channel_id=1, source_target_pairs={{0,224},{16,240},{32,0},{48,16},{64,32},{80,48},{96,64},{112,80},{... | collective-permute-start | bytes 1572872 | tf_op jit(solution)/shard_map/ppermute | solution.py:232
  52.1 22.8 %collective-permute-start.15 = (bf16[256,1024]{1,0:T(8,128)(2,1)}, bf16[256,1024]{1,0:T(8,128)(2,1)}, u32[]{:S(2)}, u32[]{:S(2)}) collective-permute-start(bf16[256,1024]{1,0:T(8,128)(2,1)} %collective-permute-done.7.refs_4_), channel_id=1, source_target_pairs={{0,224},{16,240},{32,0},{48,16},{64,32},{80,48},{96,64},{112,80},{... | collective-permute-start | bytes 1572872 | tf_op jit(solution)/shard_map/ppermute | solution.py:232
  54.4 20.4 %collective-permute-start.16 = (bf16[256,1024]{1,0:T(8,128)(2,1)}, bf16[256,1024]{1,0:T(8,128)(2,1)}, u32[]{:S(2)}, u32[]{:S(2)}) collective-permute-start(bf16[256,1024]{1,0:T(8,128)(2,1)} %collective-permute-done.6.refs_8_), channel_id=1, source_target_pairs={{0,32},{16,48},{32,64},{48,80},{64,96},{80,112},{96,128},{112,144}... | collective-permute-start | bytes 1572872 | tf_op jit(solution)/shard_map/ppermute | solution.py:232
  54.4 13.9 %collective-permute-start.14 = (bf16[384,3072]{1,0:T(8,128)(2,1)}, bf16[384,3072]{1,0:T(8,128)(2,1)}, u32[]{:S(2)}, u32[]{:S(2)}) collective-permute-start(bf16[384,3072]{1,0:T(8,128)(2,1)} %bitcast.3.own_ref), channel_id=1, source_target_pairs={{0,16},{16,0},{32,48},{48,32},{64,80},{80,64},{96,112},{112,96},{1... | collective-permute-start | bytes 7077896 | tf_op jit(solution)/shard_map/ppermute | solution.py:253
  65.3 20.4 %collective-permute-start.10 = (bf16[256,1024]{1,0:T(8,128)(2,1)S(1)}, bf16[256,1024]{1,0:T(8,128)(2,1)S(1)}, u32[]{:S(2)}, u32[]{:S(2)}) collective-permute-start(bf16[256,1024]{1,0:T(8,128)(2,1)S(1)} %collective-permute-done.8.refs_0_), channel_id=1, source_target_pairs={{0,32},{16,48},{32,64},{48,80},{64,96},{80,112},{96,128},{112,144}... | collective-permute-start | bytes 1572872 | tf_op jit(solution)/shard_map/ppermute | solution.py:232
  65.4 21.5 %collective-permute-start.12 = (bf16[256,1024]{1,0:T(8,128)(2,1)}, bf16[256,1024]{1,0:T(8,128)(2,1)S(1)}, u32[]{:S(2)}, u32[]{:S(2)}) collective-permute-start(bf16[256,1024]{1,0:T(8,128)(2,1)} %collective-permute-done.9.refs_3_), channel_id=1, source_target_pairs={{0,224},{16,240},{32,0},{48,16},{64,32},{80,48},{96,64},{112,80},{... | collective-permute-start | bytes 1572872 | tf_op jit(solution)/shard_map/ppermute | solution.py:232
  79.9 9.3 %collective-permute-start.17 = (bf16[384,1024]{1,0:T(8,128)(2,1)S(1)}, bf16[384,1024]{1,0:T(8,128)(2,1)S(1)}, u32[]{:S(2)}, u32[]{:S(2)}) collective-permute-start(bf16[384,1024]{1,0:T(8,128)(2,1)S(1)} %get-tuple-element.64), channel_id=1, source_target_pairs={{0,16},{16,0},{32,48},{48,32},{64,80},{80,64},{96,112},{112,96},{1... | collective-permute-start | bytes 2359304 | tf_op jit(solution)/shard_map/ppermute | solution.py:232
  85.7 2.8 %collective-permute-start.11 = (bf16[256,1024]{1,0:T(8,128)(2,1)S(1)}, bf16[256,1024]{1,0:T(8,128)(2,1)S(1)}, u32[]{:S(2)}, u32[]{:S(2)}) collective-permute-start(bf16[256,1024]{1,0:T(8,128)(2,1)S(1)} %collective-permute-done.10.up_ref), channel_id=1, source_target_pairs={{0,16},{16,0},{32,48},{48,32},{64,80},{80,64},{96,112},{112,96},{1... | collective-permute-start | bytes 1572872 | tf_op jit(solution)/shard_map/ppermute | solution.py:232
  86.9 2.3 %collective-permute-start.13 = (bf16[256,1024]{1,0:T(8,128)(2,1)S(1)}, bf16[256,1024]{1,0:T(8,128)(2,1)S(1)}, u32[]{:S(2)}, u32[]{:S(2)}) collective-permute-start(bf16[256,1024]{1,0:T(8,128)(2,1)S(1)} %collective-permute-done.12.down_ref), channel_id=1, source_target_pairs={{0,16},{16,0},{32,48},{48,32},{64,80},{80,64},{96,112},{112,96},{1... | collective-permute-start | bytes 1572872 | tf_op jit(solution)/shard_map/ppermute | solution.py:232

commit v11 on v8

--- a/solution.py
+++ b/solution.py
@@ -212,6 +212,23 @@
         out_specs=VMEM,
         compiler_params=params(12),
     )(*operands)
+
+
+def mix_kernel(mix_ref, returned_ref, out_ref):
+    contract = (((0,), (0,)), ((), ()))
+    out_ref[...] = lax.dot_general(mix_ref[...], returned_ref[...], contract, preferred_element_type=f32)
+
+
+def mix_call(mix, returned):
+    slots, n = mix.shape
+    width = returned.shape[1]
+    return pl.pallas_call(
+        mix_kernel,
+        out_shape=jax.ShapeDtypeStruct((n, width), f32),
+        in_specs=[VMEM, VMEM],
+        out_specs=VMEM,
+        compiler_params=params(8),
+    )(*(pltpu.with_memory_space_constraint(x, pltpu.VMEM) for x in (mix, returned)))
 
 
 def hold_kernel(*refs):
@@ -271,7 +288,7 @@
     whole = last_call(last_far_kernel, mine.shape, bf16, kept_own, factor, far_up, far_down, part, passed)
     returned = lax.all_to_all(whole.reshape(experts, CAP, width), "expert", 0, 0, tiled=True)
     returned = returned.reshape(experts * CAP, width)
-    return lax.dot_general(mix, returned, (((0,), (0,)), ((), ())), preferred_element_type=f32)
+    return mix_call(mix, returned)
 
 
 def solution(mesh):

time: 112 us -> 112 us (level)
  Pallas kernels: 25.5 us -> 26.7 us
  matrix products: 1.12 us -> 0 us
    dot_general x1 -> x0, matrix products: 1.12 us -> none  [local(): lax.dot_general(mix, returned, (((0,), (0,)), ((), ())), preferred_elemen...]
where the time goes in v11:
time: 112 us
  starting transfers between devices  35.5 us (32%)
  waiting for transfers between devices  29 us (26%)
  Pallas kernels  26.7 us (24%)
  blocking collectives  20.4 us (18%)
    ppermute x17, waiting for transfers between devices, send_on(): return lax.ppermute(x, 'dp', way)  29 us
    ppermute x17, starting transfers between devices, send_on(): return lax.ppermute(x, 'dp', way)  25.7 us
    all_to_all x1, blocking collectives, local(): lax.all_to_all(whole.reshape(experts, CAP, width), 'expert', 0, 0, tiled=...  20.4 us
    pallas_call x1, Pallas kernels, own_call(): pl.pallas_call(functools.partial(own_kernel, n_w), out_shape=(jax.ShapeDt...  7.81 us
    all_to_all x1, starting transfers between devices, local(): lax.all_to_all(send.reshape(experts, CAP, 3 * width), 'expert', 0, 0, til...  6.81 us
    pallas_call x1, Pallas kernels, other_call(): pl.pallas_call(other_kernel, out_shape=(jax.ShapeDtypeStruct((rows, width...  6.47 us
    pallas_call x1, Pallas kernels, next_call(): pl.pallas_call(functools.partial(next_kernel, n_w), out_shape=tuple((jax....  5.02 us
    pallas_call x1, Pallas kernels, prepare(): pl.pallas_call(prepare_kernel, out_shape=(jax.ShapeDtypeStruct((slots, 3...  3.13 us
  transfers between devices with their start and end apart: 19, of which 6 were waited for; matrix products, arithmetic and copies ran while one was open for 0% of the time, Pallas kernels for 22%

profile of v11, /device:TPU:1, one launch (start us, length us, event | category | flops | bytes accessed | tf_op | source)
XLA Modules:
  0.0 111.7 jit_solution(15101453659438884630)
XLA Ops:
  0.0 2.5 %collective-permute-start = (bf16[256,1024]{1,0:T(8,128)(2,1)}, bf16[256,1024]{1,0:T(8,128)(2,1)S(1)}, u32[]{:S(2)}, u32[]{:S(2)}) collective-permute-start(bf16[256,1024]{1,0:T(8,128)(2,1)} %bitcast.10), channel_id=1, source_target_pairs={{0,32},{16,48},{32,64},{48,80},{64,96},{80,112},{96,128},{112,144}... | collective-permute-start | bytes 1572872 | tf_op jit(solution)/shard_map/ppermute | solution.py:259
  2.5 3.9 %collective-permute-start.1 = (bf16[256,1024]{1,0:T(8,128)(2,1)}, bf16[256,1024]{1,0:T(8,128)(2,1)}, u32[]{:S(2)}, u32[]{:S(2)}) collective-permute-start(bf16[256,1024]{1,0:T(8,128)(2,1)} %bitcast.13), channel_id=1, source_target_pairs={{0,224},{16,240},{32,0},{48,16},{64,32},{80,48},{96,64},{112,80},{... | collective-permute-start | bytes 1572872 | tf_op jit(solution)/shard_map/ppermute | solution.py:259
  6.4 0.0 collective-permute-start.4
  6.4 2.7 %collective-permute-start.5 = (bf16[256,1024]{1,0:T(8,128)(2,1)}, bf16[256,1024]{1,0:T(8,128)(2,1)}, u32[]{:S(2)}, u32[]{:S(2)}) collective-permute-start(bf16[256,1024]{1,0:T(8,128)(2,1)} %bitcast.11), channel_id=1, source_target_pairs={{0,224},{16,240},{32,0},{48,16},{64,32},{80,48},{96,64},{112,80},{... | collective-permute-start | bytes 1572872 | tf_op jit(solution)/shard_map/ppermute | solution.py:259
  9.1 3.1 %shard_map.73 = (bf16[384,3072]{1,0:T(8,128)(2,1)}, bf16[384,128]{1,0:T(8,128)(2,1)S(1)}) custom-call(s32[2,128]{1,0:T(2,128)} %bitcast.16, s32[2,128]{1,0:T(2,128)} %bitcast.17, bf16[128,1024]{1,0:T(8,128)(2,1)} %x_hbm.1, bf16[128,1024]{1,0:T(8,128)(2,1)} %t_hbm.1, bf16[128,1024]{1,0:T(8,128)(2,1)} %c_hbm.1), custom_call_target="tpu_custom_call" | custom-call | tf_op jit(solution)/shard_map/pallas_call | solution.py:61
  12.2 6.8 %all-to-all-start = ((bf16[16,24,3072]{2,1,0:T(8,128)(2,1)}), bf16[16,24,3072]{2,1,0:T(8,128)(2,1)}, u32[]{:S(2)}, u32[]{:S(2)}) async-start(bf16[16,24,3072]{2,1,0:T(8,128)(2,1)} %bitcast.2), calls=%async_computation | async-start | bytes 4718592 | tf_op jit(solution)/shard_map/all_to_all | solution.py:265
  19.0 0.0 collective-permute-done.refs_0_.refs_1_
  19.1 0.0 copy-start
  19.1 0.0 copy-start.1
  19.1 0.0 collective-permute-done.1.refs_7_
  19.1 0.1 collective-permute-start.2
  19.2 2.7 %collective-permute-start.3 = (bf16[256,1024]{1,0:T(8,128)(2,1)}, bf16[256,1024]{1,0:T(8,128)(2,1)}, u32[]{:S(2)}, u32[]{:S(2)}) collective-permute-start(bf16[256,1024]{1,0:T(8,128)(2,1)} %collective-permute-done.1.refs_7_), channel_id=1, source_target_pairs={{0,224},{16,240},{32,0},{48,16},{64,32},{80,48},{96,64},{112,80},{... | collective-permute-start | bytes 1572872 | tf_op jit(solution)/shard_map/ppermute | solution.py:259
  21.9 7.8 %collective-permute-done.4.refs_6_ = bf16[256,1024]{1,0:T(8,128)(2,1)} collective-permute-done((bf16[256,1024]{1,0:T(8,128)(2,1)}, bf16[256,1024]{1,0:T(8,128)(2,1)}, u32[]{:S(2)}, u32[]{:S(2)}) %collective-permute-start.4) | collective-permute-done | bytes 524320 | tf_op jit(solution)/shard_map/ppermute | solution.py:259
  29.6 0.0 collective-permute-done.5.refs_2_
  29.6 0.0 collective-permute-start.6
  29.6 2.7 %collective-permute-start.7 = (bf16[256,1024]{1,0:T(8,128)(2,1)}, bf16[256,1024]{1,0:T(8,128)(2,1)}, u32[]{:S(2)}, u32[]{:S(2)}) collective-permute-start(bf16[256,1024]{1,0:T(8,128)(2,1)} %collective-permute-done.5.refs_2_), channel_id=1, source_target_pairs={{0,224},{16,240},{32,0},{48,16},{64,32},{80,48},{96,64},{112,80},{... | collective-permute-start | bytes 1572872 | tf_op jit(solution)/shard_map/ppermute | solution.py:259
  32.3 8.6 %collective-permute-done.2.refs_3_ = bf16[256,1024]{1,0:T(8,128)(2,1)S(1)} collective-permute-done((bf16[256,1024]{1,0:T(8,128)(2,1)S(1)}, bf16[256,1024]{1,0:T(8,128)(2,1)S(1)}, u32[]{:S(2)}, u32[]{:S(2)}) %collective-permute-start.2) | collective-permute-done | bytes 524320 | tf_op jit(solution)/shard_map/ppermute | solution.py:259
  40.8 0.0 collective-permute-done.3.refs_9_
  40.8 0.0 collective-permute-start.8
  40.8 2.7 %collective-permute-start.9 = (bf16[256,1024]{1,0:T(8,128)(2,1)}, bf16[256,1024]{1,0:T(8,128)(2,1)}, u32[]{:S(2)}, u32[]{:S(2)}) collective-permute-start(bf16[256,1024]{1,0:T(8,128)(2,1)} %collective-permute-done.3.refs_9_), channel_id=1, source_target_pairs={{0,224},{16,240},{32,0},{48,16},{64,32},{80,48},{96,64},{112,80},{... | collective-permute-start | bytes 1572872 | tf_op jit(solution)/shard_map/ppermute | solution.py:259
  43.5 8.6 %collective-permute-done.6.refs_8_ = bf16[256,1024]{1,0:T(8,128)(2,1)} collective-permute-done((bf16[256,1024]{1,0:T(8,128)(2,1)}, bf16[256,1024]{1,0:T(8,128)(2,1)}, u32[]{:S(2)}, u32[]{:S(2)}) %collective-permute-start.6) | collective-permute-done | bytes 524320 | tf_op jit(solution)/shard_map/ppermute | solution.py:259
  52.1 0.0 collective-permute-done.7.refs_4_
  52.1 2.4 %collective-permute-start.14 = (bf16[256,1024]{1,0:T(8,128)(2,1)}, bf16[256,1024]{1,0:T(8,128)(2,1)}, u32[]{:S(2)}, u32[]{:S(2)}) collective-permute-start(bf16[256,1024]{1,0:T(8,128)(2,1)} %collective-permute-done.7.refs_4_), channel_id=1, source_target_pairs={{0,224},{16,240},{32,0},{48,16},{64,32},{80,48},{96,64},{112,80},{... | collective-permute-start | bytes 1572872 | tf_op jit(solution)/shard_map/ppermute | solution.py:259
  54.4 0.0 collective-permute-start.15
  54.4 0.0 all-to-all-done
  54.4 3.0 %collective-permute-start.13 = (bf16[384,3072]{1,0:T(8,128)(2,1)}, bf16[384,3072]{1,0:T(8,128)(2,1)}, u32[]{:S(2)}, u32[]{:S(2)}) collective-permute-start(bf16[384,3072]{1,0:T(8,128)(2,1)} %bitcast.3.own_ref), channel_id=1, source_target_pairs={{0,16},{16,0},{32,48},{48,32},{64,80},{80,64},{96,112},{112,96},{1... | collective-permute-start | bytes 7077896 | tf_op jit(solution)/shard_map/ppermute | solution.py:280
  57.4 7.8 %shard_map.75 = (f32[384,1024]{1,0:T(8,128)S(1)}, bf16[384,3072]{1,0:T(8,128)(2,1)S(1)}, bf16[5,256,1024]{2,1,0:T(8,128)(2,1)S(1)}, bf16[5,256,1024]{2,1,0:T(8,128)(2,1)S(1)}) custom-call(bf16[384,3072]{1,0:T(8,128)(2,1)} %bitcast.3.own_ref, bf16[256,1024]{1,0:T(8,128)(2,1)S(1)} %bitcast.12, bf16[256,1024]{1,0:T(8,128)(2,1)S(1)} %collective-permute-done.refs_0_.refs_1_, ...), custom_call_target="tpu_custom_call" | custom-call | tf_op jit(solution)/shard_map/pallas_call | solution.py:122
  65.2 0.0 collective-permute-done.8.refs_0_
  65.3 0.0 collective-permute-done.9.refs_3_
  65.3 0.1 collective-permute-start.10
  65.4 3.0 %collective-permute-start.12 = (bf16[256,1024]{1,0:T(8,128)(2,1)}, bf16[256,1024]{1,0:T(8,128)(2,1)S(1)}, u32[]{:S(2)}, u32[]{:S(2)}) collective-permute-start(bf16[256,1024]{1,0:T(8,128)(2,1)} %collective-permute-done.9.refs_3_), channel_id=1, source_target_pairs={{0,224},{16,240},{32,0},{48,16},{64,32},{80,48},{96,64},{112,80},{... | collective-permute-start | bytes 1572872 | tf_op jit(solution)/shard_map/ppermute | solution.py:259
  68.4 0.0 collective-permute-done.13.other_ref
  68.4 6.5 %shard_map.77 = (f32[384,1024]{1,0:T(8,128)S(1)}, bf16[384,3072]{1,0:T(8,128)(2,1)S(1)}) custom-call(bf16[384,3072]{1,0:T(8,128)(2,1)} %collective-permute-done.13.other_ref, bf16[5,256,1024]{2,1,0:T(8,128)(2,1)S(1)} %get-tuple-element.53.up_ref, bf16[5,256,1024]{2,1,0:T(8,128)(2,1)S(1)} %get-tuple-element.54.down_ref), custom_call_target="tpu_custom_call" | custom-call | tf_op jit(solution)/shard_map/pallas_call | solution.py:143
  74.9 0.0 collective-permute-done.14.refs_1_
  74.9 0.0 collective-permute-done.15.refs_2_
  74.9 5.0 %shard_map.78 = (f32[384,1024]{1,0:T(8,128)S(1)}, bf16[384,1024]{1,0:T(8,128)(2,1)S(1)}) custom-call(bf16[384,3072]{1,0:T(8,128)(2,1)S(1)} %get-tuple-element.50.refs_1_.own_ref.rows_ref, bf16[384,3072]{1,0:T(8,128)(2,1)S(1)} %get-tuple-element.55.other_ref, bf16[256,1024]{1,0:T(8,128)(2,1)S(1)} %collective-permute-done.8.refs_0_, ...), custom_call_target="tpu_custom_call" | custom-call | tf_op jit(solution)/shard_map/pallas_call | solution.py:173
  79.9 1.8 %collective-permute-start.17 = (bf16[384,1024]{1,0:T(8,128)(2,1)S(1)}, bf16[384,1024]{1,0:T(8,128)(2,1)S(1)}, u32[]{:S(2)}, u32[]{:S(2)}) collective-permute-start(bf16[384,1024]{1,0:T(8,128)(2,1)S(1)} %get-tuple-element.62), channel_id=1, source_target_pairs={{0,16},{16,0},{32,48},{48,32},{64,80},{80,64},{96,112},{112,96},{1... | collective-permute-start | bytes 2359304 | tf_op jit(solution)/shard_map/ppermute | solution.py:259
  81.7 4.0 %collective-permute-done.10.up_ref = bf16[256,1024]{1,0:T(8,128)(2,1)S(1)} collective-permute-done((bf16[256,1024]{1,0:T(8,128)(2,1)S(1)}, bf16[256,1024]{1,0:T(8,128)(2,1)S(1)}, u32[]{:S(2)}, u32[]{:S(2)}) %collective-permute-start.10) | collective-permute-done | bytes 524320 | tf_op jit(solution)/shard_map/ppermute | solution.py:259
  85.7 1.2 %collective-permute-start.11 = (bf16[256,1024]{1,0:T(8,128)(2,1)S(1)}, bf16[256,1024]{1,0:T(8,128)(2,1)S(1)}, u32[]{:S(2)}, u32[]{:S(2)}) collective-permute-start(bf16[256,1024]{1,0:T(8,128)(2,1)S(1)} %collective-permute-done.10.up_ref), channel_id=1, source_target_pairs={{0,16},{16,0},{32,48},{48,32},{64,80},{80,64},{96,112},{112,96},{1... | collective-permute-start | bytes 1572872 | tf_op jit(solution)/shard_map/ppermute | solution.py:259
  86.9 0.0 collective-permute-start.16
  86.9 1.4 %shard_map.79.acc_ref = f32[384,1024]{1,0:T(8,128)S(1)} custom-call(bf16[384,3072]{1,0:T(8,128)(2,1)S(1)} %get-tuple-element.50.refs_1_.own_ref.rows_ref, bf16[256,1024]{1,0:T(8,128)(2,1)S(1)} %collective-permute-done.10.up_ref, bf16[256,1024]{1,0:T(8,128)(2,1)S(1)} %collective-permute-done.12.down_ref, f32[384,1024]{1,0:T(8,128)S(1)} %get-tuple-element.59.acc_ref), custom_call_target="tpu_custom_call" | custom-call | tf_op jit(solution)/shard_map/pallas_call | solution.py:208
  88.4 0.1 collective-permute-done.11.up_ref
  88.4 0.6 shard_map.80.factor_ref
  89.1 0.1 collective-permute-done.16.down_ref
  89.2 0.0 collective-permute-done.17.passed_ref
  89.2 1.0 shard_map.81
  90.2 20.4 %all_to_all.10 = bf16[16,24,1024]{2,1,0:T(8,128)(2,1)S(1)} all-to-all(bf16[16,24,1024]{2,1,0:T(8,128)(2,1)S(1)} %bitcast.9), channel_id=1, replica_groups=mesh['dp'=16,'expert'=16] {'expert'}, dimensions={0} | all-to-all | bytes 1572864 | tf_op jit(solution)/shard_map/all_to_all | solution.py:289
  110.6 1.1 shard_map.82
  (5 shorter events, 0.0 us)
Async XLA Ops:
  0.0 19.0 %collective-permute-start = (bf16[256,1024]{1,0:T(8,128)(2,1)}, bf16[256,1024]{1,0:T(8,128)(2,1)S(1)}, u32[]{:S(2)}, u32[]{:S(2)}) collective-permute-start(bf16[256,1024]{1,0:T(8,128)(2,1)} %bitcast.10), channel_id=1, source_target_pairs={{0,32},{16,48},{32,64},{48,80},{64,96},{80,112},{96,128},{112,144}... | collective-permute-start | bytes 1572872 | tf_op jit(solution)/shard_map/ppermute | solution.py:259
  2.5 16.6 %collective-permute-start.1 = (bf16[256,1024]{1,0:T(8,128)(2,1)}, bf16[256,1024]{1,0:T(8,128)(2,1)}, u32[]{:S(2)}, u32[]{:S(2)}) collective-permute-start(bf16[256,1024]{1,0:T(8,128)(2,1)} %bitcast.13), channel_id=1, source_target_pairs={{0,224},{16,240},{32,0},{48,16},{64,32},{80,48},{96,64},{112,80},{... | collective-permute-start | bytes 1572872 | tf_op jit(solution)/shard_map/ppermute | solution.py:259
  6.4 23.2 %collective-permute-start.4 = (bf16[256,1024]{1,0:T(8,128)(2,1)}, bf16[256,1024]{1,0:T(8,128)(2,1)}, u32[]{:S(2)}, u32[]{:S(2)}) collective-permute-start(bf16[256,1024]{1,0:T(8,128)(2,1)} %bitcast.14), channel_id=1, source_target_pairs={{0,32},{16,48},{32,64},{48,80},{64,96},{80,112},{96,128},{112,144}... | collective-permute-start | bytes 1572872 | tf_op jit(solution)/shard_map/ppermute | solution.py:259
  6.4 23.2 %collective-permute-start.5 = (bf16[256,1024]{1,0:T(8,128)(2,1)}, bf16[256,1024]{1,0:T(8,128)(2,1)}, u32[]{:S(2)}, u32[]{:S(2)}) collective-permute-start(bf16[256,1024]{1,0:T(8,128)(2,1)} %bitcast.11), channel_id=1, source_target_pairs={{0,224},{16,240},{32,0},{48,16},{64,32},{80,48},{96,64},{112,80},{... | collective-permute-start | bytes 1572872 | tf_op jit(solution)/shard_map/ppermute | solution.py:259
  12.2 42.2 %all-to-all-start = ((bf16[16,24,3072]{2,1,0:T(8,128)(2,1)}), bf16[16,24,3072]{2,1,0:T(8,128)(2,1)}, u32[]{:S(2)}, u32[]{:S(2)}) async-start(bf16[16,24,3072]{2,1,0:T(8,128)(2,1)} %bitcast.2), calls=%async_computation | async-start | bytes 4718592 | tf_op jit(solution)/shard_map/all_to_all | solution.py:265
  19.1 38.4 %copy-start = (bf16[1,256,1024]{2,1,0:T(8,128)(2,1)S(1)}, bf16[1,256,1024]{2,1,0:T(8,128)(2,1)}, u32[]{:S(2)}) copy-start(bf16[1,256,1024]{2,1,0:T(8,128)(2,1)} %param.12) | copy-start | bytes 1572868
  19.1 38.4 %copy-start.1 = (bf16[1,256,1024]{2,1,0:T(8,128)(2,1)S(1)}, bf16[1,256,1024]{2,1,0:T(8,128)(2,1)}, u32[]{:S(2)}) copy-start(bf16[1,256,1024]{2,1,0:T(8,128)(2,1)} %param.13) | copy-start | bytes 1572868
  19.1 21.7 %collective-permute-start.2 = (bf16[256,1024]{1,0:T(8,128)(2,1)S(1)}, bf16[256,1024]{1,0:T(8,128)(2,1)S(1)}, u32[]{:S(2)}, u32[]{:S(2)}) collective-permute-start(bf16[256,1024]{1,0:T(8,128)(2,1)S(1)} %collective-permute-done.refs_0_.refs_1_), channel_id=1, source_target_pairs={{0,32},{16,48},{32,64},{48,80},{64,96},{80,112},{96,128},{112,144}... | collective-permute-start | bytes 1572872 | tf_op jit(solution)/shard_map/ppermute | solution.py:259
  19.2 21.7 %collective-permute-start.3 = (bf16[256,1024]{1,0:T(8,128)(2,1)}, bf16[256,1024]{1,0:T(8,128)(2,1)}, u32[]{:S(2)}, u32[]{:S(2)}) collective-permute-start(bf16[256,1024]{1,0:T(8,128)(2,1)} %collective-permute-done.1.refs_7_), channel_id=1, source_target_pairs={{0,224},{16,240},{32,0},{48,16},{64,32},{80,48},{96,64},{112,80},{... | collective-permute-start | bytes 1572872 | tf_op jit(solution)/shard_map/ppermute | solution.py:259
  29.6 22.5 %collective-permute-start.6 = (bf16[256,1024]{1,0:T(8,128)(2,1)}, bf16[256,1024]{1,0:T(8,128)(2,1)}, u32[]{:S(2)}, u32[]{:S(2)}) collective-permute-start(bf16[256,1024]{1,0:T(8,128)(2,1)} %collective-permute-done.4.refs_6_), channel_id=1, source_target_pairs={{0,32},{16,48},{32,64},{48,80},{64,96},{80,112},{96,128},{112,144}... | collective-permute-start | bytes 1572872 | tf_op jit(solution)/shard_map/ppermute | solution.py:259
  29.6 22.5 %collective-permute-start.7 = (bf16[256,1024]{1,0:T(8,128)(2,1)}, bf16[256,1024]{1,0:T(8,128)(2,1)}, u32[]{:S(2)}, u32[]{:S(2)}) collective-permute-start(bf16[256,1024]{1,0:T(8,128)(2,1)} %collective-permute-done.5.refs_2_), channel_id=1, source_target_pairs={{0,224},{16,240},{32,0},{48,16},{64,32},{80,48},{96,64},{112,80},{... | collective-permute-start | bytes 1572872 | tf_op jit(solution)/shard_map/ppermute | solution.py:259
  40.8 24.4 %collective-permute-start.8 = (bf16[256,1024]{1,0:T(8,128)(2,1)S(1)}, bf16[256,1024]{1,0:T(8,128)(2,1)S(1)}, u32[]{:S(2)}, u32[]{:S(2)}) collective-permute-start(bf16[256,1024]{1,0:T(8,128)(2,1)S(1)} %collective-permute-done.2.refs_3_), channel_id=1, source_target_pairs={{0,32},{16,48},{32,64},{48,80},{64,96},{80,112},{96,128},{112,144}... | collective-permute-start | bytes 1572872 | tf_op jit(solution)/shard_map/ppermute | solution.py:259
  40.8 24.4 %collective-permute-start.9 = (bf16[256,1024]{1,0:T(8,128)(2,1)}, bf16[256,1024]{1,0:T(8,128)(2,1)}, u32[]{:S(2)}, u32[]{:S(2)}) collective-permute-start(bf16[256,1024]{1,0:T(8,128)(2,1)} %collective-permute-done.3.refs_9_), channel_id=1, source_target_pairs={{0,224},{16,240},{32,0},{48,16},{64,32},{80,48},{96,64},{112,80},{... | collective-permute-start | bytes 1572872 | tf_op jit(solution)/shard_map/ppermute | solution.py:259
  52.1 22.8 %collective-permute-start.14 = (bf16[256,1024]{1,0:T(8,128)(2,1)}, bf16[256,1024]{1,0:T(8,128)(2,1)}, u32[]{:S(2)}, u32[]{:S(2)}) collective-permute-start(bf16[256,1024]{1,0:T(8,128)(2,1)} %collective-permute-done.7.refs_4_), channel_id=1, source_target_pairs={{0,224},{16,240},{32,0},{48,16},{64,32},{80,48},{96,64},{112,80},{... | collective-permute-start | bytes 1572872 | tf_op jit(solution)/shard_map/ppermute | solution.py:259
  54.4 20.4 %collective-permute-start.15 = (bf16[256,1024]{1,0:T(8,128)(2,1)}, bf16[256,1024]{1,0:T(8,128)(2,1)}, u32[]{:S(2)}, u32[]{:S(2)}) collective-permute-start(bf16[256,1024]{1,0:T(8,128)(2,1)} %collective-permute-done.6.refs_8_), channel_id=1, source_target_pairs={{0,32},{16,48},{32,64},{48,80},{64,96},{80,112},{96,128},{112,144}... | collective-permute-start | bytes 1572872 | tf_op jit(solution)/shard_map/ppermute | solution.py:259
  54.4 13.9 %collective-permute-start.13 = (bf16[384,3072]{1,0:T(8,128)(2,1)}, bf16[384,3072]{1,0:T(8,128)(2,1)}, u32[]{:S(2)}, u32[]{:S(2)}) collective-permute-start(bf16[384,3072]{1,0:T(8,128)(2,1)} %bitcast.3.own_ref), channel_id=1, source_target_pairs={{0,16},{16,0},{32,48},{48,32},{64,80},{80,64},{96,112},{112,96},{1... | collective-permute-start | bytes 7077896 | tf_op jit(solution)/shard_map/ppermute | solution.py:280
  65.3 20.4 %collective-permute-start.10 = (bf16[256,1024]{1,0:T(8,128)(2,1)S(1)}, bf16[256,1024]{1,0:T(8,128)(2,1)S(1)}, u32[]{:S(2)}, u32[]{:S(2)}) collective-permute-start(bf16[256,1024]{1,0:T(8,128)(2,1)S(1)} %collective-permute-done.8.refs_0_), channel_id=1, source_target_pairs={{0,32},{16,48},{32,64},{48,80},{64,96},{80,112},{96,128},{112,144}... | collective-permute-start | bytes 1572872 | tf_op jit(solution)/shard_map/ppermute | solution.py:259
  65.4 21.5 %collective-permute-start.12 = (bf16[256,1024]{1,0:T(8,128)(2,1)}, bf16[256,1024]{1,0:T(8,128)(2,1)S(1)}, u32[]{:S(2)}, u32[]{:S(2)}) collective-permute-start(bf16[256,1024]{1,0:T(8,128)(2,1)} %collective-permute-done.9.refs_3_), channel_id=1, source_target_pairs={{0,224},{16,240},{32,0},{48,16},{64,32},{80,48},{96,64},{112,80},{... | collective-permute-start | bytes 1572872 | tf_op jit(solution)/shard_map/ppermute | solution.py:259
  79.9 9.3 %collective-permute-start.17 = (bf16[384,1024]{1,0:T(8,128)(2,1)S(1)}, bf16[384,1024]{1,0:T(8,128)(2,1)S(1)}, u32[]{:S(2)}, u32[]{:S(2)}) collective-permute-start(bf16[384,1024]{1,0:T(8,128)(2,1)S(1)} %get-tuple-element.62), channel_id=1, source_target_pairs={{0,16},{16,0},{32,48},{48,32},{64,80},{80,64},{96,112},{112,96},{1... | collective-permute-start | bytes 2359304 | tf_op jit(solution)/shard_map/ppermute | solution.py:259
  85.7 2.8 %collective-permute-start.11 = (bf16[256,1024]{1,0:T(8,128)(2,1)S(1)}, bf16[256,1024]{1,0:T(8,128)(2,1)S(1)}, u32[]{:S(2)}, u32[]{:S(2)}) collective-permute-start(bf16[256,1024]{1,0:T(8,128)(2,1)S(1)} %collective-permute-done.10.up_ref), channel_id=1, source_target_pairs={{0,16},{16,0},{32,48},{48,32},{64,80},{80,64},{96,112},{112,96},{1... | collective-permute-start | bytes 1572872 | tf_op jit(solution)/shard_map/ppermute | solution.py:259
  86.9 2.3 %collective-permute-start.16 = (bf16[256,1024]{1,0:T(8,128)(2,1)S(1)}, bf16[256,1024]{1,0:T(8,128)(2,1)S(1)}, u32[]{:S(2)}, u32[]{:S(2)}) collective-permute-start(bf16[256,1024]{1,0:T(8,128)(2,1)S(1)} %collective-permute-done.12.down_ref), channel_id=1, source_target_pairs={{0,16},{16,0},{32,48},{48,32},{64,80},{80,64},{96,112},{112,96},{1... | collective-permute-start | bytes 1572872 | tf_op jit(solution)/shard_map/ppermute | solution.py:259

commit v12 on v8

--- a/solution.py
+++ b/solution.py
@@ -172,7 +172,7 @@
     inside = [pltpu.with_memory_space_constraint(x, pltpu.VMEM) for x in (*rows, *acc)]
     return pl.pallas_call(
         functools.partial(next_kernel, n_w),
-        out_shape=tuple(jax.ShapeDtypeStruct(x.shape, kind) for x, kind in zip(acc, (f32, bf16))),
+        out_shape=tuple(jax.ShapeDtypeStruct(x.shape, kind) for x, kind in zip(acc, (f32, f32))),
         in_specs=[VMEM] * 2 + [ANY] * (2 * n_w) + [VMEM] * 2 + [ANY],
         out_specs=(VMEM,) * 2,
         scratch_shapes=[

time: 112 us -> 122 us (1.089)
  waiting for transfers between devices: 29 us -> 39.8 us
    ppermute x17, waiting for transfers between devices: 29 us -> 39.8 us  [send_on(): return lax.ppermute(x, 'dp', way)]
  transfers between devices with their start and end apart: 19 -> 19, of which waited for: 6 -> 8; matrix products, arithmetic and copies ran while one was open for 0% -> 0% of each run, Pallas kernels for 22% -> 16%
where the time goes in v12:
time: 122 us
  waiting for transfers between devices  39.8 us (33%)
  starting transfers between devices  34.4 us (28%)
  Pallas kernels  25.6 us (21%)
  blocking collectives  20.4 us (17%)
    ppermute x17, waiting for transfers between devices, send_on(): return lax.ppermute(x, 'dp', way)  39.8 us
    ppermute x17, starting transfers between devices, send_on(): return lax.ppermute(x, 'dp', way)  24.6 us
    all_to_all x1, blocking collectives, local(): lax.all_to_all(whole.reshape(experts, CAP, width), 'expert', 0, 0, tiled=...  20.4 us
    pallas_call x1, Pallas kernels, own_call(): pl.pallas_call(functools.partial(own_kernel, n_w), out_shape=(jax.ShapeDt...  7.81 us
    all_to_all x1, starting transfers between devices, local(): lax.all_to_all(send.reshape(experts, CAP, 3 * width), 'expert', 0, 0, til...  6.81 us
    pallas_call x1, Pallas kernels, other_call(): pl.pallas_call(other_kernel, out_shape=(jax.ShapeDtypeStruct((rows, width...  6.47 us
    pallas_call x1, Pallas kernels, next_call(): pl.pallas_call(functools.partial(next_kernel, n_w), out_shape=tuple((jax....  5.02 us
    pallas_call x1, Pallas kernels, prepare(): pl.pallas_call(prepare_kernel, out_shape=(jax.ShapeDtypeStruct((slots, 3...  3.13 us
  transfers between devices with their start and end apart: 19, of which 8 were waited for; matrix products, arithmetic and copies ran while one was open for 0% of the time, Pallas kernels for 16%

profile of v12, /device:TPU:1, one launch (start us, length us, event | category | flops | bytes accessed | tf_op | source)
XLA Modules:
  0.0 121.5 jit_solution(15685832842626989352)
XLA Ops:
  0.0 2.5 %collective-permute-start = (bf16[256,1024]{1,0:T(8,128)(2,1)}, bf16[256,1024]{1,0:T(8,128)(2,1)S(1)}, u32[]{:S(2)}, u32[]{:S(2)}) collective-permute-start(bf16[256,1024]{1,0:T(8,128)(2,1)} %bitcast.11), channel_id=1, source_target_pairs={{0,32},{16,48},{32,64},{48,80},{64,96},{80,112},{96,128},{112,144}... | collective-permute-start | bytes 1572872 | tf_op jit(solution)/shard_map/ppermute | solution.py:242
  2.5 3.9 %collective-permute-start.1 = (bf16[256,1024]{1,0:T(8,128)(2,1)}, bf16[256,1024]{1,0:T(8,128)(2,1)}, u32[]{:S(2)}, u32[]{:S(2)}) collective-permute-start(bf16[256,1024]{1,0:T(8,128)(2,1)} %bitcast.14), channel_id=1, source_target_pairs={{0,224},{16,240},{32,0},{48,16},{64,32},{80,48},{96,64},{112,80},{... | collective-permute-start | bytes 1572872 | tf_op jit(solution)/shard_map/ppermute | solution.py:242
  6.4 0.0 collective-permute-start.4
  6.4 2.7 %collective-permute-start.5 = (bf16[256,1024]{1,0:T(8,128)(2,1)}, bf16[256,1024]{1,0:T(8,128)(2,1)}, u32[]{:S(2)}, u32[]{:S(2)}) collective-permute-start(bf16[256,1024]{1,0:T(8,128)(2,1)} %bitcast.12), channel_id=1, source_target_pairs={{0,224},{16,240},{32,0},{48,16},{64,32},{80,48},{96,64},{112,80},{... | collective-permute-start | bytes 1572872 | tf_op jit(solution)/shard_map/ppermute | solution.py:242
  9.1 3.1 %shard_map.73 = (bf16[384,3072]{1,0:T(8,128)(2,1)}, bf16[384,128]{1,0:T(8,128)(2,1)S(1)}) custom-call(s32[2,128]{1,0:T(2,128)} %bitcast.18, s32[2,128]{1,0:T(2,128)} %bitcast.19, bf16[128,1024]{1,0:T(8,128)(2,1)} %x_hbm.1, bf16[128,1024]{1,0:T(8,128)(2,1)} %t_hbm.1, bf16[128,1024]{1,0:T(8,128)(2,1)} %c_hbm.1), custom_call_target="tpu_custom_call" | custom-call | tf_op jit(solution)/shard_map/pallas_call | solution.py:61
  12.2 6.8 %all-to-all-start = ((bf16[16,24,3072]{2,1,0:T(8,128)(2,1)}), bf16[16,24,3072]{2,1,0:T(8,128)(2,1)}, u32[]{:S(2)}, u32[]{:S(2)}) async-start(bf16[16,24,3072]{2,1,0:T(8,128)(2,1)} %bitcast.2), calls=%async_computation | async-start | bytes 4718592 | tf_op jit(solution)/shard_map/all_to_all | solution.py:248
  19.0 0.0 collective-permute-done.refs_0_.refs_1_
  19.1 0.0 copy-start
  19.1 0.0 copy-start.1
  19.1 0.0 collective-permute-done.1.refs_7_
  19.1 0.1 collective-permute-start.2
  19.2 2.7 %collective-permute-start.3 = (bf16[256,1024]{1,0:T(8,128)(2,1)}, bf16[256,1024]{1,0:T(8,128)(2,1)}, u32[]{:S(2)}, u32[]{:S(2)}) collective-permute-start(bf16[256,1024]{1,0:T(8,128)(2,1)} %collective-permute-done.1.refs_7_), channel_id=1, source_target_pairs={{0,224},{16,240},{32,0},{48,16},{64,32},{80,48},{96,64},{112,80},{... | collective-permute-start | bytes 1572872 | tf_op jit(solution)/shard_map/ppermute | solution.py:242
  21.9 7.8 %collective-permute-done.4.refs_6_ = bf16[256,1024]{1,0:T(8,128)(2,1)} collective-permute-done((bf16[256,1024]{1,0:T(8,128)(2,1)}, bf16[256,1024]{1,0:T(8,128)(2,1)}, u32[]{:S(2)}, u32[]{:S(2)}) %collective-permute-start.4) | collective-permute-done | bytes 524320 | tf_op jit(solution)/shard_map/ppermute | solution.py:242
  29.6 0.0 collective-permute-done.5.refs_2_
  29.6 0.0 collective-permute-start.6
  29.6 2.7 %collective-permute-start.7 = (bf16[256,1024]{1,0:T(8,128)(2,1)}, bf16[256,1024]{1,0:T(8,128)(2,1)}, u32[]{:S(2)}, u32[]{:S(2)}) collective-permute-start(bf16[256,1024]{1,0:T(8,128)(2,1)} %collective-permute-done.5.refs_2_), channel_id=1, source_target_pairs={{0,224},{16,240},{32,0},{48,16},{64,32},{80,48},{96,64},{112,80},{... | collective-permute-start | bytes 1572872 | tf_op jit(solution)/shard_map/ppermute | solution.py:242
  32.3 8.6 %collective-permute-done.2.refs_3_ = bf16[256,1024]{1,0:T(8,128)(2,1)S(1)} collective-permute-done((bf16[256,1024]{1,0:T(8,128)(2,1)S(1)}, bf16[256,1024]{1,0:T(8,128)(2,1)S(1)}, u32[]{:S(2)}, u32[]{:S(2)}) %collective-permute-start.2) | collective-permute-done | bytes 524320 | tf_op jit(solution)/shard_map/ppermute | solution.py:242
  40.8 0.0 collective-permute-done.3.refs_9_
  40.8 0.0 collective-permute-start.8
  40.8 2.7 %collective-permute-start.9 = (bf16[256,1024]{1,0:T(8,128)(2,1)}, bf16[256,1024]{1,0:T(8,128)(2,1)}, u32[]{:S(2)}, u32[]{:S(2)}) collective-permute-start(bf16[256,1024]{1,0:T(8,128)(2,1)} %collective-permute-done.3.refs_9_), channel_id=1, source_target_pairs={{0,224},{16,240},{32,0},{48,16},{64,32},{80,48},{96,64},{112,80},{... | collective-permute-start | bytes 1572872 | tf_op jit(solution)/shard_map/ppermute | solution.py:242
  43.5 8.6 %collective-permute-done.6.refs_8_ = bf16[256,1024]{1,0:T(8,128)(2,1)} collective-permute-done((bf16[256,1024]{1,0:T(8,128)(2,1)}, bf16[256,1024]{1,0:T(8,128)(2,1)}, u32[]{:S(2)}, u32[]{:S(2)}) %collective-permute-start.6) | collective-permute-done | bytes 524320 | tf_op jit(solution)/shard_map/ppermute | solution.py:242
  52.1 0.0 collective-permute-done.7.refs_4_
  52.1 2.4 %collective-permute-start.14 = (bf16[256,1024]{1,0:T(8,128)(2,1)}, bf16[256,1024]{1,0:T(8,128)(2,1)}, u32[]{:S(2)}, u32[]{:S(2)}) collective-permute-start(bf16[256,1024]{1,0:T(8,128)(2,1)} %collective-permute-done.7.refs_4_), channel_id=1, source_target_pairs={{0,224},{16,240},{32,0},{48,16},{64,32},{80,48},{96,64},{112,80},{... | collective-permute-start | bytes 1572872 | tf_op jit(solution)/shard_map/ppermute | solution.py:242
  54.4 0.0 collective-permute-start.15
  54.4 0.0 all-to-all-done
  54.4 3.0 %collective-permute-start.13 = (bf16[384,3072]{1,0:T(8,128)(2,1)}, bf16[384,3072]{1,0:T(8,128)(2,1)}, u32[]{:S(2)}, u32[]{:S(2)}) collective-permute-start(bf16[384,3072]{1,0:T(8,128)(2,1)} %bitcast.3.own_ref), channel_id=1, source_target_pairs={{0,16},{16,0},{32,48},{48,32},{64,80},{80,64},{96,112},{112,96},{1... | collective-permute-start | bytes 7077896 | tf_op jit(solution)/shard_map/ppermute | solution.py:263
  57.4 7.8 %shard_map.75 = (f32[384,1024]{1,0:T(8,128)S(1)}, bf16[384,3072]{1,0:T(8,128)(2,1)S(1)}, bf16[5,256,1024]{2,1,0:T(8,128)(2,1)S(1)}, bf16[5,256,1024]{2,1,0:T(8,128)(2,1)S(1)}) custom-call(bf16[384,3072]{1,0:T(8,128)(2,1)} %bitcast.3.own_ref, bf16[256,1024]{1,0:T(8,128)(2,1)S(1)} %bitcast.13, bf16[256,1024]{1,0:T(8,128)(2,1)S(1)} %collective-permute-done.refs_0_.refs_1_, ...), custom_call_target="tpu_custom_call" | custom-call | tf_op jit(solution)/shard_map/pallas_call | solution.py:122
  65.2 0.0 collective-permute-done.8.refs_0_
  65.3 0.0 collective-permute-done.9.refs_3_
  65.3 0.0 collective-permute-done.13.other_ref
  65.3 6.5 %shard_map.77 = (f32[384,1024]{1,0:T(8,128)S(1)}, bf16[384,3072]{1,0:T(8,128)(2,1)S(1)}) custom-call(bf16[384,3072]{1,0:T(8,128)(2,1)} %collective-permute-done.13.other_ref, bf16[5,256,1024]{2,1,0:T(8,128)(2,1)S(1)} %get-tuple-element.53.up_ref, bf16[5,256,1024]{2,1,0:T(8,128)(2,1)S(1)} %get-tuple-element.54.down_ref), custom_call_target="tpu_custom_call" | custom-call | tf_op jit(solution)/shard_map/pallas_call | solution.py:143
  71.8 1.7 %collective-permute-done.14.refs_1_ = bf16[256,1024]{1,0:T(8,128)(2,1)} collective-permute-done((bf16[256,1024]{1,0:T(8,128)(2,1)}, bf16[256,1024]{1,0:T(8,128)(2,1)}, u32[]{:S(2)}, u32[]{:S(2)}) %collective-permute-start.14) | collective-permute-done | bytes 524320 | tf_op jit(solution)/shard_map/ppermute | solution.py:242
  73.5 1.1 collective-permute-done.15.refs_2_
  74.5 5.0 %shard_map.78 = (f32[384,1024]{1,0:T(8,128)S(1)}, f32[384,1024]{1,0:T(8,128)S(1)}) custom-call(bf16[384,3072]{1,0:T(8,128)(2,1)S(1)} %get-tuple-element.50.refs_1_.own_ref.rows_ref, bf16[384,3072]{1,0:T(8,128)(2,1)S(1)} %get-tuple-element.55.other_ref, bf16[256,1024]{1,0:T(8,128)(2,1)S(1)} %collective-permute-done.8.refs_0_, ...), custom_call_target="tpu_custom_call" | custom-call | tf_op jit(solution)/shard_map/pallas_call | solution.py:173
  79.6 1.5 %collective-permute-start.17 = (f32[384,1024]{1,0:T(8,128)S(1)}, f32[384,1024]{1,0:T(8,128)S(1)}, u32[]{:S(2)}, u32[]{:S(2)}) collective-permute-start(f32[384,1024]{1,0:T(8,128)S(1)} %get-tuple-element.62), channel_id=1, source_target_pairs={{0,16},{16,0},{32,48},{48,32},{64,80},{80,64},{96,112},{112,96},{1... | collective-permute-start | bytes 4718600 | tf_op jit(solution)/shard_map/ppermute | solution.py:242
  81.1 0.0 collective-permute-start.10
  81.1 2.7 %collective-permute-start.12 = (bf16[256,1024]{1,0:T(8,128)(2,1)}, bf16[256,1024]{1,0:T(8,128)(2,1)S(1)}, u32[]{:S(2)}, u32[]{:S(2)}) collective-permute-start(bf16[256,1024]{1,0:T(8,128)(2,1)} %collective-permute-done.9.refs_3_), channel_id=1, source_target_pairs={{0,224},{16,240},{32,0},{48,16},{64,32},{80,48},{96,64},{112,80},{... | collective-permute-start | bytes 1572872 | tf_op jit(solution)/shard_map/ppermute | solution.py:242
  83.8 12.0 %collective-permute-done.10.up_ref = bf16[256,1024]{1,0:T(8,128)(2,1)S(1)} collective-permute-done((bf16[256,1024]{1,0:T(8,128)(2,1)S(1)}, bf16[256,1024]{1,0:T(8,128)(2,1)S(1)}, u32[]{:S(2)}, u32[]{:S(2)}) %collective-permute-start.10) | collective-permute-done | bytes 524320 | tf_op jit(solution)/shard_map/ppermute | solution.py:242
  95.8 0.9 collective-permute-start.11
  96.7 0.0 collective-permute-start.16
  96.7 1.4 %shard_map.79.acc_ref = f32[384,1024]{1,0:T(8,128)S(1)} custom-call(bf16[384,3072]{1,0:T(8,128)(2,1)S(1)} %get-tuple-element.50.refs_1_.own_ref.rows_ref, bf16[256,1024]{1,0:T(8,128)(2,1)S(1)} %collective-permute-done.10.up_ref, bf16[256,1024]{1,0:T(8,128)(2,1)S(1)} %collective-permute-done.12.down_ref, f32[384,1024]{1,0:T(8,128)S(1)} %get-tuple-element.59.acc_ref), custom_call_target="tpu_custom_call" | custom-call | tf_op jit(solution)/shard_map/pallas_call | solution.py:208
  98.1 0.1 collective-permute-done.11.up_ref
  98.2 0.6 shard_map.80.factor_ref
  98.9 0.1 collective-permute-done.16.down_ref
  99.0 0.0 collective-permute-done.17.passed_ref
  99.0 1.0 shard_map.81
  100.0 20.4 %all_to_all.10 = bf16[16,24,1024]{2,1,0:T(8,128)(2,1)S(1)} all-to-all(bf16[16,24,1024]{2,1,0:T(8,128)(2,1)S(1)} %bitcast.10), channel_id=1, replica_groups=mesh['dp'=16,'expert'=16] {'expert'}, dimensions={0} | all-to-all | bytes 1572864 | tf_op jit(solution)/shard_map/all_to_all | solution.py:272
  120.4 1.1 fusion
  (5 shorter events, 0.0 us)
Async XLA Ops:
  0.0 19.0 %collective-permute-start = (bf16[256,1024]{1,0:T(8,128)(2,1)}, bf16[256,1024]{1,0:T(8,128)(2,1)S(1)}, u32[]{:S(2)}, u32[]{:S(2)}) collective-permute-start(bf16[256,1024]{1,0:T(8,128)(2,1)} %bitcast.11), channel_id=1, source_target_pairs={{0,32},{16,48},{32,64},{48,80},{64,96},{80,112},{96,128},{112,144}... | collective-permute-start | bytes 1572872 | tf_op jit(solution)/shard_map/ppermute | solution.py:242
  2.5 16.6 %collective-permute-start.1 = (bf16[256,1024]{1,0:T(8,128)(2,1)}, bf16[256,1024]{1,0:T(8,128)(2,1)}, u32[]{:S(2)}, u32[]{:S(2)}) collective-permute-start(bf16[256,1024]{1,0:T(8,128)(2,1)} %bitcast.14), channel_id=1, source_target_pairs={{0,224},{16,240},{32,0},{48,16},{64,32},{80,48},{96,64},{112,80},{... | collective-permute-start | bytes 1572872 | tf_op jit(solution)/shard_map/ppermute | solution.py:242
  6.4 23.2 %collective-permute-start.4 = (bf16[256,1024]{1,0:T(8,128)(2,1)}, bf16[256,1024]{1,0:T(8,128)(2,1)}, u32[]{:S(2)}, u32[]{:S(2)}) collective-permute-start(bf16[256,1024]{1,0:T(8,128)(2,1)} %bitcast.15), channel_id=1, source_target_pairs={{0,32},{16,48},{32,64},{48,80},{64,96},{80,112},{96,128},{112,144}... | collective-permute-start | bytes 1572872 | tf_op jit(solution)/shard_map/ppermute | solution.py:242
  6.4 23.2 %collective-permute-start.5 = (bf16[256,1024]{1,0:T(8,128)(2,1)}, bf16[256,1024]{1,0:T(8,128)(2,1)}, u32[]{:S(2)}, u32[]{:S(2)}) collective-permute-start(bf16[256,1024]{1,0:T(8,128)(2,1)} %bitcast.12), channel_id=1, source_target_pairs={{0,224},{16,240},{32,0},{48,16},{64,32},{80,48},{96,64},{112,80},{... | collective-permute-start | bytes 1572872 | tf_op jit(solution)/shard_map/ppermute | solution.py:242
  12.2 42.2 %all-to-all-start = ((bf16[16,24,3072]{2,1,0:T(8,128)(2,1)}), bf16[16,24,3072]{2,1,0:T(8,128)(2,1)}, u32[]{:S(2)}, u32[]{:S(2)}) async-start(bf16[16,24,3072]{2,1,0:T(8,128)(2,1)} %bitcast.2), calls=%async_computation | async-start | bytes 4718592 | tf_op jit(solution)/shard_map/all_to_all | solution.py:248
  19.1 38.4 %copy-start = (bf16[1,256,1024]{2,1,0:T(8,128)(2,1)S(1)}, bf16[1,256,1024]{2,1,0:T(8,128)(2,1)}, u32[]{:S(2)}) copy-start(bf16[1,256,1024]{2,1,0:T(8,128)(2,1)} %param.12) | copy-start | bytes 1572868
  19.1 38.4 %copy-start.1 = (bf16[1,256,1024]{2,1,0:T(8,128)(2,1)S(1)}, bf16[1,256,1024]{2,1,0:T(8,128)(2,1)}, u32[]{:S(2)}) copy-start(bf16[1,256,1024]{2,1,0:T(8,128)(2,1)} %param.13) | copy-start | bytes 1572868
  19.1 21.7 %collective-permute-start.2 = (bf16[256,1024]{1,0:T(8,128)(2,1)S(1)}, bf16[256,1024]{1,0:T(8,128)(2,1)S(1)}, u32[]{:S(2)}, u32[]{:S(2)}) collective-permute-start(bf16[256,1024]{1,0:T(8,128)(2,1)S(1)} %collective-permute-done.refs_0_.refs_1_), channel_id=1, source_target_pairs={{0,32},{16,48},{32,64},{48,80},{64,96},{80,112},{96,128},{112,144}... | collective-permute-start | bytes 1572872 | tf_op jit(solution)/shard_map/ppermute | solution.py:242
  19.2 21.7 %collective-permute-start.3 = (bf16[256,1024]{1,0:T(8,128)(2,1)}, bf16[256,1024]{1,0:T(8,128)(2,1)}, u32[]{:S(2)}, u32[]{:S(2)}) collective-permute-start(bf16[256,1024]{1,0:T(8,128)(2,1)} %collective-permute-done.1.refs_7_), channel_id=1, source_target_pairs={{0,224},{16,240},{32,0},{48,16},{64,32},{80,48},{96,64},{112,80},{... | collective-permute-start | bytes 1572872 | tf_op jit(solution)/shard_map/ppermute | solution.py:242
  29.6 22.5 %collective-permute-start.6 = (bf16[256,1024]{1,0:T(8,128)(2,1)}, bf16[256,1024]{1,0:T(8,128)(2,1)}, u32[]{:S(2)}, u32[]{:S(2)}) collective-permute-start(bf16[256,1024]{1,0:T(8,128)(2,1)} %collective-permute-done.4.refs_6_), channel_id=1, source_target_pairs={{0,32},{16,48},{32,64},{48,80},{64,96},{80,112},{96,128},{112,144}... | collective-permute-start | bytes 1572872 | tf_op jit(solution)/shard_map/ppermute | solution.py:242
  29.6 22.5 %collective-permute-start.7 = (bf16[256,1024]{1,0:T(8,128)(2,1)}, bf16[256,1024]{1,0:T(8,128)(2,1)}, u32[]{:S(2)}, u32[]{:S(2)}) collective-permute-start(bf16[256,1024]{1,0:T(8,128)(2,1)} %collective-permute-done.5.refs_2_), channel_id=1, source_target_pairs={{0,224},{16,240},{32,0},{48,16},{64,32},{80,48},{96,64},{112,80},{... | collective-permute-start | bytes 1572872 | tf_op jit(solution)/shard_map/ppermute | solution.py:242
  40.8 24.4 %collective-permute-start.8 = (bf16[256,1024]{1,0:T(8,128)(2,1)S(1)}, bf16[256,1024]{1,0:T(8,128)(2,1)S(1)}, u32[]{:S(2)}, u32[]{:S(2)}) collective-permute-start(bf16[256,1024]{1,0:T(8,128)(2,1)S(1)} %collective-permute-done.2.refs_3_), channel_id=1, source_target_pairs={{0,32},{16,48},{32,64},{48,80},{64,96},{80,112},{96,128},{112,144}... | collective-permute-start | bytes 1572872 | tf_op jit(solution)/shard_map/ppermute | solution.py:242
  40.8 24.4 %collective-permute-start.9 = (bf16[256,1024]{1,0:T(8,128)(2,1)}, bf16[256,1024]{1,0:T(8,128)(2,1)}, u32[]{:S(2)}, u32[]{:S(2)}) collective-permute-start(bf16[256,1024]{1,0:T(8,128)(2,1)} %collective-permute-done.3.refs_9_), channel_id=1, source_target_pairs={{0,224},{16,240},{32,0},{48,16},{64,32},{80,48},{96,64},{112,80},{... | collective-permute-start | bytes 1572872 | tf_op jit(solution)/shard_map/ppermute | solution.py:242
  52.1 21.4 %collective-permute-start.14 = (bf16[256,1024]{1,0:T(8,128)(2,1)}, bf16[256,1024]{1,0:T(8,128)(2,1)}, u32[]{:S(2)}, u32[]{:S(2)}) collective-permute-start(bf16[256,1024]{1,0:T(8,128)(2,1)} %collective-permute-done.7.refs_4_), channel_id=1, source_target_pairs={{0,224},{16,240},{32,0},{48,16},{64,32},{80,48},{96,64},{112,80},{... | collective-permute-start | bytes 1572872 | tf_op jit(solution)/shard_map/ppermute | solution.py:242
  54.4 20.1 %collective-permute-start.15 = (bf16[256,1024]{1,0:T(8,128)(2,1)}, bf16[256,1024]{1,0:T(8,128)(2,1)}, u32[]{:S(2)}, u32[]{:S(2)}) collective-permute-start(bf16[256,1024]{1,0:T(8,128)(2,1)} %collective-permute-done.6.refs_8_), channel_id=1, source_target_pairs={{0,32},{16,48},{32,64},{48,80},{64,96},{80,112},{96,128},{112,144}... | collective-permute-start | bytes 1572872 | tf_op jit(solution)/shard_map/ppermute | solution.py:242
  54.4 10.8 %collective-permute-start.13 = (bf16[384,3072]{1,0:T(8,128)(2,1)}, bf16[384,3072]{1,0:T(8,128)(2,1)}, u32[]{:S(2)}, u32[]{:S(2)}) collective-permute-start(bf16[384,3072]{1,0:T(8,128)(2,1)} %bitcast.3.own_ref), channel_id=1, source_target_pairs={{0,16},{16,0},{32,48},{48,32},{64,80},{80,64},{96,112},{112,96},{1... | collective-permute-start | bytes 7077896 | tf_op jit(solution)/shard_map/ppermute | solution.py:263
  79.6 19.4 %collective-permute-start.17 = (f32[384,1024]{1,0:T(8,128)S(1)}, f32[384,1024]{1,0:T(8,128)S(1)}, u32[]{:S(2)}, u32[]{:S(2)}) collective-permute-start(f32[384,1024]{1,0:T(8,128)S(1)} %get-tuple-element.62), channel_id=1, source_target_pairs={{0,16},{16,0},{32,48},{48,32},{64,80},{80,64},{96,112},{112,96},{1... | collective-permute-start | bytes 4718600 | tf_op jit(solution)/shard_map/ppermute | solution.py:242
  81.1 14.7 %collective-permute-start.10 = (bf16[256,1024]{1,0:T(8,128)(2,1)S(1)}, bf16[256,1024]{1,0:T(8,128)(2,1)S(1)}, u32[]{:S(2)}, u32[]{:S(2)}) collective-permute-start(bf16[256,1024]{1,0:T(8,128)(2,1)S(1)} %collective-permute-done.8.refs_0_), channel_id=1, source_target_pairs={{0,32},{16,48},{32,64},{48,80},{64,96},{80,112},{96,128},{112,144}... | collective-permute-start | bytes 1572872 | tf_op jit(solution)/shard_map/ppermute | solution.py:242
  81.1 15.6 %collective-permute-start.12 = (bf16[256,1024]{1,0:T(8,128)(2,1)}, bf16[256,1024]{1,0:T(8,128)(2,1)S(1)}, u32[]{:S(2)}, u32[]{:S(2)}) collective-permute-start(bf16[256,1024]{1,0:T(8,128)(2,1)} %collective-permute-done.9.refs_3_), channel_id=1, source_target_pairs={{0,224},{16,240},{32,0},{48,16},{64,32},{80,48},{96,64},{112,80},{... | collective-permute-start | bytes 1572872 | tf_op jit(solution)/shard_map/ppermute | solution.py:242
  95.8 2.4 %collective-permute-start.11 = (bf16[256,1024]{1,0:T(8,128)(2,1)S(1)}, bf16[256,1024]{1,0:T(8,128)(2,1)S(1)}, u32[]{:S(2)}, u32[]{:S(2)}) collective-permute-start(bf16[256,1024]{1,0:T(8,128)(2,1)S(1)} %collective-permute-done.10.up_ref), channel_id=1, source_target_pairs={{0,16},{16,0},{32,48},{48,32},{64,80},{80,64},{96,112},{112,96},{1... | collective-permute-start | bytes 1572872 | tf_op jit(solution)/shard_map/ppermute | solution.py:242
  96.7 2.3 %collective-permute-start.16 = (bf16[256,1024]{1,0:T(8,128)(2,1)S(1)}, bf16[256,1024]{1,0:T(8,128)(2,1)S(1)}, u32[]{:S(2)}, u32[]{:S(2)}) collective-permute-start(bf16[256,1024]{1,0:T(8,128)(2,1)S(1)} %collective-permute-done.12.down_ref), channel_id=1, source_target_pairs={{0,16},{16,0},{32,48},{48,32},{64,80},{80,64},{96,112},{112,96},{1... | collective-permute-start | bytes 1572872 | tf_op jit(solution)/shard_map/ppermute | solution.py:242
